TPU v7x, 32 devices: a whole 2x2x4 slice. The times are simulated.
32 devices in a mesh: dp: 8 (over z, core), tensor: 4 (over y, x).
Axes of the slice: x: 2, y: 2, z: 4, core: 2. Of those that a mesh axis runs over, the one named last changes fastest.
Arguments:
- hidden_in: bfloat16 [1920, 4, 5120], P('dp', None, 'tensor'), may hold values from -6 to 6
- kv_weight: bfloat16 [2, 5120, 1024], P(None, 'tensor'), may hold values from -0.078125 to 0.078125
- factor_a: float32 [2, 64, 5120], P(None, None, 'tensor'), may hold values from -0.078125 to 0.078125
- factor_b: float32 [2, 64, 1024], P(None, None, 'tensor'), may hold values from -0.75 to 0.75
- grad_a: float32 [8, 2, 64, 5120], P('dp', None, None, 'tensor'), may hold values from -6 to 6
- grad_b: float32 [8, 2, 64, 1024], P('dp', None, None, 'tensor'), may hold values from -6 to 6
- key_gain: float32 [128], replicated, may hold values from 0.1 to 1.9
- queries: bfloat16 [1920, 4, 4096], P(('dp', 'tensor')), may hold values from -27 to 27
- cache_keys: bfloat16 [1920, 16, 1024], P(('dp', 'tensor')), may hold values from -6 to 6
- cache_values: bfloat16 [1920, 16, 1024], P(('dp', 'tensor')), may hold values from -6 to 6
- cache_lengths: int32 [1920], P(('dp', 'tensor')), may hold values from 2 to 12, as said below
- positions: int32 [1920], P(('dp', 'tensor')), may hold values from 0 to 32767
Outputs:
- attended: bfloat16 [1920, 4, 4096], P(('dp', 'tensor'))
- new_a: float32 [2, 64, 5120], P(None, None, 'tensor')
- new_b: float32 [2, 64, 1024], P(None, None, 'tensor')
Inputs may be any that keep to these rules, and one draw needn't show every extreme that they name: `cache_lengths`: some row holds 12 filled slots.
All inputs are finite; a program needn't handle non-finite values.
Results may differ from a plain program's by a relative error of at most 0.035.
Values may be sent and summed in bfloat16 or wider, within the bound.
No kernel may reach another device: no remote copies, remote signals or barrier semaphores. Data moves between devices by JAX's collectives and lax.ppermute only.
A program may use at most 64 MiB of HBM per device.

v0:
```python
import math

import jax
import jax.numpy as jnp
from jax import lax
from jax.sharding import PartitionSpec as P

D = 5120
KVH = 8
HD = 128
QH = 32
R = 64
STEPS = 4


def normed_rotated(keys, gain, position):
    scale = lax.rsqrt(jnp.mean(keys * keys, axis=-1, keepdims=True) + 1e-06)
    keys = keys * scale * gain
    half = keys.shape[-1] // 2
    freq = jnp.exp(
        -math.log(1000000.0) * (jnp.arange(half, dtype=jnp.float32) * 2.0 / keys.shape[-1])
    )
    angle = position.astype(jnp.float32)[..., None] * freq
    cosine = jnp.concatenate([jnp.cos(angle), jnp.cos(angle)], axis=-1)[..., None, :]
    sine = jnp.concatenate([jnp.sin(angle), jnp.sin(angle)], axis=-1)[..., None, :]
    turned = jnp.concatenate([-keys[..., half:], keys[..., :half]], axis=-1)
    return keys * cosine + turned * sine


def attend(queries, cache_keys, cache_values, new_keys, new_values, lengths):
    rows, steps, width = queries.shape
    slots = cache_keys.shape[1]
    slot = jnp.arange(slots, dtype=jnp.int32)
    for step in range(steps):
        hit = (slot[None, :] == lengths[:, None] + step)[:, :, None]
        cache_keys = jnp.where(hit, new_keys[:, step][:, None, :], cache_keys)
        cache_values = jnp.where(hit, new_values[:, step][:, None, :], cache_values)
    groups = QH // KVH
    query_five = queries.reshape(rows, steps, KVH, groups, HD)
    key_four = cache_keys.reshape(rows, slots, KVH, HD)
    value_four = cache_values.reshape(rows, slots, KVH, HD)
    scores = jnp.einsum(
        "rtkgd,rckd->rtkgc", query_five, key_four, preferred_element_type=jnp.float32
    ) * HD ** (-0.5)
    limit = lengths[:, None] + jnp.arange(steps, dtype=jnp.int32)[None, :]
    valid = (slot[None, None, :] <= limit[:, :, None])[:, :, None, None, :]
    scores = jnp.where(valid, scores, jnp.float32(-1e30))
    top = jnp.max(scores, axis=-1, keepdims=True)
    expo = jnp.exp(scores - top)
    weights = (expo / jnp.sum(expo, axis=-1, keepdims=True)).astype(jnp.bfloat16)
    result = jnp.einsum(
        "rtkgc,rckd->rtkgd", weights, value_four, preferred_element_type=jnp.float32
    )
    return result.reshape(rows, steps, width).astype(jnp.bfloat16)


def per_device(
    hidden_in,
    kv_weight,
    factor_a,
    factor_b,
    grad_a,
    grad_b,
    key_gain,
    queries,
    cache_keys,
    cache_values,
    cache_lengths,
    positions,
):
    groups_dp = lax.axis_size("dp")
    rate_a = 2.0 / math.sqrt(groups_dp * D)
    rate_b = 2.0 / math.sqrt(groups_dp * R)
    sum_a, sum_b = (
        lax.psum(grad_a[0].astype(jnp.bfloat16), "dp").astype(jnp.float32),
        lax.psum(grad_b[0].astype(jnp.bfloat16), "dp").astype(jnp.float32),
    )
    new_a = factor_a - rate_a * sum_a
    new_b = factor_b - rate_b * sum_b
    full_b = lax.all_gather(new_b.astype(jnp.bfloat16), "tensor", axis=2, tiled=True).astype(
        new_b.dtype
    )
    delta = jnp.einsum("prd,prk->pdk", new_a, full_b, precision=lax.Precision.HIGHEST)
    merged = (kv_weight.astype(jnp.float32) + 0.25 * delta).astype(jnp.bfloat16)
    joined = jnp.concatenate([merged[0], merged[1]], axis=1)
    rows_here = hidden_in.shape[0] // lax.axis_size("tensor")
    pieces = []
    for step in range(STEPS):
        column = hidden_in[:, step, :]

        def step_term(start, count, column=column):
            return jnp.dot(column, joined, preferred_element_type=jnp.float32)

        pieces.append(
            lax.psum_scatter(
                step_term(jnp.int32(0), rows_here * lax.axis_size("tensor")).astype(jnp.bfloat16),
                "tensor",
                scatter_dimension=0,
                tiled=True,
            ).astype(jnp.float32)
        )
    projected = jnp.stack(pieces, axis=1)
    kv_width = KVH * HD
    place = positions[:, None] + jnp.arange(STEPS, dtype=jnp.int32)[None, :]
    keys = normed_rotated(
        projected[..., :kv_width].reshape(rows_here, STEPS, KVH, HD), key_gain, place
    )
    new_keys = keys.reshape(rows_here, STEPS, kv_width).astype(jnp.bfloat16)
    new_values = projected[..., kv_width:].astype(jnp.bfloat16)
    attended = attend(queries, cache_keys, cache_values, new_keys, new_values, cache_lengths)
    return (attended, new_a, new_b)


def solution(mesh):
    return jax.shard_map(
        per_device,
        mesh=mesh,
        in_specs=(
            P("dp", None, "tensor"),
            P(None, "tensor", None),
            P(None, None, "tensor"),
            P(None, None, "tensor"),
            P("dp", None, None, "tensor"),
            P("dp", None, None, "tensor"),
            P(),
            P(("dp", "tensor"), None, None),
            P(("dp", "tensor"), None, None),
            P(("dp", "tensor"), None, None),
            P(("dp", "tensor")),
            P(("dp", "tensor")),
        ),
        out_specs=(
            P(("dp", "tensor"), None, None),
            P(None, None, "tensor"),
            P(None, None, "tensor"),
        ),
        check_vma=False,
    )
```

profile of v0, /device:TPU:0, one launch (start us, length us, event | category | flops | bytes accessed | tf_op | source)
XLA Modules:
  0.0 230.1 jit_solution(3749748746958787221)
XLA Ops:
  7.2 1.8 convert_bitcast_fusion.1
  9.1 1.5 convert_bitcast_fusion.2
  12.0 8.0 %copy.68 = bf16[2,1280,1024]{1,2,0:T(8,128)(2,1)} copy(bf16[2,1280,1024]{2,1,0:T(8,128)(2,1)} %param.13) | data formatting | bytes 10485760 | tf_op args[1]
  20.1 4.9 %fusion.27 = (bf16[240,1,1280]{2,1,0:T(2,128)(2,1)}, bf16[240,1,1280]{2,1,0:T(2,128)(2,1)}, bf16[240,1,1280]{2,1,0:T(2,128)(2,1)}, bf16[240,1,1280]{2,1,0:T(2,128)(2,1)}) fusion(bf16[240,4,1280]{2,1,0:T(4,128)(2,1)S(1)} %copy-done), kind=kLoop, calls=%fused_computation.83 | loop fusion | bytes 4915200 | tf_op jit(solution)/shard_map/slice | solution.py:89
  28.3 41.2 %all-reduce.12.cloned.1.call-done = (bf16[2,64,1280]{2,1,0:T(8,128)(2,1)}, bf16[2,64,256]{2,1,0:T(8,128)(2,1)}) async-done(((bf16[2,64,1280]{2,1,0:T(8,128)(2,1)}, bf16[2,64,256]{2,1,0:T(8,128)(2,1)}), (bf16[2,64,1280]{2,1,0:T(8,128)(2,1)}, bf16[2,64,256]{2,1,0:T(8,128)(2,1)})) %all-reduce.12.cloned.1.call-update) | async-done | bytes 393232 | tf_op jit(solution)/shard_map/psum | solution.py:75
  71.0 10.0 %all_gather.3 = bf16[2,64,1024]{2,1,0:T(8,128)(2,1)S(1)} all-gather(bf16[2,64,256]{2,1,0:T(8,128)(2,1)S(1)} %get-tuple-element.13), channel_id=1, replica_groups=mesh['dp'=8,'tensor'=4] {'tensor'}, dimensions={2}, use_global_device_ids=true | all-gather | bytes 327680 | tf_op jit(solution)/shard_map/all_gather | solution.py:80
  82.8 6.7 %add_convert_fusion = bf16[2,1280,1024]{1,2,0:T(8,128)(2,1)S(1)} fusion(bf16[2,1280,1024]{1,2,0:T(8,128)(2,1)} %copy.68, f32[2,64,1280]{2,1,0:T(8,128)S(1)} %multiply_subtract_fusion, bf16[2,64,1024]{2,1,0:T(8,128)(2,1)S(1)} %all_gather.3), kind=kOutput, calls=%fused_computation.1 | convolution fusion | flops 2023751680 | bytes 11403264 | tf_op jit(solution)/shard_map/prd,prk->pdk/dot_general | solution.py:83
  90.8 1.5 fusion.9
  92.4 1.6 fusion.8
  94.0 2.5 %fusion.7 = bf16[240,2048]{1,0:T(8,128)(2,1)} fusion(bf16[240,1,1280]{2,1,0:T(2,128)(2,1)S(1)} %copy-done.8, bf16[1280,1024]{0,1:T(8,128)(2,1)S(1)} %get-tuple-element.16, bf16[1280,1024]{0,1:T(8,128)(2,1)S(1)} %get-tuple-element.15), kind=kOutput, calls=%fused_computation.14 | convolution fusion | flops 1269268480 | bytes 6840320 | tf_op jit(solution)/shard_map/dot_general | solution.py:92
  96.5 2.5 %fusion.6 = bf16[240,2048]{1,0:T(8,128)(2,1)} fusion(bf16[240,1,1280]{2,1,0:T(2,128)(2,1)S(1)} %copy-done.7, bf16[1280,1024]{0,1:T(8,128)(2,1)S(1)} %get-tuple-element.16, bf16[1280,1024]{0,1:T(8,128)(2,1)S(1)} %get-tuple-element.15), kind=kOutput, calls=%fused_computation.13 | convolution fusion | flops 1269268480 | bytes 6840320 | tf_op jit(solution)/shard_map/dot_general | solution.py:92
  99.0 70.2 %fusion.25 = (bf16[64,2048]{1,0:T(8,128)(2,1)S(1)}, bf16[64,2048]{1,0:T(8,128)(2,1)S(1)}, bf16[64,2048]{1,0:T(8,128)(2,1)S(1)}, bf16[64,2048]{1,0:T(8,128)(2,1)S(1)}) fusion(bf16[240,2048]{1,0:T(8,128)(2,1)} %fusion.6, bf16[240,2048]{1,0:T(8,128)(2,1)} %fusion.7, bf16[240,2048]{1,0:T(8,128)(2,1)S(1)} %fusion.8, bf16[240,2048]{1,0:T(8,128)(2,1)S(1)} %fusion.9), kind=kCustom, calls=%all-reduce-scatter.4 | all-reduce-scatter fusion | flops 2097153 | bytes 4981248
  169.3 2.6 %collective-permute-start = (bf16[12,2048]{1,0:T(8,128)(2,1)S(1)}, bf16[12,2048]{1,0:T(8,128)(2,1)S(1)}, u32[]{:S(2)}, u32[]{:S(2)}) collective-permute-start(bf16[12,2048]{1,0:T(8,128)(2,1)S(1)} %slice.94), channel_id=1, source_target_pairs={{0,1},{1,2},{2,3},{4,5},{5,6},{6,7},{8,9},{9,10},{10,11},{12,13},{... | collective-permute-start | bytes 147464
  173.2 5.3 %reshape.181 = bf16[60,4,8,4,128]{4,3,2,1,0:T(4,128)(2,1)} reshape(bf16[60,4,4096]{2,1,0:T(4,128)(2,1)} %param.19) | data formatting | bytes 3932160 | tf_op jit(solution)/shard_map/reshape | solution.py:39
  179.8 4.0 %collective-permute-start.1 = (bf16[12,2048]{1,0:T(8,128)(2,1)S(1)}, bf16[12,2048]{1,0:T(8,128)(2,1)S(1)}, u32[]{:S(2)}, u32[]{:S(2)}) collective-permute-start(bf16[12,2048]{1,0:T(8,128)(2,1)S(1)} %slice.95), channel_id=1, source_target_pairs={{0,1},{1,2},{2,3},{4,5},{5,6},{6,7},{8,9},{9,10},{10,11},{12,13},{... | collective-permute-start | bytes 147464
  183.8 2.5 %collective-permute-start.2 = (bf16[12,2048]{1,0:T(8,128)(2,1)S(1)}, bf16[12,2048]{1,0:T(8,128)(2,1)S(1)}, u32[]{:S(2)}, u32[]{:S(2)}) collective-permute-start(bf16[12,2048]{1,0:T(8,128)(2,1)S(1)} %slice.96), channel_id=1, source_target_pairs={{0,1},{1,2},{2,3},{4,5},{5,6},{6,7},{8,9},{9,10},{10,11},{12,13},{... | collective-permute-start | bytes 147464
  186.3 1.9 collective-permute-start.3
  195.2 2.2 mul.116
  197.4 1.5 mul.117
  199.0 2.7 %fusion.20 = bf16[60,4,1024]{2,0,1:T(8,128)(2,1)S(1)} fusion(f32[60,4,1024]{2,1,0:T(4,128)S(1)} %mul.136, f32[60,4,1024]{2,1,0:T(4,128)S(1)} %mul.129, f32[60,4,1024]{2,1,0:T(4,128)S(1)} %mul.117, f32[1024]{0:T(1024)S(1)} %copy-done.22, bf16[60,1,2048]{2,0,1:T(8,128)(2,1)S(1)} %dynamic-slice_bitcast_fusion.3, ...), kind=kLoop, calls=%fused_computation.31 | loop fusion | flops 3194880 | bytes 4427776 | tf_op jit(solution)/shard_map/convert_element_type | solution.py:108
  201.8 2.5 %select_select_fusion.1 = (bf16[60,16,1024]{2,1,0:T(8,128)(2,1)S(1)}, bf16[60,16,1024]{2,1,0:T(8,128)(2,1)S(1)}) fusion(bf16[60,16,1024]{2,1,0:T(8,128)(2,1)S(1)} %copy-done.4, pred[60,16]{1,0:T(8,128)(4,1)S(1)} %get-tuple-element.44, pred[60,16]{1,0:T(8,128)(4,1)S(1)} %copy-done.19, pred[60,16]{1,0:T(8,128)(4,1)S(1)} %copy-done.20, ...), kind=kLoop, calls=%fused_computation.28 | loop fusion | flops 7864320 | bytes 8851200 | tf_op jit(solution)/shard_map/jit(_where)/select_n | solution.py:37
  209.2 6.8 %fusion.28 = (f32[60,4,8,4]{3,1,2,0:T(4,128)S(1)}, f32[60,4,8,4,16]{4,3,1,2,0:T(4,128)}) fusion(pred[60,4,16]{2,1,0:T(4,128)(4,1)S(1)} %copy-done.21, bf16[60,16,8,128,1]{3,2,1,0,4:T(8,128)(2,1)} %bitcast_bitcast_fusion, bf16[60,4,8,4,128]{4,3,2,1,0:T(4,128)(2,1)S(1)} %copy-done.6), kind=kOutput, calls=%fused_computation.84 | convolution fusion | flops 31948816 | bytes 4458240 | tf_op jit(solution)/shard_map/sub | solution.py:49
  216.0 4.3 %convert_bitcast_fusion = bf16[60,4,8,4,128]{4,3,1,2,0:T(4,128)(2,1)S(1)} fusion(f32[60,4,8,4,16]{4,3,1,2,0:T(4,128)} %get-tuple-element.35, f32[60,4,8,4]{3,1,2,0:T(4,128)S(1)} %get-tuple-element.34, bf16[60,16,8,128,1]{3,2,1,0,4:T(8,128)(2,1)} %bitcast_bitcast_fusion.1), kind=kOutput, calls=%fused_computation.24 | convolution fusion | flops 32686080 | bytes 4454400 | tf_op jit(solution)/shard_map/rtkgc,rckd->rtkgd/dot_general | solution.py:51
  221.2 2.0 convert_element_type.101
  (106 shorter events, 23.8 us)
Async XLA Ops:
  7.2 62.3 %all-reduce.12.cloned.1.call-start = ((), (), s32[]{:S(2)}) async-start(), calls=%async_computation | async-start | bytes 786432 | tf_op jit(solution)/shard_map/psum | solution.py:75
  12.0 8.0 %copy-start = (bf16[240,4,1280]{2,1,0:T(4,128)(2,1)S(1)}, bf16[240,4,1280]{2,1,0:T(4,128)(2,1)}, u32[]{:S(2)}) copy-start(bf16[240,4,1280]{2,1,0:T(4,128)(2,1)} %param.12) | copy-start | bytes 7372804
  20.1 5.0 %copy-start.25 = (s32[60]{0:T(128)S(1)}, s32[60]{0:T(128)}, u32[]{:S(2)}) copy-start(s32[60]{0:T(128)} %param.23) | copy-start | bytes 724
  20.1 5.1 %copy-start.23 = (s32[60]{0:T(128)S(1)}, s32[60]{0:T(128)}, u32[]{:S(2)}) copy-start(s32[60]{0:T(128)} %param.22) | copy-start | bytes 724
  20.1 7.6 %copy-start.24 = (f32[128]{0:T(128)S(1)}, f32[128]{0:T(128)}, u32[]{:S(2)}) copy-start(f32[128]{0:T(128)} %param.18) | copy-start | bytes 1540
  20.1 49.4 %copy-start.18 = (f32[2,64,256]{2,1,0:T(8,128)S(1)}, f32[2,64,256]{2,1,0:T(8,128)}, u32[]{:S(2)}) copy-start(f32[2,64,256]{2,1,0:T(8,128)} %param.15) | copy-start | bytes 393220
  20.1 60.9 %copy-start.12 = (f32[2,64,1280]{2,1,0:T(8,128)S(1)}, f32[2,64,1280]{2,1,0:T(8,128)}, u32[]{:S(2)}) copy-start(f32[2,64,1280]{2,1,0:T(8,128)} %param.14) | copy-start | bytes 1966084
  94.0 2.5 %copy-start.7 = (bf16[240,1,1280]{2,1,0:T(2,128)(2,1)S(1)}, bf16[240,1,1280]{2,1,0:T(2,128)(2,1)}, u32[]{:S(2)}) copy-start(bf16[240,1,1280]{2,1,0:T(2,128)(2,1)} %get-tuple-element.20) | copy-start | bytes 1843204
  169.3 19.0 %collective-permute-start = (bf16[12,2048]{1,0:T(8,128)(2,1)S(1)}, bf16[12,2048]{1,0:T(8,128)(2,1)S(1)}, u32[]{:S(2)}, u32[]{:S(2)}) collective-permute-start(bf16[12,2048]{1,0:T(8,128)(2,1)S(1)} %slice.94), channel_id=1, source_target_pairs={{0,1},{1,2},{2,3},{4,5},{5,6},{6,7},{8,9},{9,10},{10,11},{12,13},{... | collective-permute-start | bytes 147464
  172.9 5.6 %copy-start.26 = (u32[32]{0:T(128)S(1)}, u32[32]{0:T(128)}, u32[]{:S(2)}) copy-start(u32[32]{0:T(128)} %constant.40) | copy-start | bytes 388
  179.8 8.9 %collective-permute-start.1 = (bf16[12,2048]{1,0:T(8,128)(2,1)S(1)}, bf16[12,2048]{1,0:T(8,128)(2,1)S(1)}, u32[]{:S(2)}, u32[]{:S(2)}) collective-permute-start(bf16[12,2048]{1,0:T(8,128)(2,1)S(1)} %slice.95), channel_id=1, source_target_pairs={{0,1},{1,2},{2,3},{4,5},{5,6},{6,7},{8,9},{9,10},{10,11},{12,13},{... | collective-permute-start | bytes 147464
  183.8 5.3 %collective-permute-start.2 = (bf16[12,2048]{1,0:T(8,128)(2,1)S(1)}, bf16[12,2048]{1,0:T(8,128)(2,1)S(1)}, u32[]{:S(2)}, u32[]{:S(2)}) collective-permute-start(bf16[12,2048]{1,0:T(8,128)(2,1)S(1)} %slice.96), channel_id=1, source_target_pairs={{0,1},{1,2},{2,3},{4,5},{5,6},{6,7},{8,9},{9,10},{10,11},{12,13},{... | collective-permute-start | bytes 147464
  186.3 3.8 %collective-permute-start.3 = (bf16[12,2048]{1,0:T(8,128)(2,1)S(1)}, bf16[12,2048]{1,0:T(8,128)(2,1)S(1)}, u32[]{:S(2)}, u32[]{:S(2)}) collective-permute-start(bf16[12,2048]{1,0:T(8,128)(2,1)S(1)} %slice.97), channel_id=1, source_target_pairs={{0,1},{1,2},{2,3},{4,5},{5,6},{6,7},{8,9},{9,10},{10,11},{12,13},{... | collective-permute-start | bytes 147464
  194.8 4.0 %copy-start.22 = (f32[1024]{0:T(1024)S(1)}, f32[1024]{0:T(1024)}, u32[]{:S(2)}) copy-start(f32[1024]{0:T(1024)} %broadcast_bitcast_fusion) | copy-start | bytes 12292
  198.9 2.9 %copy-start.4 = (bf16[60,16,1024]{2,1,0:T(8,128)(2,1)S(1)}, bf16[60,16,1024]{2,1,0:T(8,128)(2,1)}, u32[]{:S(2)}) copy-start(bf16[60,16,1024]{2,1,0:T(8,128)(2,1)} %param.21) | copy-start | bytes 5898244
  198.9 2.9 %copy-start.5 = (bf16[60,16,1024]{2,1,0:T(8,128)(2,1)S(1)}, bf16[60,16,1024]{2,1,0:T(8,128)(2,1)}, u32[]{:S(2)}) copy-start(bf16[60,16,1024]{2,1,0:T(8,128)(2,1)} %param.20) | copy-start | bytes 5898244
  198.9 2.9 %copy-start.13 = (bf16[60,1024]{1,0:T(8,128)(2,1)S(1)}, bf16[60,1024]{1,0:T(8,128)(2,1)}, u32[]{:S(2)}) copy-start(bf16[60,1024]{1,0:T(8,128)(2,1)} %get-tuple-element.42) | copy-start | bytes 368644
  198.9 2.9 %copy-start.14 = (bf16[60,1024]{1,0:T(8,128)(2,1)S(1)}, bf16[60,1024]{1,0:T(8,128)(2,1)}, u32[]{:S(2)}) copy-start(bf16[60,1024]{1,0:T(8,128)(2,1)} %get-tuple-element.43) | copy-start | bytes 368644
  198.9 2.9 %copy-start.15 = (bf16[60,1024]{1,0:T(8,128)(2,1)S(1)}, bf16[60,1024]{1,0:T(8,128)(2,1)}, u32[]{:S(2)}) copy-start(bf16[60,1024]{1,0:T(8,128)(2,1)} %get-tuple-element.40) | copy-start | bytes 368644
  198.9 2.9 %copy-start.16 = (bf16[60,1024]{1,0:T(8,128)(2,1)S(1)}, bf16[60,1024]{1,0:T(8,128)(2,1)}, u32[]{:S(2)}) copy-start(bf16[60,1024]{1,0:T(8,128)(2,1)} %get-tuple-element.41) | copy-start | bytes 368644
  198.9 2.9 %copy-start.19 = (pred[60,16]{1,0:T(8,128)(4,1)S(1)}, pred[60,16]{1,0:T(8,128)(4,1)}, u32[]{:S(2)}) copy-start(pred[60,16]{1,0:T(8,128)(4,1)} %get-tuple-element.36) | copy-start | bytes 2884
  199.0 2.9 %copy-start.20 = (pred[60,16]{1,0:T(8,128)(4,1)S(1)}, pred[60,16]{1,0:T(8,128)(4,1)}, u32[]{:S(2)}) copy-start(pred[60,16]{1,0:T(8,128)(4,1)} %get-tuple-element.37) | copy-start | bytes 2884
  206.9 2.3 copy-start.6
  206.9 2.3 copy-start.21
  (8 other events, 11.0 us)
Sparse Core Ops, SparseCore 0:
  11.0 58.4 all-reduce.11
where the time goes:
time: 231 us; the launch traced here: 230 us
  blocking collectives  80.2 us (35%)
  waiting for transfers between devices  41.8 us (18%)
  local copies, waits for them, and re-layouts  37.3 us (16%)
  matrix products  26 us (11%)
  other arithmetic  18.3 us (8%)
  between operations  15.3 us (7%)
  starting transfers between devices  11.1 us (5%)
    unnamed x1, blocking collectives  70.2 us
    psum x1, waiting for transfers between devices, per_device(): lax.psum(grad_a[0].astype(jnp.bfloat16), 'dp').astype(jnp.float32)  41.2 us
    unnamed x66, local copies, waits for them, and re-layouts  13.8 us
    unnamed x4, starting transfers between devices  11 us
    all_gather x1, blocking collectives, per_device(): lax.all_gather(new_b.astype(jnp.bfloat16), 'tensor', axis=2, tiled=True)  9.99 us
    dot_general x4, matrix products, step_term(): return jnp.dot(column, joined, preferred_element_type=jnp.float32)  8.16 us
    sub x1, matrix products, attend(): expo = jnp.exp(scores - top)  6.83 us
    dot_general x1, matrix products, per_device(): jnp.einsum('prd,prk->pdk', new_a, full_b, precision=lax.Precision.HIGHEST)  6.68 us
  transfers between devices with their start and end apart: 5, of which 2 were waited for; matrix products, arithmetic and copies ran while one was open for 11% of the time, Pallas kernels for 0%

commit v1 on v0

--- a/solution.py
+++ b/solution.py
@@ -1,8 +1,11 @@
+import functools
 import math
 
 import jax
 import jax.numpy as jnp
 from jax import lax
+from jax.experimental import pallas as pl
+from jax.experimental.pallas import tpu as pltpu
 from jax.sharding import PartitionSpec as P
 
 D = 5120
@@ -11,6 +14,9 @@
 QH = 32
 R = 64
 STEPS = 4
+BF = jnp.bfloat16
+F32 = jnp.float32
+VMEM_LIMIT = 24 * 1024 * 1024
 
 
 def normed_rotated(keys, gain, position):
@@ -54,7 +60,7 @@
     return result.reshape(rows, steps, width).astype(jnp.bfloat16)
 
 
-def per_device(
+def general(
     hidden_in,
     kv_weight,
     factor_a,
@@ -86,17 +92,10 @@
     rows_here = hidden_in.shape[0] // lax.axis_size("tensor")
     pieces = []
     for step in range(STEPS):
-        column = hidden_in[:, step, :]
-
-        def step_term(start, count, column=column):
-            return jnp.dot(column, joined, preferred_element_type=jnp.float32)
-
+        term = jnp.dot(hidden_in[:, step, :], joined, preferred_element_type=jnp.float32)
         pieces.append(
             lax.psum_scatter(
-                step_term(jnp.int32(0), rows_here * lax.axis_size("tensor")).astype(jnp.bfloat16),
-                "tensor",
-                scatter_dimension=0,
-                tiled=True,
+                term.astype(jnp.bfloat16), "tensor", scatter_dimension=0, tiled=True
             ).astype(jnp.float32)
         )
     projected = jnp.stack(pieces, axis=1)
@@ -111,9 +110,460 @@
     return (attended, new_a, new_b)
 
 
+CHUNKS = (4, 4)
+GROUP = 12
+HEADS_STEP = 2
+
+
+def params(limit=VMEM_LIMIT):
+    return pltpu.CompilerParams(vmem_limit_bytes=limit)
+
+
+def cost(flops, args, outs):
+    size = sum(math.prod(x.shape) * x.dtype.itemsize for x in [*args, *outs])
+    return pl.CostEstimate(flops=flops, bytes_accessed=size, transcendentals=0)
+
+
+def dot(a, b):
+    return jnp.dot(a, b, preferred_element_type=F32)
+
+
+def dot_t(a, b):
+    return lax.dot_general(a, b, (((1,), (1,)), ((), ())), preferred_element_type=F32)
+
+
+def whole(shape):
+    return pl.BlockSpec(shape, lambda i, *_: (0,) * len(shape))
+
+
+def hbm(x):
+    return pltpu.with_memory_space_constraint(x, pltpu.HBM)
+
+
+TILE = 256
+
+
+def terms_kernel(first, ids, hidden, wk, wv, after, *outs):
+    del after
+    if first:
+        x, *outs = outs
+        tokens = x.shape[0] // 4
+
+        @pl.when(pl.program_id(0) == 0)
+        def _():
+            for r in range(4):
+                at = pl.ds((ids[0] ^ r) * (tokens // STEPS), tokens // STEPS)
+                x[r * tokens : (r + 1) * tokens] = hidden[at].reshape(tokens, x.shape[1])
+
+    else:
+        x = hidden
+        tokens = x.shape[0] // 4
+    ksend, kkeep, vsend, vkeep0, vkeep1 = outs
+    steps = x.shape[1] // TILE
+
+    def push(k):
+        at = slice(k * TILE, (k + 1) * TILE)
+        pltpu.matmul_push_rhs(wk[0, at, :], k % 2, 0)
+        pltpu.matmul_push_rhs(wv[0, at, :], k % 2, 1)
+
+    def multiply(*accs):
+        accs_k, accs_v = accs[:4], accs[4:]
+        push(0)
+        for k in range(steps):
+            if k + 1 < steps:
+                push(k + 1)
+            for r in range(4):
+                rows = x[r * tokens : (r + 1) * tokens, k * TILE : (k + 1) * TILE]
+                staged = k % 2 if r == 0 else None
+                pltpu.matmul_acc_lhs(accs_k[r], rows, load_staged_rhs=staged)
+                pltpu.matmul_acc_lhs(accs_v[r], rows, load_staged_rhs=staged)
+        key = [pltpu.matmul_pop(acc).astype(BF) for acc in accs_k]
+        value = [pltpu.matmul_pop(acc).astype(BF) for acc in accs_v]
+        kkeep[:tokens], kkeep[tokens:] = key[0], key[2]
+        ksend[:tokens], ksend[tokens:] = key[3], key[1]
+        vkeep0[...], vkeep1[...] = value[0], value[1]
+        vsend[:tokens], vsend[tokens:] = value[2], value[3]
+
+    pl.run_scoped(
+        multiply, *[pltpu.ACC(unit)((tokens, TILE), F32) for unit in range(2) for _ in range(4)]
+    )
+
+
+def projection_terms(ids, hidden, kv_weight, start, count, tokens, after):
+    first = len(hidden.shape) == 3
+    width = hidden.shape[-1]
+    wide = count * HD
+    base = start * HD // TILE
+    assert wide % TILE == 0 and start * HD % TILE == 0 and width % TILE == 0
+    rows = (2, 2, 2, 1, 1)
+    outs = [jax.ShapeDtypeStruct((n * tokens, wide), BF) for n in rows]
+    specs = [pl.BlockSpec((n * tokens, TILE), lambda i, _: (0, i)) for n in rows]
+    if first:
+        outs.insert(0, jax.ShapeDtypeStruct((4 * tokens, width), BF))
+        specs.insert(0, whole(outs[0].shape))
+    return pl.pallas_call(
+        functools.partial(terms_kernel, first),
+        out_shape=outs,
+        grid_spec=pltpu.PrefetchScalarGridSpec(
+            num_scalar_prefetch=1,
+            grid=(wide // TILE,),
+            in_specs=[
+                whole(hidden.shape),
+                pl.BlockSpec((1, width, TILE), lambda i, _: (0, 0, base + i)),
+                pl.BlockSpec((1, width, TILE), lambda i, _: (1, 0, base + i)),
+                pl.BlockSpec(memory_space=pl.ANY),
+            ],
+            out_specs=specs,
+        ),
+        compiler_params=params(),
+        cost_estimate=cost(2 * 4 * tokens * width * 2 * wide, [hidden], outs),
+        name="projection_terms",
+    )(ids, hbm(hidden) if first else hidden, hbm(kv_weight), hbm(kv_weight), after)
+
+
+def mid_kernel(kkeep, kcame, vkeep, vcame, after, kout, vout):
+    del after
+    kout[...] = (kkeep[...].astype(F32) + kcame[...].astype(F32)).astype(BF)
+    vout[...] = (vkeep[...].astype(F32) + vcame[...].astype(F32)).astype(BF)
+
+
+def mid_sums(kkeep, kcame, vkeep, vcame, after):
+    shape = vkeep.shape
+    low = pl.BlockSpec(shape, lambda i: (0, 0))
+    high = pl.BlockSpec(shape, lambda i: (1, 0))
+    return pl.pallas_call(
+        mid_kernel,
+        out_shape=[jax.ShapeDtypeStruct(shape, BF)] * 2,
+        grid=(1,),
+        in_specs=[high, low, low, high, pl.BlockSpec(memory_space=pl.ANY)],
+        out_specs=[low, low],
+        compiler_params=params(),
+        cost_estimate=cost(0, [vkeep] * 6, []),
+        name="mid_sums",
+    )(kkeep, kcame, vkeep, vcame, after)
+
+
+def pack_kernel(ids, grad_a, grad_b, out):
+    del ids
+    wide = grad_a.shape[-1]
+    out[:, :wide] = grad_a[0, 0].astype(BF)
+    out[:, wide:] = grad_b[0, 0].astype(BF)
+
+
+def chip_kernel(ids, grad_a, grad_b, other, out):
+    del ids
+    wide = grad_a.shape[-1]
+    out[:, :wide] = (grad_a[0, 0] + other[:, :wide].astype(F32)).astype(BF)
+    out[:, wide:] = (grad_b[0, 0] + other[:, wide:].astype(F32)).astype(BF)
+
+
+def grad_half(kernel, name, ids, grad_a, grad_b, flip, *rest):
+    rank, wide = grad_a.shape[2], grad_a.shape[3] + grad_b.shape[3]
+
+    def spec(x):
+        return pl.BlockSpec((1, 1) + x.shape[2:], lambda i, ids: (0, ids[2] ^ flip, 0, 0))
+
+    out = jax.ShapeDtypeStruct((rank, wide), BF)
+    return pl.pallas_call(
+        kernel,
+        out_shape=out,
+        grid_spec=pltpu.PrefetchScalarGridSpec(
+            num_scalar_prefetch=1,
+            grid=(1,),
+            in_specs=[spec(grad_a), spec(grad_b)] + [whole(x.shape) for x in rest],
+            out_specs=whole(out.shape),
+        ),
+        compiler_params=params(),
+        cost_estimate=cost(0, [out] * 4, []),
+        name=name,
+    )(ids, hbm(grad_a), hbm(grad_b), *rest)
+
+
+def small_call(kernel, name, ids, args, outs, after=()):
+    count = len(args)
+
+    def body(ids, *refs):
+        kernel(ids, *refs[:count], *refs[count + len(after) :])
+
+    return pl.pallas_call(
+        body,
+        out_shape=outs,
+        grid_spec=pltpu.PrefetchScalarGridSpec(
+            num_scalar_prefetch=1,
+            grid=(1,),
+            in_specs=[whole(x.shape) for x in args]
+            + [pl.BlockSpec(memory_space=pl.ANY)] * len(after),
+            out_specs=[whole(x.shape) for x in outs],
+        ),
+        compiler_params=params(),
+        cost_estimate=cost(0, args, outs),
+        name=name,
+    )(ids, *args, *after)
+
+
+def core_flip(x, count):
+    return lax.ppermute(x, "dp", [(i, i ^ 1) for i in range(count)])
+
+
+def plus_kernel(a, b, after, out):
+    del after
+    out[...] = (a[...].astype(F32) + b[...].astype(F32)).astype(BF)
+
+
+def plus(a, b, after):
+    out = jax.ShapeDtypeStruct(a.shape, BF)
+    return pl.pallas_call(
+        plus_kernel,
+        out_shape=out,
+        grid=(1,),
+        in_specs=[whole(a.shape)] * 2 + [pl.BlockSpec(memory_space=pl.ANY)],
+        out_specs=whole(a.shape),
+        compiler_params=params(),
+        cost_estimate=cost(0, [a, b], [out]),
+        name="plus",
+    )(a, b, after)
+
+
+def along_line(x, d, count):
+    return lax.ppermute(x, "dp", [(i, i ^ (2 * d)) for i in range(count)])
+
+
+TOP = 2 * R
+
+
+def update_kernel(rates, ids, half, other, factor_a, factor_b, new_a, new_b, a):
+    wide = factor_a.shape[-1]
+    for index, part in ((ids[2], half), (ids[2] ^ 1, other)):
+        new_a[index] = factor_a[index] - rates[0] * part[:, :wide].astype(F32)
+        new_b[index] = factor_b[index] - rates[1] * part[:, wide:].astype(F32)
+    for p in range(2):
+        a[p * R : (p + 1) * R] = new_a[p].astype(BF)
+
+
+def updated(ids, half, other, factor_a, factor_b, dp, after):
+    rates = (2.0 / math.sqrt(dp * D), 2.0 / math.sqrt(dp * R))
+    outs = [
+        jax.ShapeDtypeStruct(factor_a.shape, F32),
+        jax.ShapeDtypeStruct(factor_b.shape, F32),
+        jax.ShapeDtypeStruct((2 * R, factor_a.shape[2]), BF),
+    ]
+    return small_call(
+        functools.partial(update_kernel, rates),
+        "update_factors",
+        ids,
+        (half, other, factor_a, factor_b),
+        outs,
+        (after,),
+    )
+
+
+def payload_kernel(ids, u, new_b, *sends):
+    del ids
+    tokens = u.shape[0] // 4
+    for r, out in enumerate(sends):
+        first = r * tokens
+        for p in range(2):
+            out[p * R : (p + 1) * R, :] = new_b[p].astype(BF)
+        out[TOP:, :TOP] = u[first : first + TOP]
+        out[TOP:tokens, TOP:] = u[first + TOP : first + tokens]
+        out[tokens:, TOP:] = jnp.zeros((2 * TOP - tokens, TOP), BF)
+
+
+def payloads(ids, u, new_b):
+    outs = [jax.ShapeDtypeStruct((2 * TOP, 2 * TOP), BF)] * 4
+    return small_call(payload_kernel, "pack_terms", ids, (u, new_b), outs)
+
+
+def attend_kernel(start, ids, lengths, *refs):
+    q, cache_k, cache_v, k0, k1, k2, v0, v1, v2, *ub, cosine, sine = refs[:15]
+    out = refs[-1]
+    rows, slots, _ = cache_k.shape
+    tokens = rows * STEPS
+    u_top = sum(x[TOP:, :TOP].astype(F32) for x in ub)
+    u_low = sum(x[TOP:tokens, TOP:].astype(F32) for x in ub)
+    u = jnp.concatenate([u_top, u_low], axis=0).astype(BF)
+    rel = ids[0] ^ (start // HEADS_STEP + pl.program_id(0))
+    low = jnp.where(rel == 0, ub[0][:TOP].astype(F32), ub[1][:TOP].astype(F32))
+    high = jnp.where(rel == 2, ub[2][:TOP].astype(F32), ub[3][:TOP].astype(F32))
+    b = jnp.where(rel < 2, low, high).astype(BF)
+    k = k0[...].astype(F32) + k1[...].astype(F32) + k2[...].astype(F32) + dot(u[:, :R], b[:R])
+    v = v0[...].astype(F32) + v1[...].astype(F32) + v2[...].astype(F32) + dot(u[:, R:], b[R:])
+    v = v.astype(BF)
+    keys = []
+    for n in range(HEADS_STEP):
+        key = k[:, n * HD : (n + 1) * HD]
+        scale = lax.rsqrt(jnp.sum(key * key, axis=-1, keepdims=True) * (1.0 / HD) + 1e-06)
+        key = scale * (key * cosine[...] + pltpu.roll(key, HD // 2, 1) * sine[...])
+        keys.append(key.astype(BF))
+    n_q, n_c = GROUP * STEPS, GROUP * slots
+    shape = (n_q, n_c + n_q)
+    here = lax.broadcasted_iota(jnp.int32, shape, 0)
+    col = lax.broadcasted_iota(jnp.int32, shape, 1)
+    fresh = col - n_c
+    cached = (col < n_c) & (here // STEPS == col // slots)
+    new = (col >= n_c) & (here // STEPS == fresh // STEPS) & (fresh % STEPS <= here % STEPS)
+    bias_here = jnp.where(cached | new, 0.0, -1e30)
+    col = lax.broadcasted_iota(jnp.int32, (1, n_c + n_q), 1)
+    ones = jnp.ones((n_c + n_q, HD), BF)
+    factor = math.log2(math.e) * HD**-0.5
+    heads = QH // KVH
+    blocks = rows // GROUP
+    query = q[...].reshape(tokens, HEADS_STEP * heads * HD)
+
+    def block(n, g, cache, fresh):
+        old = cache[g * GROUP : (g + 1) * GROUP, :, n * HD : (n + 1) * HD].reshape(n_c, HD)
+        return jnp.concatenate([old, fresh[g * n_q : (g + 1) * n_q]], axis=0)
+
+    every = [(n, g) for n in range(HEADS_STEP) for g in range(blocks)]
+    scores = []
+    for n, g in every:
+        part = [query[g * n_q : (g + 1) * n_q, h * HD : (h + 1) * HD] for h in range(n * heads, (n + 1) * heads)]
+        scores.append(dot_t(jnp.concatenate(part, axis=0), block(n, g, cache_k, keys[n])))
+    biases = []
+    for g in range(blocks):
+        filled = jnp.full(col.shape, lengths[g * GROUP], jnp.int32)
+        for i in range(1, GROUP):
+            filled = jnp.where(col // slots == i, lengths[g * GROUP + i], filled)
+        bias = jnp.where((col >= n_c) | (col % slots < filled), 0.0, -1e30) + bias_here
+        biases.append(jnp.concatenate([bias] * heads, axis=0))
+    weights = []
+    for (n, g), s in zip(every, scores):
+        s = s * factor + biases[g]
+        top = jnp.max(s, axis=-1, keepdims=True)
+        weights.append(jnp.exp2(s - top).astype(BF))
+    results = []
+    for (n, g), w in zip(every, weights):
+        here_v = block(n, g, cache_v, v[:, n * HD : (n + 1) * HD])
+        r = dot(w, jnp.concatenate([here_v, ones], axis=1))
+        total = r[:, HD:]
+        inverse = pl.reciprocal(total, approx=True)
+        inverse = inverse * (2.0 - total * inverse)
+        results.append((r[:, :HD] * inverse).astype(BF))
+    for n in range(HEADS_STEP):
+        for h in range(heads):
+            part = [r[h * n_q : (h + 1) * n_q] for r in results[n * blocks : (n + 1) * blocks]]
+            at = (n * heads + h) * HD
+            out[:, :, at : at + HD] = jnp.concatenate(part, axis=0).reshape(rows, STEPS, HD)
+
+
+def attend_chunk(
+    ids, lengths, start, count, queries, cache_keys, cache_values, terms, ub, tables, before
+):
+    rows, slots, _ = cache_keys.shape
+    tokens = rows * STEPS
+    heads = QH // KVH
+    args = [queries, cache_keys, cache_values, *terms, *ub, *tables]
+    assert start % HEADS_STEP == 0 and count % HEADS_STEP == 0
+    first = start // HEADS_STEP
+    size = HEADS_STEP * HD
+    part = pl.BlockSpec((tokens, size), lambda i, *_: (0, i))
+    low = pl.BlockSpec((tokens, size), lambda i, *_: (1, i))
+    cache = pl.BlockSpec((rows, slots, size), lambda i, *_: (0, 0, first + i))
+    wide = pl.BlockSpec((rows, STEPS, heads * size), lambda i, *_: (0, 0, first + i))
+    specs = [wide, cache, cache, part, low, part, part, part, part]
+    specs += [whole(x.shape) for x in (*ub, *tables)]
+    aliases = {}
+    if before is not None:
+        args.append(before)
+        specs.append(pl.BlockSpec(memory_space=pl.ANY))
+        aliases = {len(args) + 1: 0}
+    return pl.pallas_call(
+        functools.partial(attend_kernel, start),
+        out_shape=jax.ShapeDtypeStruct(queries.shape, BF),
+        grid_spec=pltpu.PrefetchScalarGridSpec(
+            num_scalar_prefetch=2, grid=(count // HEADS_STEP,), in_specs=specs, out_specs=wide
+        ),
+        input_output_aliases=aliases,
+        compiler_params=params(),
+        cost_estimate=cost(count * 4 * 10**9, args, []),
+        name="attend_chunk",
+    )(ids, lengths, *args)
+
+
+def rotary_tables(key_gain, positions):
+    half = HD // 2
+    place = positions[:, None] + jnp.arange(STEPS, dtype=jnp.int32)[None, :]
+    freq = jnp.exp(-math.log(1000000.0) * (jnp.arange(half, dtype=F32) * 2.0 / HD))
+    angle = place.reshape(-1).astype(F32)[:, None] * jnp.concatenate([freq, freq])
+    turned = jnp.concatenate([-key_gain[half:], key_gain[:half]])
+    return jnp.cos(angle) * key_gain, jnp.sin(angle) * turned
+
+
+def across(x, r):
+    return lax.ppermute(x, "tensor", [(i, i ^ r) for i in range(4)])
+
+
+def square(
+    hidden_in,
+    kv_weight,
+    factor_a,
+    factor_b,
+    grad_a,
+    grad_b,
+    key_gain,
+    queries,
+    cache_keys,
+    cache_values,
+    cache_lengths,
+    positions,
+):
+    tokens = cache_keys.shape[0] * STEPS
+    count_dp = lax.axis_size("dp")
+    dp = lax.axis_index("dp")
+    ids = jnp.stack([lax.axis_index("tensor"), dp // 2, dp % 2]).astype(jnp.int32)
+    tables = rotary_tables(key_gain, positions)
+
+    packed = grad_half(pack_kernel, "pack_grads", ids, grad_a, grad_b, 1)
+    other = core_flip(packed, count_dp)
+    half = grad_half(chip_kernel, "chip_grads", ids, grad_a, grad_b, 0, other)
+    x, *first = projection_terms(ids, hidden_in, kv_weight, 0, CHUNKS[0], tokens, half)
+    step, before = 1, first[0]
+    while 4 * step < count_dp:
+        half = plus(half, along_line(half, step, count_dp), before)
+        step, before = 2 * step, half
+    second = projection_terms(ids, x, kv_weight, CHUNKS[0], CHUNKS[1], tokens, half)
+    if step * 2 < count_dp:
+        half = plus(half, along_line(half, step, count_dp), second[0])
+    other = core_flip(half, count_dp)
+
+    def first_exchange(term, after):
+        ksend, kkeep, vsend, vkeep0, vkeep1 = term
+        kcame, vcame = across(ksend, 1), across(vsend, 2)
+        mids = mid_sums(kkeep, kcame, vkeep1, vcame, after)
+        return mids, (kkeep, kcame, vkeep0, vcame)
+
+    def second_exchange(mids, parts):
+        kkeep, kcame, vkeep0, vcame = parts
+        return kkeep, kcame, across(mids[0], 2), vkeep0, vcame, across(mids[1], 1)
+
+    mids, parts = first_exchange(first, half)
+    first = second_exchange(mids, parts)
+    new_a, new_b, a = updated(ids, half, other, factor_a, factor_b, count_dp, mids[0])
+    sends = payloads(ids, (0.25 * dot_t(x, a)).astype(BF), new_b)
+    ub = [sends[0]] + [across(sends[r], r) for r in (1, 2, 3)]
+    second = second_exchange(*first_exchange(second, sends[0]))
+    attended = None
+    for start, count, came in ((0, CHUNKS[0], first), (CHUNKS[0], CHUNKS[1], second)):
+        attended = attend_chunk(
+            ids,
+            cache_lengths,
+            start,
+            count,
+            queries,
+            cache_keys,
+            cache_values,
+            came,
+            ub,
+            tables,
+            attended,
+        )
+    return attended, new_a, new_b
+
+
 def solution(mesh):
+    fits = mesh.shape["tensor"] == 4 and mesh.shape["dp"] in (2, 4, 8)
     return jax.shard_map(
-        per_device,
+        square if fits else general,
         mesh=mesh,
         in_specs=(
             P("dp", None, "tensor"),

time: 231 us -> 64.8 us (0.28)
  blocking collectives: 80.2 us -> 0 us
  local copies, waits for them, and re-layouts: 37.3 us -> 1.69 us
  Pallas kernels: 0 us -> 29.6 us
  waiting for transfers between devices: 41.8 us -> 12.7 us
  matrix products: 26 us -> 0.8 us
  other arithmetic: 18.3 us -> 1.47 us
  between operations: 15.3 us -> 0.84 us
  starting transfers between devices: 11.1 us -> 17.4 us
    unnamed x1 -> x0, blocking collectives: 70.2 us -> none
    psum x1 -> x0, waiting for transfers between devices: 41.2 us -> none  [per_device(): lax.psum(grad_a[0].astype(jnp.bfloat16), 'dp').astype(jnp.float32)]
    pallas_call x0 -> x12, Pallas kernels: none -> 29.6 us  [the longest x2 11.5 us: projection_terms(): pl.pallas_call(functools.partial(terms_kernel, first), out_shape=outs, gr...]
    dot_general x6 -> x1, matrix products: 19.2 us -> 0.8 us  [dot_t(): lax.dot_general(a, b, (((1,), (1,)), ((), ())), preferred_element_type=F32)]
    ppermute x0 -> x15, starting transfers between devices: none -> 17.4 us  [the longest x11 11.2 us: across(): return lax.ppermute(x, 'tensor', [(i, i ^ r) for i in range(4)])]
    ppermute x0 -> x15, waiting for transfers between devices: none -> 12.7 us  [the longest x11 9.92 us: across(): return lax.ppermute(x, 'tensor', [(i, i ^ r) for i in range(4)])]
    unnamed x66 -> x24, local copies, waits for them, and re-layouts: 13.8 us -> 1.58 us
    unnamed x4 -> x0, starting transfers between devices: 11 us -> none
  transfers between devices with their start and end apart: 5 -> 15, of which waited for: 2 -> 6; matrix products, arithmetic and copies ran while one was open for 11% -> 4% of each run, Pallas kernels for 0% -> 33%
where the time goes in v1:
time: 64.8 us; the launch traced here: 64.5 us
  Pallas kernels  29.6 us (46%)
  starting transfers between devices  17.4 us (27%)
  waiting for transfers between devices  12.7 us (20%)
  local copies, waits for them, and re-layouts  1.69 us (3%)
  other arithmetic  1.47 us (2%)
  between operations  0.84 us (1%)
  matrix products  0.8 us (1%)
    pallas_call x2, Pallas kernels, projection_terms(): pl.pallas_call(functools.partial(terms_kernel, first), out_shape=outs, gr...  11.5 us
    ppermute x11, starting transfers between devices, across(): return lax.ppermute(x, 'tensor', [(i, i ^ r) for i in range(4)])  11.2 us
    pallas_call x2, Pallas kernels, attend_chunk(): pl.pallas_call(functools.partial(attend_kernel, start), out_shape=jax.Sha...  10.5 us
    ppermute x11, waiting for transfers between devices, across(): return lax.ppermute(x, 'tensor', [(i, i ^ r) for i in range(4)])  9.92 us
    ppermute x2, starting transfers between devices, along_line(): return lax.ppermute(x, 'dp', [(i, i ^ 2 * d) for i in range(count)])  5.67 us
    pallas_call x2, Pallas kernels, grad_half(): pl.pallas_call(kernel, out_shape=out, grid_spec=pltpu.PrefetchScalarGridS...  3.1 us
    ppermute x2, waiting for transfers between devices, along_line(): return lax.ppermute(x, 'dp', [(i, i ^ 2 * d) for i in range(count)])  2.46 us
    pallas_call x2, Pallas kernels, small_call(): pl.pallas_call(body, out_shape=outs, grid_spec=pltpu.PrefetchScalarGridSp...  2.1 us
  transfers between devices with their start and end apart: 15, of which 6 were waited for; matrix products, arithmetic and copies ran while one was open for 4% of the time, Pallas kernels for 33%

profile of v1, /device:TPU:0, one launch (start us, length us, event | category | flops | bytes accessed | tf_op | source)
XLA Modules:
  0.0 64.5 jit_solution(3281117977603399474)
XLA Ops:
  0.7 1.5 %pack_grads.1 = bf16[64,1536]{1,0:T(8,128)(2,1)S(1)} custom-call(s32[3]{0:T(128)S(1)} %pad_add_fusion.ids, f32[1,2,64,1280]{3,2,1,0:T(8,128)} %grad_a.3, f32[1,2,64,256]{3,2,1,0:T(8,128)} %grad_b.3), custom_call_target="tpu_custom_call" | custom-call | bytes 786432 | tf_op jit(solution)/shard_map/pack_grads/pallas_call | solution.py:267
  2.8 0.7 %add_convert_fusion = f32[60,4]{1,0:T(8,128)S(1)} fusion(s32[60]{0:T(128)} %param.23), kind=kLoop, calls=%fused_computation.6 | loop fusion | flops 480 | bytes 1200 | tf_op jit(solution)/shard_map/convert_element_type | solution.py:487
  3.9 1.6 %chip_grads.1.after.a = bf16[64,1536]{1,0:T(8,128)(2,1)S(1)} custom-call(s32[3]{0:T(128)S(1)} %pad_add_fusion.ids, f32[1,2,64,1280]{3,2,1,0:T(8,128)} %grad_a.3, f32[1,2,64,256]{3,2,1,0:T(8,128)} %grad_b.3, bf16[64,1536]{1,0:T(8,128)(2,1)S(1)} %collective-permute-done.other), custom_call_target="tpu_custom_call" | custom-call | bytes 786432 | tf_op jit(solution)/shard_map/chip_grads/pallas_call | solution.py:267
  5.4 3.0 %collective-permute-start.1 = (bf16[64,1536]{1,0:T(8,128)(2,1)S(1)}, bf16[64,1536]{1,0:T(8,128)(2,1)}, u32[]{:S(2)}, u32[]{:S(2)}) collective-permute-start(bf16[64,1536]{1,0:T(8,128)(2,1)S(1)} %chip_grads.1.after.a), channel_id=1, source_target_pairs={{0,8},{4,12},{8,0},{12,4},{16,24},{20,28},{24,16},{28,20},{1,9},{5... | collective-permute-start | bytes 589832 | tf_op jit(solution)/shard_map/ppermute | solution.py:328
  8.4 6.6 %projection_terms.2 = (bf16[960,1280]{1,0:T(8,128)(2,1)S(1)}, bf16[480,512]{1,0:T(8,128)(2,1)S(1)}, bf16[480,512]{1,0:T(8,128)(2,1)S(1)}, bf16[480,512]{1,0:T(8,...) custom-call(s32[3]{0:T(128)S(1)} %pad_add_fusion.ids, bf16[240,4,1280]{2,1,0:T(4,128)(2,1)} %hidden.1, ...), custom_call_target="tpu_custom_call" | custom-call | flops 2516582400 | bytes 6881280 | tf_op jit(solution)/shard_map/projection_terms/pallas_call | solution.py:204
  15.1 0.8 %copy-done.1 = bf16[480,512]{1,0:T(8,128)(2,1)} copy-done((bf16[480,512]{1,0:T(8,128)(2,1)}, bf16[480,512]{1,0:T(8,128)(2,1)S(1)}, u32[]{:S(2)}) %copy-start.1) | copy-done | bytes 491544
  16.6 1.5 %collective-permute-start.6 = (bf16[480,512]{1,0:T(8,128)(2,1)S(1)}, bf16[480,512]{1,0:T(8,128)(2,1)}, u32[]{:S(2)}, u32[]{:S(2)}) collective-permute-start(bf16[480,512]{1,0:T(8,128)(2,1)S(1)} %get-tuple-element.26.after), channel_id=1, source_target_pairs={{0,1},{1,0},{2,3},{3,2},{4,5},{5,4},{6,7},{7,6},{8,9},{9,8},{10,11... | collective-permute-start | bytes 1474568 | tf_op jit(solution)/shard_map/ppermute | solution.py:493
  18.1 1.5 %collective-permute-start.7 = (bf16[480,512]{1,0:T(8,128)(2,1)}, bf16[480,512]{1,0:T(8,128)(2,1)}, u32[]{:S(2)}, u32[]{:S(2)}) collective-permute-start(bf16[480,512]{1,0:T(8,128)(2,1)} %get-tuple-element.33), channel_id=1, source_target_pairs={{0,2},{1,3},{2,0},{3,1},{4,6},{5,7},{6,4},{7,5},{8,10},{9,11},{10,... | collective-permute-start | bytes 1474568 | tf_op jit(solution)/shard_map/ppermute | solution.py:493
  19.8 1.0 %plus.2.after.a = bf16[64,1536]{1,0:T(8,128)(2,1)S(1)} custom-call(bf16[64,1536]{1,0:T(8,128)(2,1)S(1)} %chip_grads.1.after.a, bf16[64,1536]{1,0:T(8,128)(2,1)} %collective-permute-done.1.b, bf16[480,512]{1,0:T(8,128)(2,1)S(1)} %get-tuple-element.26.after), custom_call_target="tpu_custom_call" | custom-call | bytes 589824 | tf_op jit(solution)/shard_map/plus/pallas_call | solution.py:315
  20.7 2.7 %collective-permute-start.4 = (bf16[64,1536]{1,0:T(8,128)(2,1)S(1)}, bf16[64,1536]{1,0:T(8,128)(2,1)S(1)}, u32[]{:S(2)}, u32[]{:S(2)}) collective-permute-start(bf16[64,1536]{1,0:T(8,128)(2,1)S(1)} %plus.2.after.a), channel_id=1, source_target_pairs={{0,16},{4,20},{8,24},{12,28},{16,0},{20,4},{24,8},{28,12},{1,17},{... | collective-permute-start | bytes 589832 | tf_op jit(solution)/shard_map/ppermute | solution.py:328
  23.4 4.9 %projection_terms.3 = (bf16[480,512]{1,0:T(8,128)(2,1)S(1)}, bf16[480,512]{1,0:T(8,128)(2,1)S(1)}, bf16[480,512]{1,0:T(8,128)(2,1)S(1)}, bf16[240,512]{1,0:T(8,128)(2,1)S(1)}, bf16[240,512]{1,0:T(8,128)(2,1)S(1)}) custom-call(s32[3]{0:T(128)S(1)} %pad_add_fusion.ids, bf16[960,1280]{1,0:T(8,128)(2,1)S(1)} %get-tuple-element.25.hidden, ...), custom_call_target="tpu_custom_call" | custom-call | flops 2516582400 | bytes 4423680 | tf_op jit(solution)/shard_map/projection_terms/pallas_call | solution.py:204
  29.4 2.5 %collective-permute-done.4.b = bf16[64,1536]{1,0:T(8,128)(2,1)S(1)} collective-permute-done((bf16[64,1536]{1,0:T(8,128)(2,1)S(1)}, bf16[64,1536]{1,0:T(8,128)(2,1)S(1)}, u32[]{:S(2)}, u32[]{:S(2)}) %collective-permute-start.4) | collective-permute-done | bytes 196640 | tf_op jit(solution)/shard_map/ppermute | solution.py:328
  32.1 1.2 %mid_sums.2 = (bf16[240,512]{1,0:T(8,128)(2,1)S(1)}, bf16[240,512]{1,0:T(8,128)(2,1)S(1)}) custom-call(bf16[480,512]{1,0:T(8,128)(2,1)S(1)} %copy-done.2, bf16[480,512]{1,0:T(8,128)(2,1)} %collective-permute-done.6.kcame.refs_4_, bf16[240,512]{1,0:T(8,128)(2,1)S(1)} %get-tuple-element.32.vkeep, bf16[480,512]{1,0:T(8,128)(2,1)} %collective-permute-done.7.vcame.refs_7_, ...), custom_call_target="tpu_custom_call" | custom-call | bytes 1474560 | tf_op jit(solution)/shard_map/mid_sums/pallas_call | solution.py:234
  33.3 1.9 %collective-permute-start.13 = (bf16[240,512]{1,0:T(8,128)(2,1)S(1)}, bf16[240,512]{1,0:T(8,128)(2,1)S(1)}, u32[]{:S(2)}, u32[]{:S(2)}) collective-permute-start(bf16[240,512]{1,0:T(8,128)(2,1)S(1)} %get-tuple-element.34.refs_4_), channel_id=1, source_target_pairs={{0,2},{1,3},{2,0},{3,1},{4,6},{5,7},{6,4},{7,5},{8,10},{9,11},{10,... | collective-permute-start | bytes 737288 | tf_op jit(solution)/shard_map/ppermute | solution.py:493
  35.3 1.5 %update_factors.1 = (f32[2,64,1280]{2,1,0:T(8,128)}, f32[2,64,256]{2,1,0:T(8,128)}, bf16[128,1280]{1,0:T(8,128)(2,1)S(1)}) custom-call(s32[3]{0:T(128)S(1)} %pad_add_fusion.ids, bf16[64,1536]{1,0:T(8,128)(2,1)S(1)} %plus.3.after.refs_0_, bf16[64,1536]{1,0:T(8,128)(2,1)S(1)} %collective-permute-done.5.refs_1_, f32[2,64,1280]{2,1,0:T(8,128)S(1)} %copy-done, ...), custom_call_target="tpu_custom_call" | custom-call | bytes 2293760 | tf_op jit(solution)/shard_map/update_factors/pallas_call | solution.py:288
  36.8 0.8 %fusion.refs_0_ = bf16[960,128]{1,0:T(8,128)(2,1)S(1)} fusion(bf16[960,1280]{1,0:T(8,128)(2,1)S(1)} %get-tuple-element.25.hidden, bf16[128,1280]{1,0:T(8,128)(2,1)S(1)} %get-tuple-element.35), kind=kOutput, calls=%fused_computation.1 | convolution fusion | flops 314818560 | bytes 3031040 | tf_op jit(solution)/shard_map/dot_general | solution.py:132
  38.3 2.1 %collective-permute-start.10 = (bf16[256,256]{1,0:T(8,128)(2,1)S(1)}, bf16[256,256]{1,0:T(8,128)(2,1)S(1)}, u32[]{:S(2)}, u32[]{:S(2)}) collective-permute-start(bf16[256,256]{1,0:T(8,128)(2,1)S(1)} %get-tuple-element.41), channel_id=1, source_target_pairs={{0,1},{1,0},{2,3},{3,2},{4,5},{5,4},{6,7},{7,6},{8,9},{9,8},{10,11... | collective-permute-start | bytes 393224 | tf_op jit(solution)/shard_map/ppermute | solution.py:493
  40.4 2.2 %collective-permute-done.2.kcame.refs_4_ = bf16[480,512]{1,0:T(8,128)(2,1)S(1)} collective-permute-done((bf16[480,512]{1,0:T(8,128)(2,1)S(1)}, bf16[480,512]{1,0:T(8,128)(2,1)S(1)}, u32[]{:S(2)}, u32[]{:S(2)}) %collective-permute-start.2) | collective-permute-done | bytes 491552 | tf_op jit(solution)/shard_map/ppermute | solution.py:493
  43.1 1.5 %collective-permute-start.12 = (bf16[256,256]{1,0:T(8,128)(2,1)S(1)}, bf16[256,256]{1,0:T(8,128)(2,1)S(1)}, u32[]{:S(2)}, u32[]{:S(2)}) collective-permute-start(bf16[256,256]{1,0:T(8,128)(2,1)S(1)} %get-tuple-element.43), channel_id=1, source_target_pairs={{0,3},{1,2},{2,1},{3,0},{4,7},{5,6},{6,5},{7,4},{8,11},{9,10},{10,... | collective-permute-start | bytes 393224 | tf_op jit(solution)/shard_map/ppermute | solution.py:493
  45.2 4.8 %collective-permute-done.10.refs_10_ = bf16[256,256]{1,0:T(8,128)(2,1)S(1)} collective-permute-done((bf16[256,256]{1,0:T(8,128)(2,1)S(1)}, bf16[256,256]{1,0:T(8,128)(2,1)S(1)}, u32[]{:S(2)}, u32[]{:S(2)}) %collective-permute-start.10) | collective-permute-done | bytes 131104 | tf_op jit(solution)/shard_map/ppermute | solution.py:493
  50.0 1.1 %collective-permute-start.8 = (bf16[240,512]{1,0:T(8,128)(2,1)S(1)}, bf16[240,512]{1,0:T(8,128)(2,1)S(1)}, u32[]{:S(2)}, u32[]{:S(2)}) collective-permute-start(bf16[240,512]{1,0:T(8,128)(2,1)S(1)} %get-tuple-element.38), channel_id=1, source_target_pairs={{0,2},{1,3},{2,0},{3,1},{4,6},{5,7},{6,4},{7,5},{8,10},{9,11},{10,... | collective-permute-start | bytes 737288 | tf_op jit(solution)/shard_map/ppermute | solution.py:493
  51.1 2.3 %collective-permute-done.11.refs_11_ = bf16[256,256]{1,0:T(8,128)(2,1)S(1)} collective-permute-done((bf16[256,256]{1,0:T(8,128)(2,1)S(1)}, bf16[256,256]{1,0:T(8,128)(2,1)S(1)}, u32[]{:S(2)}, u32[]{:S(2)}) %collective-permute-start.11) | collective-permute-done | bytes 131104 | tf_op jit(solution)/shard_map/ppermute | solution.py:493
  53.5 5.6 %attend_chunk.2.refs_15_ = bf16[60,4,4096]{2,1,0:T(4,128)(2,1)} custom-call(s32[3]{0:T(128)S(1)} %pad_add_fusion.ids, s32[60]{0:T(128)S(1)} %copy-done.10, bf16[60,4,4096]{2,1,0:T(4,128)(2,1)S(1)} %copy-done.5, bf16[60,16,1024]{2,1,0:T(8,128)(2,1)S(1)} %copy-done.6, bf16[60,16,1024]{2,1,0:T(8,128)(2,1)S(1)} %copy-done.7, bf16[480,512]{1,0:T(8,128)(2,1)S(1)} %copy-done.2, ...), custom_call_target="tpu_custom_call" | custom-call | flops 16000000000 | bytes 8880128 | tf_op jit(solution)/shard_map/attend_chunk/pallas_call | solution.py:470
  59.6 4.9 %attend_chunk.3 = bf16[60,4,4096]{2,1,0:T(4,128)(2,1)} custom-call(s32[3]{0:T(128)S(1)} %pad_add_fusion.ids, s32[60]{0:T(128)S(1)} %copy-done.10, bf16[60,4,4096]{2,1,0:T(4,128)(2,1)S(1)} %copy-done.5, bf16[60,16,1024]{2,1,0:T(8,128)(2,1)S(1)} %copy-done.6, bf16[60,16,1024]{2,1,0:T(8,128)(2,1)S(1)} %copy-done.7, ...), custom_call_target="tpu_custom_call", output_to_operand_aliasing={{}: (17, {})} | custom-call | flops 16000000000 | bytes 10846208 | tf_op jit(solution)/shard_map/attend_chunk/pallas_call | solution.py:470
  (50 shorter events, 5.6 us)
Async XLA Ops:
  2.3 1.6 %collective-permute-start = (bf16[64,1536]{1,0:T(8,128)(2,1)S(1)}, bf16[64,1536]{1,0:T(8,128)(2,1)S(1)}, u32[]{:S(2)}, u32[]{:S(2)}) collective-permute-start(bf16[64,1536]{1,0:T(8,128)(2,1)S(1)} %pack_grads.1), channel_id=1, source_target_pairs={{0,4},{4,0},{8,12},{12,8},{16,20},{20,16},{24,28},{28,24},{1,5},{5... | collective-permute-start | bytes 589832 | tf_op jit(solution)/shard_map/ppermute | solution.py:305
  5.4 14.1 %copy-start.11 = (f32[128]{0:T(128)S(1)}, f32[128]{0:T(128)}, u32[]{:S(2)}) copy-start(f32[128]{0:T(128)} %param.18) | copy-start | bytes 1540
  5.4 14.3 %collective-permute-start.1 = (bf16[64,1536]{1,0:T(8,128)(2,1)S(1)}, bf16[64,1536]{1,0:T(8,128)(2,1)}, u32[]{:S(2)}, u32[]{:S(2)}) collective-permute-start(bf16[64,1536]{1,0:T(8,128)(2,1)S(1)} %chip_grads.1.after.a), channel_id=1, source_target_pairs={{0,8},{4,12},{8,0},{12,4},{16,24},{20,28},{24,16},{28,20},{1,9},{5... | collective-permute-start | bytes 589832 | tf_op jit(solution)/shard_map/ppermute | solution.py:328
  16.6 15.6 %collective-permute-start.6 = (bf16[480,512]{1,0:T(8,128)(2,1)S(1)}, bf16[480,512]{1,0:T(8,128)(2,1)}, u32[]{:S(2)}, u32[]{:S(2)}) collective-permute-start(bf16[480,512]{1,0:T(8,128)(2,1)S(1)} %get-tuple-element.26.after), channel_id=1, source_target_pairs={{0,1},{1,0},{2,3},{3,2},{4,5},{5,4},{6,7},{7,6},{8,9},{9,8},{10,11... | collective-permute-start | bytes 1474568 | tf_op jit(solution)/shard_map/ppermute | solution.py:493
  18.1 14.1 %collective-permute-start.7 = (bf16[480,512]{1,0:T(8,128)(2,1)}, bf16[480,512]{1,0:T(8,128)(2,1)}, u32[]{:S(2)}, u32[]{:S(2)}) collective-permute-start(bf16[480,512]{1,0:T(8,128)(2,1)} %get-tuple-element.33), channel_id=1, source_target_pairs={{0,2},{1,3},{2,0},{3,1},{4,6},{5,7},{6,4},{7,5},{8,10},{9,11},{10,... | collective-permute-start | bytes 1474568 | tf_op jit(solution)/shard_map/ppermute | solution.py:493
  20.7 11.2 %collective-permute-start.4 = (bf16[64,1536]{1,0:T(8,128)(2,1)S(1)}, bf16[64,1536]{1,0:T(8,128)(2,1)S(1)}, u32[]{:S(2)}, u32[]{:S(2)}) collective-permute-start(bf16[64,1536]{1,0:T(8,128)(2,1)S(1)} %plus.2.after.a), channel_id=1, source_target_pairs={{0,16},{4,20},{8,24},{12,28},{16,0},{20,4},{24,8},{28,12},{1,17},{... | collective-permute-start | bytes 589832 | tf_op jit(solution)/shard_map/ppermute | solution.py:328
  23.4 8.7 %copy-start.2 = (bf16[480,512]{1,0:T(8,128)(2,1)S(1)}, bf16[480,512]{1,0:T(8,128)(2,1)}, u32[]{:S(2)}) copy-start(bf16[480,512]{1,0:T(8,128)(2,1)} %copy-done.1) | copy-start | bytes 1474564
  28.3 7.0 %copy-start = (f32[2,64,1280]{2,1,0:T(8,128)S(1)}, f32[2,64,1280]{2,1,0:T(8,128)}, u32[]{:S(2)}) copy-start(f32[2,64,1280]{2,1,0:T(8,128)} %refs_2_.3) | copy-start | bytes 1966084
  28.3 7.0 %copy-start.4 = (f32[2,64,256]{2,1,0:T(8,128)S(1)}, f32[2,64,256]{2,1,0:T(8,128)}, u32[]{:S(2)}) copy-start(f32[2,64,256]{2,1,0:T(8,128)} %refs_3_.1) | copy-start | bytes 393220
  28.3 14.2 %collective-permute-start.2 = (bf16[480,512]{1,0:T(8,128)(2,1)S(1)}, bf16[480,512]{1,0:T(8,128)(2,1)S(1)}, u32[]{:S(2)}, u32[]{:S(2)}) collective-permute-start(bf16[480,512]{1,0:T(8,128)(2,1)S(1)} %get-tuple-element.28.after), channel_id=1, source_target_pairs={{0,1},{1,0},{2,3},{3,2},{4,5},{5,4},{6,7},{7,6},{8,9},{9,8},{10,11... | collective-permute-start | bytes 1474568 | tf_op jit(solution)/shard_map/ppermute | solution.py:493
  28.9 14.2 %collective-permute-start.3 = (bf16[480,512]{1,0:T(8,128)(2,1)S(1)}, bf16[480,512]{1,0:T(8,128)(2,1)S(1)}, u32[]{:S(2)}, u32[]{:S(2)}) collective-permute-start(bf16[480,512]{1,0:T(8,128)(2,1)S(1)} %get-tuple-element.30), channel_id=1, source_target_pairs={{0,2},{1,3},{2,0},{3,1},{4,6},{5,7},{6,4},{7,5},{8,10},{9,11},{10,... | collective-permute-start | bytes 1474568 | tf_op jit(solution)/shard_map/ppermute | solution.py:493
  32.0 3.3 %collective-permute-start.5 = (bf16[64,1536]{1,0:T(8,128)(2,1)S(1)}, bf16[64,1536]{1,0:T(8,128)(2,1)S(1)}, u32[]{:S(2)}, u32[]{:S(2)}) collective-permute-start(bf16[64,1536]{1,0:T(8,128)(2,1)S(1)} %plus.3.after.refs_0_), channel_id=1, source_target_pairs={{0,4},{4,0},{8,12},{12,8},{16,20},{20,16},{24,28},{28,24},{1,5},{5... | collective-permute-start | bytes 589832 | tf_op jit(solution)/shard_map/ppermute | solution.py:305
  33.3 20.1 %collective-permute-start.13 = (bf16[240,512]{1,0:T(8,128)(2,1)S(1)}, bf16[240,512]{1,0:T(8,128)(2,1)S(1)}, u32[]{:S(2)}, u32[]{:S(2)}) collective-permute-start(bf16[240,512]{1,0:T(8,128)(2,1)S(1)} %get-tuple-element.34.refs_4_), channel_id=1, source_target_pairs={{0,2},{1,3},{2,0},{3,1},{4,6},{5,7},{6,4},{7,5},{8,10},{9,11},{10,... | collective-permute-start | bytes 737288 | tf_op jit(solution)/shard_map/ppermute | solution.py:493
  35.3 18.2 %collective-permute-start.14 = (bf16[240,512]{1,0:T(8,128)(2,1)S(1)}, bf16[240,512]{1,0:T(8,128)(2,1)S(1)}, u32[]{:S(2)}, u32[]{:S(2)}) collective-permute-start(bf16[240,512]{1,0:T(8,128)(2,1)S(1)} %get-tuple-element.45), channel_id=1, source_target_pairs={{0,1},{1,0},{2,3},{3,2},{4,5},{5,4},{6,7},{7,6},{8,9},{9,8},{10,11... | collective-permute-start | bytes 737288 | tf_op jit(solution)/shard_map/ppermute | solution.py:493
  36.8 16.6 %copy-start.6 = (bf16[60,16,1024]{2,1,0:T(8,128)(2,1)S(1)}, bf16[60,16,1024]{2,1,0:T(8,128)(2,1)}, u32[]{:S(2)}) copy-start(bf16[60,16,1024]{2,1,0:T(8,128)(2,1)} %refs_1_.3) | copy-start | bytes 5898244
  36.8 16.6 %copy-start.7 = (bf16[60,16,1024]{2,1,0:T(8,128)(2,1)S(1)}, bf16[60,16,1024]{2,1,0:T(8,128)(2,1)}, u32[]{:S(2)}) copy-start(bf16[60,16,1024]{2,1,0:T(8,128)(2,1)} %refs_2_.5) | copy-start | bytes 5898244
  37.6 15.8 %copy-start.5 = (bf16[60,4,4096]{2,1,0:T(4,128)(2,1)S(1)}, bf16[60,4,4096]{2,1,0:T(4,128)(2,1)}, u32[]{:S(2)}) copy-start(bf16[60,4,4096]{2,1,0:T(4,128)(2,1)} %refs_0_.3) | copy-start | bytes 5898244
  37.6 15.8 %copy-start.9 = (bf16[240,512]{1,0:T(8,128)(2,1)S(1)}, bf16[240,512]{1,0:T(8,128)(2,1)}, u32[]{:S(2)}) copy-start(bf16[240,512]{1,0:T(8,128)(2,1)} %copy-done.8) | copy-start | bytes 737284
  37.6 15.8 %copy-start.10 = (s32[60]{0:T(128)S(1)}, s32[60]{0:T(128)}, u32[]{:S(2)}) copy-start(s32[60]{0:T(128)} %lengths.3) | copy-start | bytes 724
  38.3 11.7 %collective-permute-start.10 = (bf16[256,256]{1,0:T(8,128)(2,1)S(1)}, bf16[256,256]{1,0:T(8,128)(2,1)S(1)}, u32[]{:S(2)}, u32[]{:S(2)}) collective-permute-start(bf16[256,256]{1,0:T(8,128)(2,1)S(1)} %get-tuple-element.41), channel_id=1, source_target_pairs={{0,1},{1,0},{2,3},{3,2},{4,5},{5,4},{6,7},{7,6},{8,9},{9,8},{10,11... | collective-permute-start | bytes 393224 | tf_op jit(solution)/shard_map/ppermute | solution.py:493
  42.6 10.9 %collective-permute-start.11 = (bf16[256,256]{1,0:T(8,128)(2,1)S(1)}, bf16[256,256]{1,0:T(8,128)(2,1)S(1)}, u32[]{:S(2)}, u32[]{:S(2)}) collective-permute-start(bf16[256,256]{1,0:T(8,128)(2,1)S(1)} %get-tuple-element.42), channel_id=1, source_target_pairs={{0,2},{1,3},{2,0},{3,1},{4,6},{5,7},{6,4},{7,5},{8,10},{9,11},{10,... | collective-permute-start | bytes 393224 | tf_op jit(solution)/shard_map/ppermute | solution.py:493
  43.1 10.3 %collective-permute-start.12 = (bf16[256,256]{1,0:T(8,128)(2,1)S(1)}, bf16[256,256]{1,0:T(8,128)(2,1)S(1)}, u32[]{:S(2)}, u32[]{:S(2)}) collective-permute-start(bf16[256,256]{1,0:T(8,128)(2,1)S(1)} %get-tuple-element.43), channel_id=1, source_target_pairs={{0,3},{1,2},{2,1},{3,0},{4,7},{5,6},{6,5},{7,4},{8,11},{9,10},{10,... | collective-permute-start | bytes 393224 | tf_op jit(solution)/shard_map/ppermute | solution.py:493
  50.0 9.0 %collective-permute-start.8 = (bf16[240,512]{1,0:T(8,128)(2,1)S(1)}, bf16[240,512]{1,0:T(8,128)(2,1)S(1)}, u32[]{:S(2)}, u32[]{:S(2)}) collective-permute-start(bf16[240,512]{1,0:T(8,128)(2,1)S(1)} %get-tuple-element.38), channel_id=1, source_target_pairs={{0,2},{1,3},{2,0},{3,1},{4,6},{5,7},{6,4},{7,5},{8,10},{9,11},{10,... | collective-permute-start | bytes 737288 | tf_op jit(solution)/shard_map/ppermute | solution.py:493
  53.4 6.2 %collective-permute-start.9 = (bf16[240,512]{1,0:T(8,128)(2,1)S(1)}, bf16[240,512]{1,0:T(8,128)(2,1)S(1)}, u32[]{:S(2)}, u32[]{:S(2)}) collective-permute-start(bf16[240,512]{1,0:T(8,128)(2,1)S(1)} %get-tuple-element.40), channel_id=1, source_target_pairs={{0,1},{1,0},{2,3},{3,2},{4,5},{5,4},{6,7},{7,6},{8,9},{9,8},{10,11... | collective-permute-start | bytes 737288 | tf_op jit(solution)/shard_map/ppermute | solution.py:493
  (3 other events, 2.4 us)

commit v2 on v1

--- a/solution.py
+++ b/solution.py
@@ -143,82 +143,110 @@
 TILE = 256
 
 
-def terms_kernel(first, ids, hidden, wk, wv, after, *outs):
-    del after
+def terms_kernel(first, ids, hidden, weight, *rest):
+    *outs, w, sems = rest[1:]
+    wide = w.shape[1] * TILE
+    start = 0 if first else weight.shape[2] - wide
+    tiles = w.shape[1]
+
+    def weight_copy(p, i):
+        at = pl.ds(start + i * TILE, TILE)
+        return pltpu.make_async_copy(weight.at[p, :, at], w.at[p, i], sems.at[p, i])
+
     if first:
-        x, *outs = outs
+        x, *outs, held, hidden_sems = outs
         tokens = x.shape[0] // 4
-
-        @pl.when(pl.program_id(0) == 0)
-        def _():
-            for r in range(4):
-                at = pl.ds((ids[0] ^ r) * (tokens // STEPS), tokens // STEPS)
-                x[r * tokens : (r + 1) * tokens] = hidden[at].reshape(tokens, x.shape[1])
-
+        rows = tokens // STEPS
+
+        def hidden_copy(r):
+            at = pl.ds((ids[0] ^ r) * rows, rows)
+            return pltpu.make_async_copy(hidden.at[at], held.at[r], hidden_sems.at[r])
+
+        for r in range(4):
+            hidden_copy(r).start()
     else:
         x = hidden
         tokens = x.shape[0] // 4
+    for i in range(tiles):
+        for p in range(2):
+            weight_copy(p, i).start()
+    if first:
+        for r in range(4):
+            hidden_copy(r).wait()
+            x[r * tokens : (r + 1) * tokens] = held[r].reshape(tokens, x.shape[1])
     ksend, kkeep, vsend, vkeep0, vkeep1 = outs
     steps = x.shape[1] // TILE
 
-    def push(k):
-        at = slice(k * TILE, (k + 1) * TILE)
-        pltpu.matmul_push_rhs(wk[0, at, :], k % 2, 0)
-        pltpu.matmul_push_rhs(wv[0, at, :], k % 2, 1)
-
     def multiply(*accs):
         accs_k, accs_v = accs[:4], accs[4:]
-        push(0)
-        for k in range(steps):
-            if k + 1 < steps:
-                push(k + 1)
-            for r in range(4):
-                rows = x[r * tokens : (r + 1) * tokens, k * TILE : (k + 1) * TILE]
-                staged = k % 2 if r == 0 else None
-                pltpu.matmul_acc_lhs(accs_k[r], rows, load_staged_rhs=staged)
-                pltpu.matmul_acc_lhs(accs_v[r], rows, load_staged_rhs=staged)
-        key = [pltpu.matmul_pop(acc).astype(BF) for acc in accs_k]
-        value = [pltpu.matmul_pop(acc).astype(BF) for acc in accs_v]
-        kkeep[:tokens], kkeep[tokens:] = key[0], key[2]
-        ksend[:tokens], ksend[tokens:] = key[3], key[1]
-        vkeep0[...], vkeep1[...] = value[0], value[1]
-        vsend[:tokens], vsend[tokens:] = value[2], value[3]
+
+        @pl.loop(0, tiles)
+        def _(i):
+            for p in range(2):
+                weight_copy(p, i).wait()
+
+            def push(k):
+                for p in range(2):
+                    pltpu.matmul_push_rhs(w[p, i, k * TILE : (k + 1) * TILE, :], k % 2, p)
+
+            push(0)
+            for k in range(steps):
+                if k + 1 < steps:
+                    push(k + 1)
+                for r in range(4):
+                    rows = x[r * tokens : (r + 1) * tokens, k * TILE : (k + 1) * TILE]
+                    staged = k % 2 if r == 0 else None
+                    pltpu.matmul_acc_lhs(accs_k[r], rows, load_staged_rhs=staged)
+                    pltpu.matmul_acc_lhs(accs_v[r], rows, load_staged_rhs=staged)
+            at = pl.ds(pl.multiple_of(i * TILE, TILE), TILE)
+            low, high = slice(0, tokens), slice(tokens, 2 * tokens)
+            kkeep[low, at] = pltpu.matmul_pop(accs_k[0]).astype(BF)
+            vkeep0[:, at] = pltpu.matmul_pop(accs_v[0]).astype(BF)
+            ksend[high, at] = pltpu.matmul_pop(accs_k[1]).astype(BF)
+            vkeep1[:, at] = pltpu.matmul_pop(accs_v[1]).astype(BF)
+            kkeep[high, at] = pltpu.matmul_pop(accs_k[2]).astype(BF)
+            vsend[low, at] = pltpu.matmul_pop(accs_v[2]).astype(BF)
+            ksend[low, at] = pltpu.matmul_pop(accs_k[3]).astype(BF)
+            vsend[high, at] = pltpu.matmul_pop(accs_v[3]).astype(BF)
 
     pl.run_scoped(
         multiply, *[pltpu.ACC(unit)((tokens, TILE), F32) for unit in range(2) for _ in range(4)]
     )
 
 
-def projection_terms(ids, hidden, kv_weight, start, count, tokens, after):
+def projection_terms(ids, hidden, kv_weight, count, tokens, after):
     first = len(hidden.shape) == 3
     width = hidden.shape[-1]
     wide = count * HD
-    base = start * HD // TILE
-    assert wide % TILE == 0 and start * HD % TILE == 0 and width % TILE == 0
+    assert wide % TILE == 0 and width % TILE == 0
     rows = (2, 2, 2, 1, 1)
     outs = [jax.ShapeDtypeStruct((n * tokens, wide), BF) for n in rows]
-    specs = [pl.BlockSpec((n * tokens, TILE), lambda i, _: (0, i)) for n in rows]
+    scratch = []
     if first:
         outs.insert(0, jax.ShapeDtypeStruct((4 * tokens, width), BF))
-        specs.insert(0, whole(outs[0].shape))
+        scratch += [
+            pltpu.VMEM((4, tokens // STEPS, STEPS, width), BF),
+            pltpu.SemaphoreType.DMA((4,)),
+        ]
+    scratch += [
+        pltpu.VMEM((2, wide // TILE, width, TILE), BF),
+        pltpu.SemaphoreType.DMA((2, wide // TILE)),
+    ]
+    here = pl.BlockSpec(memory_space=pl.ANY)
     return pl.pallas_call(
         functools.partial(terms_kernel, first),
         out_shape=outs,
         grid_spec=pltpu.PrefetchScalarGridSpec(
             num_scalar_prefetch=1,
-            grid=(wide // TILE,),
-            in_specs=[
-                whole(hidden.shape),
-                pl.BlockSpec((1, width, TILE), lambda i, _: (0, 0, base + i)),
-                pl.BlockSpec((1, width, TILE), lambda i, _: (1, 0, base + i)),
-                pl.BlockSpec(memory_space=pl.ANY),
-            ],
-            out_specs=specs,
+            grid=(1,),
+            in_specs=[here if first else whole(hidden.shape), here, here],
+            out_specs=[whole(x.shape) for x in outs],
+            scratch_shapes=scratch,
         ),
         compiler_params=params(),
         cost_estimate=cost(2 * 4 * tokens * width * 2 * wide, [hidden], outs),
         name="projection_terms",
-    )(ids, hbm(hidden) if first else hidden, hbm(kv_weight), hbm(kv_weight), after)
+    )(ids, hbm(hidden) if first else hidden, hbm(kv_weight), after)
 
 
 def mid_kernel(kkeep, kcame, vkeep, vcame, after, kout, vout):
@@ -243,8 +271,8 @@
     )(kkeep, kcame, vkeep, vcame, after)
 
 
-def pack_kernel(ids, grad_a, grad_b, out):
-    del ids
+def pack_kernel(ids, grad_a, grad_b, after, out, unwritten):
+    del ids, after, unwritten
     wide = grad_a.shape[-1]
     out[:, :wide] = grad_a[0, 0].astype(BF)
     out[:, wide:] = grad_b[0, 0].astype(BF)
@@ -257,7 +285,7 @@
     out[:, wide:] = (grad_b[0, 0] + other[:, wide:].astype(F32)).astype(BF)
 
 
-def grad_half(kernel, name, ids, grad_a, grad_b, flip, *rest):
+def grad_half(kernel, name, ids, grad_a, grad_b, flip, rest, rest_specs, more_outs=()):
     rank, wide = grad_a.shape[2], grad_a.shape[3] + grad_b.shape[3]
 
     def spec(x):
@@ -266,12 +294,12 @@
     out = jax.ShapeDtypeStruct((rank, wide), BF)
     return pl.pallas_call(
         kernel,
-        out_shape=out,
+        out_shape=[out, *more_outs],
         grid_spec=pltpu.PrefetchScalarGridSpec(
             num_scalar_prefetch=1,
             grid=(1,),
-            in_specs=[spec(grad_a), spec(grad_b)] + [whole(x.shape) for x in rest],
-            out_specs=whole(out.shape),
+            in_specs=[spec(grad_a), spec(grad_b), *rest_specs],
+            out_specs=[whole(out.shape)] + [pl.BlockSpec(memory_space=pl.ANY)] * len(more_outs),
         ),
         compiler_params=params(),
         cost_estimate=cost(0, [out] * 4, []),
@@ -279,7 +307,7 @@
     )(ids, hbm(grad_a), hbm(grad_b), *rest)
 
 
-def small_call(kernel, name, ids, args, outs, after=()):
+def small_call(kernel, name, ids, args, outs, after=(), scratch=()):
     count = len(args)
 
     def body(ids, *refs):
@@ -294,9 +322,10 @@
             in_specs=[whole(x.shape) for x in args]
             + [pl.BlockSpec(memory_space=pl.ANY)] * len(after),
             out_specs=[whole(x.shape) for x in outs],
+            scratch_shapes=list(scratch),
         ),
         compiler_params=params(),
-        cost_estimate=cost(0, args, outs),
+        cost_estimate=cost(0, args, []),
         name=name,
     )(ids, *args, *after)
 
@@ -331,50 +360,60 @@
 TOP = 2 * R
 
 
-def update_kernel(rates, ids, half, other, factor_a, factor_b, new_a, new_b, a):
+def update_kernel(rates, ids, half, other, factor_a, factor_b, x, new_a, new_b, *rest):
+    *sends, a = rest
     wide = factor_a.shape[-1]
     for index, part in ((ids[2], half), (ids[2] ^ 1, other)):
         new_a[index] = factor_a[index] - rates[0] * part[:, :wide].astype(F32)
         new_b[index] = factor_b[index] - rates[1] * part[:, wide:].astype(F32)
     for p in range(2):
         a[p * R : (p + 1) * R] = new_a[p].astype(BF)
-
-
-def updated(ids, half, other, factor_a, factor_b, dp, after):
+    a[TOP:] = jnp.zeros((TILE - TOP, wide), BF)
+    tokens = x.shape[0] // 4
+
+    def multiply(*accs):
+        steps = wide // TILE
+
+        def push(k):
+            for unit in range(2):
+                tile = a[:, k * TILE : (k + 1) * TILE]
+                pltpu.matmul_push_rhs(tile, k % 2, unit, transpose=True)
+
+        push(0)
+        for k in range(steps):
+            if k + 1 < steps:
+                push(k + 1)
+            for r in range(4):
+                rows = x[r * tokens : (r + 1) * tokens, k * TILE : (k + 1) * TILE]
+                staged = k % 2 if r < 2 else None
+                pltpu.matmul_acc_lhs(accs[r], rows, load_staged_rhs=staged)
+        for r, send in enumerate(sends):
+            u = (0.25 * pltpu.matmul_pop(accs[r])[:, :TOP]).astype(BF)
+            for p in range(2):
+                send[p * R : (p + 1) * R, :] = new_b[p].astype(BF)
+            send[TOP:, :TOP] = u[:TOP]
+            send[TOP:tokens, TOP:] = u[TOP:]
+            send[tokens:, TOP:] = jnp.zeros((2 * TOP - tokens, TOP), BF)
+
+    pl.run_scoped(multiply, *[pltpu.ACC(r % 2)((tokens, TILE), F32) for r in range(4)])
+
+
+def updated(ids, half, other, factor_a, factor_b, x, dp, after):
     rates = (2.0 / math.sqrt(dp * D), 2.0 / math.sqrt(dp * R))
-    outs = [
-        jax.ShapeDtypeStruct(factor_a.shape, F32),
-        jax.ShapeDtypeStruct(factor_b.shape, F32),
-        jax.ShapeDtypeStruct((2 * R, factor_a.shape[2]), BF),
-    ]
+    outs = [pltpu.VMEM(f.shape, F32) for f in (factor_a, factor_b)]
+    outs += [jax.ShapeDtypeStruct((2 * TOP, 2 * TOP), BF)] * 4
     return small_call(
         functools.partial(update_kernel, rates),
         "update_factors",
         ids,
-        (half, other, factor_a, factor_b),
+        (half, other, factor_a, factor_b, x),
         outs,
         (after,),
-    )
-
-
-def payload_kernel(ids, u, new_b, *sends):
-    del ids
-    tokens = u.shape[0] // 4
-    for r, out in enumerate(sends):
-        first = r * tokens
-        for p in range(2):
-            out[p * R : (p + 1) * R, :] = new_b[p].astype(BF)
-        out[TOP:, :TOP] = u[first : first + TOP]
-        out[TOP:tokens, TOP:] = u[first + TOP : first + tokens]
-        out[tokens:, TOP:] = jnp.zeros((2 * TOP - tokens, TOP), BF)
-
-
-def payloads(ids, u, new_b):
-    outs = [jax.ShapeDtypeStruct((2 * TOP, 2 * TOP), BF)] * 4
-    return small_call(payload_kernel, "pack_terms", ids, (u, new_b), outs)
-
-
-def attend_kernel(start, ids, lengths, *refs):
+        [pltpu.VMEM((TILE, factor_a.shape[-1]), BF)],
+    )
+
+
+def attend_kernel(ids, first, lengths, *refs):
     q, cache_k, cache_v, k0, k1, k2, v0, v1, v2, *ub, cosine, sine = refs[:15]
     out = refs[-1]
     rows, slots, _ = cache_k.shape
@@ -382,7 +421,7 @@
     u_top = sum(x[TOP:, :TOP].astype(F32) for x in ub)
     u_low = sum(x[TOP:tokens, TOP:].astype(F32) for x in ub)
     u = jnp.concatenate([u_top, u_low], axis=0).astype(BF)
-    rel = ids[0] ^ (start // HEADS_STEP + pl.program_id(0))
+    rel = ids[0] ^ (first[0] + pl.program_id(0))
     low = jnp.where(rel == 0, ub[0][:TOP].astype(F32), ub[1][:TOP].astype(F32))
     high = jnp.where(rel == 2, ub[2][:TOP].astype(F32), ub[3][:TOP].astype(F32))
     b = jnp.where(rel < 2, low, high).astype(BF)
@@ -454,30 +493,27 @@
     heads = QH // KVH
     args = [queries, cache_keys, cache_values, *terms, *ub, *tables]
     assert start % HEADS_STEP == 0 and count % HEADS_STEP == 0
-    first = start // HEADS_STEP
+    first = jnp.full((1,), start // HEADS_STEP, jnp.int32)
     size = HEADS_STEP * HD
     part = pl.BlockSpec((tokens, size), lambda i, *_: (0, i))
     low = pl.BlockSpec((tokens, size), lambda i, *_: (1, i))
-    cache = pl.BlockSpec((rows, slots, size), lambda i, *_: (0, 0, first + i))
-    wide = pl.BlockSpec((rows, STEPS, heads * size), lambda i, *_: (0, 0, first + i))
+    cache = pl.BlockSpec((rows, slots, size), lambda i, _, first, *__: (0, 0, first[0] + i))
+    wide = pl.BlockSpec((rows, STEPS, heads * size), lambda i, _, first, *__: (0, 0, first[0] + i))
     specs = [wide, cache, cache, part, low, part, part, part, part]
     specs += [whole(x.shape) for x in (*ub, *tables)]
-    aliases = {}
-    if before is not None:
-        args.append(before)
-        specs.append(pl.BlockSpec(memory_space=pl.ANY))
-        aliases = {len(args) + 1: 0}
+    args.append(before)
+    specs.append(pl.BlockSpec(memory_space=pl.ANY))
     return pl.pallas_call(
-        functools.partial(attend_kernel, start),
+        attend_kernel,
         out_shape=jax.ShapeDtypeStruct(queries.shape, BF),
         grid_spec=pltpu.PrefetchScalarGridSpec(
-            num_scalar_prefetch=2, grid=(count // HEADS_STEP,), in_specs=specs, out_specs=wide
+            num_scalar_prefetch=3, grid=(count // HEADS_STEP,), in_specs=specs, out_specs=wide
         ),
-        input_output_aliases=aliases,
+        input_output_aliases={len(args) + 2: 0},
         compiler_params=params(),
         cost_estimate=cost(count * 4 * 10**9, args, []),
         name="attend_chunk",
-    )(ids, lengths, *args)
+    )(ids, first, lengths, *args)
 
 
 def rotary_tables(key_gain, positions):
@@ -513,16 +549,33 @@
     ids = jnp.stack([lax.axis_index("tensor"), dp // 2, dp % 2]).astype(jnp.int32)
     tables = rotary_tables(key_gain, positions)
 
-    packed = grad_half(pack_kernel, "pack_grads", ids, grad_a, grad_b, 1)
+    x, *first = projection_terms(ids, hidden_in, kv_weight, CHUNKS[0], tokens, ids)
+    here = pl.BlockSpec(memory_space=pl.ANY)
+    packed, attended = grad_half(
+        pack_kernel,
+        "pack_grads",
+        ids,
+        grad_a,
+        grad_b,
+        1,
+        [first[0]],
+        [here],
+        [jax.ShapeDtypeStruct(queries.shape, BF)],
+    )
     other = core_flip(packed, count_dp)
-    half = grad_half(chip_kernel, "chip_grads", ids, grad_a, grad_b, 0, other)
-    x, *first = projection_terms(ids, hidden_in, kv_weight, 0, CHUNKS[0], tokens, half)
-    step, before = 1, first[0]
+    (half,) = grad_half(
+        chip_kernel, "chip_grads", ids, grad_a, grad_b, 0, [other], [whole(other.shape)]
+    )
+    step = 1
     while 4 * step < count_dp:
-        half = plus(half, along_line(half, step, count_dp), before)
-        step, before = 2 * step, half
-    second = projection_terms(ids, x, kv_weight, CHUNKS[0], CHUNKS[1], tokens, half)
-    if step * 2 < count_dp:
+        came = along_line(half, step, count_dp)
+        if step == 1:
+            second = projection_terms(ids, x, kv_weight, CHUNKS[1], tokens, half)
+        half = plus(half, came, second[0])
+        step *= 2
+    if step == 1:
+        second = projection_terms(ids, x, kv_weight, CHUNKS[1], tokens, half)
+    if 2 * step < count_dp:
         half = plus(half, along_line(half, step, count_dp), second[0])
     other = core_flip(half, count_dp)
 
@@ -538,11 +591,11 @@
 
     mids, parts = first_exchange(first, half)
     first = second_exchange(mids, parts)
-    new_a, new_b, a = updated(ids, half, other, factor_a, factor_b, count_dp, mids[0])
-    sends = payloads(ids, (0.25 * dot_t(x, a)).astype(BF), new_b)
+    new_a, new_b, *sends = updated(
+        ids, half, other, factor_a, factor_b, x, count_dp, mids[0]
+    )
     ub = [sends[0]] + [across(sends[r], r) for r in (1, 2, 3)]
     second = second_exchange(*first_exchange(second, sends[0]))
-    attended = None
     for start, count, came in ((0, CHUNKS[0], first), (CHUNKS[0], CHUNKS[1], second)):
         attended = attend_chunk(
             ids,

time: 64.8 us -> 65.8 us (1.015)
  local copies, waits for them, and re-layouts: 1.69 us -> 5.93 us
  waiting for transfers between devices: 12.7 us -> 8.48 us
  Pallas kernels: 29.6 us -> 30.5 us
  matrix products: 0.8 us -> 0 us
    ppermute x11, waiting for transfers between devices: 9.92 us -> 0.03 us  [across(): return lax.ppermute(x, 'tensor', [(i, i ^ r) for i in range(4)])]
    ppermute x2, waiting for transfers between devices: 2.46 us -> 8.44 us  [along_line(): return lax.ppermute(x, 'dp', [(i, i ^ 2 * d) for i in range(count)])]
    unnamed x24 -> x42, local copies, waits for them, and re-layouts: 1.58 us -> 5.07 us
    ppermute x11, starting transfers between devices: 11.2 us -> 13.1 us  [across(): return lax.ppermute(x, 'tensor', [(i, i ^ r) for i in range(4)])]
    ppermute x2, starting transfers between devices: 5.67 us -> 4.3 us  [along_line(): return lax.ppermute(x, 'dp', [(i, i ^ 2 * d) for i in range(count)])]
    pallas_call x2, Pallas kernels: 1.02 us -> 0.1 us  [plus(): pl.pallas_call(plus_kernel, out_shape=out, grid=(1,), in_specs=[whole(a.s...]
    pallas_call x2, Pallas kernels: 1.31 us -> 2.22 us  [mid_sums(): pl.pallas_call(mid_kernel, out_shape=[jax.ShapeDtypeStruct(shape, BF)] *...]
    dot_general x1 -> x0, matrix products: 0.8 us -> none  [dot_t(): lax.dot_general(a, b, (((1,), (1,)), ((), ())), preferred_element_type=F32)]
  transfers between devices with their start and end apart: 15 -> 15, of which waited for: 6 -> 1; matrix products, arithmetic and copies ran while one was open for 4% -> 6% of each run, Pallas kernels for 33% -> 27%
where the time goes in v2:
time: 65.8 us; the launch traced here: 65.3 us
  Pallas kernels  30.5 us (46%)
  starting transfers between devices  18 us (27%)
  waiting for transfers between devices  8.48 us (13%)
  local copies, waits for them, and re-layouts  5.93 us (9%)
  other arithmetic  1.44 us (2%)
  between operations  0.95 us (1%)
    ppermute x11, starting transfers between devices, across(): return lax.ppermute(x, 'tensor', [(i, i ^ r) for i in range(4)])  13.1 us
    pallas_call x2, Pallas kernels, projection_terms(): pl.pallas_call(functools.partial(terms_kernel, first), out_shape=outs, gr...  11.3 us
    pallas_call x2, Pallas kernels, attend_chunk(): pl.pallas_call(attend_kernel, out_shape=jax.ShapeDtypeStruct(queries.shap...  11.2 us
    ppermute x2, waiting for transfers between devices, along_line(): return lax.ppermute(x, 'dp', [(i, i ^ 2 * d) for i in range(count)])  8.44 us
    unnamed x42, local copies, waits for them, and re-layouts  5.07 us
    ppermute x2, starting transfers between devices, along_line(): return lax.ppermute(x, 'dp', [(i, i ^ 2 * d) for i in range(count)])  4.3 us
    pallas_call x2, Pallas kernels, grad_half(): pl.pallas_call(kernel, out_shape=[out, *more_outs], grid_spec=pltpu.Prefe...  3.1 us
    pallas_call x1, Pallas kernels, small_call(): pl.pallas_call(body, out_shape=outs, grid_spec=pltpu.PrefetchScalarGridSp...  2.6 us
  transfers between devices with their start and end apart: 15, of which 1 were waited for; matrix products, arithmetic and copies ran while one was open for 6% of the time, Pallas kernels for 27%

profile of v2, /device:TPU:0, one launch (start us, length us, event | category | flops | bytes accessed | tf_op | source)
XLA Modules:
  0.0 65.3 jit_solution(2082073506875516150)
XLA Ops:
  0.7 5.8 %projection_terms.2 = (bf16[960,1280]{1,0:T(8,128)(2,1)S(1)}, bf16[480,512]{1,0:T(8,128)(2,1)S(1)}, bf16[480,512]{1,0:T(8,128)(2,1)S(1)}, bf16[480,512]{1,0:T(8,...) custom-call(s32[3]{0:T(128)S(1)} %pad_add_fusion.ids.rest_0_, bf16[240,4,1280]{2,1,0:T(4,128)(2,1)} %hidden.1, ...), custom_call_target="tpu_custom_call" | custom-call | flops 2516582400 | bytes 6881280 | tf_op jit(solution)/shard_map/projection_terms/pallas_call | solution.py:236
  6.6 1.5 %pack_grads.1 = (bf16[64,1536]{1,0:T(8,128)(2,1)S(1)}, bf16[60,4,4096]{2,1,0:T(4,128)(2,1)}) custom-call(s32[3]{0:T(128)S(1)} %pad_add_fusion.ids.rest_0_, f32[1,2,64,1280]{3,2,1,0:T(8,128)} %grad_a.3, f32[1,2,64,256]{3,2,1,0:T(8,128)} %grad_b.3, bf16[480,512]{1,0:T(8,128)(2,1)S(1)} %get-tuple-element.27.after), custom_call_target="tpu_custom_call" | custom-call | bytes 786432 | tf_op jit(solution)/shard_map/pack_grads/pallas_call | solution.py:295
  8.6 2.6 %collective-permute-start.6 = (bf16[480,512]{1,0:T(8,128)(2,1)S(1)}, bf16[480,512]{1,0:T(8,128)(2,1)S(1)}, u32[]{:S(2)}, u32[]{:S(2)}) collective-permute-start(bf16[480,512]{1,0:T(8,128)(2,1)S(1)} %get-tuple-element.27.after), channel_id=1, source_target_pairs={{0,1},{1,0},{2,3},{3,2},{4,5},{5,4},{6,7},{7,6},{8,9},{9,8},{10,11... | collective-permute-start | bytes 1474568 | tf_op jit(solution)/shard_map/ppermute | solution.py:529
  11.2 1.5 %collective-permute-start.7 = (bf16[480,512]{1,0:T(8,128)(2,1)S(1)}, bf16[480,512]{1,0:T(8,128)(2,1)S(1)}, u32[]{:S(2)}, u32[]{:S(2)}) collective-permute-start(bf16[480,512]{1,0:T(8,128)(2,1)S(1)} %get-tuple-element.35), channel_id=1, source_target_pairs={{0,2},{1,3},{2,0},{3,1},{4,6},{5,7},{6,4},{7,5},{8,10},{9,11},{10,... | collective-permute-start | bytes 1474568 | tf_op jit(solution)/shard_map/ppermute | solution.py:529
  12.7 1.6 %chip_grads.1.rest_0_.a = bf16[64,1536]{1,0:T(8,128)(2,1)S(1)} custom-call(s32[3]{0:T(128)S(1)} %pad_add_fusion.ids.rest_0_, f32[1,2,64,1280]{3,2,1,0:T(8,128)} %grad_a.3, f32[1,2,64,256]{3,2,1,0:T(8,128)} %grad_b.3, bf16[64,1536]{1,0:T(8,128)(2,1)S(1)} %collective-permute-done.other), custom_call_target="tpu_custom_call" | custom-call | bytes 786432 | tf_op jit(solution)/shard_map/chip_grads/pallas_call | solution.py:295
  14.3 1.6 %collective-permute-start.3 = (bf16[64,1536]{1,0:T(8,128)(2,1)S(1)}, bf16[64,1536]{1,0:T(8,128)(2,1)S(1)}, u32[]{:S(2)}, u32[]{:S(2)}) collective-permute-start(bf16[64,1536]{1,0:T(8,128)(2,1)S(1)} %chip_grads.1.rest_0_.a), channel_id=1, source_target_pairs={{0,8},{4,12},{8,0},{12,4},{16,24},{20,28},{24,16},{28,20},{1,9},{5... | collective-permute-start | bytes 589832 | tf_op jit(solution)/shard_map/ppermute | solution.py:357
  15.9 5.5 %projection_terms.3 = (bf16[480,512]{1,0:T(8,128)(2,1)S(1)}, bf16[480,512]{1,0:T(8,128)(2,1)S(1)}, bf16[480,512]{1,0:T(8,128)(2,1)}, bf16[240,512]{1,0:T(8,128)(2,1)S(1)}, bf16[240,512]{1,0:T(8,128)(2,1)S(1)}) custom-call(s32[3]{0:T(128)S(1)} %pad_add_fusion.ids.rest_0_, bf16[960,1280]{1,0:T(8,128)(2,1)S(1)} %get-tuple-element.26.hidden.refs_4_, ...), custom_call_target="tpu_custom_call" | custom-call | flops 2516582400 | bytes 4423680 | tf_op jit(solution)/shard_map/projection_terms/pallas_call | solution.py:236
  22.8 0.8 %collective-permute-start.2 = (bf16[480,512]{1,0:T(8,128)(2,1)}, bf16[480,512]{1,0:T(8,128)(2,1)}, u32[]{:S(2)}, u32[]{:S(2)}) collective-permute-start(bf16[480,512]{1,0:T(8,128)(2,1)} %get-tuple-element.32), channel_id=1, source_target_pairs={{0,2},{1,3},{2,0},{3,1},{4,6},{5,7},{6,4},{7,5},{8,10},{9,11},{10,... | collective-permute-start | bytes 1474568 | tf_op jit(solution)/shard_map/ppermute | solution.py:529
  24.4 2.7 %collective-permute-start.4 = (bf16[64,1536]{1,0:T(8,128)(2,1)S(1)}, bf16[64,1536]{1,0:T(8,128)(2,1)S(1)}, u32[]{:S(2)}, u32[]{:S(2)}) collective-permute-start(bf16[64,1536]{1,0:T(8,128)(2,1)S(1)} %plus.2.a), channel_id=1, source_target_pairs={{0,16},{4,20},{8,24},{12,28},{16,0},{20,4},{24,8},{28,12},{1,17},{... | collective-permute-start | bytes 589832 | tf_op jit(solution)/shard_map/ppermute | solution.py:357
  27.1 8.4 %collective-permute-done.4.b = bf16[64,1536]{1,0:T(8,128)(2,1)S(1)} collective-permute-done((bf16[64,1536]{1,0:T(8,128)(2,1)S(1)}, bf16[64,1536]{1,0:T(8,128)(2,1)S(1)}, u32[]{:S(2)}, u32[]{:S(2)}) %collective-permute-start.4) | collective-permute-done | bytes 196640 | tf_op jit(solution)/shard_map/ppermute | solution.py:357
  35.7 1.0 %mid_sums.2 = (bf16[240,512]{1,0:T(8,128)(2,1)}, bf16[240,512]{1,0:T(8,128)(2,1)}) custom-call(bf16[480,512]{1,0:T(8,128)(2,1)S(1)} %get-tuple-element.33.kkeep.refs_3_, bf16[480,512]{1,0:T(8,128)(2,1)S(1)} %collective-permute-done.6.kcame.refs_4_, bf16[240,512]{1,0:T(8,128)(2,1)S(1)} %get-tuple-element.34.vkeep, ...), custom_call_target="tpu_custom_call" | custom-call | bytes 1474560 | tf_op jit(solution)/shard_map/mid_sums/pallas_call | solution.py:262
  36.8 0.9 %collective-permute-start.13 = (bf16[240,512]{1,0:T(8,128)(2,1)}, bf16[240,512]{1,0:T(8,128)(2,1)}, u32[]{:S(2)}, u32[]{:S(2)}) collective-permute-start(bf16[240,512]{1,0:T(8,128)(2,1)} %get-tuple-element.36.refs_5_), channel_id=1, source_target_pairs={{0,2},{1,3},{2,0},{3,1},{4,6},{5,7},{6,4},{7,5},{8,10},{9,11},{10,... | collective-permute-start | bytes 737288 | tf_op jit(solution)/shard_map/ppermute | solution.py:529
  37.8 1.5 %collective-permute-start.14 = (bf16[240,512]{1,0:T(8,128)(2,1)}, bf16[240,512]{1,0:T(8,128)(2,1)}, u32[]{:S(2)}, u32[]{:S(2)}) collective-permute-start(bf16[240,512]{1,0:T(8,128)(2,1)} %get-tuple-element.45), channel_id=1, source_target_pairs={{0,1},{1,0},{2,3},{3,2},{4,5},{5,4},{6,7},{7,6},{8,9},{9,8},{10,11... | collective-permute-start | bytes 737288 | tf_op jit(solution)/shard_map/ppermute | solution.py:529
  39.4 0.9 %convert_element_type.11 = f32[240]{0:T(256)S(1)} reshape(f32[60,4]{1,0:T(8,128)} %add_convert_fusion) | data formatting | bytes 1920 | tf_op jit(solution)/shard_map/convert_element_type | solution.py:523
  40.3 1.1 %copy-done = f32[2,64,1280]{2,1,0:T(8,128)S(1)} copy-done((f32[2,64,1280]{2,1,0:T(8,128)S(1)}, f32[2,64,1280]{2,1,0:T(8,128)}, u32[]{:S(2)}) %copy-start) | copy-done | bytes 655384
  41.3 2.6 %update_factors.1 = (f32[2,64,1280]{2,1,0:T(8,128)S(1)}, f32[2,64,256]{2,1,0:T(8,128)S(1)}, bf16[256,256]{1,0:T(8,128)(2,1)S(1)}, bf16[256,256]{1,0:T(8,128)(2,1...) custom-call(s32[3]{0:T(128)S(1)} %pad_add_fusion.ids.rest_0_, bf16[64,1536]{1,0:T(8,128)(2,1)S(1)} %plus.3.after.refs_0_, ...), custom_call_target="tpu_custom_call" | custom-call | bytes 3637248 | tf_op jit(solution)/shard_map/update_factors/pallas_call | solution.py:316
  44.6 1.1 %collective-permute-start.11 = (bf16[256,256]{1,0:T(8,128)(2,1)S(1)}, bf16[256,256]{1,0:T(8,128)(2,1)S(1)}, u32[]{:S(2)}, u32[]{:S(2)}) collective-permute-start(bf16[256,256]{1,0:T(8,128)(2,1)S(1)} %get-tuple-element.42), channel_id=1, source_target_pairs={{0,2},{1,3},{2,0},{3,1},{4,6},{5,7},{6,4},{7,5},{8,10},{9,11},{10,... | collective-permute-start | bytes 393224 | tf_op jit(solution)/shard_map/ppermute | solution.py:529
  45.7 1.9 %collective-permute-start.12 = (bf16[256,256]{1,0:T(8,128)(2,1)S(1)}, bf16[256,256]{1,0:T(8,128)(2,1)S(1)}, u32[]{:S(2)}, u32[]{:S(2)}) collective-permute-start(bf16[256,256]{1,0:T(8,128)(2,1)S(1)} %get-tuple-element.43), channel_id=1, source_target_pairs={{0,3},{1,2},{2,1},{3,0},{4,7},{5,6},{6,5},{7,4},{8,11},{9,10},{10,... | collective-permute-start | bytes 393224 | tf_op jit(solution)/shard_map/ppermute | solution.py:529
  48.1 0.8 %copy.19 = f32[2,64,1280]{2,1,0:T(8,128)} copy(f32[2,64,1280]{2,1,0:T(8,128)S(1)} %get-tuple-element.56) | data formatting | bytes 1310720
  49.6 1.2 %mid_sums.3 = (bf16[240,512]{1,0:T(8,128)(2,1)S(1)}, bf16[240,512]{1,0:T(8,128)(2,1)S(1)}) custom-call(bf16[480,512]{1,0:T(8,128)(2,1)S(1)} %copy-done.2, bf16[480,512]{1,0:T(8,128)(2,1)} %collective-permute-done.1.kcame.refs_4_, bf16[240,512]{1,0:T(8,128)(2,1)S(1)} %get-tuple-element.31.vkeep, bf16[480,512]{1,0:T(8,128)(2,1)} %collective-permute-done.2.vcame.refs_7_, ...), custom_call_target="tpu_custom_call" | custom-call | bytes 1474560 | tf_op jit(solution)/shard_map/mid_sums/pallas_call | solution.py:262
  51.4 1.1 %collective-permute-start.9 = (bf16[240,512]{1,0:T(8,128)(2,1)S(1)}, bf16[240,512]{1,0:T(8,128)(2,1)S(1)}, u32[]{:S(2)}, u32[]{:S(2)}) collective-permute-start(bf16[240,512]{1,0:T(8,128)(2,1)S(1)} %get-tuple-element.40), channel_id=1, source_target_pairs={{0,1},{1,0},{2,3},{3,2},{4,5},{5,4},{6,7},{7,6},{8,9},{9,8},{10,11... | collective-permute-start | bytes 737288 | tf_op jit(solution)/shard_map/ppermute | solution.py:529
  52.6 1.5 %copy-done.12 = bf16[60,16,1024]{2,1,0:T(8,128)(2,1)S(1)} copy-done((bf16[60,16,1024]{2,1,0:T(8,128)(2,1)S(1)}, bf16[60,16,1024]{2,1,0:T(8,128)(2,1)}, u32[]{:S(2)}) %copy-start.12) | copy-done | bytes 1966104
  54.1 5.6 %attend_chunk.2.refs_15_ = bf16[60,4,4096]{2,1,0:T(4,128)(2,1)} custom-call(s32[3]{0:T(128)S(1)} %pad_add_fusion.ids.rest_0_, s32[1]{0:T(128)} %constant.43.clone.1.first, s32[60]{0:T(128)S(1)} %copy-done.13, bf16[60,4,4096]{2,1,0:T(4,128)(2,1)S(1)} %copy-done.10, bf16[60,16,1024]{2,1,0:T(8,128)(2,1)S(1)} %copy-done.11, ...), custom_call_target="tpu_custom_call", output_to_operand_aliasing={{}: (18, {})} | custom-call | flops 16000000000 | bytes 10846208 | tf_op jit(solution)/shard_map/attend_chunk/pallas_call | solution.py:506
  59.8 5.6 %attend_chunk.3 = bf16[60,4,4096]{2,1,0:T(4,128)(2,1)} custom-call(s32[3]{0:T(128)S(1)} %pad_add_fusion.ids.rest_0_, s32[1]{0:T(128)} %constant.41.clone.1.first, s32[60]{0:T(128)S(1)} %copy-done.13, bf16[60,4,4096]{2,1,0:T(4,128)(2,1)S(1)} %copy-done.10, bf16[60,16,1024]{2,1,0:T(8,128)(2,1)S(1)} %copy-done.11, ...), custom_call_target="tpu_custom_call", output_to_operand_aliasing={{}: (18, {})} | custom-call | flops 16000000000 | bytes 10846208 | tf_op jit(solution)/shard_map/attend_chunk/pallas_call | solution.py:506
  (66 shorter events, 5.5 us)
Async XLA Ops:
  6.5 14.9 %copy-start.16 = (bf16[240,512]{1,0:T(8,128)(2,1)}, bf16[240,512]{1,0:T(8,128)(2,1)S(1)}, u32[]{:S(2)}) copy-start(bf16[240,512]{1,0:T(8,128)(2,1)S(1)} %get-tuple-element.44.refs_6_) | copy-start | bytes 737284
  6.6 29.2 %copy-start.3 = (bf16[480,512]{1,0:T(8,128)(2,1)}, bf16[480,512]{1,0:T(8,128)(2,1)S(1)}, u32[]{:S(2)}) copy-start(bf16[480,512]{1,0:T(8,128)(2,1)S(1)} %get-tuple-element.33.kkeep.refs_3_) | copy-start | bytes 1474564
  8.1 4.6 %collective-permute-start = (bf16[64,1536]{1,0:T(8,128)(2,1)S(1)}, bf16[64,1536]{1,0:T(8,128)(2,1)S(1)}, u32[]{:S(2)}, u32[]{:S(2)}) collective-permute-start(bf16[64,1536]{1,0:T(8,128)(2,1)S(1)} %get-tuple-element.28), channel_id=1, source_target_pairs={{0,4},{4,0},{8,12},{12,8},{16,20},{20,16},{24,28},{28,24},{1,5},{5... | collective-permute-start | bytes 589832 | tf_op jit(solution)/shard_map/ppermute | solution.py:334
  8.6 27.1 %collective-permute-start.6 = (bf16[480,512]{1,0:T(8,128)(2,1)S(1)}, bf16[480,512]{1,0:T(8,128)(2,1)S(1)}, u32[]{:S(2)}, u32[]{:S(2)}) collective-permute-start(bf16[480,512]{1,0:T(8,128)(2,1)S(1)} %get-tuple-element.27.after), channel_id=1, source_target_pairs={{0,1},{1,0},{2,3},{3,2},{4,5},{5,4},{6,7},{7,6},{8,9},{9,8},{10,11... | collective-permute-start | bytes 1474568 | tf_op jit(solution)/shard_map/ppermute | solution.py:529
  11.2 24.5 %collective-permute-start.7 = (bf16[480,512]{1,0:T(8,128)(2,1)S(1)}, bf16[480,512]{1,0:T(8,128)(2,1)S(1)}, u32[]{:S(2)}, u32[]{:S(2)}) collective-permute-start(bf16[480,512]{1,0:T(8,128)(2,1)S(1)} %get-tuple-element.35), channel_id=1, source_target_pairs={{0,2},{1,3},{2,0},{3,1},{4,6},{5,7},{6,4},{7,5},{8,10},{9,11},{10,... | collective-permute-start | bytes 1474568 | tf_op jit(solution)/shard_map/ppermute | solution.py:529
  14.3 10.0 %collective-permute-start.3 = (bf16[64,1536]{1,0:T(8,128)(2,1)S(1)}, bf16[64,1536]{1,0:T(8,128)(2,1)S(1)}, u32[]{:S(2)}, u32[]{:S(2)}) collective-permute-start(bf16[64,1536]{1,0:T(8,128)(2,1)S(1)} %chip_grads.1.rest_0_.a), channel_id=1, source_target_pairs={{0,8},{4,12},{8,0},{12,4},{16,24},{20,28},{24,16},{28,20},{1,9},{5... | collective-permute-start | bytes 589832 | tf_op jit(solution)/shard_map/ppermute | solution.py:357
  15.9 11.1 %copy-start.18 = (f32[128]{0:T(128)S(1)}, f32[128]{0:T(128)}, u32[]{:S(2)}) copy-start(f32[128]{0:T(128)} %param.18) | copy-start | bytes 1540
  22.3 14.5 %copy-start.14 = (bf16[240,512]{1,0:T(8,128)(2,1)}, bf16[240,512]{1,0:T(8,128)(2,1)S(1)}, u32[]{:S(2)}) copy-start(bf16[240,512]{1,0:T(8,128)(2,1)S(1)} %get-tuple-element.39.refs_6_) | copy-start | bytes 737284
  22.3 22.4 %collective-permute-start.1 = (bf16[480,512]{1,0:T(8,128)(2,1)S(1)}, bf16[480,512]{1,0:T(8,128)(2,1)}, u32[]{:S(2)}, u32[]{:S(2)}) collective-permute-start(bf16[480,512]{1,0:T(8,128)(2,1)S(1)} %get-tuple-element.30.after), channel_id=1, source_target_pairs={{0,1},{1,0},{2,3},{3,2},{4,5},{5,4},{6,7},{7,6},{8,9},{9,8},{10,11... | collective-permute-start | bytes 1474568 | tf_op jit(solution)/shard_map/ppermute | solution.py:529
  22.8 22.9 %collective-permute-start.2 = (bf16[480,512]{1,0:T(8,128)(2,1)}, bf16[480,512]{1,0:T(8,128)(2,1)}, u32[]{:S(2)}, u32[]{:S(2)}) collective-permute-start(bf16[480,512]{1,0:T(8,128)(2,1)} %get-tuple-element.32), channel_id=1, source_target_pairs={{0,2},{1,3},{2,0},{3,1},{4,6},{5,7},{6,4},{7,5},{8,10},{9,11},{10,... | collective-permute-start | bytes 1474568 | tf_op jit(solution)/shard_map/ppermute | solution.py:529
  24.3 15.9 %copy-start.9 = (f32[2,64,256]{2,1,0:T(8,128)S(1)}, f32[2,64,256]{2,1,0:T(8,128)}, u32[]{:S(2)}) copy-start(f32[2,64,256]{2,1,0:T(8,128)} %refs_3_.1) | copy-start | bytes 393220
  24.4 11.2 %collective-permute-start.4 = (bf16[64,1536]{1,0:T(8,128)(2,1)S(1)}, bf16[64,1536]{1,0:T(8,128)(2,1)S(1)}, u32[]{:S(2)}, u32[]{:S(2)}) collective-permute-start(bf16[64,1536]{1,0:T(8,128)(2,1)S(1)} %plus.2.a), channel_id=1, source_target_pairs={{0,16},{4,20},{8,24},{12,28},{16,0},{20,4},{24,8},{28,12},{1,17},{... | collective-permute-start | bytes 589832 | tf_op jit(solution)/shard_map/ppermute | solution.py:357
  35.6 4.6 %collective-permute-start.5 = (bf16[64,1536]{1,0:T(8,128)(2,1)S(1)}, bf16[64,1536]{1,0:T(8,128)(2,1)}, u32[]{:S(2)}, u32[]{:S(2)}) collective-permute-start(bf16[64,1536]{1,0:T(8,128)(2,1)S(1)} %plus.3.after.refs_0_), channel_id=1, source_target_pairs={{0,4},{4,0},{8,12},{12,8},{16,20},{20,16},{24,28},{28,24},{1,5},{5... | collective-permute-start | bytes 589832 | tf_op jit(solution)/shard_map/ppermute | solution.py:334
  36.8 14.0 %collective-permute-start.13 = (bf16[240,512]{1,0:T(8,128)(2,1)}, bf16[240,512]{1,0:T(8,128)(2,1)}, u32[]{:S(2)}, u32[]{:S(2)}) collective-permute-start(bf16[240,512]{1,0:T(8,128)(2,1)} %get-tuple-element.36.refs_5_), channel_id=1, source_target_pairs={{0,2},{1,3},{2,0},{3,1},{4,6},{5,7},{6,4},{7,5},{8,10},{9,11},{10,... | collective-permute-start | bytes 737288 | tf_op jit(solution)/shard_map/ppermute | solution.py:529
  37.8 13.6 %collective-permute-start.14 = (bf16[240,512]{1,0:T(8,128)(2,1)}, bf16[240,512]{1,0:T(8,128)(2,1)}, u32[]{:S(2)}, u32[]{:S(2)}) collective-permute-start(bf16[240,512]{1,0:T(8,128)(2,1)} %get-tuple-element.45), channel_id=1, source_target_pairs={{0,1},{1,0},{2,3},{3,2},{4,5},{5,4},{6,7},{7,6},{8,9},{9,8},{10,11... | collective-permute-start | bytes 737288 | tf_op jit(solution)/shard_map/ppermute | solution.py:529
  41.3 11.2 %copy-start.11 = (bf16[60,16,1024]{2,1,0:T(8,128)(2,1)S(1)}, bf16[60,16,1024]{2,1,0:T(8,128)(2,1)}, u32[]{:S(2)}) copy-start(bf16[60,16,1024]{2,1,0:T(8,128)(2,1)} %refs_1_.3) | copy-start | bytes 5898244
  44.0 8.6 %copy-start.4 = (bf16[480,512]{1,0:T(8,128)(2,1)S(1)}, bf16[480,512]{1,0:T(8,128)(2,1)}, u32[]{:S(2)}) copy-start(bf16[480,512]{1,0:T(8,128)(2,1)} %copy-done.3) | copy-start | bytes 1474564
  44.0 8.6 %copy-start.6 = (bf16[480,512]{1,0:T(8,128)(2,1)S(1)}, bf16[480,512]{1,0:T(8,128)(2,1)}, u32[]{:S(2)}) copy-start(bf16[480,512]{1,0:T(8,128)(2,1)} %copy-done.5) | copy-start | bytes 1474564
  44.0 8.6 %copy-start.8 = (bf16[480,512]{1,0:T(8,128)(2,1)S(1)}, bf16[480,512]{1,0:T(8,128)(2,1)}, u32[]{:S(2)}) copy-start(bf16[480,512]{1,0:T(8,128)(2,1)} %copy-done.7) | copy-start | bytes 1474564
  44.0 8.5 %collective-permute-start.10 = (bf16[256,256]{1,0:T(8,128)(2,1)S(1)}, bf16[256,256]{1,0:T(8,128)(2,1)S(1)}, u32[]{:S(2)}, u32[]{:S(2)}) collective-permute-start(bf16[256,256]{1,0:T(8,128)(2,1)S(1)} %get-tuple-element.41), channel_id=1, source_target_pairs={{0,1},{1,0},{2,3},{3,2},{4,5},{5,4},{6,7},{7,6},{8,9},{9,8},{10,11... | collective-permute-start | bytes 393224 | tf_op jit(solution)/shard_map/ppermute | solution.py:529
  44.6 7.9 %collective-permute-start.11 = (bf16[256,256]{1,0:T(8,128)(2,1)S(1)}, bf16[256,256]{1,0:T(8,128)(2,1)S(1)}, u32[]{:S(2)}, u32[]{:S(2)}) collective-permute-start(bf16[256,256]{1,0:T(8,128)(2,1)S(1)} %get-tuple-element.42), channel_id=1, source_target_pairs={{0,2},{1,3},{2,0},{3,1},{4,6},{5,7},{6,4},{7,5},{8,10},{9,11},{10,... | collective-permute-start | bytes 393224 | tf_op jit(solution)/shard_map/ppermute | solution.py:529
  45.7 6.8 %collective-permute-start.12 = (bf16[256,256]{1,0:T(8,128)(2,1)S(1)}, bf16[256,256]{1,0:T(8,128)(2,1)S(1)}, u32[]{:S(2)}, u32[]{:S(2)}) collective-permute-start(bf16[256,256]{1,0:T(8,128)(2,1)S(1)} %get-tuple-element.43), channel_id=1, source_target_pairs={{0,3},{1,2},{2,1},{3,0},{4,7},{5,6},{6,5},{7,4},{8,11},{9,10},{10,... | collective-permute-start | bytes 393224 | tf_op jit(solution)/shard_map/ppermute | solution.py:529
  50.8 8.9 %collective-permute-start.8 = (bf16[240,512]{1,0:T(8,128)(2,1)S(1)}, bf16[240,512]{1,0:T(8,128)(2,1)S(1)}, u32[]{:S(2)}, u32[]{:S(2)}) collective-permute-start(bf16[240,512]{1,0:T(8,128)(2,1)S(1)} %get-tuple-element.38), channel_id=1, source_target_pairs={{0,2},{1,3},{2,0},{3,1},{4,6},{5,7},{6,4},{7,5},{8,10},{9,11},{10,... | collective-permute-start | bytes 737288 | tf_op jit(solution)/shard_map/ppermute | solution.py:529
  51.4 8.3 %collective-permute-start.9 = (bf16[240,512]{1,0:T(8,128)(2,1)S(1)}, bf16[240,512]{1,0:T(8,128)(2,1)S(1)}, u32[]{:S(2)}, u32[]{:S(2)}) collective-permute-start(bf16[240,512]{1,0:T(8,128)(2,1)S(1)} %get-tuple-element.40), channel_id=1, source_target_pairs={{0,1},{1,0},{2,3},{3,2},{4,5},{5,4},{6,7},{7,6},{8,9},{9,8},{10,11... | collective-permute-start | bytes 737288 | tf_op jit(solution)/shard_map/ppermute | solution.py:529
  (11 other events, 52.9 us)

commit v3 on v2

--- a/solution.py
+++ b/solution.py
@@ -16,7 +16,7 @@
 STEPS = 4
 BF = jnp.bfloat16
 F32 = jnp.float32
-VMEM_LIMIT = 24 * 1024 * 1024
+VMEM_LIMIT = 16 * 1024 * 1024
 
 
 def normed_rotated(keys, gain, position):
@@ -144,17 +144,9 @@
 
 
 def terms_kernel(first, ids, hidden, weight, *rest):
-    *outs, w, sems = rest[1:]
-    wide = w.shape[1] * TILE
-    start = 0 if first else weight.shape[2] - wide
-    tiles = w.shape[1]
-
-    def weight_copy(p, i):
-        at = pl.ds(start + i * TILE, TILE)
-        return pltpu.make_async_copy(weight.at[p, :, at], w.at[p, i], sems.at[p, i])
-
     if first:
-        x, *outs, held, hidden_sems = outs
+        x, *outs, held, hidden_sems, w, sems = rest[1:]
+        tiles = w.shape[1]
         tokens = x.shape[0] // 4
         rows = tokens // STEPS
 
@@ -162,18 +154,23 @@
             at = pl.ds((ids[0] ^ r) * rows, rows)
             return pltpu.make_async_copy(hidden.at[at], held.at[r], hidden_sems.at[r])
 
+        def weight_copy(p, i):
+            at = pl.ds(i * TILE, TILE)
+            return pltpu.make_async_copy(weight.at[p, :, at], w.at[p, i], sems.at[p, i])
+
         for r in range(4):
             hidden_copy(r).start()
-    else:
-        x = hidden
-        tokens = x.shape[0] // 4
-    for i in range(tiles):
-        for p in range(2):
-            weight_copy(p, i).start()
-    if first:
+        for i in range(tiles):
+            for p in range(2):
+                weight_copy(p, i).start()
         for r in range(4):
             hidden_copy(r).wait()
             x[r * tokens : (r + 1) * tokens] = held[r].reshape(tokens, x.shape[1])
+    else:
+        x, outs = hidden, rest[1:]
+        tokens = x.shape[0] // 4
+        tiles = outs[0].shape[1] // TILE
+        base = weight.shape[2] - tiles * TILE
     ksend, kkeep, vsend, vkeep0, vkeep1 = outs
     steps = x.shape[1] // TILE
 
@@ -182,12 +179,18 @@
 
         @pl.loop(0, tiles)
         def _(i):
-            for p in range(2):
-                weight_copy(p, i).wait()
+            if first:
+                for p in range(2):
+                    weight_copy(p, i).wait()
 
             def push(k):
+                rows = slice(k * TILE, (k + 1) * TILE)
                 for p in range(2):
-                    pltpu.matmul_push_rhs(w[p, i, k * TILE : (k + 1) * TILE, :], k % 2, p)
+                    if first:
+                        tile = w[p, i, rows, :]
+                    else:
+                        tile = weight[p, rows, pl.ds(pl.multiple_of(base + i * TILE, TILE), TILE)]
+                    pltpu.matmul_push_rhs(tile, k % 2, p)
 
             push(0)
             for k in range(steps):
@@ -227,11 +230,9 @@
         scratch += [
             pltpu.VMEM((4, tokens // STEPS, STEPS, width), BF),
             pltpu.SemaphoreType.DMA((4,)),
+            pltpu.VMEM((2, wide // TILE, width, TILE), BF),
+            pltpu.SemaphoreType.DMA((2, wide // TILE)),
         ]
-    scratch += [
-        pltpu.VMEM((2, wide // TILE, width, TILE), BF),
-        pltpu.SemaphoreType.DMA((2, wide // TILE)),
-    ]
     here = pl.BlockSpec(memory_space=pl.ANY)
     return pl.pallas_call(
         functools.partial(terms_kernel, first),
@@ -239,14 +240,16 @@
         grid_spec=pltpu.PrefetchScalarGridSpec(
             num_scalar_prefetch=1,
             grid=(1,),
-            in_specs=[here if first else whole(hidden.shape), here, here],
+            in_specs=[here, here, here]
+            if first
+            else [whole(hidden.shape), whole(kv_weight.shape), here],
             out_specs=[whole(x.shape) for x in outs],
             scratch_shapes=scratch,
         ),
         compiler_params=params(),
         cost_estimate=cost(2 * 4 * tokens * width * 2 * wide, [hidden], outs),
         name="projection_terms",
-    )(ids, hbm(hidden) if first else hidden, hbm(kv_weight), after)
+    )(ids, *(map(hbm, (hidden, kv_weight)) if first else (hidden, kv_weight)), after)
 
 
 def mid_kernel(kkeep, kcame, vkeep, vcame, after, kout, vout):
@@ -307,7 +310,7 @@
     )(ids, hbm(grad_a), hbm(grad_b), *rest)
 
 
-def small_call(kernel, name, ids, args, outs, after=(), scratch=()):
+def small_call(kernel, name, ids, args, outs, after=(), scratch=(), copied=0):
     count = len(args)
 
     def body(ids, *refs):
@@ -321,7 +324,8 @@
             grid=(1,),
             in_specs=[whole(x.shape) for x in args]
             + [pl.BlockSpec(memory_space=pl.ANY)] * len(after),
-            out_specs=[whole(x.shape) for x in outs],
+            out_specs=[pl.BlockSpec(memory_space=pltpu.HBM)] * copied
+            + [whole(x.shape) for x in outs[copied:]],
             scratch_shapes=list(scratch),
         ),
         compiler_params=params(),
@@ -334,23 +338,22 @@
     return lax.ppermute(x, "dp", [(i, i ^ 1) for i in range(count)])
 
 
-def plus_kernel(a, b, after, out):
-    del after
-    out[...] = (a[...].astype(F32) + b[...].astype(F32)).astype(BF)
-
-
-def plus(a, b, after):
+def plus_kernel(a, b, *rest):
+    rest[-1][...] = (a[...].astype(F32) + b[...].astype(F32)).astype(BF)
+
+
+def plus(a, b, *after):
     out = jax.ShapeDtypeStruct(a.shape, BF)
     return pl.pallas_call(
         plus_kernel,
         out_shape=out,
         grid=(1,),
-        in_specs=[whole(a.shape)] * 2 + [pl.BlockSpec(memory_space=pl.ANY)],
+        in_specs=[whole(a.shape)] * 2 + [pl.BlockSpec(memory_space=pl.ANY)] * len(after),
         out_specs=whole(a.shape),
         compiler_params=params(),
         cost_estimate=cost(0, [a, b], [out]),
         name="plus",
-    )(a, b, after)
+    )(a, b, *after)
 
 
 def along_line(x, d, count):
@@ -360,12 +363,18 @@
 TOP = 2 * R
 
 
-def update_kernel(rates, ids, half, other, factor_a, factor_b, x, new_a, new_b, *rest):
-    *sends, a = rest
+def update_kernel(rates, ids, half, other, factor_a, factor_b, x, out_a, out_b, *rest):
+    *sends, a, new_a, new_b, sems = rest
+    copies = [
+        pltpu.make_async_copy(new_a, out_a, sems.at[0]),
+        pltpu.make_async_copy(new_b, out_b, sems.at[1]),
+    ]
     wide = factor_a.shape[-1]
     for index, part in ((ids[2], half), (ids[2] ^ 1, other)):
         new_a[index] = factor_a[index] - rates[0] * part[:, :wide].astype(F32)
         new_b[index] = factor_b[index] - rates[1] * part[:, wide:].astype(F32)
+    for copy in copies:
+        copy.start()
     for p in range(2):
         a[p * R : (p + 1) * R] = new_a[p].astype(BF)
     a[TOP:] = jnp.zeros((TILE - TOP, wide), BF)
@@ -396,11 +405,13 @@
             send[tokens:, TOP:] = jnp.zeros((2 * TOP - tokens, TOP), BF)
 
     pl.run_scoped(multiply, *[pltpu.ACC(r % 2)((tokens, TILE), F32) for r in range(4)])
+    for copy in copies:
+        copy.wait()
 
 
 def updated(ids, half, other, factor_a, factor_b, x, dp, after):
     rates = (2.0 / math.sqrt(dp * D), 2.0 / math.sqrt(dp * R))
-    outs = [pltpu.VMEM(f.shape, F32) for f in (factor_a, factor_b)]
+    outs = [pltpu.HBM(f.shape, F32) for f in (factor_a, factor_b)]
     outs += [jax.ShapeDtypeStruct((2 * TOP, 2 * TOP), BF)] * 4
     return small_call(
         functools.partial(update_kernel, rates),
@@ -409,7 +420,13 @@
         (half, other, factor_a, factor_b, x),
         outs,
         (after,),
-        [pltpu.VMEM((TILE, factor_a.shape[-1]), BF)],
+        [
+            pltpu.VMEM((TILE, factor_a.shape[-1]), BF),
+            pltpu.VMEM(factor_a.shape, F32),
+            pltpu.VMEM(factor_b.shape, F32),
+            pltpu.SemaphoreType.DMA((2,)),
+        ],
+        2,
     )
 
 
@@ -566,19 +583,6 @@
     (half,) = grad_half(
         chip_kernel, "chip_grads", ids, grad_a, grad_b, 0, [other], [whole(other.shape)]
     )
-    step = 1
-    while 4 * step < count_dp:
-        came = along_line(half, step, count_dp)
-        if step == 1:
-            second = projection_terms(ids, x, kv_weight, CHUNKS[1], tokens, half)
-        half = plus(half, came, second[0])
-        step *= 2
-    if step == 1:
-        second = projection_terms(ids, x, kv_weight, CHUNKS[1], tokens, half)
-    if 2 * step < count_dp:
-        half = plus(half, along_line(half, step, count_dp), second[0])
-    other = core_flip(half, count_dp)
-
     def first_exchange(term, after):
         ksend, kkeep, vsend, vkeep0, vkeep1 = term
         kcame, vcame = across(ksend, 1), across(vsend, 2)
@@ -589,7 +593,17 @@
         kkeep, kcame, vkeep0, vcame = parts
         return kkeep, kcame, across(mids[0], 2), vkeep0, vcame, across(mids[1], 1)
 
-    mids, parts = first_exchange(first, half)
+    second = projection_terms(ids, x, kv_weight, CHUNKS[1], tokens, half)
+    step, after = 1, second[:1]
+    while 2 * step < count_dp:
+        half = plus(half, along_line(half, step, count_dp), *after)
+        step *= 2
+        if step == 2:
+            mids, parts = first_exchange(first, half)
+            after = (mids[0], tables[0])
+    if step == 1:
+        mids, parts = first_exchange(first, half)
+    other = core_flip(half, count_dp)
     first = second_exchange(mids, parts)
     new_a, new_b, *sends = updated(
         ids, half, other, factor_a, factor_b, x, count_dp, mids[0]

time: 65.8 us -> 64.6 us (0.982)
  waiting for transfers between devices: 8.48 us -> 12.9 us
  local copies, waits for them, and re-layouts: 5.93 us -> 2.64 us
  Pallas kernels: 30.5 us -> 27.5 us
  starting transfers between devices: 18 us -> 19.7 us
    ppermute x11, waiting for transfers between devices: 0.03 us -> 4.63 us  [across(): return lax.ppermute(x, 'tensor', [(i, i ^ r) for i in range(4)])]
    unnamed x42 -> x26, local copies, waits for them, and re-layouts: 5.07 us -> 2.54 us
    ppermute x11, starting transfers between devices: 13.1 us -> 15.4 us  [across(): return lax.ppermute(x, 'tensor', [(i, i ^ r) for i in range(4)])]
    ppermute x2, waiting for transfers between devices: 8.44 us -> 6.74 us  [along_line(): return lax.ppermute(x, 'dp', [(i, i ^ 2 * d) for i in range(count)])]
    ppermute x2, waiting for transfers between devices: 0.01 us -> 1.48 us  [core_flip(): return lax.ppermute(x, 'dp', [(i, i ^ 1) for i in range(count)])]
    pallas_call x2, Pallas kernels: 11.3 us -> 10.1 us  [projection_terms(): pl.pallas_call(functools.partial(terms_kernel, first), out_shape=outs, gr...]
    pallas_call x1, Pallas kernels: 2.6 us -> 1.52 us  [small_call(): pl.pallas_call(body, out_shape=outs, grid_spec=pltpu.PrefetchScalarGridSp...]
    pallas_call x2, Pallas kernels: 2.22 us -> 1.29 us  [mid_sums(): pl.pallas_call(mid_kernel, out_shape=[jax.ShapeDtypeStruct(shape, BF)] *...]
  transfers between devices with their start and end apart: 15 -> 15, of which waited for: 1 -> 4; matrix products, arithmetic and copies ran while one was open for 6% -> 1% of each run, Pallas kernels for 27% -> 25%
where the time goes in v3:
time: 64.6 us; the launch traced here: 64.4 us
  Pallas kernels  27.5 us (43%)
  starting transfers between devices  19.7 us (30%)
  waiting for transfers between devices  12.9 us (20%)
  local copies, waits for them, and re-layouts  2.64 us (4%)
  between operations  0.85 us (1%)
  other arithmetic  0.82 us (1%)
    ppermute x11, starting transfers between devices, across(): return lax.ppermute(x, 'tensor', [(i, i ^ r) for i in range(4)])  15.4 us
    pallas_call x2, Pallas kernels, attend_chunk(): pl.pallas_call(attend_kernel, out_shape=jax.ShapeDtypeStruct(queries.shap...  10.6 us
    pallas_call x2, Pallas kernels, projection_terms(): pl.pallas_call(functools.partial(terms_kernel, first), out_shape=outs, gr...  10.1 us
    ppermute x2, waiting for transfers between devices, along_line(): return lax.ppermute(x, 'dp', [(i, i ^ 2 * d) for i in range(count)])  6.74 us
    ppermute x11, waiting for transfers between devices, across(): return lax.ppermute(x, 'tensor', [(i, i ^ r) for i in range(4)])  4.63 us
    ppermute x2, starting transfers between devices, along_line(): return lax.ppermute(x, 'dp', [(i, i ^ 2 * d) for i in range(count)])  4.29 us
    pallas_call x2, Pallas kernels, grad_half(): pl.pallas_call(kernel, out_shape=[out, *more_outs], grid_spec=pltpu.Prefe...  3.88 us
    unnamed x26, local copies, waits for them, and re-layouts  2.54 us
  transfers between devices with their start and end apart: 15, of which 4 were waited for; matrix products, arithmetic and copies ran while one was open for 1% of the time, Pallas kernels for 25%

profile of v3, /device:TPU:0, one launch (start us, length us, event | category | flops | bytes accessed | tf_op | source)
XLA Modules:
  0.0 64.4 jit_solution(7680248346213846843)
XLA Ops:
  0.7 6.6 %projection_terms.2 = (bf16[960,1280]{1,0:T(8,128)(2,1)S(1)}, bf16[480,512]{1,0:T(8,128)(2,1)S(1)}, bf16[480,512]{1,0:T(8,128)(2,1)S(1)}, bf16[480,512]{1,0:T(8,...) custom-call(s32[3]{0:T(128)S(1)} %pad_add_fusion.ids.rest_0_, bf16[240,4,1280]{2,1,0:T(4,128)(2,1)} %hidden.1, ...), custom_call_target="tpu_custom_call" | custom-call | flops 2516582400 | bytes 6881280 | tf_op jit(solution)/shard_map/projection_terms/pallas_call | solution.py:237
  7.3 3.0 %collective-permute-start.6 = (bf16[480,512]{1,0:T(8,128)(2,1)}, bf16[480,512]{1,0:T(8,128)(2,1)}, u32[]{:S(2)}, u32[]{:S(2)}) collective-permute-start(bf16[480,512]{1,0:T(8,128)(2,1)} %get-tuple-element.35), channel_id=1, source_target_pairs={{0,2},{1,3},{2,0},{3,1},{4,6},{5,7},{6,4},{7,5},{8,10},{9,11},{10,... | collective-permute-start | bytes 1474568 | tf_op jit(solution)/shard_map/ppermute | solution.py:546
  10.4 1.5 %collective-permute-start.5 = (bf16[480,512]{1,0:T(8,128)(2,1)S(1)}, bf16[480,512]{1,0:T(8,128)(2,1)}, u32[]{:S(2)}, u32[]{:S(2)}) collective-permute-start(bf16[480,512]{1,0:T(8,128)(2,1)S(1)} %get-tuple-element.27.after), channel_id=1, source_target_pairs={{0,1},{1,0},{2,3},{3,2},{4,5},{5,4},{6,7},{7,6},{8,9},{9,8},{10,11... | collective-permute-start | bytes 1474568 | tf_op jit(solution)/shard_map/ppermute | solution.py:546
  11.9 2.2 %pack_grads.1 = (bf16[64,1536]{1,0:T(8,128)(2,1)}, bf16[60,4,4096]{2,1,0:T(4,128)(2,1)}) custom-call(s32[3]{0:T(128)S(1)} %pad_add_fusion.ids.rest_0_, f32[1,2,64,1280]{3,2,1,0:T(8,128)} %grad_a.3, f32[1,2,64,256]{3,2,1,0:T(8,128)} %grad_b.3, bf16[480,512]{1,0:T(8,128)(2,1)S(1)} %get-tuple-element.27.after), custom_call_target="tpu_custom_call" | custom-call | bytes 786432 | tf_op jit(solution)/shard_map/pack_grads/pallas_call | solution.py:298
  14.4 1.5 %collective-permute-done.other = bf16[64,1536]{1,0:T(8,128)(2,1)} collective-permute-done((bf16[64,1536]{1,0:T(8,128)(2,1)}, bf16[64,1536]{1,0:T(8,128)(2,1)}, u32[]{:S(2)}, u32[]{:S(2)}) %collective-permute-start) | collective-permute-done | bytes 196640 | tf_op jit(solution)/shard_map/ppermute | solution.py:338
  15.9 1.6 %chip_grads.1.rest_0_.a = bf16[64,1536]{1,0:T(8,128)(2,1)S(1)} custom-call(s32[3]{0:T(128)S(1)} %pad_add_fusion.ids.rest_0_, f32[1,2,64,1280]{3,2,1,0:T(8,128)} %grad_a.3, f32[1,2,64,256]{3,2,1,0:T(8,128)} %grad_b.3, bf16[64,1536]{1,0:T(8,128)(2,1)} %collective-permute-done.other), custom_call_target="tpu_custom_call" | custom-call | bytes 786432 | tf_op jit(solution)/shard_map/chip_grads/pallas_call | solution.py:298
  17.5 1.6 %collective-permute-start.3 = (bf16[64,1536]{1,0:T(8,128)(2,1)S(1)}, bf16[64,1536]{1,0:T(8,128)(2,1)S(1)}, u32[]{:S(2)}, u32[]{:S(2)}) collective-permute-start(bf16[64,1536]{1,0:T(8,128)(2,1)S(1)} %chip_grads.1.rest_0_.a), channel_id=1, source_target_pairs={{0,8},{4,12},{8,0},{12,4},{16,24},{20,28},{24,16},{28,20},{1,9},{5... | collective-permute-start | bytes 589832 | tf_op jit(solution)/shard_map/ppermute | solution.py:360
  19.2 2.5 %copy-done.4 = bf16[2,1280,1024]{2,1,0:T(8,128)(2,1)S(1)} copy-done((bf16[2,1280,1024]{2,1,0:T(8,128)(2,1)S(1)}, bf16[2,1280,1024]{2,1,0:T(8,128)(2,1)}, u32[]{:S(2)}) %copy-start.4) | copy-done | bytes 5242904
  21.7 3.5 %projection_terms.3 = (bf16[480,512]{1,0:T(8,128)(2,1)S(1)}, bf16[480,512]{1,0:T(8,128)(2,1)S(1)}, bf16[480,512]{1,0:T(8,128)(2,1)S(1)}, bf16[240,512]{1,0:T(8,128)(2,1)S(1)}, bf16[240,512]{1,0:T(8,128)(2,1)S(1)}) custom-call(s32[3]{0:T(128)S(1)} %pad_add_fusion.ids.rest_0_, bf16[960,1280]{1,0:T(8,128)(2,1)S(1)} %get-tuple-element.26.hidden.refs_4_, ...), custom_call_target="tpu_custom_call" | custom-call | flops 2516582400 | bytes 4423680 | tf_op jit(solution)/shard_map/projection_terms/pallas_call | solution.py:237
  25.2 0.6 collective-permute-start.2
  26.4 2.6 %collective-permute-start.4 = (bf16[64,1536]{1,0:T(8,128)(2,1)S(1)}, bf16[64,1536]{1,0:T(8,128)(2,1)S(1)}, u32[]{:S(2)}, u32[]{:S(2)}) collective-permute-start(bf16[64,1536]{1,0:T(8,128)(2,1)S(1)} %plus.2.after.a), channel_id=1, source_target_pairs={{0,16},{4,20},{8,24},{12,28},{16,0},{20,4},{24,8},{28,12},{1,17},{... | collective-permute-start | bytes 589832 | tf_op jit(solution)/shard_map/ppermute | solution.py:360
  29.6 1.2 %mid_sums.2 = (bf16[240,512]{1,0:T(8,128)(2,1)S(1)}, bf16[240,512]{1,0:T(8,128)(2,1)S(1)}) custom-call(bf16[480,512]{1,0:T(8,128)(2,1)S(1)} %get-tuple-element.33.kkeep.refs_3_, bf16[480,512]{1,0:T(8,128)(2,1)} %collective-permute-done.5.kcame.refs_4_, bf16[240,512]{1,0:T(8,128)(2,1)S(1)} %copy-done.2, ...), custom_call_target="tpu_custom_call" | custom-call | bytes 1474560 | tf_op jit(solution)/shard_map/mid_sums/pallas_call | solution.py:265
  30.8 6.7 %collective-permute-done.4.b = bf16[64,1536]{1,0:T(8,128)(2,1)S(1)} collective-permute-done((bf16[64,1536]{1,0:T(8,128)(2,1)S(1)}, bf16[64,1536]{1,0:T(8,128)(2,1)S(1)}, u32[]{:S(2)}, u32[]{:S(2)}) %collective-permute-start.4) | collective-permute-done | bytes 196640 | tf_op jit(solution)/shard_map/ppermute | solution.py:360
  37.7 1.6 %collective-permute-start.14 = (bf16[240,512]{1,0:T(8,128)(2,1)S(1)}, bf16[240,512]{1,0:T(8,128)(2,1)S(1)}, u32[]{:S(2)}, u32[]{:S(2)}) collective-permute-start(bf16[240,512]{1,0:T(8,128)(2,1)S(1)} %get-tuple-element.45), channel_id=1, source_target_pairs={{0,1},{1,0},{2,3},{3,2},{4,5},{5,4},{6,7},{7,6},{8,9},{9,8},{10,11... | collective-permute-start | bytes 737288 | tf_op jit(solution)/shard_map/ppermute | solution.py:546
  39.3 1.5 %collective-permute-start.13 = (bf16[240,512]{1,0:T(8,128)(2,1)S(1)}, bf16[240,512]{1,0:T(8,128)(2,1)S(1)}, u32[]{:S(2)}, u32[]{:S(2)}) collective-permute-start(bf16[240,512]{1,0:T(8,128)(2,1)S(1)} %get-tuple-element.36.rest_0_.refs_5_), channel_id=1, source_target_pairs={{0,2},{1,3},{2,0},{3,1},{4,6},{5,7},{6,4},{7,5},{8,10},{9,11},{10,... | collective-permute-start | bytes 737288 | tf_op jit(solution)/shard_map/ppermute | solution.py:546
  40.8 1.5 %update_factors.1 = (f32[2,64,1280]{2,1,0:T(8,128)}, f32[2,64,256]{2,1,0:T(8,128)}, bf16[256,256]{1,0:T(8,128)(2,1)S(1)}, bf16[256,256]{1,0:T(8,128)(2,1)S(1)}, ...) custom-call(s32[3]{0:T(128)S(1)} %pad_add_fusion.ids.rest_0_, bf16[64,1536]{1,0:T(8,128)(2,1)S(1)} %plus.3.refs_0_, ...), custom_call_target="tpu_custom_call" | custom-call | bytes 3637248 | tf_op jit(solution)/shard_map/update_factors/pallas_call | solution.py:319
  42.4 0.6 collective-permute-start.10
  43.0 0.8 %collective-permute-start.11 = (bf16[256,256]{1,0:T(8,128)(2,1)S(1)}, bf16[256,256]{1,0:T(8,128)(2,1)S(1)}, u32[]{:S(2)}, u32[]{:S(2)}) collective-permute-start(bf16[256,256]{1,0:T(8,128)(2,1)S(1)} %get-tuple-element.42), channel_id=1, source_target_pairs={{0,2},{1,3},{2,0},{3,1},{4,6},{5,7},{6,4},{7,5},{8,10},{9,11},{10,... | collective-permute-start | bytes 393224 | tf_op jit(solution)/shard_map/ppermute | solution.py:546
  43.8 2.2 %collective-permute-start.12 = (bf16[256,256]{1,0:T(8,128)(2,1)S(1)}, bf16[256,256]{1,0:T(8,128)(2,1)S(1)}, u32[]{:S(2)}, u32[]{:S(2)}) collective-permute-start(bf16[256,256]{1,0:T(8,128)(2,1)S(1)} %get-tuple-element.43), channel_id=1, source_target_pairs={{0,3},{1,2},{2,1},{3,0},{4,7},{5,6},{6,5},{7,4},{8,11},{9,10},{10,... | collective-permute-start | bytes 393224 | tf_op jit(solution)/shard_map/ppermute | solution.py:546
  46.5 1.6 %collective-permute-start.8 = (bf16[240,512]{1,0:T(8,128)(2,1)S(1)}, bf16[240,512]{1,0:T(8,128)(2,1)S(1)}, u32[]{:S(2)}, u32[]{:S(2)}) collective-permute-start(bf16[240,512]{1,0:T(8,128)(2,1)S(1)} %get-tuple-element.38), channel_id=1, source_target_pairs={{0,2},{1,3},{2,0},{3,1},{4,6},{5,7},{6,4},{7,5},{8,10},{9,11},{10,... | collective-permute-start | bytes 737288 | tf_op jit(solution)/shard_map/ppermute | solution.py:546
  48.1 1.5 %collective-permute-start.9 = (bf16[240,512]{1,0:T(8,128)(2,1)S(1)}, bf16[240,512]{1,0:T(8,128)(2,1)S(1)}, u32[]{:S(2)}, u32[]{:S(2)}) collective-permute-start(bf16[240,512]{1,0:T(8,128)(2,1)S(1)} %get-tuple-element.40), channel_id=1, source_target_pairs={{0,1},{1,0},{2,3},{3,2},{4,5},{5,4},{6,7},{7,6},{8,9},{9,8},{10,11... | collective-permute-start | bytes 737288 | tf_op jit(solution)/shard_map/ppermute | solution.py:546
  49.6 4.1 %collective-permute-done.11.refs_11_ = bf16[256,256]{1,0:T(8,128)(2,1)S(1)} collective-permute-done((bf16[256,256]{1,0:T(8,128)(2,1)S(1)}, bf16[256,256]{1,0:T(8,128)(2,1)S(1)}, u32[]{:S(2)}, u32[]{:S(2)}) %collective-permute-start.11) | collective-permute-done | bytes 131104 | tf_op jit(solution)/shard_map/ppermute | solution.py:546
  53.8 5.6 %attend_chunk.2.refs_15_ = bf16[60,4,4096]{2,1,0:T(4,128)(2,1)} custom-call(s32[3]{0:T(128)S(1)} %pad_add_fusion.ids.rest_0_, s32[1]{0:T(128)} %constant.43.clone.1.first, s32[60]{0:T(128)S(1)} %copy-done.8, bf16[60,4,4096]{2,1,0:T(4,128)(2,1)S(1)} %copy-done.5, bf16[60,16,1024]{2,1,0:T(8,128)(2,1)S(1)} %copy-done.6, ...), custom_call_target="tpu_custom_call", output_to_operand_aliasing={{}: (18, {})} | custom-call | flops 16000000000 | bytes 10846208 | tf_op jit(solution)/shard_map/attend_chunk/pallas_call | solution.py:523
  59.4 5.0 %attend_chunk.3 = bf16[60,4,4096]{2,1,0:T(4,128)(2,1)} custom-call(s32[3]{0:T(128)S(1)} %pad_add_fusion.ids.rest_0_, s32[1]{0:T(128)} %constant.41.clone.1.first, s32[60]{0:T(128)S(1)} %copy-done.8, bf16[60,4,4096]{2,1,0:T(4,128)(2,1)S(1)} %copy-done.5, bf16[60,16,1024]{2,1,0:T(8,128)(2,1)S(1)} %copy-done.6, ...), custom_call_target="tpu_custom_call", output_to_operand_aliasing={{}: (18, {})} | custom-call | flops 16000000000 | bytes 10846208 | tf_op jit(solution)/shard_map/attend_chunk/pallas_call | solution.py:523
  (50 shorter events, 2.3 us)
Async XLA Ops:
  0.7 13.4 %copy-start.12 = (s32[60]{0:T(128)S(1)}, s32[60]{0:T(128)}, u32[]{:S(2)}) copy-start(s32[60]{0:T(128)} %param.23) | copy-start | bytes 724
  0.7 13.6 %copy-start.11 = (f32[128]{0:T(128)S(1)}, f32[128]{0:T(128)}, u32[]{:S(2)}) copy-start(f32[128]{0:T(128)} %param.18) | copy-start | bytes 1540
  7.3 22.2 %collective-permute-start.6 = (bf16[480,512]{1,0:T(8,128)(2,1)}, bf16[480,512]{1,0:T(8,128)(2,1)}, u32[]{:S(2)}, u32[]{:S(2)}) collective-permute-start(bf16[480,512]{1,0:T(8,128)(2,1)} %get-tuple-element.35), channel_id=1, source_target_pairs={{0,2},{1,3},{2,0},{3,1},{4,6},{5,7},{6,4},{7,5},{8,10},{9,11},{10,... | collective-permute-start | bytes 1474568 | tf_op jit(solution)/shard_map/ppermute | solution.py:546
  10.4 19.2 %collective-permute-start.5 = (bf16[480,512]{1,0:T(8,128)(2,1)S(1)}, bf16[480,512]{1,0:T(8,128)(2,1)}, u32[]{:S(2)}, u32[]{:S(2)}) collective-permute-start(bf16[480,512]{1,0:T(8,128)(2,1)S(1)} %get-tuple-element.27.after), channel_id=1, source_target_pairs={{0,1},{1,0},{2,3},{3,2},{4,5},{5,4},{6,7},{7,6},{8,9},{9,8},{10,11... | collective-permute-start | bytes 1474568 | tf_op jit(solution)/shard_map/ppermute | solution.py:546
  14.1 1.8 %collective-permute-start = (bf16[64,1536]{1,0:T(8,128)(2,1)}, bf16[64,1536]{1,0:T(8,128)(2,1)}, u32[]{:S(2)}, u32[]{:S(2)}) collective-permute-start(bf16[64,1536]{1,0:T(8,128)(2,1)} %get-tuple-element.28), channel_id=1, source_target_pairs={{0,4},{4,0},{8,12},{12,8},{16,20},{20,16},{24,28},{28,24},{1,5},{5... | collective-permute-start | bytes 589832 | tf_op jit(solution)/shard_map/ppermute | solution.py:338
  17.5 8.8 %collective-permute-start.3 = (bf16[64,1536]{1,0:T(8,128)(2,1)S(1)}, bf16[64,1536]{1,0:T(8,128)(2,1)S(1)}, u32[]{:S(2)}, u32[]{:S(2)}) collective-permute-start(bf16[64,1536]{1,0:T(8,128)(2,1)S(1)} %chip_grads.1.rest_0_.a), channel_id=1, source_target_pairs={{0,8},{4,12},{8,0},{12,4},{16,24},{20,28},{24,16},{28,20},{1,9},{5... | collective-permute-start | bytes 589832 | tf_op jit(solution)/shard_map/ppermute | solution.py:360
  25.2 17.8 %collective-permute-start.2 = (bf16[480,512]{1,0:T(8,128)(2,1)S(1)}, bf16[480,512]{1,0:T(8,128)(2,1)S(1)}, u32[]{:S(2)}, u32[]{:S(2)}) collective-permute-start(bf16[480,512]{1,0:T(8,128)(2,1)S(1)} %get-tuple-element.32), channel_id=1, source_target_pairs={{0,2},{1,3},{2,0},{3,1},{4,6},{5,7},{6,4},{7,5},{8,10},{9,11},{10,... | collective-permute-start | bytes 1474568 | tf_op jit(solution)/shard_map/ppermute | solution.py:546
  25.7 18.0 %collective-permute-start.1 = (bf16[480,512]{1,0:T(8,128)(2,1)S(1)}, bf16[480,512]{1,0:T(8,128)(2,1)S(1)}, u32[]{:S(2)}, u32[]{:S(2)}) collective-permute-start(bf16[480,512]{1,0:T(8,128)(2,1)S(1)} %get-tuple-element.30.rest_0_), channel_id=1, source_target_pairs={{0,1},{1,0},{2,3},{3,2},{4,5},{5,4},{6,7},{7,6},{8,9},{9,8},{10,11... | collective-permute-start | bytes 1474568 | tf_op jit(solution)/shard_map/ppermute | solution.py:546
  26.3 14.5 %copy-start = (f32[2,64,1280]{2,1,0:T(8,128)S(1)}, f32[2,64,1280]{2,1,0:T(8,128)}, u32[]{:S(2)}) copy-start(f32[2,64,1280]{2,1,0:T(8,128)} %refs_2_.3) | copy-start | bytes 1966084
  26.3 14.5 %copy-start.3 = (f32[2,64,256]{2,1,0:T(8,128)S(1)}, f32[2,64,256]{2,1,0:T(8,128)}, u32[]{:S(2)}) copy-start(f32[2,64,256]{2,1,0:T(8,128)} %refs_3_.1) | copy-start | bytes 393220
  26.4 11.1 %collective-permute-start.4 = (bf16[64,1536]{1,0:T(8,128)(2,1)S(1)}, bf16[64,1536]{1,0:T(8,128)(2,1)S(1)}, u32[]{:S(2)}, u32[]{:S(2)}) collective-permute-start(bf16[64,1536]{1,0:T(8,128)(2,1)S(1)} %plus.2.after.a), channel_id=1, source_target_pairs={{0,16},{4,20},{8,24},{12,28},{16,0},{20,4},{24,8},{28,12},{1,17},{... | collective-permute-start | bytes 589832 | tf_op jit(solution)/shard_map/ppermute | solution.py:360
  37.5 16.2 %copy-start.7 = (bf16[60,16,1024]{2,1,0:T(8,128)(2,1)S(1)}, bf16[60,16,1024]{2,1,0:T(8,128)(2,1)}, u32[]{:S(2)}) copy-start(bf16[60,16,1024]{2,1,0:T(8,128)(2,1)} %refs_2_.5) | copy-start | bytes 5898244
  37.6 3.3 %collective-permute-start.7 = (bf16[64,1536]{1,0:T(8,128)(2,1)S(1)}, bf16[64,1536]{1,0:T(8,128)(2,1)S(1)}, u32[]{:S(2)}, u32[]{:S(2)}) collective-permute-start(bf16[64,1536]{1,0:T(8,128)(2,1)S(1)} %plus.3.refs_0_), channel_id=1, source_target_pairs={{0,4},{4,0},{8,12},{12,8},{16,20},{20,16},{24,28},{28,24},{1,5},{5... | collective-permute-start | bytes 589832 | tf_op jit(solution)/shard_map/ppermute | solution.py:338
  37.7 16.1 %copy-start.5 = (bf16[60,4,4096]{2,1,0:T(4,128)(2,1)S(1)}, bf16[60,4,4096]{2,1,0:T(4,128)(2,1)}, u32[]{:S(2)}) copy-start(bf16[60,4,4096]{2,1,0:T(4,128)(2,1)} %refs_0_.3) | copy-start | bytes 5898244
  37.7 16.1 %copy-start.6 = (bf16[60,16,1024]{2,1,0:T(8,128)(2,1)S(1)}, bf16[60,16,1024]{2,1,0:T(8,128)(2,1)}, u32[]{:S(2)}) copy-start(bf16[60,16,1024]{2,1,0:T(8,128)(2,1)} %refs_1_.3) | copy-start | bytes 5898244
  37.7 16.1 %copy-start.8 = (s32[60]{0:T(128)S(1)}, s32[60]{0:T(128)}, u32[]{:S(2)}) copy-start(s32[60]{0:T(128)} %lengths.3) | copy-start | bytes 724
  37.7 16.1 %copy-start.10 = (bf16[240,512]{1,0:T(8,128)(2,1)S(1)}, bf16[240,512]{1,0:T(8,128)(2,1)}, u32[]{:S(2)}) copy-start(bf16[240,512]{1,0:T(8,128)(2,1)} %copy-done.9) | copy-start | bytes 737284
  37.7 8.8 %collective-permute-start.14 = (bf16[240,512]{1,0:T(8,128)(2,1)S(1)}, bf16[240,512]{1,0:T(8,128)(2,1)S(1)}, u32[]{:S(2)}, u32[]{:S(2)}) collective-permute-start(bf16[240,512]{1,0:T(8,128)(2,1)S(1)} %get-tuple-element.45), channel_id=1, source_target_pairs={{0,1},{1,0},{2,3},{3,2},{4,5},{5,4},{6,7},{7,6},{8,9},{9,8},{10,11... | collective-permute-start | bytes 737288 | tf_op jit(solution)/shard_map/ppermute | solution.py:546
  39.3 8.8 %collective-permute-start.13 = (bf16[240,512]{1,0:T(8,128)(2,1)S(1)}, bf16[240,512]{1,0:T(8,128)(2,1)S(1)}, u32[]{:S(2)}, u32[]{:S(2)}) collective-permute-start(bf16[240,512]{1,0:T(8,128)(2,1)S(1)} %get-tuple-element.36.rest_0_.refs_5_), channel_id=1, source_target_pairs={{0,2},{1,3},{2,0},{3,1},{4,6},{5,7},{6,4},{7,5},{8,10},{9,11},{10,... | collective-permute-start | bytes 737288 | tf_op jit(solution)/shard_map/ppermute | solution.py:546
  42.4 7.2 %collective-permute-start.10 = (bf16[256,256]{1,0:T(8,128)(2,1)S(1)}, bf16[256,256]{1,0:T(8,128)(2,1)S(1)}, u32[]{:S(2)}, u32[]{:S(2)}) collective-permute-start(bf16[256,256]{1,0:T(8,128)(2,1)S(1)} %get-tuple-element.41), channel_id=1, source_target_pairs={{0,1},{1,0},{2,3},{3,2},{4,5},{5,4},{6,7},{7,6},{8,9},{9,8},{10,11... | collective-permute-start | bytes 393224 | tf_op jit(solution)/shard_map/ppermute | solution.py:546
  43.0 10.7 %collective-permute-start.11 = (bf16[256,256]{1,0:T(8,128)(2,1)S(1)}, bf16[256,256]{1,0:T(8,128)(2,1)S(1)}, u32[]{:S(2)}, u32[]{:S(2)}) collective-permute-start(bf16[256,256]{1,0:T(8,128)(2,1)S(1)} %get-tuple-element.42), channel_id=1, source_target_pairs={{0,2},{1,3},{2,0},{3,1},{4,6},{5,7},{6,4},{7,5},{8,10},{9,11},{10,... | collective-permute-start | bytes 393224 | tf_op jit(solution)/shard_map/ppermute | solution.py:546
  43.8 10.0 %collective-permute-start.12 = (bf16[256,256]{1,0:T(8,128)(2,1)S(1)}, bf16[256,256]{1,0:T(8,128)(2,1)S(1)}, u32[]{:S(2)}, u32[]{:S(2)}) collective-permute-start(bf16[256,256]{1,0:T(8,128)(2,1)S(1)} %get-tuple-element.43), channel_id=1, source_target_pairs={{0,3},{1,2},{2,1},{3,0},{4,7},{5,6},{6,5},{7,4},{8,11},{9,10},{10,... | collective-permute-start | bytes 393224 | tf_op jit(solution)/shard_map/ppermute | solution.py:546
  46.5 12.8 %collective-permute-start.8 = (bf16[240,512]{1,0:T(8,128)(2,1)S(1)}, bf16[240,512]{1,0:T(8,128)(2,1)S(1)}, u32[]{:S(2)}, u32[]{:S(2)}) collective-permute-start(bf16[240,512]{1,0:T(8,128)(2,1)S(1)} %get-tuple-element.38), channel_id=1, source_target_pairs={{0,2},{1,3},{2,0},{3,1},{4,6},{5,7},{6,4},{7,5},{8,10},{9,11},{10,... | collective-permute-start | bytes 737288 | tf_op jit(solution)/shard_map/ppermute | solution.py:546
  48.1 11.3 %collective-permute-start.9 = (bf16[240,512]{1,0:T(8,128)(2,1)S(1)}, bf16[240,512]{1,0:T(8,128)(2,1)S(1)}, u32[]{:S(2)}, u32[]{:S(2)}) collective-permute-start(bf16[240,512]{1,0:T(8,128)(2,1)S(1)} %get-tuple-element.40), channel_id=1, source_target_pairs={{0,1},{1,0},{2,3},{3,2},{4,5},{5,4},{6,7},{7,6},{8,9},{9,8},{10,11... | collective-permute-start | bytes 737288 | tf_op jit(solution)/shard_map/ppermute | solution.py:546
  (4 other events, 24.0 us)

commit v4 on v3

--- a/solution.py
+++ b/solution.py
@@ -119,11 +119,6 @@
     return pltpu.CompilerParams(vmem_limit_bytes=limit)
 
 
-def cost(flops, args, outs):
-    size = sum(math.prod(x.shape) * x.dtype.itemsize for x in [*args, *outs])
-    return pl.CostEstimate(flops=flops, bytes_accessed=size, transcendentals=0)
-
-
 def dot(a, b):
     return jnp.dot(a, b, preferred_element_type=F32)
 
@@ -143,54 +138,22 @@
 TILE = 256
 
 
-def terms_kernel(first, ids, hidden, weight, *rest):
-    if first:
-        x, *outs, held, hidden_sems, w, sems = rest[1:]
-        tiles = w.shape[1]
-        tokens = x.shape[0] // 4
-        rows = tokens // STEPS
-
-        def hidden_copy(r):
-            at = pl.ds((ids[0] ^ r) * rows, rows)
-            return pltpu.make_async_copy(hidden.at[at], held.at[r], hidden_sems.at[r])
-
-        def weight_copy(p, i):
-            at = pl.ds(i * TILE, TILE)
-            return pltpu.make_async_copy(weight.at[p, :, at], w.at[p, i], sems.at[p, i])
-
-        for r in range(4):
-            hidden_copy(r).start()
-        for i in range(tiles):
-            for p in range(2):
-                weight_copy(p, i).start()
-        for r in range(4):
-            hidden_copy(r).wait()
-            x[r * tokens : (r + 1) * tokens] = held[r].reshape(tokens, x.shape[1])
-    else:
-        x, outs = hidden, rest[1:]
-        tokens = x.shape[0] // 4
-        tiles = outs[0].shape[1] // TILE
-        base = weight.shape[2] - tiles * TILE
+def multiply_terms(x, w, outs, ready):
     ksend, kkeep, vsend, vkeep0, vkeep1 = outs
+    tokens = x.shape[0] // 4
     steps = x.shape[1] // TILE
+    low, high = slice(0, tokens), slice(tokens, 2 * tokens)
 
     def multiply(*accs):
         accs_k, accs_v = accs[:4], accs[4:]
 
-        @pl.loop(0, tiles)
+        @pl.loop(0, w.shape[1])
         def _(i):
-            if first:
+            ready(i)
+
+            def push(k):
                 for p in range(2):
-                    weight_copy(p, i).wait()
-
-            def push(k):
-                rows = slice(k * TILE, (k + 1) * TILE)
-                for p in range(2):
-                    if first:
-                        tile = w[p, i, rows, :]
-                    else:
-                        tile = weight[p, rows, pl.ds(pl.multiple_of(base + i * TILE, TILE), TILE)]
-                    pltpu.matmul_push_rhs(tile, k % 2, p)
+                    pltpu.matmul_push_rhs(w[p, i, k * TILE : (k + 1) * TILE, :], k % 2, p)
 
             push(0)
             for k in range(steps):
@@ -202,7 +165,6 @@
                     pltpu.matmul_acc_lhs(accs_k[r], rows, load_staged_rhs=staged)
                     pltpu.matmul_acc_lhs(accs_v[r], rows, load_staged_rhs=staged)
             at = pl.ds(pl.multiple_of(i * TILE, TILE), TILE)
-            low, high = slice(0, tokens), slice(tokens, 2 * tokens)
             kkeep[low, at] = pltpu.matmul_pop(accs_k[0]).astype(BF)
             vkeep0[:, at] = pltpu.matmul_pop(accs_v[0]).astype(BF)
             ksend[high, at] = pltpu.matmul_pop(accs_k[1]).astype(BF)
@@ -217,39 +179,108 @@
     )
 
 
-def projection_terms(ids, hidden, kv_weight, count, tokens, after):
-    first = len(hidden.shape) == 3
-    width = hidden.shape[-1]
-    wide = count * HD
-    assert wide % TILE == 0 and width % TILE == 0
-    rows = (2, 2, 2, 1, 1)
-    outs = [jax.ShapeDtypeStruct((n * tokens, wide), BF) for n in rows]
-    scratch = []
-    if first:
-        outs.insert(0, jax.ShapeDtypeStruct((4 * tokens, width), BF))
-        scratch += [
-            pltpu.VMEM((4, tokens // STEPS, STEPS, width), BF),
-            pltpu.SemaphoreType.DMA((4,)),
-            pltpu.VMEM((2, wide // TILE, width, TILE), BF),
-            pltpu.SemaphoreType.DMA((2, wide // TILE)),
-        ]
+def first_kernel(ids, hidden, weight, grad_a, grad_b, *rest):
+    x, *outs = rest[:6]
+    send, own, later, _ = rest[6:10]
+    held, w, held_a, held_b, hidden_sems, sems, later_sems, grad_sems = rest[10:]
+    tokens = x.shape[0] // 4
+    rows = tokens // STEPS
+
+    def hidden_copy(r):
+        at = pl.ds((ids[0] ^ r) * rows, rows)
+        return pltpu.make_async_copy(hidden.at[at], held.at[r], hidden_sems.at[r])
+
+    def weight_copy(p, i):
+        at = pl.ds(i * TILE, TILE)
+        return pltpu.make_async_copy(weight.at[p, :, at], w.at[p, i], sems.at[p, i])
+
+    def later_copy(p, i):
+        at = pl.ds((w.shape[1] + i) * TILE, TILE)
+        return pltpu.make_async_copy(weight.at[p, :, at], later.at[p, i], later_sems.at[p, i])
+
+    others = [
+        pltpu.make_async_copy(grad_a.at[0], held_a, grad_sems.at[0]),
+        pltpu.make_async_copy(grad_b.at[0], held_b, grad_sems.at[1]),
+    ]
+    others += [later_copy(p, i) for i in range(later.shape[1]) for p in range(2)]
+    for r in range(4):
+        hidden_copy(r).start()
+    for i in range(w.shape[1]):
+        for p in range(2):
+            weight_copy(p, i).start()
+    for r in range(4):
+        hidden_copy(r).wait()
+        x[r * tokens : (r + 1) * tokens] = held[r].reshape(tokens, x.shape[1])
+    for copy in others:
+        copy.start()
+
+    def ready(i):
+        for p in range(2):
+            weight_copy(p, i).wait()
+
+    multiply_terms(x, w, outs, ready)
+    for copy in others:
+        copy.wait()
+    wide = grad_a.shape[-1]
+    for out, p in ((send, ids[2] ^ 1), (own, ids[2])):
+        out[:, :wide] = held_a[p].astype(BF)
+        out[:, wide:] = held_b[p].astype(BF)
+
+
+def later_kernel(x, w, after, *outs):
+    del after
+    multiply_terms(x, w, outs, lambda i: None)
+
+
+def term_shapes(tokens, count):
+    return [jax.ShapeDtypeStruct((n * tokens, count * HD), BF) for n in (2, 2, 2, 1, 1)]
+
+
+def first_terms(ids, hidden, kv_weight, grad_a, grad_b, queries, tokens):
+    width = hidden.shape[2]
+    rank, wide = grad_a.shape[2], grad_a.shape[3] + grad_b.shape[3]
     here = pl.BlockSpec(memory_space=pl.ANY)
+    outs = [jax.ShapeDtypeStruct((4 * tokens, width), BF), *term_shapes(tokens, CHUNKS[0])]
+    outs += [jax.ShapeDtypeStruct((rank, wide), BF)] * 2
+    tiles = [count * HD // TILE for count in CHUNKS]
+    outs.append(pltpu.VMEM((2, tiles[1], width, TILE), BF))
+    specs = [whole(x.shape) for x in outs] + [here]
+    outs.append(jax.ShapeDtypeStruct(queries.shape, BF))
     return pl.pallas_call(
-        functools.partial(terms_kernel, first),
+        first_kernel,
         out_shape=outs,
         grid_spec=pltpu.PrefetchScalarGridSpec(
             num_scalar_prefetch=1,
             grid=(1,),
-            in_specs=[here, here, here]
-            if first
-            else [whole(hidden.shape), whole(kv_weight.shape), here],
-            out_specs=[whole(x.shape) for x in outs],
-            scratch_shapes=scratch,
+            in_specs=[here] * 4,
+            out_specs=specs,
+            scratch_shapes=[
+                pltpu.VMEM((4, tokens // STEPS, STEPS, width), BF),
+                pltpu.VMEM((2, tiles[0], width, TILE), BF),
+                pltpu.VMEM(grad_a.shape[1:], F32),
+                pltpu.VMEM(grad_b.shape[1:], F32),
+                pltpu.SemaphoreType.DMA((4,)),
+                pltpu.SemaphoreType.DMA((2, tiles[0])),
+                pltpu.SemaphoreType.DMA((2, tiles[1])),
+                pltpu.SemaphoreType.DMA((2,)),
+            ],
         ),
         compiler_params=params(),
-        cost_estimate=cost(2 * 4 * tokens * width * 2 * wide, [hidden], outs),
-        name="projection_terms",
-    )(ids, *(map(hbm, (hidden, kv_weight)) if first else (hidden, kv_weight)), after)
+        name="first_terms",
+    )(ids, *map(hbm, (hidden, kv_weight, grad_a, grad_b)))
+
+
+def later_terms(x, w, after):
+    outs = term_shapes(x.shape[0] // 4, CHUNKS[1])
+    return pl.pallas_call(
+        later_kernel,
+        out_shape=outs,
+        grid=(1,),
+        in_specs=[whole(x.shape), whole(w.shape), pl.BlockSpec(memory_space=pl.ANY)],
+        out_specs=[whole(out.shape) for out in outs],
+        compiler_params=params(),
+        name="later_terms",
+    )(x, w, after)
 
 
 def mid_kernel(kkeep, kcame, vkeep, vcame, after, kout, vout):
@@ -269,45 +300,8 @@
         in_specs=[high, low, low, high, pl.BlockSpec(memory_space=pl.ANY)],
         out_specs=[low, low],
         compiler_params=params(),
-        cost_estimate=cost(0, [vkeep] * 6, []),
         name="mid_sums",
     )(kkeep, kcame, vkeep, vcame, after)
-
-
-def pack_kernel(ids, grad_a, grad_b, after, out, unwritten):
-    del ids, after, unwritten
-    wide = grad_a.shape[-1]
-    out[:, :wide] = grad_a[0, 0].astype(BF)
-    out[:, wide:] = grad_b[0, 0].astype(BF)
-
-
-def chip_kernel(ids, grad_a, grad_b, other, out):
-    del ids
-    wide = grad_a.shape[-1]
-    out[:, :wide] = (grad_a[0, 0] + other[:, :wide].astype(F32)).astype(BF)
-    out[:, wide:] = (grad_b[0, 0] + other[:, wide:].astype(F32)).astype(BF)
-
-
-def grad_half(kernel, name, ids, grad_a, grad_b, flip, rest, rest_specs, more_outs=()):
-    rank, wide = grad_a.shape[2], grad_a.shape[3] + grad_b.shape[3]
-
-    def spec(x):
-        return pl.BlockSpec((1, 1) + x.shape[2:], lambda i, ids: (0, ids[2] ^ flip, 0, 0))
-
-    out = jax.ShapeDtypeStruct((rank, wide), BF)
-    return pl.pallas_call(
-        kernel,
-        out_shape=[out, *more_outs],
-        grid_spec=pltpu.PrefetchScalarGridSpec(
-            num_scalar_prefetch=1,
-            grid=(1,),
-            in_specs=[spec(grad_a), spec(grad_b), *rest_specs],
-            out_specs=[whole(out.shape)] + [pl.BlockSpec(memory_space=pl.ANY)] * len(more_outs),
-        ),
-        compiler_params=params(),
-        cost_estimate=cost(0, [out] * 4, []),
-        name=name,
-    )(ids, hbm(grad_a), hbm(grad_b), *rest)
 
 
 def small_call(kernel, name, ids, args, outs, after=(), scratch=(), copied=0):
@@ -329,7 +323,6 @@
             scratch_shapes=list(scratch),
         ),
         compiler_params=params(),
-        cost_estimate=cost(0, args, []),
         name=name,
     )(ids, *args, *after)
 
@@ -351,7 +344,6 @@
         in_specs=[whole(a.shape)] * 2 + [pl.BlockSpec(memory_space=pl.ANY)] * len(after),
         out_specs=whole(a.shape),
         compiler_params=params(),
-        cost_estimate=cost(0, [a, b], [out]),
         name="plus",
     )(a, b, *after)
 
@@ -508,7 +500,7 @@
     rows, slots, _ = cache_keys.shape
     tokens = rows * STEPS
     heads = QH // KVH
-    args = [queries, cache_keys, cache_values, *terms, *ub, *tables]
+    args = [*map(hbm, (queries, cache_keys, cache_values)), *terms, *ub, *tables]
     assert start % HEADS_STEP == 0 and count % HEADS_STEP == 0
     first = jnp.full((1,), start // HEADS_STEP, jnp.int32)
     size = HEADS_STEP * HD
@@ -528,7 +520,6 @@
         ),
         input_output_aliases={len(args) + 2: 0},
         compiler_params=params(),
-        cost_estimate=cost(count * 4 * 10**9, args, []),
         name="attend_chunk",
     )(ids, first, lengths, *args)
 
@@ -566,23 +557,11 @@
     ids = jnp.stack([lax.axis_index("tensor"), dp // 2, dp % 2]).astype(jnp.int32)
     tables = rotary_tables(key_gain, positions)
 
-    x, *first = projection_terms(ids, hidden_in, kv_weight, CHUNKS[0], tokens, ids)
-    here = pl.BlockSpec(memory_space=pl.ANY)
-    packed, attended = grad_half(
-        pack_kernel,
-        "pack_grads",
-        ids,
-        grad_a,
-        grad_b,
-        1,
-        [first[0]],
-        [here],
-        [jax.ShapeDtypeStruct(queries.shape, BF)],
-    )
-    other = core_flip(packed, count_dp)
-    (half,) = grad_half(
-        chip_kernel, "chip_grads", ids, grad_a, grad_b, 0, [other], [whole(other.shape)]
-    )
+    x, *first, packed, own, weights, attended = first_terms(
+        ids, hidden_in, kv_weight, grad_a, grad_b, queries, tokens
+    )
+    half = plus(own, core_flip(packed, count_dp))
+
     def first_exchange(term, after):
         ksend, kkeep, vsend, vkeep0, vkeep1 = term
         kcame, vcame = across(ksend, 1), across(vsend, 2)
@@ -593,7 +572,7 @@
         kkeep, kcame, vkeep0, vcame = parts
         return kkeep, kcame, across(mids[0], 2), vkeep0, vcame, across(mids[1], 1)
 
-    second = projection_terms(ids, x, kv_weight, CHUNKS[1], tokens, half)
+    second = later_terms(x, weights, half)
     step, after = 1, second[:1]
     while 2 * step < count_dp:
         half = plus(half, along_line(half, step, count_dp), *after)
@@ -603,13 +582,14 @@
             after = (mids[0], tables[0])
     if step == 1:
         mids, parts = first_exchange(first, half)
+    first = second_exchange(mids, parts)
     other = core_flip(half, count_dp)
-    first = second_exchange(mids, parts)
+    mids, parts = first_exchange(second, half)
+    second = second_exchange(mids, parts)
     new_a, new_b, *sends = updated(
         ids, half, other, factor_a, factor_b, x, count_dp, mids[0]
     )
     ub = [sends[0]] + [across(sends[r], r) for r in (1, 2, 3)]
-    second = second_exchange(*first_exchange(second, sends[0]))
     for start, count, came in ((0, CHUNKS[0], first), (CHUNKS[0], CHUNKS[1], second)):
         attended = attend_chunk(
             ids,

time: 64.6 us -> 66.3 us (1.026)
  local copies, waits for them, and re-layouts: 2.64 us -> 6.35 us
  Pallas kernels: 27.5 us -> 25.2 us
    ppermute x11, waiting for transfers between devices: 4.63 us -> 9.13 us  [across(): return lax.ppermute(x, 'tensor', [(i, i ^ r) for i in range(4)])]
    pallas_call x4 -> x2, Pallas kernels: 13.9 us -> 9.77 us  [the longest x1 6.89 us: first_terms(): pl.pallas_call(first_kernel, out_shape=outs, grid_spec=pltpu.PrefetchScal...]
    unnamed x26, local copies, waits for them, and re-layouts: 2.54 us -> 6.25 us
    ppermute x2, waiting for transfers between devices: 6.74 us -> 4.28 us  [along_line(): return lax.ppermute(x, 'dp', [(i, i ^ 2 * d) for i in range(count)])]
    ppermute x2, waiting for transfers between devices: 1.48 us -> 0.01 us  [core_flip(): return lax.ppermute(x, 'dp', [(i, i ^ 1) for i in range(count)])]
    pallas_call x2, Pallas kernels: 10.6 us -> 11.7 us  [attend_chunk(): pl.pallas_call(attend_kernel, out_shape=jax.ShapeDtypeStruct(queries.shap...]
    pallas_call x2 -> x3, Pallas kernels: 0.1 us -> 1.07 us  [plus(): pl.pallas_call(plus_kernel, out_shape=out, grid=(1,), in_specs=[whole(a.s...]
    ppermute x11, starting transfers between devices: 15.4 us -> 14.6 us  [across(): return lax.ppermute(x, 'tensor', [(i, i ^ r) for i in range(4)])]
  transfers between devices with their start and end apart: 15 -> 15, of which waited for: 4 -> 5; matrix products, arithmetic and copies ran while one was open for 1% -> 1% of each run, Pallas kernels for 25% -> 19%
where the time goes in v4:
time: 66.3 us; the launch traced here: 66.1 us
  Pallas kernels  25.2 us (38%)
  starting transfers between devices  19.5 us (29%)
  waiting for transfers between devices  13.4 us (20%)
  local copies, waits for them, and re-layouts  6.35 us (10%)
  other arithmetic  0.82 us (1%)
  between operations  0.78 us (1%)
    ppermute x11, starting transfers between devices, across(): return lax.ppermute(x, 'tensor', [(i, i ^ r) for i in range(4)])  14.6 us
    pallas_call x2, Pallas kernels, attend_chunk(): pl.pallas_call(attend_kernel, out_shape=jax.ShapeDtypeStruct(queries.shap...  11.7 us
    ppermute x11, waiting for transfers between devices, across(): return lax.ppermute(x, 'tensor', [(i, i ^ r) for i in range(4)])  9.13 us
    pallas_call x1, Pallas kernels, first_terms(): pl.pallas_call(first_kernel, out_shape=outs, grid_spec=pltpu.PrefetchScal...  6.89 us
    unnamed x26, local copies, waits for them, and re-layouts  6.25 us
    ppermute x2, starting transfers between devices, along_line(): return lax.ppermute(x, 'dp', [(i, i ^ 2 * d) for i in range(count)])  4.3 us
    ppermute x2, waiting for transfers between devices, along_line(): return lax.ppermute(x, 'dp', [(i, i ^ 2 * d) for i in range(count)])  4.28 us
    pallas_call x1, Pallas kernels, later_terms(): pl.pallas_call(later_kernel, out_shape=outs, grid=(1,), in_specs=[whole(x...  2.88 us
  transfers between devices with their start and end apart: 15, of which 5 were waited for; matrix products, arithmetic and copies ran while one was open for 1% of the time, Pallas kernels for 19%

profile of v4, /device:TPU:0, one launch (start us, length us, event | category | flops | bytes accessed | tf_op | source)
XLA Modules:
  0.0 66.1 jit_solution(16685559070735181473)
XLA Ops:
  0.7 6.9 %first_terms.1 = (bf16[960,1280]{1,0:T(8,128)(2,1)S(1)}, bf16[480,512]{1,0:T(8,128)(2,1)}, bf16[480,512]{1,0:T(8,128)(2,1)S(1)}, bf16[480,512]{1,0:T(8,128)(2,1)...) custom-call(s32[3]{0:T(128)S(1)} %pad_add_fusion.ids, ...), custom_call_target="tpu_custom_call" | custom-call | tf_op jit(solution)/shard_map/first_terms/pallas_call | solution.py:249
  7.6 1.5 %copy-done = bf16[2,2,1280,256]{3,2,1,0:T(8,128)(2,1)} copy-done((bf16[2,2,1280,256]{3,2,1,0:T(8,128)(2,1)}, bf16[2,2,1280,256]{3,2,1,0:T(8,128)(2,1)S(1)}, u32[]{:S(2)}) %copy-start) | copy-done | bytes 2621464
  11.6 2.5 %collective-permute-start.5 = (bf16[480,512]{1,0:T(8,128)(2,1)}, bf16[480,512]{1,0:T(8,128)(2,1)S(1)}, u32[]{:S(2)}, u32[]{:S(2)}) collective-permute-start(bf16[480,512]{1,0:T(8,128)(2,1)} %get-tuple-element.37), channel_id=1, source_target_pairs={{0,1},{1,0},{2,3},{3,2},{4,5},{5,4},{6,7},{7,6},{8,9},{9,8},{10,11... | collective-permute-start | bytes 1474568 | tf_op jit(solution)/shard_map/ppermute | solution.py:537
  14.1 1.5 %collective-permute-start.6 = (bf16[480,512]{1,0:T(8,128)(2,1)}, bf16[480,512]{1,0:T(8,128)(2,1)}, u32[]{:S(2)}, u32[]{:S(2)}) collective-permute-start(bf16[480,512]{1,0:T(8,128)(2,1)} %get-tuple-element.39), channel_id=1, source_target_pairs={{0,2},{1,3},{2,0},{3,1},{4,6},{5,7},{6,4},{7,5},{8,10},{9,11},{10,... | collective-permute-start | bytes 1474568 | tf_op jit(solution)/shard_map/ppermute | solution.py:537
  16.8 1.0 %plus.3.after.a = bf16[64,1536]{1,0:T(8,128)(2,1)S(1)} custom-call(bf16[64,1536]{1,0:T(8,128)(2,1)S(1)} %copy-done.8, bf16[64,1536]{1,0:T(8,128)(2,1)} %collective-permute-done.b), custom_call_target="tpu_custom_call" | custom-call | tf_op jit(solution)/shard_map/plus/pallas_call | solution.py:340
  17.8 1.6 %collective-permute-start.3 = (bf16[64,1536]{1,0:T(8,128)(2,1)S(1)}, bf16[64,1536]{1,0:T(8,128)(2,1)S(1)}, u32[]{:S(2)}, u32[]{:S(2)}) collective-permute-start(bf16[64,1536]{1,0:T(8,128)(2,1)S(1)} %plus.3.after.a), channel_id=1, source_target_pairs={{0,8},{4,12},{8,0},{12,4},{16,24},{20,28},{24,16},{28,20},{1,9},{5... | collective-permute-start | bytes 589832 | tf_op jit(solution)/shard_map/ppermute | solution.py:352
  19.5 1.7 %copy-done.1 = bf16[2,2,1280,256]{3,2,1,0:T(8,128)(2,1)S(1)} copy-done((bf16[2,2,1280,256]{3,2,1,0:T(8,128)(2,1)S(1)}, bf16[2,2,1280,256]{3,2,1,0:T(8,128)(2,1)}, u32[]{:S(2)}) %copy-start.1) | copy-done | bytes 2621464
  21.2 2.9 %later_terms.1 = (bf16[480,512]{1,0:T(8,128)(2,1)S(1)}, bf16[480,512]{1,0:T(8,128)(2,1)S(1)}, bf16[480,512]{1,0:T(8,128)(2,1)S(1)}, bf16[240,512]{1,0:T(8,128)(2,1)S(1)}, bf16[240,512]{1,0:T(8,128)(2,1)S(1)}) custom-call(bf16[960,1280]{1,0:T(8,128)(2,1)S(1)} %get-tuple-element.28.x.refs_4_, bf16[2,2,1280,256]{3,2,1,0:T(8,128)(2,1)S(1)} %copy-done.1, ...), custom_call_target="tpu_custom_call" | custom-call | tf_op jit(solution)/shard_map/later_terms/pallas_call | solution.py:275
  24.7 1.0 %collective-permute-start.2 = (bf16[480,512]{1,0:T(8,128)(2,1)S(1)}, bf16[480,512]{1,0:T(8,128)(2,1)S(1)}, u32[]{:S(2)}, u32[]{:S(2)}) collective-permute-start(bf16[480,512]{1,0:T(8,128)(2,1)S(1)} %get-tuple-element.35), channel_id=1, source_target_pairs={{0,2},{1,3},{2,0},{3,1},{4,6},{5,7},{6,4},{7,5},{8,10},{9,11},{10,... | collective-permute-start | bytes 1474568 | tf_op jit(solution)/shard_map/ppermute | solution.py:537
  25.8 2.7 %collective-permute-start.4 = (bf16[64,1536]{1,0:T(8,128)(2,1)S(1)}, bf16[64,1536]{1,0:T(8,128)(2,1)S(1)}, u32[]{:S(2)}, u32[]{:S(2)}) collective-permute-start(bf16[64,1536]{1,0:T(8,128)(2,1)S(1)} %plus.4.after.a), channel_id=1, source_target_pairs={{0,16},{4,20},{8,24},{12,28},{16,0},{20,4},{24,8},{28,12},{1,17},{... | collective-permute-start | bytes 589832 | tf_op jit(solution)/shard_map/ppermute | solution.py:352
  28.5 1.1 %mid_sums.2 = (bf16[240,512]{1,0:T(8,128)(2,1)S(1)}, bf16[240,512]{1,0:T(8,128)(2,1)S(1)}) custom-call(bf16[480,512]{1,0:T(8,128)(2,1)S(1)} %get-tuple-element.36.kkeep.refs_3_, bf16[480,512]{1,0:T(8,128)(2,1)S(1)} %collective-permute-done.5.kcame.refs_4_, bf16[240,512]{1,0:T(8,128)(2,1)S(1)} %copy-done.4, ...), custom_call_target="tpu_custom_call" | custom-call | tf_op jit(solution)/shard_map/mid_sums/pallas_call | solution.py:296
  29.6 1.6 %collective-permute-start.13 = (bf16[240,512]{1,0:T(8,128)(2,1)S(1)}, bf16[240,512]{1,0:T(8,128)(2,1)S(1)}, u32[]{:S(2)}, u32[]{:S(2)}) collective-permute-start(bf16[240,512]{1,0:T(8,128)(2,1)S(1)} %get-tuple-element.40.rest_0_), channel_id=1, source_target_pairs={{0,2},{1,3},{2,0},{3,1},{4,6},{5,7},{6,4},{7,5},{8,10},{9,11},{10,... | collective-permute-start | bytes 737288 | tf_op jit(solution)/shard_map/ppermute | solution.py:537
  31.2 1.0 %collective-permute-start.14 = (bf16[240,512]{1,0:T(8,128)(2,1)S(1)}, bf16[240,512]{1,0:T(8,128)(2,1)S(1)}, u32[]{:S(2)}, u32[]{:S(2)}) collective-permute-start(bf16[240,512]{1,0:T(8,128)(2,1)S(1)} %get-tuple-element.49), channel_id=1, source_target_pairs={{0,1},{1,0},{2,3},{3,2},{4,5},{5,4},{6,7},{7,6},{8,9},{9,8},{10,11... | collective-permute-start | bytes 737288 | tf_op jit(solution)/shard_map/ppermute | solution.py:537
  32.7 4.3 %collective-permute-done.4.b = bf16[64,1536]{1,0:T(8,128)(2,1)S(1)} collective-permute-done((bf16[64,1536]{1,0:T(8,128)(2,1)S(1)}, bf16[64,1536]{1,0:T(8,128)(2,1)S(1)}, u32[]{:S(2)}, u32[]{:S(2)}) %collective-permute-start.4) | collective-permute-done | bytes 196640 | tf_op jit(solution)/shard_map/ppermute | solution.py:352
  37.1 1.2 %collective-permute-done.1.kcame.refs_4_ = bf16[480,512]{1,0:T(8,128)(2,1)S(1)} collective-permute-done((bf16[480,512]{1,0:T(8,128)(2,1)S(1)}, bf16[480,512]{1,0:T(8,128)(2,1)S(1)}, u32[]{:S(2)}, u32[]{:S(2)}) %collective-permute-start.1) | collective-permute-done | bytes 491552 | tf_op jit(solution)/shard_map/ppermute | solution.py:537
  39.1 1.6 %collective-permute-start.7 = (bf16[240,512]{1,0:T(8,128)(2,1)S(1)}, bf16[240,512]{1,0:T(8,128)(2,1)S(1)}, u32[]{:S(2)}, u32[]{:S(2)}) collective-permute-start(bf16[240,512]{1,0:T(8,128)(2,1)S(1)} %get-tuple-element.41.refs_5_), channel_id=1, source_target_pairs={{0,2},{1,3},{2,0},{3,1},{4,6},{5,7},{6,4},{7,5},{8,10},{9,11},{10,... | collective-permute-start | bytes 737288 | tf_op jit(solution)/shard_map/ppermute | solution.py:537
  41.2 1.5 %update_factors.1 = (f32[2,64,1280]{2,1,0:T(8,128)}, f32[2,64,256]{2,1,0:T(8,128)}, bf16[256,256]{1,0:T(8,128)(2,1)S(1)}, bf16[256,256]{1,0:T(8,128)(2,1)S(1)}, ...) custom-call(s32[3]{0:T(128)S(1)} %pad_add_fusion.ids, bf16[64,1536]{1,0:T(8,128)(2,1)S(1)} %plus.5.after.refs_0_, ...), custom_call_target="tpu_custom_call" | custom-call | tf_op jit(solution)/shard_map/update_factors/pallas_call | solution.py:313
  42.7 1.6 %collective-permute-start.10 = (bf16[256,256]{1,0:T(8,128)(2,1)S(1)}, bf16[256,256]{1,0:T(8,128)(2,1)S(1)}, u32[]{:S(2)}, u32[]{:S(2)}) collective-permute-start(bf16[256,256]{1,0:T(8,128)(2,1)S(1)} %get-tuple-element.45), channel_id=1, source_target_pairs={{0,1},{1,0},{2,3},{3,2},{4,5},{5,4},{6,7},{7,6},{8,9},{9,8},{10,11... | collective-permute-start | bytes 393224 | tf_op jit(solution)/shard_map/ppermute | solution.py:537
  44.3 1.4 %collective-permute-start.11 = (bf16[256,256]{1,0:T(8,128)(2,1)S(1)}, bf16[256,256]{1,0:T(8,128)(2,1)S(1)}, u32[]{:S(2)}, u32[]{:S(2)}) collective-permute-start(bf16[256,256]{1,0:T(8,128)(2,1)S(1)} %get-tuple-element.46), channel_id=1, source_target_pairs={{0,2},{1,3},{2,0},{3,1},{4,6},{5,7},{6,4},{7,5},{8,10},{9,11},{10,... | collective-permute-start | bytes 393224 | tf_op jit(solution)/shard_map/ppermute | solution.py:537
  45.7 1.4 %collective-permute-start.12 = (bf16[256,256]{1,0:T(8,128)(2,1)S(1)}, bf16[256,256]{1,0:T(8,128)(2,1)S(1)}, u32[]{:S(2)}, u32[]{:S(2)}) collective-permute-start(bf16[256,256]{1,0:T(8,128)(2,1)S(1)} %get-tuple-element.47), channel_id=1, source_target_pairs={{0,3},{1,2},{2,1},{3,0},{4,7},{5,6},{6,5},{7,4},{8,11},{9,10},{10,... | collective-permute-start | bytes 393224 | tf_op jit(solution)/shard_map/ppermute | solution.py:537
  47.1 4.6 %collective-permute-done.10.refs_10_ = bf16[256,256]{1,0:T(8,128)(2,1)S(1)} collective-permute-done((bf16[256,256]{1,0:T(8,128)(2,1)S(1)}, bf16[256,256]{1,0:T(8,128)(2,1)S(1)}, u32[]{:S(2)}, u32[]{:S(2)}) %collective-permute-start.10) | collective-permute-done | bytes 131104 | tf_op jit(solution)/shard_map/ppermute | solution.py:537
  51.7 2.7 %collective-permute-done.11.refs_11_ = bf16[256,256]{1,0:T(8,128)(2,1)S(1)} collective-permute-done((bf16[256,256]{1,0:T(8,128)(2,1)S(1)}, bf16[256,256]{1,0:T(8,128)(2,1)S(1)}, u32[]{:S(2)}, u32[]{:S(2)}) %collective-permute-start.11) | collective-permute-done | bytes 131104 | tf_op jit(solution)/shard_map/ppermute | solution.py:537
  54.4 5.9 %attend_chunk.2.refs_15_ = bf16[60,4,4096]{2,1,0:T(4,128)(2,1)} custom-call(s32[3]{0:T(128)S(1)} %pad_add_fusion.ids, s32[1]{0:T(128)} %constant.43.clone.1.first, s32[60]{0:T(128)S(1)} %copy-done.10, bf16[60,4,4096]{2,1,0:T(4,128)(2,1)} %refs_0_.3, bf16[60,16,1024]{2,1,0:T(8,128)(2,1)} %refs_1_.3, ...), custom_call_target="tpu_custom_call", output_to_operand_aliasing={{}: (18, {})} | custom-call | tf_op jit(solution)/shard_map/attend_chunk/pallas_call | solution.py:515
  60.3 5.8 %attend_chunk.3 = bf16[60,4,4096]{2,1,0:T(4,128)(2,1)} custom-call(s32[3]{0:T(128)S(1)} %pad_add_fusion.ids, s32[1]{0:T(128)} %constant.41.clone.1.first, s32[60]{0:T(128)S(1)} %copy-done.10, bf16[60,4,4096]{2,1,0:T(4,128)(2,1)} %refs_0_.3, bf16[60,16,1024]{2,1,0:T(8,128)(2,1)} %refs_1_.3, ...), custom_call_target="tpu_custom_call", output_to_operand_aliasing={{}: (18, {})} | custom-call | tf_op jit(solution)/shard_map/attend_chunk/pallas_call | solution.py:515
  (49 shorter events, 6.5 us)
Async XLA Ops:
  0.7 14.9 %copy-start.12 = (s32[60]{0:T(128)S(1)}, s32[60]{0:T(128)}, u32[]{:S(2)}) copy-start(s32[60]{0:T(128)} %param.23) | copy-start | bytes 724
  0.7 15.1 %copy-start.11 = (f32[128]{0:T(128)S(1)}, f32[128]{0:T(128)}, u32[]{:S(2)}) copy-start(f32[128]{0:T(128)} %param.18) | copy-start | bytes 1540
  7.6 1.5 %copy-start = (bf16[2,2,1280,256]{3,2,1,0:T(8,128)(2,1)}, bf16[2,2,1280,256]{3,2,1,0:T(8,128)(2,1)S(1)}, u32[]{:S(2)}) copy-start(bf16[2,2,1280,256]{3,2,1,0:T(8,128)(2,1)S(1)} %get-tuple-element.29.w) | copy-start | bytes 7864324
  11.2 4.7 %collective-permute-start = (bf16[64,1536]{1,0:T(8,128)(2,1)}, bf16[64,1536]{1,0:T(8,128)(2,1)}, u32[]{:S(2)}, u32[]{:S(2)}) collective-permute-start(bf16[64,1536]{1,0:T(8,128)(2,1)} %get-tuple-element.31), channel_id=1, source_target_pairs={{0,4},{4,0},{8,12},{12,8},{16,20},{20,16},{24,28},{28,24},{1,5},{5... | collective-permute-start | bytes 589832 | tf_op jit(solution)/shard_map/ppermute | solution.py:331
  11.6 16.8 %collective-permute-start.5 = (bf16[480,512]{1,0:T(8,128)(2,1)}, bf16[480,512]{1,0:T(8,128)(2,1)S(1)}, u32[]{:S(2)}, u32[]{:S(2)}) collective-permute-start(bf16[480,512]{1,0:T(8,128)(2,1)} %get-tuple-element.37), channel_id=1, source_target_pairs={{0,1},{1,0},{2,3},{3,2},{4,5},{5,4},{6,7},{7,6},{8,9},{9,8},{10,11... | collective-permute-start | bytes 1474568 | tf_op jit(solution)/shard_map/ppermute | solution.py:537
  14.1 14.4 %collective-permute-start.6 = (bf16[480,512]{1,0:T(8,128)(2,1)}, bf16[480,512]{1,0:T(8,128)(2,1)}, u32[]{:S(2)}, u32[]{:S(2)}) collective-permute-start(bf16[480,512]{1,0:T(8,128)(2,1)} %get-tuple-element.39), channel_id=1, source_target_pairs={{0,2},{1,3},{2,0},{3,1},{4,6},{5,7},{6,4},{7,5},{8,10},{9,11},{10,... | collective-permute-start | bytes 1474568 | tf_op jit(solution)/shard_map/ppermute | solution.py:537
  17.8 7.9 %collective-permute-start.3 = (bf16[64,1536]{1,0:T(8,128)(2,1)S(1)}, bf16[64,1536]{1,0:T(8,128)(2,1)S(1)}, u32[]{:S(2)}, u32[]{:S(2)}) collective-permute-start(bf16[64,1536]{1,0:T(8,128)(2,1)S(1)} %plus.3.after.a), channel_id=1, source_target_pairs={{0,8},{4,12},{8,0},{12,4},{16,24},{20,28},{24,16},{28,20},{1,9},{5... | collective-permute-start | bytes 589832 | tf_op jit(solution)/shard_map/ppermute | solution.py:352
  19.5 1.7 %copy-start.1 = (bf16[2,2,1280,256]{3,2,1,0:T(8,128)(2,1)S(1)}, bf16[2,2,1280,256]{3,2,1,0:T(8,128)(2,1)}, u32[]{:S(2)}) copy-start(bf16[2,2,1280,256]{3,2,1,0:T(8,128)(2,1)} %copy-done) | copy-start | bytes 7864324
  21.2 7.3 %copy-start.4 = (bf16[240,512]{1,0:T(8,128)(2,1)S(1)}, bf16[240,512]{1,0:T(8,128)(2,1)}, u32[]{:S(2)}) copy-start(bf16[240,512]{1,0:T(8,128)(2,1)} %copy-done.3) | copy-start | bytes 737284
  24.1 14.2 %collective-permute-start.1 = (bf16[480,512]{1,0:T(8,128)(2,1)S(1)}, bf16[480,512]{1,0:T(8,128)(2,1)S(1)}, u32[]{:S(2)}, u32[]{:S(2)}) collective-permute-start(bf16[480,512]{1,0:T(8,128)(2,1)S(1)} %get-tuple-element.33.rest_0_), channel_id=1, source_target_pairs={{0,1},{1,0},{2,3},{3,2},{4,5},{5,4},{6,7},{7,6},{8,9},{9,8},{10,11... | collective-permute-start | bytes 1474568 | tf_op jit(solution)/shard_map/ppermute | solution.py:537
  24.7 14.2 %collective-permute-start.2 = (bf16[480,512]{1,0:T(8,128)(2,1)S(1)}, bf16[480,512]{1,0:T(8,128)(2,1)S(1)}, u32[]{:S(2)}, u32[]{:S(2)}) collective-permute-start(bf16[480,512]{1,0:T(8,128)(2,1)S(1)} %get-tuple-element.35), channel_id=1, source_target_pairs={{0,2},{1,3},{2,0},{3,1},{4,6},{5,7},{6,4},{7,5},{8,10},{9,11},{10,... | collective-permute-start | bytes 1474568 | tf_op jit(solution)/shard_map/ppermute | solution.py:537
  25.8 11.2 %collective-permute-start.4 = (bf16[64,1536]{1,0:T(8,128)(2,1)S(1)}, bf16[64,1536]{1,0:T(8,128)(2,1)S(1)}, u32[]{:S(2)}, u32[]{:S(2)}) collective-permute-start(bf16[64,1536]{1,0:T(8,128)(2,1)S(1)} %plus.4.after.a), channel_id=1, source_target_pairs={{0,16},{4,20},{8,24},{12,28},{16,0},{20,4},{24,8},{28,12},{1,17},{... | collective-permute-start | bytes 589832 | tf_op jit(solution)/shard_map/ppermute | solution.py:352
  29.6 11.6 %copy-start.2 = (f32[2,64,1280]{2,1,0:T(8,128)S(1)}, f32[2,64,1280]{2,1,0:T(8,128)}, u32[]{:S(2)}) copy-start(f32[2,64,1280]{2,1,0:T(8,128)} %refs_2_.3) | copy-start | bytes 1966084
  29.6 11.6 %copy-start.9 = (f32[2,64,256]{2,1,0:T(8,128)S(1)}, f32[2,64,256]{2,1,0:T(8,128)}, u32[]{:S(2)}) copy-start(f32[2,64,256]{2,1,0:T(8,128)} %refs_3_.1) | copy-start | bytes 393220
  29.6 14.7 %collective-permute-start.13 = (bf16[240,512]{1,0:T(8,128)(2,1)S(1)}, bf16[240,512]{1,0:T(8,128)(2,1)S(1)}, u32[]{:S(2)}, u32[]{:S(2)}) collective-permute-start(bf16[240,512]{1,0:T(8,128)(2,1)S(1)} %get-tuple-element.40.rest_0_), channel_id=1, source_target_pairs={{0,2},{1,3},{2,0},{3,1},{4,6},{5,7},{6,4},{7,5},{8,10},{9,11},{10,... | collective-permute-start | bytes 737288 | tf_op jit(solution)/shard_map/ppermute | solution.py:537
  31.2 14.5 %collective-permute-start.14 = (bf16[240,512]{1,0:T(8,128)(2,1)S(1)}, bf16[240,512]{1,0:T(8,128)(2,1)S(1)}, u32[]{:S(2)}, u32[]{:S(2)}) collective-permute-start(bf16[240,512]{1,0:T(8,128)(2,1)S(1)} %get-tuple-element.49), channel_id=1, source_target_pairs={{0,1},{1,0},{2,3},{3,2},{4,5},{5,4},{6,7},{7,6},{8,9},{9,8},{10,11... | collective-permute-start | bytes 737288 | tf_op jit(solution)/shard_map/ppermute | solution.py:537
  37.0 4.2 %collective-permute-start.9 = (bf16[64,1536]{1,0:T(8,128)(2,1)S(1)}, bf16[64,1536]{1,0:T(8,128)(2,1)S(1)}, u32[]{:S(2)}, u32[]{:S(2)}) collective-permute-start(bf16[64,1536]{1,0:T(8,128)(2,1)S(1)} %plus.5.after.refs_0_), channel_id=1, source_target_pairs={{0,4},{4,0},{8,12},{12,8},{16,20},{20,16},{24,28},{28,24},{1,5},{5... | collective-permute-start | bytes 589832 | tf_op jit(solution)/shard_map/ppermute | solution.py:331
  39.1 15.3 %copy-start.6 = (bf16[240,512]{1,0:T(8,128)(2,1)S(1)}, bf16[240,512]{1,0:T(8,128)(2,1)}, u32[]{:S(2)}) copy-start(bf16[240,512]{1,0:T(8,128)(2,1)} %copy-done.5) | copy-start | bytes 737284
  39.1 15.3 %copy-start.10 = (s32[60]{0:T(128)S(1)}, s32[60]{0:T(128)}, u32[]{:S(2)}) copy-start(s32[60]{0:T(128)} %lengths.3) | copy-start | bytes 724
  39.1 21.2 %collective-permute-start.7 = (bf16[240,512]{1,0:T(8,128)(2,1)S(1)}, bf16[240,512]{1,0:T(8,128)(2,1)S(1)}, u32[]{:S(2)}, u32[]{:S(2)}) collective-permute-start(bf16[240,512]{1,0:T(8,128)(2,1)S(1)} %get-tuple-element.41.refs_5_), channel_id=1, source_target_pairs={{0,2},{1,3},{2,0},{3,1},{4,6},{5,7},{6,4},{7,5},{8,10},{9,11},{10,... | collective-permute-start | bytes 737288 | tf_op jit(solution)/shard_map/ppermute | solution.py:537
  40.7 19.6 %collective-permute-start.8 = (bf16[240,512]{1,0:T(8,128)(2,1)S(1)}, bf16[240,512]{1,0:T(8,128)(2,1)S(1)}, u32[]{:S(2)}, u32[]{:S(2)}) collective-permute-start(bf16[240,512]{1,0:T(8,128)(2,1)S(1)} %get-tuple-element.43), channel_id=1, source_target_pairs={{0,1},{1,0},{2,3},{3,2},{4,5},{5,4},{6,7},{7,6},{8,9},{9,8},{10,11... | collective-permute-start | bytes 737288 | tf_op jit(solution)/shard_map/ppermute | solution.py:537
  42.7 9.0 %collective-permute-start.10 = (bf16[256,256]{1,0:T(8,128)(2,1)S(1)}, bf16[256,256]{1,0:T(8,128)(2,1)S(1)}, u32[]{:S(2)}, u32[]{:S(2)}) collective-permute-start(bf16[256,256]{1,0:T(8,128)(2,1)S(1)} %get-tuple-element.45), channel_id=1, source_target_pairs={{0,1},{1,0},{2,3},{3,2},{4,5},{5,4},{6,7},{7,6},{8,9},{9,8},{10,11... | collective-permute-start | bytes 393224 | tf_op jit(solution)/shard_map/ppermute | solution.py:537
  44.3 10.1 %collective-permute-start.11 = (bf16[256,256]{1,0:T(8,128)(2,1)S(1)}, bf16[256,256]{1,0:T(8,128)(2,1)S(1)}, u32[]{:S(2)}, u32[]{:S(2)}) collective-permute-start(bf16[256,256]{1,0:T(8,128)(2,1)S(1)} %get-tuple-element.46), channel_id=1, source_target_pairs={{0,2},{1,3},{2,0},{3,1},{4,6},{5,7},{6,4},{7,5},{8,10},{9,11},{10,... | collective-permute-start | bytes 393224 | tf_op jit(solution)/shard_map/ppermute | solution.py:537
  45.7 8.7 %collective-permute-start.12 = (bf16[256,256]{1,0:T(8,128)(2,1)S(1)}, bf16[256,256]{1,0:T(8,128)(2,1)S(1)}, u32[]{:S(2)}, u32[]{:S(2)}) collective-permute-start(bf16[256,256]{1,0:T(8,128)(2,1)S(1)} %get-tuple-element.47), channel_id=1, source_target_pairs={{0,3},{1,2},{2,1},{3,0},{4,7},{5,6},{6,5},{7,4},{8,11},{9,10},{10,... | collective-permute-start | bytes 393224 | tf_op jit(solution)/shard_map/ppermute | solution.py:537
  (4 other events, 3.0 us)

commit v5 on v4

--- a/solution.py
+++ b/solution.py
@@ -16,7 +16,7 @@
 STEPS = 4
 BF = jnp.bfloat16
 F32 = jnp.float32
-VMEM_LIMIT = 16 * 1024 * 1024
+MIB = 1024 * 1024
 
 
 def normed_rotated(keys, gain, position):
@@ -115,8 +115,8 @@
 HEADS_STEP = 2
 
 
-def params(limit=VMEM_LIMIT):
-    return pltpu.CompilerParams(vmem_limit_bytes=limit)
+def params(mib):
+    return pltpu.CompilerParams(vmem_limit_bytes=mib * MIB)
 
 
 def dot(a, b):
@@ -181,8 +181,8 @@
 
 def first_kernel(ids, hidden, weight, grad_a, grad_b, *rest):
     x, *outs = rest[:6]
-    send, own, later, _ = rest[6:10]
-    held, w, held_a, held_b, hidden_sems, sems, later_sems, grad_sems = rest[10:]
+    send, own, _ = rest[6:9]
+    held, w, held_a, held_b, hidden_sems, sems, grad_sems = rest[9:]
     tokens = x.shape[0] // 4
     rows = tokens // STEPS
 
@@ -193,16 +193,11 @@
     def weight_copy(p, i):
         at = pl.ds(i * TILE, TILE)
         return pltpu.make_async_copy(weight.at[p, :, at], w.at[p, i], sems.at[p, i])
-
-    def later_copy(p, i):
-        at = pl.ds((w.shape[1] + i) * TILE, TILE)
-        return pltpu.make_async_copy(weight.at[p, :, at], later.at[p, i], later_sems.at[p, i])
 
     others = [
         pltpu.make_async_copy(grad_a.at[0], held_a, grad_sems.at[0]),
         pltpu.make_async_copy(grad_b.at[0], held_b, grad_sems.at[1]),
     ]
-    others += [later_copy(p, i) for i in range(later.shape[1]) for p in range(2)]
     for r in range(4):
         hidden_copy(r).start()
     for i in range(w.shape[1]):
@@ -227,9 +222,24 @@
         out[:, wide:] = held_b[p].astype(BF)
 
 
-def later_kernel(x, w, after, *outs):
+def later_kernel(x, weight, after, *rest):
     del after
-    multiply_terms(x, w, outs, lambda i: None)
+    *outs, w, sems = rest
+    base = weight.shape[2] - w.shape[1] * TILE
+
+    def weight_copy(p, i):
+        at = pl.ds(base + i * TILE, TILE)
+        return pltpu.make_async_copy(weight.at[p, :, at], w.at[p, i], sems.at[p, i])
+
+    for i in range(w.shape[1]):
+        for p in range(2):
+            weight_copy(p, i).start()
+
+    def ready(i):
+        for p in range(2):
+            weight_copy(p, i).wait()
+
+    multiply_terms(x, w, outs, ready)
 
 
 def term_shapes(tokens, count):
@@ -242,8 +252,7 @@
     here = pl.BlockSpec(memory_space=pl.ANY)
     outs = [jax.ShapeDtypeStruct((4 * tokens, width), BF), *term_shapes(tokens, CHUNKS[0])]
     outs += [jax.ShapeDtypeStruct((rank, wide), BF)] * 2
-    tiles = [count * HD // TILE for count in CHUNKS]
-    outs.append(pltpu.VMEM((2, tiles[1], width, TILE), BF))
+    tiles = CHUNKS[0] * HD // TILE
     specs = [whole(x.shape) for x in outs] + [here]
     outs.append(jax.ShapeDtypeStruct(queries.shape, BF))
     return pl.pallas_call(
@@ -256,31 +265,36 @@
             out_specs=specs,
             scratch_shapes=[
                 pltpu.VMEM((4, tokens // STEPS, STEPS, width), BF),
-                pltpu.VMEM((2, tiles[0], width, TILE), BF),
+                pltpu.VMEM((2, tiles, width, TILE), BF),
                 pltpu.VMEM(grad_a.shape[1:], F32),
                 pltpu.VMEM(grad_b.shape[1:], F32),
                 pltpu.SemaphoreType.DMA((4,)),
-                pltpu.SemaphoreType.DMA((2, tiles[0])),
-                pltpu.SemaphoreType.DMA((2, tiles[1])),
+                pltpu.SemaphoreType.DMA((2, tiles)),
                 pltpu.SemaphoreType.DMA((2,)),
             ],
         ),
-        compiler_params=params(),
+        compiler_params=params(16),
         name="first_terms",
     )(ids, *map(hbm, (hidden, kv_weight, grad_a, grad_b)))
 
 
-def later_terms(x, w, after):
+def later_terms(x, kv_weight, after):
     outs = term_shapes(x.shape[0] // 4, CHUNKS[1])
+    here = pl.BlockSpec(memory_space=pl.ANY)
+    tiles = CHUNKS[1] * HD // TILE
     return pl.pallas_call(
         later_kernel,
         out_shape=outs,
         grid=(1,),
-        in_specs=[whole(x.shape), whole(w.shape), pl.BlockSpec(memory_space=pl.ANY)],
+        in_specs=[whole(x.shape), here, here],
         out_specs=[whole(out.shape) for out in outs],
-        compiler_params=params(),
+        scratch_shapes=[
+            pltpu.VMEM((2, tiles, x.shape[1], TILE), BF),
+            pltpu.SemaphoreType.DMA((2, tiles)),
+        ],
+        compiler_params=params(12),
         name="later_terms",
-    )(x, w, after)
+    )(x, hbm(kv_weight), after)
 
 
 def mid_kernel(kkeep, kcame, vkeep, vcame, after, kout, vout):
@@ -299,7 +313,7 @@
         grid=(1,),
         in_specs=[high, low, low, high, pl.BlockSpec(memory_space=pl.ANY)],
         out_specs=[low, low],
-        compiler_params=params(),
+        compiler_params=params(4),
         name="mid_sums",
     )(kkeep, kcame, vkeep, vcame, after)
 
@@ -322,7 +336,7 @@
             + [whole(x.shape) for x in outs[copied:]],
             scratch_shapes=list(scratch),
         ),
-        compiler_params=params(),
+        compiler_params=params(8),
         name=name,
     )(ids, *args, *after)
 
@@ -343,7 +357,7 @@
         grid=(1,),
         in_specs=[whole(a.shape)] * 2 + [pl.BlockSpec(memory_space=pl.ANY)] * len(after),
         out_specs=whole(a.shape),
-        compiler_params=params(),
+        compiler_params=params(2),
         name="plus",
     )(a, b, *after)
 
@@ -519,7 +533,7 @@
             num_scalar_prefetch=3, grid=(count // HEADS_STEP,), in_specs=specs, out_specs=wide
         ),
         input_output_aliases={len(args) + 2: 0},
-        compiler_params=params(),
+        compiler_params=params(14),
         name="attend_chunk",
     )(ids, first, lengths, *args)
 
@@ -557,7 +571,7 @@
     ids = jnp.stack([lax.axis_index("tensor"), dp // 2, dp % 2]).astype(jnp.int32)
     tables = rotary_tables(key_gain, positions)
 
-    x, *first, packed, own, weights, attended = first_terms(
+    x, *first, packed, own, attended = first_terms(
         ids, hidden_in, kv_weight, grad_a, grad_b, queries, tokens
     )
     half = plus(own, core_flip(packed, count_dp))
@@ -572,7 +586,7 @@
         kkeep, kcame, vkeep0, vcame = parts
         return kkeep, kcame, across(mids[0], 2), vkeep0, vcame, across(mids[1], 1)
 
-    second = later_terms(x, weights, half)
+    second = later_terms(x, kv_weight, half)
     step, after = 1, second[:1]
     while 2 * step < count_dp:
         half = plus(half, along_line(half, step, count_dp), *after)
@@ -584,12 +598,11 @@
         mids, parts = first_exchange(first, half)
     first = second_exchange(mids, parts)
     other = core_flip(half, count_dp)
-    mids, parts = first_exchange(second, half)
-    second = second_exchange(mids, parts)
     new_a, new_b, *sends = updated(
         ids, half, other, factor_a, factor_b, x, count_dp, mids[0]
     )
     ub = [sends[0]] + [across(sends[r], r) for r in (1, 2, 3)]
+    second = second_exchange(*first_exchange(second, ub[1]))
     for start, count, came in ((0, CHUNKS[0], first), (CHUNKS[0], CHUNKS[1], second)):
         attended = attend_chunk(
             ids,

time: 66.3 us -> 71.8 us (1.083)
  waiting for transfers between devices: 13.4 us -> 22.5 us
  local copies, waits for them, and re-layouts: 6.35 us -> 3.12 us
  starting transfers between devices: 19.5 us -> 17.8 us
  Pallas kernels: 25.2 us -> 26.5 us
    ppermute x11, waiting for transfers between devices: 9.13 us -> 14.8 us  [across(): return lax.ppermute(x, 'tensor', [(i, i ^ r) for i in range(4)])]
    unnamed x26 -> x22, local copies, waits for them, and re-layouts: 6.25 us -> 3.02 us
    ppermute x2, waiting for transfers between devices: 4.28 us -> 7.02 us  [along_line(): return lax.ppermute(x, 'dp', [(i, i ^ 2 * d) for i in range(count)])]
    ppermute x11, starting transfers between devices: 14.6 us -> 13 us  [across(): return lax.ppermute(x, 'tensor', [(i, i ^ r) for i in range(4)])]
    pallas_call x1, Pallas kernels: 2.88 us -> 4.26 us  [later_terms(): pl.pallas_call(later_kernel, out_shape=outs, grid=(1,), in_specs=[whole(x...]
  transfers between devices with their start and end apart: 15 -> 15, of which waited for: 5 -> 4; matrix products, arithmetic and copies ran while one was open for 1% -> 1% of each run, Pallas kernels for 19% -> 19%
where the time goes in v5:
time: 71.8 us; the launch traced here: 71.5 us
  Pallas kernels  26.5 us (37%)
  waiting for transfers between devices  22.5 us (31%)
  starting transfers between devices  17.8 us (25%)
  local copies, waits for them, and re-layouts  3.12 us (4%)
  other arithmetic  0.82 us (1%)
  between operations  0.79 us (1%)
    ppermute x11, waiting for transfers between devices, across(): return lax.ppermute(x, 'tensor', [(i, i ^ r) for i in range(4)])  14.8 us
    ppermute x11, starting transfers between devices, across(): return lax.ppermute(x, 'tensor', [(i, i ^ r) for i in range(4)])  13 us
    pallas_call x2, Pallas kernels, attend_chunk(): pl.pallas_call(attend_kernel, out_shape=jax.ShapeDtypeStruct(queries.shap...  11.7 us
    ppermute x2, waiting for transfers between devices, along_line(): return lax.ppermute(x, 'dp', [(i, i ^ 2 * d) for i in range(count)])  7.02 us
    pallas_call x1, Pallas kernels, first_terms(): pl.pallas_call(first_kernel, out_shape=outs, grid_spec=pltpu.PrefetchScal...  6.84 us
    ppermute x2, starting transfers between devices, along_line(): return lax.ppermute(x, 'dp', [(i, i ^ 2 * d) for i in range(count)])  4.3 us
    pallas_call x1, Pallas kernels, later_terms(): pl.pallas_call(later_kernel, out_shape=outs, grid=(1,), in_specs=[whole(x...  4.26 us
    unnamed x22, local copies, waits for them, and re-layouts  3.02 us
  transfers between devices with their start and end apart: 15, of which 4 were waited for; matrix products, arithmetic and copies ran while one was open for 1% of the time, Pallas kernels for 19%

profile of v5, /device:TPU:0, one launch (start us, length us, event | category | flops | bytes accessed | tf_op | source)
XLA Modules:
  0.0 71.5 jit_solution(14320954724556320973)
XLA Ops:
  0.7 6.8 %first_terms.1 = (bf16[960,1280]{1,0:T(8,128)(2,1)S(1)}, bf16[480,512]{1,0:T(8,128)(2,1)}, bf16[480,512]{1,0:T(8,128)(2,1)S(1)}, bf16[480,512]{1,0:T(8,128)(2,1)...) custom-call(s32[3]{0:T(128)S(1)} %pad_add_fusion.ids, ...), custom_call_target="tpu_custom_call" | custom-call | tf_op jit(solution)/shard_map/first_terms/pallas_call | solution.py:258
  7.6 0.7 copy-done.1
  8.3 0.7 copy-done.3
  10.1 2.5 %collective-permute-start.5 = (bf16[480,512]{1,0:T(8,128)(2,1)}, bf16[480,512]{1,0:T(8,128)(2,1)S(1)}, u32[]{:S(2)}, u32[]{:S(2)}) collective-permute-start(bf16[480,512]{1,0:T(8,128)(2,1)} %get-tuple-element.35), channel_id=1, source_target_pairs={{0,1},{1,0},{2,3},{3,2},{4,5},{5,4},{6,7},{7,6},{8,9},{9,8},{10,11... | collective-permute-start | bytes 1474568 | tf_op jit(solution)/shard_map/ppermute | solution.py:551
  12.6 1.5 %collective-permute-start.6 = (bf16[480,512]{1,0:T(8,128)(2,1)}, bf16[480,512]{1,0:T(8,128)(2,1)}, u32[]{:S(2)}, u32[]{:S(2)}) collective-permute-start(bf16[480,512]{1,0:T(8,128)(2,1)} %get-tuple-element.37), channel_id=1, source_target_pairs={{0,2},{1,3},{2,0},{3,1},{4,6},{5,7},{6,4},{7,5},{8,10},{9,11},{10,... | collective-permute-start | bytes 1474568 | tf_op jit(solution)/shard_map/ppermute | solution.py:551
  14.4 0.9 %copy-done.6 = bf16[64,1536]{1,0:T(8,128)(2,1)S(1)} copy-done((bf16[64,1536]{1,0:T(8,128)(2,1)S(1)}, bf16[64,1536]{1,0:T(8,128)(2,1)}, u32[]{:S(2)}) %copy-start.6) | copy-done | bytes 196632
  15.3 1.0 %plus.3.after.a = bf16[64,1536]{1,0:T(8,128)(2,1)S(1)} custom-call(bf16[64,1536]{1,0:T(8,128)(2,1)S(1)} %copy-done.6, bf16[64,1536]{1,0:T(8,128)(2,1)} %collective-permute-done.b), custom_call_target="tpu_custom_call" | custom-call | tf_op jit(solution)/shard_map/plus/pallas_call | solution.py:354
  16.3 1.6 %collective-permute-start.3 = (bf16[64,1536]{1,0:T(8,128)(2,1)S(1)}, bf16[64,1536]{1,0:T(8,128)(2,1)S(1)}, u32[]{:S(2)}, u32[]{:S(2)}) collective-permute-start(bf16[64,1536]{1,0:T(8,128)(2,1)S(1)} %plus.3.after.a), channel_id=1, source_target_pairs={{0,8},{4,12},{8,0},{12,4},{16,24},{20,28},{24,16},{28,20},{1,9},{5... | collective-permute-start | bytes 589832 | tf_op jit(solution)/shard_map/ppermute | solution.py:366
  18.0 4.3 %later_terms.1 = (bf16[480,512]{1,0:T(8,128)(2,1)S(1)}, bf16[480,512]{1,0:T(8,128)(2,1)S(1)}, bf16[480,512]{1,0:T(8,128)(2,1)S(1)}, bf16[240,512]{1,0:T(8,128)(2,1)S(1)}, bf16[240,512]{1,0:T(8,128)(2,1)S(1)}) custom-call(bf16[960,1280]{1,0:T(8,128)(2,1)S(1)} %get-tuple-element.27.x.refs_4_, bf16[2,1280,1024]{2,1,0:T(8,128)(2,1)} %weight.3, ...), custom_call_target="tpu_custom_call" | custom-call | tf_op jit(solution)/shard_map/later_terms/pallas_call | solution.py:285
  22.9 1.0 %collective-permute-start.1 = (bf16[480,512]{1,0:T(8,128)(2,1)S(1)}, bf16[480,512]{1,0:T(8,128)(2,1)S(1)}, u32[]{:S(2)}, u32[]{:S(2)}) collective-permute-start(bf16[480,512]{1,0:T(8,128)(2,1)S(1)} %get-tuple-element.31.rest_0_), channel_id=1, source_target_pairs={{0,1},{1,0},{2,3},{3,2},{4,5},{5,4},{6,7},{7,6},{8,9},{9,8},{10,11... | collective-permute-start | bytes 1474568 | tf_op jit(solution)/shard_map/ppermute | solution.py:551
  23.9 2.7 %collective-permute-start.4 = (bf16[64,1536]{1,0:T(8,128)(2,1)S(1)}, bf16[64,1536]{1,0:T(8,128)(2,1)S(1)}, u32[]{:S(2)}, u32[]{:S(2)}) collective-permute-start(bf16[64,1536]{1,0:T(8,128)(2,1)S(1)} %plus.4.after.a), channel_id=1, source_target_pairs={{0,16},{4,20},{8,24},{12,28},{16,0},{20,4},{24,8},{28,12},{1,17},{... | collective-permute-start | bytes 589832 | tf_op jit(solution)/shard_map/ppermute | solution.py:366
  27.1 1.1 %mid_sums.2 = (bf16[240,512]{1,0:T(8,128)(2,1)S(1)}, bf16[240,512]{1,0:T(8,128)(2,1)S(1)}) custom-call(bf16[480,512]{1,0:T(8,128)(2,1)S(1)} %get-tuple-element.34.kkeep.refs_3_, bf16[480,512]{1,0:T(8,128)(2,1)S(1)} %collective-permute-done.5.kcame.refs_4_, bf16[240,512]{1,0:T(8,128)(2,1)S(1)} %copy-done.2, ...), custom_call_target="tpu_custom_call" | custom-call | tf_op jit(solution)/shard_map/mid_sums/pallas_call | solution.py:310
  28.2 7.0 %collective-permute-done.4.b = bf16[64,1536]{1,0:T(8,128)(2,1)S(1)} collective-permute-done((bf16[64,1536]{1,0:T(8,128)(2,1)S(1)}, bf16[64,1536]{1,0:T(8,128)(2,1)S(1)}, u32[]{:S(2)}, u32[]{:S(2)}) %collective-permute-start.4) | collective-permute-done | bytes 196640 | tf_op jit(solution)/shard_map/ppermute | solution.py:366
  35.4 0.8 %collective-permute-start.14 = (bf16[240,512]{1,0:T(8,128)(2,1)S(1)}, bf16[240,512]{1,0:T(8,128)(2,1)S(1)}, u32[]{:S(2)}, u32[]{:S(2)}) collective-permute-start(bf16[240,512]{1,0:T(8,128)(2,1)S(1)} %get-tuple-element.47), channel_id=1, source_target_pairs={{0,1},{1,0},{2,3},{3,2},{4,5},{5,4},{6,7},{7,6},{8,9},{9,8},{10,11... | collective-permute-start | bytes 737288 | tf_op jit(solution)/shard_map/ppermute | solution.py:551
  36.8 1.5 %update_factors.1 = (f32[2,64,1280]{2,1,0:T(8,128)}, f32[2,64,256]{2,1,0:T(8,128)}, bf16[256,256]{1,0:T(8,128)(2,1)S(1)}, bf16[256,256]{1,0:T(8,128)(2,1)S(1)}, ...) custom-call(s32[3]{0:T(128)S(1)} %pad_add_fusion.ids, bf16[64,1536]{1,0:T(8,128)(2,1)S(1)} %plus.5.refs_0_, ...), custom_call_target="tpu_custom_call" | custom-call | tf_op jit(solution)/shard_map/update_factors/pallas_call | solution.py:327
  38.3 0.8 %collective-permute-start.8 = (bf16[256,256]{1,0:T(8,128)(2,1)S(1)}, bf16[256,256]{1,0:T(8,128)(2,1)S(1)}, u32[]{:S(2)}, u32[]{:S(2)}) collective-permute-start(bf16[256,256]{1,0:T(8,128)(2,1)S(1)} %get-tuple-element.39), channel_id=1, source_target_pairs={{0,1},{1,0},{2,3},{3,2},{4,5},{5,4},{6,7},{7,6},{8,9},{9,8},{10,11... | collective-permute-start | bytes 393224 | tf_op jit(solution)/shard_map/ppermute | solution.py:551
  39.1 1.5 %collective-permute-start.13 = (bf16[240,512]{1,0:T(8,128)(2,1)S(1)}, bf16[240,512]{1,0:T(8,128)(2,1)S(1)}, u32[]{:S(2)}, u32[]{:S(2)}) collective-permute-start(bf16[240,512]{1,0:T(8,128)(2,1)S(1)} %get-tuple-element.38.rest_0_.refs_5_), channel_id=1, source_target_pairs={{0,2},{1,3},{2,0},{3,1},{4,6},{5,7},{6,4},{7,5},{8,10},{9,11},{10,... | collective-permute-start | bytes 737288 | tf_op jit(solution)/shard_map/ppermute | solution.py:551
  40.6 5.9 %collective-permute-done.8.after.refs_10_ = bf16[256,256]{1,0:T(8,128)(2,1)S(1)} collective-permute-done((bf16[256,256]{1,0:T(8,128)(2,1)S(1)}, bf16[256,256]{1,0:T(8,128)(2,1)S(1)}, u32[]{:S(2)}, u32[]{:S(2)}) %collective-permute-start.8) | collective-permute-done | bytes 131104 | tf_op jit(solution)/shard_map/ppermute | solution.py:551
  46.6 0.8 %collective-permute-start.9 = (bf16[240,512]{1,0:T(8,128)(2,1)S(1)}, bf16[240,512]{1,0:T(8,128)(2,1)S(1)}, u32[]{:S(2)}, u32[]{:S(2)}) collective-permute-start(bf16[240,512]{1,0:T(8,128)(2,1)S(1)} %get-tuple-element.40), channel_id=1, source_target_pairs={{0,2},{1,3},{2,0},{3,1},{4,6},{5,7},{6,4},{7,5},{8,10},{9,11},{10,... | collective-permute-start | bytes 737288 | tf_op jit(solution)/shard_map/ppermute | solution.py:551
  47.5 1.5 %collective-permute-start.10 = (bf16[240,512]{1,0:T(8,128)(2,1)S(1)}, bf16[240,512]{1,0:T(8,128)(2,1)S(1)}, u32[]{:S(2)}, u32[]{:S(2)}) collective-permute-start(bf16[240,512]{1,0:T(8,128)(2,1)S(1)} %get-tuple-element.42), channel_id=1, source_target_pairs={{0,1},{1,0},{2,3},{3,2},{4,5},{5,4},{6,7},{7,6},{8,9},{9,8},{10,11... | collective-permute-start | bytes 737288 | tf_op jit(solution)/shard_map/ppermute | solution.py:551
  49.5 1.5 %collective-permute-start.12 = (bf16[256,256]{1,0:T(8,128)(2,1)S(1)}, bf16[256,256]{1,0:T(8,128)(2,1)S(1)}, u32[]{:S(2)}, u32[]{:S(2)}) collective-permute-start(bf16[256,256]{1,0:T(8,128)(2,1)S(1)} %get-tuple-element.45), channel_id=1, source_target_pairs={{0,3},{1,2},{2,1},{3,0},{4,7},{5,6},{6,5},{7,4},{8,11},{9,10},{10,... | collective-permute-start | bytes 393224 | tf_op jit(solution)/shard_map/ppermute | solution.py:551
  51.0 8.9 %collective-permute-done.11.refs_11_ = bf16[256,256]{1,0:T(8,128)(2,1)S(1)} collective-permute-done((bf16[256,256]{1,0:T(8,128)(2,1)S(1)}, bf16[256,256]{1,0:T(8,128)(2,1)S(1)}, u32[]{:S(2)}, u32[]{:S(2)}) %collective-permute-start.11) | collective-permute-done | bytes 131104 | tf_op jit(solution)/shard_map/ppermute | solution.py:551
  59.8 5.8 %attend_chunk.2.refs_15_ = bf16[60,4,4096]{2,1,0:T(4,128)(2,1)} custom-call(s32[3]{0:T(128)S(1)} %pad_add_fusion.ids, s32[1]{0:T(128)} %constant.43.clone.1.first, s32[60]{0:T(128)S(1)} %copy-done.8, bf16[60,4,4096]{2,1,0:T(4,128)(2,1)} %refs_0_.3, bf16[60,16,1024]{2,1,0:T(8,128)(2,1)} %refs_1_.3, ...), custom_call_target="tpu_custom_call", output_to_operand_aliasing={{}: (18, {})} | custom-call | tf_op jit(solution)/shard_map/attend_chunk/pallas_call | solution.py:529
  65.7 5.8 %attend_chunk.3 = bf16[60,4,4096]{2,1,0:T(4,128)(2,1)} custom-call(s32[3]{0:T(128)S(1)} %pad_add_fusion.ids, s32[1]{0:T(128)} %constant.41.clone.1.first, s32[60]{0:T(128)S(1)} %copy-done.8, bf16[60,4,4096]{2,1,0:T(4,128)(2,1)} %refs_0_.3, bf16[60,16,1024]{2,1,0:T(8,128)(2,1)} %refs_1_.3, ...), custom_call_target="tpu_custom_call", output_to_operand_aliasing={{}: (18, {})} | custom-call | tf_op jit(solution)/shard_map/attend_chunk/pallas_call | solution.py:529
  (45 shorter events, 4.1 us)
Async XLA Ops:
  0.7 13.4 %copy-start.10 = (s32[60]{0:T(128)S(1)}, s32[60]{0:T(128)}, u32[]{:S(2)}) copy-start(s32[60]{0:T(128)} %param.23) | copy-start | bytes 724
  0.7 13.5 %copy-start.9 = (f32[128]{0:T(128)S(1)}, f32[128]{0:T(128)}, u32[]{:S(2)}) copy-start(f32[128]{0:T(128)} %param.18) | copy-start | bytes 1540
  7.6 0.7 copy-start.1
  9.7 4.7 %collective-permute-start = (bf16[64,1536]{1,0:T(8,128)(2,1)}, bf16[64,1536]{1,0:T(8,128)(2,1)}, u32[]{:S(2)}, u32[]{:S(2)}) collective-permute-start(bf16[64,1536]{1,0:T(8,128)(2,1)} %get-tuple-element.29), channel_id=1, source_target_pairs={{0,4},{4,0},{8,12},{12,8},{16,20},{20,16},{24,28},{28,24},{1,5},{5... | collective-permute-start | bytes 589832 | tf_op jit(solution)/shard_map/ppermute | solution.py:345
  10.1 17.0 %collective-permute-start.5 = (bf16[480,512]{1,0:T(8,128)(2,1)}, bf16[480,512]{1,0:T(8,128)(2,1)S(1)}, u32[]{:S(2)}, u32[]{:S(2)}) collective-permute-start(bf16[480,512]{1,0:T(8,128)(2,1)} %get-tuple-element.35), channel_id=1, source_target_pairs={{0,1},{1,0},{2,3},{3,2},{4,5},{5,4},{6,7},{7,6},{8,9},{9,8},{10,11... | collective-permute-start | bytes 1474568 | tf_op jit(solution)/shard_map/ppermute | solution.py:551
  12.6 14.5 %collective-permute-start.6 = (bf16[480,512]{1,0:T(8,128)(2,1)}, bf16[480,512]{1,0:T(8,128)(2,1)}, u32[]{:S(2)}, u32[]{:S(2)}) collective-permute-start(bf16[480,512]{1,0:T(8,128)(2,1)} %get-tuple-element.37), channel_id=1, source_target_pairs={{0,2},{1,3},{2,0},{3,1},{4,6},{5,7},{6,4},{7,5},{8,10},{9,11},{10,... | collective-permute-start | bytes 1474568 | tf_op jit(solution)/shard_map/ppermute | solution.py:551
  14.4 0.9 %copy-start.6 = (bf16[64,1536]{1,0:T(8,128)(2,1)S(1)}, bf16[64,1536]{1,0:T(8,128)(2,1)}, u32[]{:S(2)}) copy-start(bf16[64,1536]{1,0:T(8,128)(2,1)} %copy-done.5) | copy-start | bytes 589828
  16.3 7.6 %collective-permute-start.3 = (bf16[64,1536]{1,0:T(8,128)(2,1)S(1)}, bf16[64,1536]{1,0:T(8,128)(2,1)S(1)}, u32[]{:S(2)}, u32[]{:S(2)}) collective-permute-start(bf16[64,1536]{1,0:T(8,128)(2,1)S(1)} %plus.3.after.a), channel_id=1, source_target_pairs={{0,8},{4,12},{8,0},{12,4},{16,24},{20,28},{24,16},{28,20},{1,9},{5... | collective-permute-start | bytes 589832 | tf_op jit(solution)/shard_map/ppermute | solution.py:366
  18.0 9.1 %copy-start.2 = (bf16[240,512]{1,0:T(8,128)(2,1)S(1)}, bf16[240,512]{1,0:T(8,128)(2,1)}, u32[]{:S(2)}) copy-start(bf16[240,512]{1,0:T(8,128)(2,1)} %copy-done.1) | copy-start | bytes 737284
  22.3 18.3 %collective-permute-start.2 = (bf16[480,512]{1,0:T(8,128)(2,1)S(1)}, bf16[480,512]{1,0:T(8,128)(2,1)S(1)}, u32[]{:S(2)}, u32[]{:S(2)}) collective-permute-start(bf16[480,512]{1,0:T(8,128)(2,1)S(1)} %get-tuple-element.33), channel_id=1, source_target_pairs={{0,2},{1,3},{2,0},{3,1},{4,6},{5,7},{6,4},{7,5},{8,10},{9,11},{10,... | collective-permute-start | bytes 1474568 | tf_op jit(solution)/shard_map/ppermute | solution.py:551
  22.9 13.9 %copy-start = (f32[2,64,1280]{2,1,0:T(8,128)S(1)}, f32[2,64,1280]{2,1,0:T(8,128)}, u32[]{:S(2)}) copy-start(f32[2,64,1280]{2,1,0:T(8,128)} %refs_2_.3) | copy-start | bytes 1966084
  22.9 13.9 %copy-start.7 = (f32[2,64,256]{2,1,0:T(8,128)S(1)}, f32[2,64,256]{2,1,0:T(8,128)}, u32[]{:S(2)}) copy-start(f32[2,64,256]{2,1,0:T(8,128)} %refs_3_.1) | copy-start | bytes 393220
  22.9 17.7 %collective-permute-start.1 = (bf16[480,512]{1,0:T(8,128)(2,1)S(1)}, bf16[480,512]{1,0:T(8,128)(2,1)S(1)}, u32[]{:S(2)}, u32[]{:S(2)}) collective-permute-start(bf16[480,512]{1,0:T(8,128)(2,1)S(1)} %get-tuple-element.31.rest_0_), channel_id=1, source_target_pairs={{0,1},{1,0},{2,3},{3,2},{4,5},{5,4},{6,7},{7,6},{8,9},{9,8},{10,11... | collective-permute-start | bytes 1474568 | tf_op jit(solution)/shard_map/ppermute | solution.py:551
  23.9 11.3 %collective-permute-start.4 = (bf16[64,1536]{1,0:T(8,128)(2,1)S(1)}, bf16[64,1536]{1,0:T(8,128)(2,1)S(1)}, u32[]{:S(2)}, u32[]{:S(2)}) collective-permute-start(bf16[64,1536]{1,0:T(8,128)(2,1)S(1)} %plus.4.after.a), channel_id=1, source_target_pairs={{0,16},{4,20},{8,24},{12,28},{16,0},{20,4},{24,8},{28,12},{1,17},{... | collective-permute-start | bytes 589832 | tf_op jit(solution)/shard_map/ppermute | solution.py:366
  35.3 1.5 %collective-permute-start.7 = (bf16[64,1536]{1,0:T(8,128)(2,1)S(1)}, bf16[64,1536]{1,0:T(8,128)(2,1)S(1)}, u32[]{:S(2)}, u32[]{:S(2)}) collective-permute-start(bf16[64,1536]{1,0:T(8,128)(2,1)S(1)} %plus.5.refs_0_), channel_id=1, source_target_pairs={{0,4},{4,0},{8,12},{12,8},{16,20},{20,16},{24,28},{28,24},{1,5},{5... | collective-permute-start | bytes 589832 | tf_op jit(solution)/shard_map/ppermute | solution.py:345
  35.3 24.5 %copy-start.4 = (bf16[240,512]{1,0:T(8,128)(2,1)S(1)}, bf16[240,512]{1,0:T(8,128)(2,1)}, u32[]{:S(2)}) copy-start(bf16[240,512]{1,0:T(8,128)(2,1)} %copy-done.3) | copy-start | bytes 737284
  35.3 24.5 %copy-start.8 = (s32[60]{0:T(128)S(1)}, s32[60]{0:T(128)}, u32[]{:S(2)}) copy-start(s32[60]{0:T(128)} %lengths.3) | copy-start | bytes 724
  35.4 14.1 %collective-permute-start.14 = (bf16[240,512]{1,0:T(8,128)(2,1)S(1)}, bf16[240,512]{1,0:T(8,128)(2,1)S(1)}, u32[]{:S(2)}, u32[]{:S(2)}) collective-permute-start(bf16[240,512]{1,0:T(8,128)(2,1)S(1)} %get-tuple-element.47), channel_id=1, source_target_pairs={{0,1},{1,0},{2,3},{3,2},{4,5},{5,4},{6,7},{7,6},{8,9},{9,8},{10,11... | collective-permute-start | bytes 737288 | tf_op jit(solution)/shard_map/ppermute | solution.py:551
  38.3 8.2 %collective-permute-start.8 = (bf16[256,256]{1,0:T(8,128)(2,1)S(1)}, bf16[256,256]{1,0:T(8,128)(2,1)S(1)}, u32[]{:S(2)}, u32[]{:S(2)}) collective-permute-start(bf16[256,256]{1,0:T(8,128)(2,1)S(1)} %get-tuple-element.39), channel_id=1, source_target_pairs={{0,1},{1,0},{2,3},{3,2},{4,5},{5,4},{6,7},{7,6},{8,9},{9,8},{10,11... | collective-permute-start | bytes 393224 | tf_op jit(solution)/shard_map/ppermute | solution.py:551
  39.1 11.9 %collective-permute-start.13 = (bf16[240,512]{1,0:T(8,128)(2,1)S(1)}, bf16[240,512]{1,0:T(8,128)(2,1)S(1)}, u32[]{:S(2)}, u32[]{:S(2)}) collective-permute-start(bf16[240,512]{1,0:T(8,128)(2,1)S(1)} %get-tuple-element.38.rest_0_.refs_5_), channel_id=1, source_target_pairs={{0,2},{1,3},{2,0},{3,1},{4,6},{5,7},{6,4},{7,5},{8,10},{9,11},{10,... | collective-permute-start | bytes 737288 | tf_op jit(solution)/shard_map/ppermute | solution.py:551
  46.6 19.0 %collective-permute-start.9 = (bf16[240,512]{1,0:T(8,128)(2,1)S(1)}, bf16[240,512]{1,0:T(8,128)(2,1)S(1)}, u32[]{:S(2)}, u32[]{:S(2)}) collective-permute-start(bf16[240,512]{1,0:T(8,128)(2,1)S(1)} %get-tuple-element.40), channel_id=1, source_target_pairs={{0,2},{1,3},{2,0},{3,1},{4,6},{5,7},{6,4},{7,5},{8,10},{9,11},{10,... | collective-permute-start | bytes 737288 | tf_op jit(solution)/shard_map/ppermute | solution.py:551
  47.5 18.2 %collective-permute-start.10 = (bf16[240,512]{1,0:T(8,128)(2,1)S(1)}, bf16[240,512]{1,0:T(8,128)(2,1)S(1)}, u32[]{:S(2)}, u32[]{:S(2)}) collective-permute-start(bf16[240,512]{1,0:T(8,128)(2,1)S(1)} %get-tuple-element.42), channel_id=1, source_target_pairs={{0,1},{1,0},{2,3},{3,2},{4,5},{5,4},{6,7},{7,6},{8,9},{9,8},{10,11... | collective-permute-start | bytes 737288 | tf_op jit(solution)/shard_map/ppermute | solution.py:551
  48.9 10.9 %collective-permute-start.11 = (bf16[256,256]{1,0:T(8,128)(2,1)S(1)}, bf16[256,256]{1,0:T(8,128)(2,1)S(1)}, u32[]{:S(2)}, u32[]{:S(2)}) collective-permute-start(bf16[256,256]{1,0:T(8,128)(2,1)S(1)} %get-tuple-element.44), channel_id=1, source_target_pairs={{0,2},{1,3},{2,0},{3,1},{4,6},{5,7},{6,4},{7,5},{8,10},{9,11},{10,... | collective-permute-start | bytes 393224 | tf_op jit(solution)/shard_map/ppermute | solution.py:551
  49.5 10.4 %collective-permute-start.12 = (bf16[256,256]{1,0:T(8,128)(2,1)S(1)}, bf16[256,256]{1,0:T(8,128)(2,1)S(1)}, u32[]{:S(2)}, u32[]{:S(2)}) collective-permute-start(bf16[256,256]{1,0:T(8,128)(2,1)S(1)} %get-tuple-element.45), channel_id=1, source_target_pairs={{0,3},{1,2},{2,1},{3,0},{4,7},{5,6},{6,5},{7,4},{8,11},{9,10},{10,... | collective-permute-start | bytes 393224 | tf_op jit(solution)/shard_map/ppermute | solution.py:551
  (2 other events, 1.4 us)

commit v6 on v5

--- a/solution.py
+++ b/solution.py
@@ -251,7 +251,8 @@
     rank, wide = grad_a.shape[2], grad_a.shape[3] + grad_b.shape[3]
     here = pl.BlockSpec(memory_space=pl.ANY)
     outs = [jax.ShapeDtypeStruct((4 * tokens, width), BF), *term_shapes(tokens, CHUNKS[0])]
-    outs += [jax.ShapeDtypeStruct((rank, wide), BF)] * 2
+    outs[4:] = [pltpu.HBM(x.shape, BF) for x in outs[4:]]
+    outs += [jax.ShapeDtypeStruct((rank, wide), BF), pltpu.VMEM((rank, wide), BF)]
     tiles = CHUNKS[0] * HD // TILE
     specs = [whole(x.shape) for x in outs] + [here]
     outs.append(jax.ShapeDtypeStruct(queries.shape, BF))
@@ -297,13 +298,13 @@
     )(x, hbm(kv_weight), after)
 
 
-def mid_kernel(kkeep, kcame, vkeep, vcame, after, kout, vout):
-    del after
+def mid_kernel(kkeep, kcame, vkeep, vcame, *rest):
+    kout, vout = rest[-2:]
     kout[...] = (kkeep[...].astype(F32) + kcame[...].astype(F32)).astype(BF)
     vout[...] = (vkeep[...].astype(F32) + vcame[...].astype(F32)).astype(BF)
 
 
-def mid_sums(kkeep, kcame, vkeep, vcame, after):
+def mid_sums(kkeep, kcame, vkeep, vcame, *after):
     shape = vkeep.shape
     low = pl.BlockSpec(shape, lambda i: (0, 0))
     high = pl.BlockSpec(shape, lambda i: (1, 0))
@@ -311,11 +312,11 @@
         mid_kernel,
         out_shape=[jax.ShapeDtypeStruct(shape, BF)] * 2,
         grid=(1,),
-        in_specs=[high, low, low, high, pl.BlockSpec(memory_space=pl.ANY)],
+        in_specs=[high, low, low, high] + [pl.BlockSpec(memory_space=pl.ANY)] * len(after),
         out_specs=[low, low],
         compiler_params=params(4),
         name="mid_sums",
-    )(kkeep, kcame, vkeep, vcame, after)
+    )(kkeep, kcame, vkeep, vcame, *after)
 
 
 def small_call(kernel, name, ids, args, outs, after=(), scratch=(), copied=0):
@@ -415,7 +416,7 @@
         copy.wait()
 
 
-def updated(ids, half, other, factor_a, factor_b, x, dp, after):
+def updated(ids, half, other, factor_a, factor_b, x, dp, *after):
     rates = (2.0 / math.sqrt(dp * D), 2.0 / math.sqrt(dp * R))
     outs = [pltpu.HBM(f.shape, F32) for f in (factor_a, factor_b)]
     outs += [jax.ShapeDtypeStruct((2 * TOP, 2 * TOP), BF)] * 4
@@ -425,7 +426,7 @@
         ids,
         (half, other, factor_a, factor_b, x),
         outs,
-        (after,),
+        after,
         [
             pltpu.VMEM((TILE, factor_a.shape[-1]), BF),
             pltpu.VMEM(factor_a.shape, F32),
@@ -574,12 +575,13 @@
     x, *first, packed, own, attended = first_terms(
         ids, hidden_in, kv_weight, grad_a, grad_b, queries, tokens
     )
+    own = pltpu.with_memory_space_constraint(own, pltpu.VMEM)
     half = plus(own, core_flip(packed, count_dp))
 
-    def first_exchange(term, after):
+    def first_exchange(term, *after):
         ksend, kkeep, vsend, vkeep0, vkeep1 = term
         kcame, vcame = across(ksend, 1), across(vsend, 2)
-        mids = mid_sums(kkeep, kcame, vkeep1, vcame, after)
+        mids = mid_sums(kkeep, kcame, vkeep1, vcame, *after)
         return mids, (kkeep, kcame, vkeep0, vcame)
 
     def second_exchange(mids, parts):
@@ -599,10 +601,10 @@
     first = second_exchange(mids, parts)
     other = core_flip(half, count_dp)
     new_a, new_b, *sends = updated(
-        ids, half, other, factor_a, factor_b, x, count_dp, mids[0]
+        ids, half, other, factor_a, factor_b, x, count_dp, first[2], first[5]
     )
     ub = [sends[0]] + [across(sends[r], r) for r in (1, 2, 3)]
-    second = second_exchange(*first_exchange(second, ub[1]))
+    second = second_exchange(*first_exchange(second, *ub[1:]))
     for start, count, came in ((0, CHUNKS[0], first), (CHUNKS[0], CHUNKS[1], second)):
         attended = attend_chunk(
             ids,

time: 71.8 us -> 65.4 us (0.911)
  waiting for transfers between devices: 22.5 us -> 16.6 us
  local copies, waits for them, and re-layouts: 3.12 us -> 1.75 us
  starting transfers between devices: 17.8 us -> 18.6 us
    ppermute x11, waiting for transfers between devices: 14.8 us -> 12.1 us  [across(): return lax.ppermute(x, 'tensor', [(i, i ^ r) for i in range(4)])]
    ppermute x2, waiting for transfers between devices: 7.02 us -> 4.42 us  [along_line(): return lax.ppermute(x, 'dp', [(i, i ^ 2 * d) for i in range(count)])]
    unnamed x22 -> x18, local copies, waits for them, and re-layouts: 3.02 us -> 1.64 us
    ppermute x11, starting transfers between devices: 13 us -> 13.8 us  [across(): return lax.ppermute(x, 'tensor', [(i, i ^ r) for i in range(4)])]
  transfers between devices with their start and end apart: 15 -> 15, of which waited for: 4 -> 7; matrix products, arithmetic and copies ran while one was open for 1% -> 1% of each run, Pallas kernels for 19% -> 21%
where the time goes in v6:
time: 65.4 us; the launch traced here: 65.2 us
  Pallas kernels  26.7 us (41%)
  starting transfers between devices  18.6 us (28%)
  waiting for transfers between devices  16.6 us (25%)
  local copies, waits for them, and re-layouts  1.75 us (3%)
  other arithmetic  0.82 us (1%)
  between operations  0.76 us (1%)
    ppermute x11, starting transfers between devices, across(): return lax.ppermute(x, 'tensor', [(i, i ^ r) for i in range(4)])  13.8 us
    ppermute x11, waiting for transfers between devices, across(): return lax.ppermute(x, 'tensor', [(i, i ^ r) for i in range(4)])  12.1 us
    pallas_call x2, Pallas kernels, attend_chunk(): pl.pallas_call(attend_kernel, out_shape=jax.ShapeDtypeStruct(queries.shap...  11.6 us
    pallas_call x1, Pallas kernels, first_terms(): pl.pallas_call(first_kernel, out_shape=outs, grid_spec=pltpu.PrefetchScal...  6.99 us
    ppermute x2, waiting for transfers between devices, along_line(): return lax.ppermute(x, 'dp', [(i, i ^ 2 * d) for i in range(count)])  4.42 us
    ppermute x2, starting transfers between devices, along_line(): return lax.ppermute(x, 'dp', [(i, i ^ 2 * d) for i in range(count)])  4.3 us
    pallas_call x1, Pallas kernels, later_terms(): pl.pallas_call(later_kernel, out_shape=outs, grid=(1,), in_specs=[whole(x...  4.26 us
    unnamed x18, local copies, waits for them, and re-layouts  1.64 us
  transfers between devices with their start and end apart: 15, of which 7 were waited for; matrix products, arithmetic and copies ran while one was open for 1% of the time, Pallas kernels for 21%

profile of v6, /device:TPU:0, one launch (start us, length us, event | category | flops | bytes accessed | tf_op | source)
XLA Modules:
  0.0 65.2 jit_solution(15315793080898153820)
XLA Ops:
  0.7 7.0 %first_terms.1 = (bf16[960,1280]{1,0:T(8,128)(2,1)S(1)}, bf16[480,512]{1,0:T(8,128)(2,1)}, bf16[480,512]{1,0:T(8,128)(2,1)S(1)}, bf16[480,512]{1,0:T(8,128)(2,1)...) custom-call(s32[3]{0:T(128)S(1)} %pad_add_fusion.ids, ...), custom_call_target="tpu_custom_call" | custom-call | tf_op jit(solution)/shard_map/first_terms/pallas_call | solution.py:259
  8.9 2.5 %collective-permute-start.5 = (bf16[480,512]{1,0:T(8,128)(2,1)}, bf16[480,512]{1,0:T(8,128)(2,1)S(1)}, u32[]{:S(2)}, u32[]{:S(2)}) collective-permute-start(bf16[480,512]{1,0:T(8,128)(2,1)} %get-tuple-element.35), channel_id=1, source_target_pairs={{0,1},{1,0},{2,3},{3,2},{4,5},{5,4},{6,7},{7,6},{8,9},{9,8},{10,11... | collective-permute-start | bytes 1474568 | tf_op jit(solution)/shard_map/ppermute | solution.py:552
  11.4 1.5 %collective-permute-start.6 = (bf16[480,512]{1,0:T(8,128)(2,1)}, bf16[480,512]{1,0:T(8,128)(2,1)}, u32[]{:S(2)}, u32[]{:S(2)}) collective-permute-start(bf16[480,512]{1,0:T(8,128)(2,1)} %get-tuple-element.37), channel_id=1, source_target_pairs={{0,2},{1,3},{2,0},{3,1},{4,6},{5,7},{6,4},{7,5},{8,10},{9,11},{10,... | collective-permute-start | bytes 1474568 | tf_op jit(solution)/shard_map/ppermute | solution.py:552
  13.2 0.9 %copy-done.4 = bf16[64,1536]{1,0:T(8,128)(2,1)S(1)} copy-done((bf16[64,1536]{1,0:T(8,128)(2,1)S(1)}, bf16[64,1536]{1,0:T(8,128)(2,1)}, u32[]{:S(2)}) %copy-start.4) | copy-done | bytes 196632
  14.1 1.0 %plus.3.after.a = bf16[64,1536]{1,0:T(8,128)(2,1)S(1)} custom-call(bf16[64,1536]{1,0:T(8,128)(2,1)S(1)} %copy-done.4, bf16[64,1536]{1,0:T(8,128)(2,1)} %collective-permute-done.b), custom_call_target="tpu_custom_call" | custom-call | tf_op jit(solution)/shard_map/plus/pallas_call | solution.py:355
  15.1 1.6 %collective-permute-start.3 = (bf16[64,1536]{1,0:T(8,128)(2,1)S(1)}, bf16[64,1536]{1,0:T(8,128)(2,1)S(1)}, u32[]{:S(2)}, u32[]{:S(2)}) collective-permute-start(bf16[64,1536]{1,0:T(8,128)(2,1)S(1)} %plus.3.after.a), channel_id=1, source_target_pairs={{0,8},{4,12},{8,0},{12,4},{16,24},{20,28},{24,16},{28,20},{1,9},{5... | collective-permute-start | bytes 589832 | tf_op jit(solution)/shard_map/ppermute | solution.py:367
  16.8 4.3 %later_terms.1 = (bf16[480,512]{1,0:T(8,128)(2,1)S(1)}, bf16[480,512]{1,0:T(8,128)(2,1)S(1)}, bf16[480,512]{1,0:T(8,128)(2,1)S(1)}, bf16[240,512]{1,0:T(8,128)(2,1)S(1)}, bf16[240,512]{1,0:T(8,128)(2,1)S(1)}) custom-call(bf16[960,1280]{1,0:T(8,128)(2,1)S(1)} %get-tuple-element.27.x.refs_4_, bf16[2,1280,1024]{2,1,0:T(8,128)(2,1)} %weight.3, ...), custom_call_target="tpu_custom_call" | custom-call | tf_op jit(solution)/shard_map/later_terms/pallas_call | solution.py:286
  21.6 1.0 %collective-permute-start.1 = (bf16[480,512]{1,0:T(8,128)(2,1)S(1)}, bf16[480,512]{1,0:T(8,128)(2,1)S(1)}, u32[]{:S(2)}, u32[]{:S(2)}) collective-permute-start(bf16[480,512]{1,0:T(8,128)(2,1)S(1)} %get-tuple-element.31.rest_0_), channel_id=1, source_target_pairs={{0,1},{1,0},{2,3},{3,2},{4,5},{5,4},{6,7},{7,6},{8,9},{9,8},{10,11... | collective-permute-start | bytes 1474568 | tf_op jit(solution)/shard_map/ppermute | solution.py:552
  22.7 2.7 %collective-permute-start.4 = (bf16[64,1536]{1,0:T(8,128)(2,1)S(1)}, bf16[64,1536]{1,0:T(8,128)(2,1)S(1)}, u32[]{:S(2)}, u32[]{:S(2)}) collective-permute-start(bf16[64,1536]{1,0:T(8,128)(2,1)S(1)} %plus.4.rest_0_.a), channel_id=1, source_target_pairs={{0,16},{4,20},{8,24},{12,28},{16,0},{20,4},{24,8},{28,12},{1,17},{... | collective-permute-start | bytes 589832 | tf_op jit(solution)/shard_map/ppermute | solution.py:367
  25.7 1.1 %mid_sums.2 = (bf16[240,512]{1,0:T(8,128)(2,1)S(1)}, bf16[240,512]{1,0:T(8,128)(2,1)S(1)}) custom-call(bf16[480,512]{1,0:T(8,128)(2,1)S(1)} %get-tuple-element.34.kkeep.refs_3_, bf16[480,512]{1,0:T(8,128)(2,1)S(1)} %collective-permute-done.5.kcame.refs_4_, bf16[240,512]{1,0:T(8,128)(2,1)S(1)} %copy-done.1, ...), custom_call_target="tpu_custom_call" | custom-call | tf_op jit(solution)/shard_map/mid_sums/pallas_call | solution.py:311
  26.8 0.7 %collective-permute-start.9 = (bf16[240,512]{1,0:T(8,128)(2,1)S(1)}, bf16[240,512]{1,0:T(8,128)(2,1)S(1)}, u32[]{:S(2)}, u32[]{:S(2)}) collective-permute-start(bf16[240,512]{1,0:T(8,128)(2,1)S(1)} %get-tuple-element.39), channel_id=1, source_target_pairs={{0,1},{1,0},{2,3},{3,2},{4,5},{5,4},{6,7},{7,6},{8,9},{9,8},{10,11... | collective-permute-start | bytes 737288 | tf_op jit(solution)/shard_map/ppermute | solution.py:552
  27.5 1.5 %collective-permute-start.8 = (bf16[240,512]{1,0:T(8,128)(2,1)S(1)}, bf16[240,512]{1,0:T(8,128)(2,1)S(1)}, u32[]{:S(2)}, u32[]{:S(2)}) collective-permute-start(bf16[240,512]{1,0:T(8,128)(2,1)S(1)} %get-tuple-element.38.rest_0_), channel_id=1, source_target_pairs={{0,2},{1,3},{2,0},{3,1},{4,6},{5,7},{6,4},{7,5},{8,10},{9,11},{10,... | collective-permute-start | bytes 737288 | tf_op jit(solution)/shard_map/ppermute | solution.py:552
  29.5 4.4 %collective-permute-done.4.b = bf16[64,1536]{1,0:T(8,128)(2,1)S(1)} collective-permute-done((bf16[64,1536]{1,0:T(8,128)(2,1)S(1)}, bf16[64,1536]{1,0:T(8,128)(2,1)S(1)}, u32[]{:S(2)}, u32[]{:S(2)}) %collective-permute-start.4) | collective-permute-done | bytes 196640 | tf_op jit(solution)/shard_map/ppermute | solution.py:367
  34.1 5.3 %collective-permute-done.9.refs_6_.refs_8_ = bf16[240,512]{1,0:T(8,128)(2,1)S(1)} collective-permute-done((bf16[240,512]{1,0:T(8,128)(2,1)S(1)}, bf16[240,512]{1,0:T(8,128)(2,1)S(1)}, u32[]{:S(2)}, u32[]{:S(2)}) %collective-permute-start.9) | collective-permute-done | bytes 245792 | tf_op jit(solution)/shard_map/ppermute | solution.py:552
  39.4 1.3 %collective-permute-done.8.refs_5_ = bf16[240,512]{1,0:T(8,128)(2,1)S(1)} collective-permute-done((bf16[240,512]{1,0:T(8,128)(2,1)S(1)}, bf16[240,512]{1,0:T(8,128)(2,1)S(1)}, u32[]{:S(2)}, u32[]{:S(2)}) %collective-permute-start.8) | collective-permute-done | bytes 245792 | tf_op jit(solution)/shard_map/ppermute | solution.py:552
  40.7 1.5 %update_factors.1 = (f32[2,64,1280]{2,1,0:T(8,128)}, f32[2,64,256]{2,1,0:T(8,128)}, bf16[256,256]{1,0:T(8,128)(2,1)S(1)}, bf16[256,256]{1,0:T(8,128)(2,1)S(1)}, ...) custom-call(s32[3]{0:T(128)S(1)} %pad_add_fusion.ids, bf16[64,1536]{1,0:T(8,128)(2,1)S(1)} %plus.5.refs_0_, ...), custom_call_target="tpu_custom_call" | custom-call | tf_op jit(solution)/shard_map/update_factors/pallas_call | solution.py:328
  42.7 1.7 %collective-permute-start.11 = (bf16[256,256]{1,0:T(8,128)(2,1)S(1)}, bf16[256,256]{1,0:T(8,128)(2,1)S(1)}, u32[]{:S(2)}, u32[]{:S(2)}) collective-permute-start(bf16[256,256]{1,0:T(8,128)(2,1)S(1)} %get-tuple-element.41), channel_id=1, source_target_pairs={{0,2},{1,3},{2,0},{3,1},{4,6},{5,7},{6,4},{7,5},{8,10},{9,11},{10,... | collective-permute-start | bytes 393224 | tf_op jit(solution)/shard_map/ppermute | solution.py:552
  44.4 1.4 %collective-permute-start.12 = (bf16[256,256]{1,0:T(8,128)(2,1)S(1)}, bf16[256,256]{1,0:T(8,128)(2,1)S(1)}, u32[]{:S(2)}, u32[]{:S(2)}) collective-permute-start(bf16[256,256]{1,0:T(8,128)(2,1)S(1)} %get-tuple-element.42), channel_id=1, source_target_pairs={{0,3},{1,2},{2,1},{3,0},{4,7},{5,6},{6,5},{7,4},{8,11},{9,10},{10,... | collective-permute-start | bytes 393224 | tf_op jit(solution)/shard_map/ppermute | solution.py:552
  45.9 2.9 %collective-permute-done.10.rest_0_.refs_10_ = bf16[256,256]{1,0:T(8,128)(2,1)S(1)} collective-permute-done((bf16[256,256]{1,0:T(8,128)(2,1)S(1)}, bf16[256,256]{1,0:T(8,128)(2,1)S(1)}, u32[]{:S(2)}, u32[]{:S(2)}) %collective-permute-start.10) | collective-permute-done | bytes 131104 | tf_op jit(solution)/shard_map/ppermute | solution.py:552
  49.4 1.5 %collective-permute-done.12.rest_2_.refs_12_ = bf16[256,256]{1,0:T(8,128)(2,1)S(1)} collective-permute-done((bf16[256,256]{1,0:T(8,128)(2,1)S(1)}, bf16[256,256]{1,0:T(8,128)(2,1)S(1)}, u32[]{:S(2)}, u32[]{:S(2)}) %collective-permute-start.12) | collective-permute-done | bytes 131104 | tf_op jit(solution)/shard_map/ppermute | solution.py:552
  51.1 1.0 %collective-permute-start.13 = (bf16[240,512]{1,0:T(8,128)(2,1)S(1)}, bf16[240,512]{1,0:T(8,128)(2,1)S(1)}, u32[]{:S(2)}, u32[]{:S(2)}) collective-permute-start(bf16[240,512]{1,0:T(8,128)(2,1)S(1)} %get-tuple-element.43), channel_id=1, source_target_pairs={{0,2},{1,3},{2,0},{3,1},{4,6},{5,7},{6,4},{7,5},{8,10},{9,11},{10,... | collective-permute-start | bytes 737288 | tf_op jit(solution)/shard_map/ppermute | solution.py:552
  52.1 1.5 %collective-permute-start.14 = (bf16[240,512]{1,0:T(8,128)(2,1)S(1)}, bf16[240,512]{1,0:T(8,128)(2,1)S(1)}, u32[]{:S(2)}, u32[]{:S(2)}) collective-permute-start(bf16[240,512]{1,0:T(8,128)(2,1)S(1)} %get-tuple-element.45), channel_id=1, source_target_pairs={{0,1},{1,0},{2,3},{3,2},{4,5},{5,4},{6,7},{7,6},{8,9},{9,8},{10,11... | collective-permute-start | bytes 737288 | tf_op jit(solution)/shard_map/ppermute | solution.py:552
  53.5 5.8 %attend_chunk.2.refs_15_ = bf16[60,4,4096]{2,1,0:T(4,128)(2,1)} custom-call(s32[3]{0:T(128)S(1)} %pad_add_fusion.ids, s32[1]{0:T(128)} %constant.43.clone.1.first, s32[60]{0:T(128)S(1)} %copy-done.6, bf16[60,4,4096]{2,1,0:T(4,128)(2,1)} %refs_0_.3, bf16[60,16,1024]{2,1,0:T(8,128)(2,1)} %refs_1_.3, ...), custom_call_target="tpu_custom_call", output_to_operand_aliasing={{}: (18, {})} | custom-call | tf_op jit(solution)/shard_map/attend_chunk/pallas_call | solution.py:530
  59.4 5.8 %attend_chunk.3 = bf16[60,4,4096]{2,1,0:T(4,128)(2,1)} custom-call(s32[3]{0:T(128)S(1)} %pad_add_fusion.ids, s32[1]{0:T(128)} %constant.41.clone.1.first, s32[60]{0:T(128)S(1)} %copy-done.6, bf16[60,4,4096]{2,1,0:T(4,128)(2,1)} %refs_0_.3, bf16[60,16,1024]{2,1,0:T(8,128)(2,1)} %refs_1_.3, ...), custom_call_target="tpu_custom_call", output_to_operand_aliasing={{}: (18, {})} | custom-call | tf_op jit(solution)/shard_map/attend_chunk/pallas_call | solution.py:530
  (41 shorter events, 4.4 us)
Async XLA Ops:
  0.7 12.2 %copy-start.8 = (s32[60]{0:T(128)S(1)}, s32[60]{0:T(128)}, u32[]{:S(2)}) copy-start(s32[60]{0:T(128)} %param.23) | copy-start | bytes 724
  0.7 12.3 %copy-start.7 = (f32[128]{0:T(128)S(1)}, f32[128]{0:T(128)}, u32[]{:S(2)}) copy-start(f32[128]{0:T(128)} %param.18) | copy-start | bytes 1540
  7.7 0.7 %copy-start.3 = (bf16[64,1536]{1,0:T(8,128)(2,1)}, bf16[64,1536]{1,0:T(8,128)(2,1)S(1)}, u32[]{:S(2)}) copy-start(bf16[64,1536]{1,0:T(8,128)(2,1)S(1)} %get-tuple-element.28.a) | copy-start | bytes 589828
  8.4 4.7 %collective-permute-start = (bf16[64,1536]{1,0:T(8,128)(2,1)}, bf16[64,1536]{1,0:T(8,128)(2,1)}, u32[]{:S(2)}, u32[]{:S(2)}) collective-permute-start(bf16[64,1536]{1,0:T(8,128)(2,1)} %get-tuple-element.29), channel_id=1, source_target_pairs={{0,4},{4,0},{8,12},{12,8},{16,20},{20,16},{24,28},{28,24},{1,5},{5... | collective-permute-start | bytes 589832 | tf_op jit(solution)/shard_map/ppermute | solution.py:346
  8.9 16.5 %collective-permute-start.5 = (bf16[480,512]{1,0:T(8,128)(2,1)}, bf16[480,512]{1,0:T(8,128)(2,1)S(1)}, u32[]{:S(2)}, u32[]{:S(2)}) collective-permute-start(bf16[480,512]{1,0:T(8,128)(2,1)} %get-tuple-element.35), channel_id=1, source_target_pairs={{0,1},{1,0},{2,3},{3,2},{4,5},{5,4},{6,7},{7,6},{8,9},{9,8},{10,11... | collective-permute-start | bytes 1474568 | tf_op jit(solution)/shard_map/ppermute | solution.py:552
  11.4 14.4 %collective-permute-start.6 = (bf16[480,512]{1,0:T(8,128)(2,1)}, bf16[480,512]{1,0:T(8,128)(2,1)}, u32[]{:S(2)}, u32[]{:S(2)}) collective-permute-start(bf16[480,512]{1,0:T(8,128)(2,1)} %get-tuple-element.37), channel_id=1, source_target_pairs={{0,2},{1,3},{2,0},{3,1},{4,6},{5,7},{6,4},{7,5},{8,10},{9,11},{10,... | collective-permute-start | bytes 1474568 | tf_op jit(solution)/shard_map/ppermute | solution.py:552
  13.2 0.9 %copy-start.4 = (bf16[64,1536]{1,0:T(8,128)(2,1)S(1)}, bf16[64,1536]{1,0:T(8,128)(2,1)}, u32[]{:S(2)}) copy-start(bf16[64,1536]{1,0:T(8,128)(2,1)} %copy-done.3) | copy-start | bytes 589828
  15.1 7.6 %collective-permute-start.3 = (bf16[64,1536]{1,0:T(8,128)(2,1)S(1)}, bf16[64,1536]{1,0:T(8,128)(2,1)S(1)}, u32[]{:S(2)}, u32[]{:S(2)}) collective-permute-start(bf16[64,1536]{1,0:T(8,128)(2,1)S(1)} %plus.3.after.a), channel_id=1, source_target_pairs={{0,8},{4,12},{8,0},{12,4},{16,24},{20,28},{24,16},{28,20},{1,9},{5... | collective-permute-start | bytes 589832 | tf_op jit(solution)/shard_map/ppermute | solution.py:367
  16.8 8.9 %copy-start.1 = (bf16[240,512]{1,0:T(8,128)(2,1)S(1)}, bf16[240,512]{1,0:T(8,128)(2,1)}, u32[]{:S(2)}) copy-start(bf16[240,512]{1,0:T(8,128)(2,1)} %get-tuple-element.36.vkeep) | copy-start | bytes 737284
  21.1 24.8 %collective-permute-start.2 = (bf16[480,512]{1,0:T(8,128)(2,1)S(1)}, bf16[480,512]{1,0:T(8,128)(2,1)S(1)}, u32[]{:S(2)}, u32[]{:S(2)}) collective-permute-start(bf16[480,512]{1,0:T(8,128)(2,1)S(1)} %get-tuple-element.33), channel_id=1, source_target_pairs={{0,2},{1,3},{2,0},{3,1},{4,6},{5,7},{6,4},{7,5},{8,10},{9,11},{10,... | collective-permute-start | bytes 1474568 | tf_op jit(solution)/shard_map/ppermute | solution.py:552
  21.6 19.1 %copy-start = (f32[2,64,1280]{2,1,0:T(8,128)S(1)}, f32[2,64,1280]{2,1,0:T(8,128)}, u32[]{:S(2)}) copy-start(f32[2,64,1280]{2,1,0:T(8,128)} %refs_2_.3) | copy-start | bytes 1966084
  21.6 19.1 %copy-start.5 = (f32[2,64,256]{2,1,0:T(8,128)S(1)}, f32[2,64,256]{2,1,0:T(8,128)}, u32[]{:S(2)}) copy-start(f32[2,64,256]{2,1,0:T(8,128)} %refs_3_.1) | copy-start | bytes 393220
  21.6 24.2 %collective-permute-start.1 = (bf16[480,512]{1,0:T(8,128)(2,1)S(1)}, bf16[480,512]{1,0:T(8,128)(2,1)S(1)}, u32[]{:S(2)}, u32[]{:S(2)}) collective-permute-start(bf16[480,512]{1,0:T(8,128)(2,1)S(1)} %get-tuple-element.31.rest_0_), channel_id=1, source_target_pairs={{0,1},{1,0},{2,3},{3,2},{4,5},{5,4},{6,7},{7,6},{8,9},{9,8},{10,11... | collective-permute-start | bytes 1474568 | tf_op jit(solution)/shard_map/ppermute | solution.py:552
  22.7 11.3 %collective-permute-start.4 = (bf16[64,1536]{1,0:T(8,128)(2,1)S(1)}, bf16[64,1536]{1,0:T(8,128)(2,1)S(1)}, u32[]{:S(2)}, u32[]{:S(2)}) collective-permute-start(bf16[64,1536]{1,0:T(8,128)(2,1)S(1)} %plus.4.rest_0_.a), channel_id=1, source_target_pairs={{0,16},{4,20},{8,24},{12,28},{16,0},{20,4},{24,8},{28,12},{1,17},{... | collective-permute-start | bytes 589832 | tf_op jit(solution)/shard_map/ppermute | solution.py:367
  26.8 12.6 %collective-permute-start.9 = (bf16[240,512]{1,0:T(8,128)(2,1)S(1)}, bf16[240,512]{1,0:T(8,128)(2,1)S(1)}, u32[]{:S(2)}, u32[]{:S(2)}) collective-permute-start(bf16[240,512]{1,0:T(8,128)(2,1)S(1)} %get-tuple-element.39), channel_id=1, source_target_pairs={{0,1},{1,0},{2,3},{3,2},{4,5},{5,4},{6,7},{7,6},{8,9},{9,8},{10,11... | collective-permute-start | bytes 737288 | tf_op jit(solution)/shard_map/ppermute | solution.py:552
  27.5 13.2 %collective-permute-start.8 = (bf16[240,512]{1,0:T(8,128)(2,1)S(1)}, bf16[240,512]{1,0:T(8,128)(2,1)S(1)}, u32[]{:S(2)}, u32[]{:S(2)}) collective-permute-start(bf16[240,512]{1,0:T(8,128)(2,1)S(1)} %get-tuple-element.38.rest_0_), channel_id=1, source_target_pairs={{0,2},{1,3},{2,0},{3,1},{4,6},{5,7},{6,4},{7,5},{8,10},{9,11},{10,... | collective-permute-start | bytes 737288 | tf_op jit(solution)/shard_map/ppermute | solution.py:552
  34.0 6.7 %collective-permute-start.7 = (bf16[64,1536]{1,0:T(8,128)(2,1)S(1)}, bf16[64,1536]{1,0:T(8,128)(2,1)S(1)}, u32[]{:S(2)}, u32[]{:S(2)}) collective-permute-start(bf16[64,1536]{1,0:T(8,128)(2,1)S(1)} %plus.5.refs_0_), channel_id=1, source_target_pairs={{0,4},{4,0},{8,12},{12,8},{16,20},{20,16},{24,28},{28,24},{1,5},{5... | collective-permute-start | bytes 589832 | tf_op jit(solution)/shard_map/ppermute | solution.py:346
  42.3 11.2 %copy-start.2 = (bf16[240,512]{1,0:T(8,128)(2,1)S(1)}, bf16[240,512]{1,0:T(8,128)(2,1)}, u32[]{:S(2)}) copy-start(bf16[240,512]{1,0:T(8,128)(2,1)} %get-tuple-element.47.refs_6_) | copy-start | bytes 737284
  42.3 11.2 %copy-start.6 = (s32[60]{0:T(128)S(1)}, s32[60]{0:T(128)}, u32[]{:S(2)}) copy-start(s32[60]{0:T(128)} %lengths.3) | copy-start | bytes 724
  42.3 6.4 %collective-permute-start.10 = (bf16[256,256]{1,0:T(8,128)(2,1)S(1)}, bf16[256,256]{1,0:T(8,128)(2,1)S(1)}, u32[]{:S(2)}, u32[]{:S(2)}) collective-permute-start(bf16[256,256]{1,0:T(8,128)(2,1)S(1)} %get-tuple-element.40), channel_id=1, source_target_pairs={{0,1},{1,0},{2,3},{3,2},{4,5},{5,4},{6,7},{7,6},{8,9},{9,8},{10,11... | collective-permute-start | bytes 393224 | tf_op jit(solution)/shard_map/ppermute | solution.py:552
  42.7 6.7 %collective-permute-start.11 = (bf16[256,256]{1,0:T(8,128)(2,1)S(1)}, bf16[256,256]{1,0:T(8,128)(2,1)S(1)}, u32[]{:S(2)}, u32[]{:S(2)}) collective-permute-start(bf16[256,256]{1,0:T(8,128)(2,1)S(1)} %get-tuple-element.41), channel_id=1, source_target_pairs={{0,2},{1,3},{2,0},{3,1},{4,6},{5,7},{6,4},{7,5},{8,10},{9,11},{10,... | collective-permute-start | bytes 393224 | tf_op jit(solution)/shard_map/ppermute | solution.py:552
  44.4 6.6 %collective-permute-start.12 = (bf16[256,256]{1,0:T(8,128)(2,1)S(1)}, bf16[256,256]{1,0:T(8,128)(2,1)S(1)}, u32[]{:S(2)}, u32[]{:S(2)}) collective-permute-start(bf16[256,256]{1,0:T(8,128)(2,1)S(1)} %get-tuple-element.42), channel_id=1, source_target_pairs={{0,3},{1,2},{2,1},{3,0},{4,7},{5,6},{6,5},{7,4},{8,11},{9,10},{10,... | collective-permute-start | bytes 393224 | tf_op jit(solution)/shard_map/ppermute | solution.py:552
  51.1 8.3 %collective-permute-start.13 = (bf16[240,512]{1,0:T(8,128)(2,1)S(1)}, bf16[240,512]{1,0:T(8,128)(2,1)S(1)}, u32[]{:S(2)}, u32[]{:S(2)}) collective-permute-start(bf16[240,512]{1,0:T(8,128)(2,1)S(1)} %get-tuple-element.43), channel_id=1, source_target_pairs={{0,2},{1,3},{2,0},{3,1},{4,6},{5,7},{6,4},{7,5},{8,10},{9,11},{10,... | collective-permute-start | bytes 737288 | tf_op jit(solution)/shard_map/ppermute | solution.py:552
  52.1 7.3 %collective-permute-start.14 = (bf16[240,512]{1,0:T(8,128)(2,1)S(1)}, bf16[240,512]{1,0:T(8,128)(2,1)S(1)}, u32[]{:S(2)}, u32[]{:S(2)}) collective-permute-start(bf16[240,512]{1,0:T(8,128)(2,1)S(1)} %get-tuple-element.45), channel_id=1, source_target_pairs={{0,1},{1,0},{2,3},{3,2},{4,5},{5,4},{6,7},{7,6},{8,9},{9,8},{10,11... | collective-permute-start | bytes 737288 | tf_op jit(solution)/shard_map/ppermute | solution.py:552

commit v7 on v6

--- a/solution.py
+++ b/solution.py
@@ -111,12 +111,17 @@
 
 
 CHUNKS = (4, 4)
-GROUP = 12
+GROUP = 4
 HEADS_STEP = 2
 
 
 def params(mib):
     return pltpu.CompilerParams(vmem_limit_bytes=mib * MIB)
+
+
+def cost(flops, *arrays):
+    size = sum(math.prod(x.shape) * x.dtype.itemsize for x in arrays)
+    return pl.CostEstimate(flops=flops, bytes_accessed=size, transcendentals=0)
 
 
 def dot(a, b):
@@ -251,8 +256,7 @@
     rank, wide = grad_a.shape[2], grad_a.shape[3] + grad_b.shape[3]
     here = pl.BlockSpec(memory_space=pl.ANY)
     outs = [jax.ShapeDtypeStruct((4 * tokens, width), BF), *term_shapes(tokens, CHUNKS[0])]
-    outs[4:] = [pltpu.HBM(x.shape, BF) for x in outs[4:]]
-    outs += [jax.ShapeDtypeStruct((rank, wide), BF), pltpu.VMEM((rank, wide), BF)]
+    outs += [jax.ShapeDtypeStruct((rank, wide), BF)] * 2
     tiles = CHUNKS[0] * HD // TILE
     specs = [whole(x.shape) for x in outs] + [here]
     outs.append(jax.ShapeDtypeStruct(queries.shape, BF))
@@ -275,6 +279,7 @@
             ],
         ),
         compiler_params=params(16),
+        cost_estimate=cost(16 * tokens * width * CHUNKS[0] * HD, hidden),
         name="first_terms",
     )(ids, *map(hbm, (hidden, kv_weight, grad_a, grad_b)))
 
@@ -294,6 +299,7 @@
             pltpu.SemaphoreType.DMA((2, tiles)),
         ],
         compiler_params=params(12),
+        cost_estimate=cost(4 * math.prod(x.shape) * CHUNKS[1] * HD, x, *outs),
         name="later_terms",
     )(x, hbm(kv_weight), after)
 
@@ -315,6 +321,7 @@
         in_specs=[high, low, low, high] + [pl.BlockSpec(memory_space=pl.ANY)] * len(after),
         out_specs=[low, low],
         compiler_params=params(4),
+        cost_estimate=cost(0, *[vkeep] * 6),
         name="mid_sums",
     )(kkeep, kcame, vkeep, vcame, *after)
 
@@ -338,6 +345,7 @@
             scratch_shapes=list(scratch),
         ),
         compiler_params=params(8),
+        cost_estimate=cost(0, *args),
         name=name,
     )(ids, *args, *after)
 
@@ -359,6 +367,7 @@
         in_specs=[whole(a.shape)] * 2 + [pl.BlockSpec(memory_space=pl.ANY)] * len(after),
         out_specs=whole(a.shape),
         compiler_params=params(2),
+        cost_estimate=cost(0, a, b, out),
         name="plus",
     )(a, b, *after)
 
@@ -439,16 +448,24 @@
 
 def attend_kernel(ids, first, lengths, *refs):
     q, cache_k, cache_v, k0, k1, k2, v0, v1, v2, *ub, cosine, sine = refs[:15]
-    out = refs[-1]
+    out = refs[-3]
     rows, slots, _ = cache_k.shape
     tokens = rows * STEPS
-    u_top = sum(x[TOP:, :TOP].astype(F32) for x in ub)
-    u_low = sum(x[TOP:tokens, TOP:].astype(F32) for x in ub)
-    u = jnp.concatenate([u_top, u_low], axis=0).astype(BF)
+    u_held, b_held = refs[-2:]
+
+    @pl.when(pl.program_id(0) == 0)
+    def _():
+        u_held[:TOP] = sum(x[TOP:, :TOP].astype(F32) for x in ub).astype(BF)
+        u_held[TOP:] = sum(x[TOP:tokens, TOP:].astype(F32) for x in ub).astype(BF)
+
     rel = ids[0] ^ (first[0] + pl.program_id(0))
-    low = jnp.where(rel == 0, ub[0][:TOP].astype(F32), ub[1][:TOP].astype(F32))
-    high = jnp.where(rel == 2, ub[2][:TOP].astype(F32), ub[3][:TOP].astype(F32))
-    b = jnp.where(rel < 2, low, high).astype(BF)
+    for r, x in enumerate(ub):
+
+        @pl.when(rel == r)
+        def _():
+            b_held[...] = x[:TOP]
+
+    u, b = u_held[...], b_held[...]
     k = k0[...].astype(F32) + k1[...].astype(F32) + k2[...].astype(F32) + dot(u[:, :R], b[:R])
     v = v0[...].astype(F32) + v1[...].astype(F32) + v2[...].astype(F32) + dot(u[:, R:], b[R:])
     v = v.astype(BF)
@@ -515,7 +532,7 @@
     rows, slots, _ = cache_keys.shape
     tokens = rows * STEPS
     heads = QH // KVH
-    args = [*map(hbm, (queries, cache_keys, cache_values)), *terms, *ub, *tables]
+    args = [queries, cache_keys, cache_values, *terms, *ub, *tables]
     assert start % HEADS_STEP == 0 and count % HEADS_STEP == 0
     first = jnp.full((1,), start // HEADS_STEP, jnp.int32)
     size = HEADS_STEP * HD
@@ -531,10 +548,12 @@
         attend_kernel,
         out_shape=jax.ShapeDtypeStruct(queries.shape, BF),
         grid_spec=pltpu.PrefetchScalarGridSpec(
-            num_scalar_prefetch=3, grid=(count // HEADS_STEP,), in_specs=specs, out_specs=wide
+            num_scalar_prefetch=3, grid=(count // HEADS_STEP,), in_specs=specs, out_specs=wide,
+            scratch_shapes=[pltpu.VMEM((tokens, TOP), BF), pltpu.VMEM((TOP, size), BF)],
         ),
         input_output_aliases={len(args) + 2: 0},
         compiler_params=params(14),
+        cost_estimate=cost(count * 4 * 10**9, *args),
         name="attend_chunk",
     )(ids, first, lengths, *args)
 
@@ -575,7 +594,6 @@
     x, *first, packed, own, attended = first_terms(
         ids, hidden_in, kv_weight, grad_a, grad_b, queries, tokens
     )
-    own = pltpu.with_memory_space_constraint(own, pltpu.VMEM)
     half = plus(own, core_flip(packed, count_dp))
 
     def first_exchange(term, *after):
@@ -601,7 +619,7 @@
     first = second_exchange(mids, parts)
     other = core_flip(half, count_dp)
     new_a, new_b, *sends = updated(
-        ids, half, other, factor_a, factor_b, x, count_dp, first[2], first[5]
+        ids, half, other, factor_a, factor_b, x, count_dp
     )
     ub = [sends[0]] + [across(sends[r], r) for r in (1, 2, 3)]
     second = second_exchange(*first_exchange(second, *ub[1:]))

time: 65.4 us -> 63.2 us (0.966)
  Pallas kernels: 26.7 us -> 24.8 us
  waiting for transfers between devices: 16.6 us -> 14.9 us
  local copies, waits for them, and re-layouts: 1.75 us -> 3.16 us
    ppermute x11, waiting for transfers between devices: 12.1 us -> 7.91 us  [across(): return lax.ppermute(x, 'tensor', [(i, i ^ r) for i in range(4)])]
    ppermute x2, waiting for transfers between devices: 4.42 us -> 7.01 us  [along_line(): return lax.ppermute(x, 'dp', [(i, i ^ 2 * d) for i in range(count)])]
    pallas_call x2, Pallas kernels: 11.6 us -> 9.89 us  [attend_chunk(): pl.pallas_call(attend_kernel, out_shape=jax.ShapeDtypeStruct(queries.shap...]
    unnamed x18 -> x28, local copies, waits for them, and re-layouts: 1.64 us -> 3.05 us
  transfers between devices with their start and end apart: 15 -> 15, of which waited for: 7 -> 4; matrix products, arithmetic and copies ran while one was open for 1% -> 1% of each run, Pallas kernels for 21% -> 21%
where the time goes in v7:
time: 63.2 us; the launch traced here: 62.9 us
  Pallas kernels  24.8 us (39%)
  starting transfers between devices  18.4 us (29%)
  waiting for transfers between devices  14.9 us (24%)
  local copies, waits for them, and re-layouts  3.16 us (5%)
  between operations  0.84 us (1%)
  other arithmetic  0.82 us (1%)
    ppermute x11, starting transfers between devices, across(): return lax.ppermute(x, 'tensor', [(i, i ^ r) for i in range(4)])  13.6 us
    pallas_call x2, Pallas kernels, attend_chunk(): pl.pallas_call(attend_kernel, out_shape=jax.ShapeDtypeStruct(queries.shap...  9.89 us
    ppermute x11, waiting for transfers between devices, across(): return lax.ppermute(x, 'tensor', [(i, i ^ r) for i in range(4)])  7.91 us
    ppermute x2, waiting for transfers between devices, along_line(): return lax.ppermute(x, 'dp', [(i, i ^ 2 * d) for i in range(count)])  7.01 us
    pallas_call x1, Pallas kernels, first_terms(): pl.pallas_call(first_kernel, out_shape=outs, grid_spec=pltpu.PrefetchScal...  6.87 us
    ppermute x2, starting transfers between devices, along_line(): return lax.ppermute(x, 'dp', [(i, i ^ 2 * d) for i in range(count)])  4.3 us
    pallas_call x1, Pallas kernels, later_terms(): pl.pallas_call(later_kernel, out_shape=outs, grid=(1,), in_specs=[whole(x...  4.25 us
    unnamed x28, local copies, waits for them, and re-layouts  3.05 us
  transfers between devices with their start and end apart: 15, of which 4 were waited for; matrix products, arithmetic and copies ran while one was open for 1% of the time, Pallas kernels for 21%

profile of v7, /device:TPU:0, one launch (start us, length us, event | category | flops | bytes accessed | tf_op | source)
XLA Modules:
  0.0 62.9 jit_solution(3228451980730351022)
XLA Ops:
  0.7 6.9 %first_terms.1 = (bf16[960,1280]{1,0:T(8,128)(2,1)S(1)}, bf16[480,512]{1,0:T(8,128)(2,1)}, bf16[480,512]{1,0:T(8,128)(2,1)S(1)}, bf16[480,512]{1,0:T(8,128)(2,1)...) custom-call(s32[3]{0:T(128)S(1)} %pad_add_fusion.ids, ...), custom_call_target="tpu_custom_call" | custom-call | flops 2516582400 | bytes 2457600 | tf_op jit(solution)/shard_map/first_terms/pallas_call | solution.py:263
  7.6 0.7 %copy-done.1 = bf16[240,512]{1,0:T(8,128)(2,1)} copy-done((bf16[240,512]{1,0:T(8,128)(2,1)}, bf16[240,512]{1,0:T(8,128)(2,1)S(1)}, u32[]{:S(2)}) %copy-start.1) | copy-done | bytes 245784
  9.0 0.7 %copy-done.10 = bf16[240,512]{1,0:T(8,128)(2,1)} copy-done((bf16[240,512]{1,0:T(8,128)(2,1)}, bf16[240,512]{1,0:T(8,128)(2,1)S(1)}, u32[]{:S(2)}) %copy-start.10) | copy-done | bytes 245784
  10.1 2.5 %collective-permute-start.5 = (bf16[480,512]{1,0:T(8,128)(2,1)}, bf16[480,512]{1,0:T(8,128)(2,1)S(1)}, u32[]{:S(2)}, u32[]{:S(2)}) collective-permute-start(bf16[480,512]{1,0:T(8,128)(2,1)} %get-tuple-element.35), channel_id=1, source_target_pairs={{0,1},{1,0},{2,3},{3,2},{4,5},{5,4},{6,7},{7,6},{8,9},{9,8},{10,11... | collective-permute-start | bytes 1474568 | tf_op jit(solution)/shard_map/ppermute | solution.py:571
  12.6 1.5 %collective-permute-start.6 = (bf16[480,512]{1,0:T(8,128)(2,1)}, bf16[480,512]{1,0:T(8,128)(2,1)}, u32[]{:S(2)}, u32[]{:S(2)}) collective-permute-start(bf16[480,512]{1,0:T(8,128)(2,1)} %get-tuple-element.37), channel_id=1, source_target_pairs={{0,2},{1,3},{2,0},{3,1},{4,6},{5,7},{6,4},{7,5},{8,10},{9,11},{10,... | collective-permute-start | bytes 1474568 | tf_op jit(solution)/shard_map/ppermute | solution.py:571
  14.4 0.9 %copy-done.4 = bf16[64,1536]{1,0:T(8,128)(2,1)S(1)} copy-done((bf16[64,1536]{1,0:T(8,128)(2,1)S(1)}, bf16[64,1536]{1,0:T(8,128)(2,1)}, u32[]{:S(2)}) %copy-start.4) | copy-done | bytes 196632
  15.4 1.0 %plus.3.after.a = bf16[64,1536]{1,0:T(8,128)(2,1)S(1)} custom-call(bf16[64,1536]{1,0:T(8,128)(2,1)S(1)} %copy-done.4, bf16[64,1536]{1,0:T(8,128)(2,1)} %collective-permute-done.b), custom_call_target="tpu_custom_call" | custom-call | bytes 589824 | tf_op jit(solution)/shard_map/plus/pallas_call | solution.py:363
  16.3 1.6 %collective-permute-start.3 = (bf16[64,1536]{1,0:T(8,128)(2,1)S(1)}, bf16[64,1536]{1,0:T(8,128)(2,1)S(1)}, u32[]{:S(2)}, u32[]{:S(2)}) collective-permute-start(bf16[64,1536]{1,0:T(8,128)(2,1)S(1)} %plus.3.after.a), channel_id=1, source_target_pairs={{0,8},{4,12},{8,0},{12,4},{16,24},{20,28},{24,16},{28,20},{1,9},{5... | collective-permute-start | bytes 589832 | tf_op jit(solution)/shard_map/ppermute | solution.py:376
  18.0 4.3 %later_terms.1 = (bf16[480,512]{1,0:T(8,128)(2,1)S(1)}, bf16[480,512]{1,0:T(8,128)(2,1)S(1)}, bf16[480,512]{1,0:T(8,128)(2,1)S(1)}, bf16[240,512]{1,0:T(8,128)(2,1)S(1)}, bf16[240,512]{1,0:T(8,128)(2,1)S(1)}) custom-call(bf16[960,1280]{1,0:T(8,128)(2,1)S(1)} %get-tuple-element.27.x.refs_4_, bf16[2,1280,1024]{2,1,0:T(8,128)(2,1)} %weight.3, ...), custom_call_target="tpu_custom_call" | custom-call | flops 2516582400 | bytes 4423680 | tf_op jit(solution)/shard_map/later_terms/pallas_call | solution.py:291
  22.8 1.0 %collective-permute-start.1 = (bf16[480,512]{1,0:T(8,128)(2,1)S(1)}, bf16[480,512]{1,0:T(8,128)(2,1)S(1)}, u32[]{:S(2)}, u32[]{:S(2)}) collective-permute-start(bf16[480,512]{1,0:T(8,128)(2,1)S(1)} %get-tuple-element.31.rest_0_), channel_id=1, source_target_pairs={{0,1},{1,0},{2,3},{3,2},{4,5},{5,4},{6,7},{7,6},{8,9},{9,8},{10,11... | collective-permute-start | bytes 1474568 | tf_op jit(solution)/shard_map/ppermute | solution.py:571
  23.9 2.7 %collective-permute-start.4 = (bf16[64,1536]{1,0:T(8,128)(2,1)S(1)}, bf16[64,1536]{1,0:T(8,128)(2,1)S(1)}, u32[]{:S(2)}, u32[]{:S(2)}) collective-permute-start(bf16[64,1536]{1,0:T(8,128)(2,1)S(1)} %plus.4.rest_0_.a), channel_id=1, source_target_pairs={{0,16},{4,20},{8,24},{12,28},{16,0},{20,4},{24,8},{28,12},{1,17},{... | collective-permute-start | bytes 589832 | tf_op jit(solution)/shard_map/ppermute | solution.py:376
  27.2 1.1 %mid_sums.2 = (bf16[240,512]{1,0:T(8,128)(2,1)S(1)}, bf16[240,512]{1,0:T(8,128)(2,1)S(1)}) custom-call(bf16[480,512]{1,0:T(8,128)(2,1)S(1)} %get-tuple-element.34.kkeep.refs_3_, bf16[480,512]{1,0:T(8,128)(2,1)S(1)} %collective-permute-done.5.kcame.refs_4_, bf16[240,512]{1,0:T(8,128)(2,1)S(1)} %copy-done.2, ...), custom_call_target="tpu_custom_call" | custom-call | bytes 1474560 | tf_op jit(solution)/shard_map/mid_sums/pallas_call | solution.py:317
  28.2 7.0 %collective-permute-done.4.b = bf16[64,1536]{1,0:T(8,128)(2,1)S(1)} collective-permute-done((bf16[64,1536]{1,0:T(8,128)(2,1)S(1)}, bf16[64,1536]{1,0:T(8,128)(2,1)S(1)}, u32[]{:S(2)}, u32[]{:S(2)}) %collective-permute-start.4) | collective-permute-done | bytes 196640 | tf_op jit(solution)/shard_map/ppermute | solution.py:376
  35.4 0.8 %collective-permute-start.14 = (bf16[240,512]{1,0:T(8,128)(2,1)S(1)}, bf16[240,512]{1,0:T(8,128)(2,1)S(1)}, u32[]{:S(2)}, u32[]{:S(2)}) collective-permute-start(bf16[240,512]{1,0:T(8,128)(2,1)S(1)} %get-tuple-element.47), channel_id=1, source_target_pairs={{0,1},{1,0},{2,3},{3,2},{4,5},{5,4},{6,7},{7,6},{8,9},{9,8},{10,11... | collective-permute-start | bytes 737288 | tf_op jit(solution)/shard_map/ppermute | solution.py:571
  36.2 1.5 %collective-permute-start.13 = (bf16[240,512]{1,0:T(8,128)(2,1)S(1)}, bf16[240,512]{1,0:T(8,128)(2,1)S(1)}, u32[]{:S(2)}, u32[]{:S(2)}) collective-permute-start(bf16[240,512]{1,0:T(8,128)(2,1)S(1)} %get-tuple-element.38.rest_0_), channel_id=1, source_target_pairs={{0,2},{1,3},{2,0},{3,1},{4,6},{5,7},{6,4},{7,5},{8,10},{9,11},{10,... | collective-permute-start | bytes 737288 | tf_op jit(solution)/shard_map/ppermute | solution.py:571
  37.7 1.5 %update_factors.1 = (f32[2,64,1280]{2,1,0:T(8,128)}, f32[2,64,256]{2,1,0:T(8,128)}, bf16[256,256]{1,0:T(8,128)(2,1)S(1)}, bf16[256,256]{1,0:T(8,128)(2,1)S(1)}, ...) custom-call(s32[3]{0:T(128)S(1)} %pad_add_fusion.ids, bf16[64,1536]{1,0:T(8,128)(2,1)S(1)} %plus.5.refs_0_, ...), custom_call_target="tpu_custom_call" | custom-call | bytes 3637248 | tf_op jit(solution)/shard_map/update_factors/pallas_call | solution.py:335
  39.9 1.3 %collective-permute-start.9 = (bf16[256,256]{1,0:T(8,128)(2,1)S(1)}, bf16[256,256]{1,0:T(8,128)(2,1)S(1)}, u32[]{:S(2)}, u32[]{:S(2)}) collective-permute-start(bf16[256,256]{1,0:T(8,128)(2,1)S(1)} %get-tuple-element.40), channel_id=1, source_target_pairs={{0,2},{1,3},{2,0},{3,1},{4,6},{5,7},{6,4},{7,5},{8,10},{9,11},{10,... | collective-permute-start | bytes 393224 | tf_op jit(solution)/shard_map/ppermute | solution.py:571
  41.1 1.7 %collective-permute-start.10 = (bf16[256,256]{1,0:T(8,128)(2,1)S(1)}, bf16[256,256]{1,0:T(8,128)(2,1)S(1)}, u32[]{:S(2)}, u32[]{:S(2)}) collective-permute-start(bf16[256,256]{1,0:T(8,128)(2,1)S(1)} %get-tuple-element.41), channel_id=1, source_target_pairs={{0,3},{1,2},{2,1},{3,0},{4,7},{5,6},{6,5},{7,4},{8,11},{9,10},{10,... | collective-permute-start | bytes 393224 | tf_op jit(solution)/shard_map/ppermute | solution.py:571
  42.8 4.2 %collective-permute-done.8.rest_0_.refs_10_ = bf16[256,256]{1,0:T(8,128)(2,1)S(1)} collective-permute-done((bf16[256,256]{1,0:T(8,128)(2,1)S(1)}, bf16[256,256]{1,0:T(8,128)(2,1)S(1)}, u32[]{:S(2)}, u32[]{:S(2)}) %collective-permute-start.8) | collective-permute-done | bytes 131104 | tf_op jit(solution)/shard_map/ppermute | solution.py:571
  47.0 2.8 %collective-permute-done.9.rest_1_.refs_11_ = bf16[256,256]{1,0:T(8,128)(2,1)S(1)} collective-permute-done((bf16[256,256]{1,0:T(8,128)(2,1)S(1)}, bf16[256,256]{1,0:T(8,128)(2,1)S(1)}, u32[]{:S(2)}, u32[]{:S(2)}) %collective-permute-start.9) | collective-permute-done | bytes 131104 | tf_op jit(solution)/shard_map/ppermute | solution.py:571
  49.9 1.6 %collective-permute-start.11 = (bf16[240,512]{1,0:T(8,128)(2,1)S(1)}, bf16[240,512]{1,0:T(8,128)(2,1)S(1)}, u32[]{:S(2)}, u32[]{:S(2)}) collective-permute-start(bf16[240,512]{1,0:T(8,128)(2,1)S(1)} %get-tuple-element.42), channel_id=1, source_target_pairs={{0,2},{1,3},{2,0},{3,1},{4,6},{5,7},{6,4},{7,5},{8,10},{9,11},{10,... | collective-permute-start | bytes 737288 | tf_op jit(solution)/shard_map/ppermute | solution.py:571
  52.1 5.2 %attend_chunk.2.refs_15_ = bf16[60,4,4096]{2,1,0:T(4,128)(2,1)} custom-call(s32[3]{0:T(128)S(1)} %pad_add_fusion.ids, s32[1]{0:T(128)} %constant.43.clone.1.first, s32[60]{0:T(128)S(1)} %copy-done.9, bf16[60,4,4096]{2,1,0:T(4,128)(2,1)S(1)} %copy-done.6, bf16[60,16,1024]{2,1,0:T(8,128)(2,1)S(1)} %copy-done.7, ...), custom_call_target="tpu_custom_call", output_to_operand_aliasing={{}: (18, {})} | custom-call | flops 16000000000 | bytes 10846208 | tf_op jit(solution)/shard_map/attend_chunk/pallas_call | solution.py:547
  57.4 0.9 %collective-permute-done.12.refs_8_ = bf16[240,512]{1,0:T(8,128)(2,1)S(1)} collective-permute-done((bf16[240,512]{1,0:T(8,128)(2,1)S(1)}, bf16[240,512]{1,0:T(8,128)(2,1)S(1)}, u32[]{:S(2)}, u32[]{:S(2)}) %collective-permute-start.12) | collective-permute-done | bytes 245792 | tf_op jit(solution)/shard_map/ppermute | solution.py:571
  58.3 4.6 %attend_chunk.3 = bf16[60,4,4096]{2,1,0:T(4,128)(2,1)} custom-call(s32[3]{0:T(128)S(1)} %pad_add_fusion.ids, s32[1]{0:T(128)} %constant.41.clone.1.first, s32[60]{0:T(128)S(1)} %copy-done.9, bf16[60,4,4096]{2,1,0:T(4,128)(2,1)S(1)} %copy-done.6, bf16[60,16,1024]{2,1,0:T(8,128)(2,1)S(1)} %copy-done.7, ...), custom_call_target="tpu_custom_call", output_to_operand_aliasing={{}: (18, {})} | custom-call | flops 16000000000 | bytes 10846208 | tf_op jit(solution)/shard_map/attend_chunk/pallas_call | solution.py:547
  (51 shorter events, 4.1 us)
Async XLA Ops:
  0.7 13.4 %copy-start.13 = (s32[60]{0:T(128)S(1)}, s32[60]{0:T(128)}, u32[]{:S(2)}) copy-start(s32[60]{0:T(128)} %param.23) | copy-start | bytes 724
  0.7 13.6 %copy-start.12 = (f32[128]{0:T(128)S(1)}, f32[128]{0:T(128)}, u32[]{:S(2)}) copy-start(f32[128]{0:T(128)} %param.18) | copy-start | bytes 1540
  9.7 4.7 %collective-permute-start = (bf16[64,1536]{1,0:T(8,128)(2,1)}, bf16[64,1536]{1,0:T(8,128)(2,1)}, u32[]{:S(2)}, u32[]{:S(2)}) collective-permute-start(bf16[64,1536]{1,0:T(8,128)(2,1)} %get-tuple-element.29), channel_id=1, source_target_pairs={{0,4},{4,0},{8,12},{12,8},{16,20},{20,16},{24,28},{28,24},{1,5},{5... | collective-permute-start | bytes 589832 | tf_op jit(solution)/shard_map/ppermute | solution.py:354
  10.1 17.0 %collective-permute-start.5 = (bf16[480,512]{1,0:T(8,128)(2,1)}, bf16[480,512]{1,0:T(8,128)(2,1)S(1)}, u32[]{:S(2)}, u32[]{:S(2)}) collective-permute-start(bf16[480,512]{1,0:T(8,128)(2,1)} %get-tuple-element.35), channel_id=1, source_target_pairs={{0,1},{1,0},{2,3},{3,2},{4,5},{5,4},{6,7},{7,6},{8,9},{9,8},{10,11... | collective-permute-start | bytes 1474568 | tf_op jit(solution)/shard_map/ppermute | solution.py:571
  12.6 14.5 %collective-permute-start.6 = (bf16[480,512]{1,0:T(8,128)(2,1)}, bf16[480,512]{1,0:T(8,128)(2,1)}, u32[]{:S(2)}, u32[]{:S(2)}) collective-permute-start(bf16[480,512]{1,0:T(8,128)(2,1)} %get-tuple-element.37), channel_id=1, source_target_pairs={{0,2},{1,3},{2,0},{3,1},{4,6},{5,7},{6,4},{7,5},{8,10},{9,11},{10,... | collective-permute-start | bytes 1474568 | tf_op jit(solution)/shard_map/ppermute | solution.py:571
  16.3 7.5 %collective-permute-start.3 = (bf16[64,1536]{1,0:T(8,128)(2,1)S(1)}, bf16[64,1536]{1,0:T(8,128)(2,1)S(1)}, u32[]{:S(2)}, u32[]{:S(2)}) collective-permute-start(bf16[64,1536]{1,0:T(8,128)(2,1)S(1)} %plus.3.after.a), channel_id=1, source_target_pairs={{0,8},{4,12},{8,0},{12,4},{16,24},{20,28},{24,16},{28,20},{1,9},{5... | collective-permute-start | bytes 589832 | tf_op jit(solution)/shard_map/ppermute | solution.py:376
  22.2 17.6 %collective-permute-start.2 = (bf16[480,512]{1,0:T(8,128)(2,1)S(1)}, bf16[480,512]{1,0:T(8,128)(2,1)S(1)}, u32[]{:S(2)}, u32[]{:S(2)}) collective-permute-start(bf16[480,512]{1,0:T(8,128)(2,1)S(1)} %get-tuple-element.33), channel_id=1, source_target_pairs={{0,2},{1,3},{2,0},{3,1},{4,6},{5,7},{6,4},{7,5},{8,10},{9,11},{10,... | collective-permute-start | bytes 1474568 | tf_op jit(solution)/shard_map/ppermute | solution.py:571
  22.8 18.3 %collective-permute-start.1 = (bf16[480,512]{1,0:T(8,128)(2,1)S(1)}, bf16[480,512]{1,0:T(8,128)(2,1)S(1)}, u32[]{:S(2)}, u32[]{:S(2)}) collective-permute-start(bf16[480,512]{1,0:T(8,128)(2,1)S(1)} %get-tuple-element.31.rest_0_), channel_id=1, source_target_pairs={{0,1},{1,0},{2,3},{3,2},{4,5},{5,4},{6,7},{7,6},{8,9},{9,8},{10,11... | collective-permute-start | bytes 1474568 | tf_op jit(solution)/shard_map/ppermute | solution.py:571
  23.9 13.8 %copy-start = (f32[2,64,1280]{2,1,0:T(8,128)S(1)}, f32[2,64,1280]{2,1,0:T(8,128)}, u32[]{:S(2)}) copy-start(f32[2,64,1280]{2,1,0:T(8,128)} %refs_2_.3) | copy-start | bytes 1966084
  23.9 13.8 %copy-start.5 = (f32[2,64,256]{2,1,0:T(8,128)S(1)}, f32[2,64,256]{2,1,0:T(8,128)}, u32[]{:S(2)}) copy-start(f32[2,64,256]{2,1,0:T(8,128)} %refs_3_.1) | copy-start | bytes 393220
  23.9 11.3 %collective-permute-start.4 = (bf16[64,1536]{1,0:T(8,128)(2,1)S(1)}, bf16[64,1536]{1,0:T(8,128)(2,1)S(1)}, u32[]{:S(2)}, u32[]{:S(2)}) collective-permute-start(bf16[64,1536]{1,0:T(8,128)(2,1)S(1)} %plus.4.rest_0_.a), channel_id=1, source_target_pairs={{0,16},{4,20},{8,24},{12,28},{16,0},{20,4},{24,8},{28,12},{1,17},{... | collective-permute-start | bytes 589832 | tf_op jit(solution)/shard_map/ppermute | solution.py:376
  35.2 16.8 %copy-start.8 = (bf16[60,16,1024]{2,1,0:T(8,128)(2,1)S(1)}, bf16[60,16,1024]{2,1,0:T(8,128)(2,1)}, u32[]{:S(2)}) copy-start(bf16[60,16,1024]{2,1,0:T(8,128)(2,1)} %refs_2_.5) | copy-start | bytes 5898244
  35.3 2.4 %collective-permute-start.7 = (bf16[64,1536]{1,0:T(8,128)(2,1)S(1)}, bf16[64,1536]{1,0:T(8,128)(2,1)S(1)}, u32[]{:S(2)}, u32[]{:S(2)}) collective-permute-start(bf16[64,1536]{1,0:T(8,128)(2,1)S(1)} %plus.5.refs_0_), channel_id=1, source_target_pairs={{0,4},{4,0},{8,12},{12,8},{16,20},{20,16},{24,28},{28,24},{1,5},{5... | collective-permute-start | bytes 589832 | tf_op jit(solution)/shard_map/ppermute | solution.py:354
  35.4 16.7 %collective-permute-start.14 = (bf16[240,512]{1,0:T(8,128)(2,1)S(1)}, bf16[240,512]{1,0:T(8,128)(2,1)S(1)}, u32[]{:S(2)}, u32[]{:S(2)}) collective-permute-start(bf16[240,512]{1,0:T(8,128)(2,1)S(1)} %get-tuple-element.47), channel_id=1, source_target_pairs={{0,1},{1,0},{2,3},{3,2},{4,5},{5,4},{6,7},{7,6},{8,9},{9,8},{10,11... | collective-permute-start | bytes 737288 | tf_op jit(solution)/shard_map/ppermute | solution.py:571
  36.2 15.9 %collective-permute-start.13 = (bf16[240,512]{1,0:T(8,128)(2,1)S(1)}, bf16[240,512]{1,0:T(8,128)(2,1)S(1)}, u32[]{:S(2)}, u32[]{:S(2)}) collective-permute-start(bf16[240,512]{1,0:T(8,128)(2,1)S(1)} %get-tuple-element.38.rest_0_), channel_id=1, source_target_pairs={{0,2},{1,3},{2,0},{3,1},{4,6},{5,7},{6,4},{7,5},{8,10},{9,11},{10,... | collective-permute-start | bytes 737288 | tf_op jit(solution)/shard_map/ppermute | solution.py:571
  37.7 14.4 %copy-start.7 = (bf16[60,16,1024]{2,1,0:T(8,128)(2,1)S(1)}, bf16[60,16,1024]{2,1,0:T(8,128)(2,1)}, u32[]{:S(2)}) copy-start(bf16[60,16,1024]{2,1,0:T(8,128)(2,1)} %refs_1_.3) | copy-start | bytes 5898244
  37.7 14.4 %copy-start.11 = (bf16[240,512]{1,0:T(8,128)(2,1)S(1)}, bf16[240,512]{1,0:T(8,128)(2,1)}, u32[]{:S(2)}) copy-start(bf16[240,512]{1,0:T(8,128)(2,1)} %copy-done.10) | copy-start | bytes 737284
  39.2 12.8 %copy-start.6 = (bf16[60,4,4096]{2,1,0:T(4,128)(2,1)S(1)}, bf16[60,4,4096]{2,1,0:T(4,128)(2,1)}, u32[]{:S(2)}) copy-start(bf16[60,4,4096]{2,1,0:T(4,128)(2,1)} %refs_0_.3) | copy-start | bytes 5898244
  39.3 12.8 %copy-start.9 = (s32[60]{0:T(128)S(1)}, s32[60]{0:T(128)}, u32[]{:S(2)}) copy-start(s32[60]{0:T(128)} %lengths.3) | copy-start | bytes 724
  39.3 7.7 %collective-permute-start.8 = (bf16[256,256]{1,0:T(8,128)(2,1)S(1)}, bf16[256,256]{1,0:T(8,128)(2,1)S(1)}, u32[]{:S(2)}, u32[]{:S(2)}) collective-permute-start(bf16[256,256]{1,0:T(8,128)(2,1)S(1)} %get-tuple-element.39), channel_id=1, source_target_pairs={{0,1},{1,0},{2,3},{3,2},{4,5},{5,4},{6,7},{7,6},{8,9},{9,8},{10,11... | collective-permute-start | bytes 393224 | tf_op jit(solution)/shard_map/ppermute | solution.py:571
  39.9 9.9 %collective-permute-start.9 = (bf16[256,256]{1,0:T(8,128)(2,1)S(1)}, bf16[256,256]{1,0:T(8,128)(2,1)S(1)}, u32[]{:S(2)}, u32[]{:S(2)}) collective-permute-start(bf16[256,256]{1,0:T(8,128)(2,1)S(1)} %get-tuple-element.40), channel_id=1, source_target_pairs={{0,2},{1,3},{2,0},{3,1},{4,6},{5,7},{6,4},{7,5},{8,10},{9,11},{10,... | collective-permute-start | bytes 393224 | tf_op jit(solution)/shard_map/ppermute | solution.py:571
  41.1 8.7 %collective-permute-start.10 = (bf16[256,256]{1,0:T(8,128)(2,1)S(1)}, bf16[256,256]{1,0:T(8,128)(2,1)S(1)}, u32[]{:S(2)}, u32[]{:S(2)}) collective-permute-start(bf16[256,256]{1,0:T(8,128)(2,1)S(1)} %get-tuple-element.41), channel_id=1, source_target_pairs={{0,3},{1,2},{2,1},{3,0},{4,7},{5,6},{6,5},{7,4},{8,11},{9,10},{10,... | collective-permute-start | bytes 393224 | tf_op jit(solution)/shard_map/ppermute | solution.py:571
  49.9 7.4 %collective-permute-start.11 = (bf16[240,512]{1,0:T(8,128)(2,1)S(1)}, bf16[240,512]{1,0:T(8,128)(2,1)S(1)}, u32[]{:S(2)}, u32[]{:S(2)}) collective-permute-start(bf16[240,512]{1,0:T(8,128)(2,1)S(1)} %get-tuple-element.42), channel_id=1, source_target_pairs={{0,2},{1,3},{2,0},{3,1},{4,6},{5,7},{6,4},{7,5},{8,10},{9,11},{10,... | collective-permute-start | bytes 737288 | tf_op jit(solution)/shard_map/ppermute | solution.py:571
  51.5 6.8 %collective-permute-start.12 = (bf16[240,512]{1,0:T(8,128)(2,1)S(1)}, bf16[240,512]{1,0:T(8,128)(2,1)S(1)}, u32[]{:S(2)}, u32[]{:S(2)}) collective-permute-start(bf16[240,512]{1,0:T(8,128)(2,1)S(1)} %get-tuple-element.44), channel_id=1, source_target_pairs={{0,1},{1,0},{2,3},{3,2},{4,5},{5,4},{6,7},{7,6},{8,9},{9,8},{10,11... | collective-permute-start | bytes 737288 | tf_op jit(solution)/shard_map/ppermute | solution.py:571
  (5 other events, 12.2 us)

commit v8 on v7

--- a/solution.py
+++ b/solution.py
@@ -143,18 +143,27 @@
 TILE = 256
 
 
-def multiply_terms(x, w, outs, ready):
-    ksend, kkeep, vsend, vkeep0, vkeep1 = outs
+def multiply_terms(x, weight, base, w, sems, keys, values):
     tokens = x.shape[0] // 4
     steps = x.shape[1] // TILE
-    low, high = slice(0, tokens), slice(tokens, 2 * tokens)
+    units = (keys, values)
+
+    def copy(p, i):
+        at = pl.ds(base + i * TILE, TILE)
+        return pltpu.make_async_copy(weight.at[p, :, at], w.at[p, i], sems.at[p, i])
+
+    def start():
+        for i in range(w.shape[1]):
+            for p in range(2):
+                copy(p, i).start()
 
     def multiply(*accs):
-        accs_k, accs_v = accs[:4], accs[4:]
+        accs = (accs[: len(keys)], accs[len(keys) :])
 
         @pl.loop(0, w.shape[1])
         def _(i):
-            ready(i)
+            for p in range(2):
+                copy(p, i).wait()
 
             def push(k):
                 for p in range(2):
@@ -164,140 +173,142 @@
             for k in range(steps):
                 if k + 1 < steps:
                     push(k + 1)
-                for r in range(4):
-                    rows = x[r * tokens : (r + 1) * tokens, k * TILE : (k + 1) * TILE]
-                    staged = k % 2 if r == 0 else None
-                    pltpu.matmul_acc_lhs(accs_k[r], rows, load_staged_rhs=staged)
-                    pltpu.matmul_acc_lhs(accs_v[r], rows, load_staged_rhs=staged)
+                for n in range(len(keys)):
+                    for p in range(2):
+                        r = units[p][n][0]
+                        rows = x[r * tokens : (r + 1) * tokens, k * TILE : (k + 1) * TILE]
+                        staged = k % 2 if n == 0 else None
+                        pltpu.matmul_acc_lhs(accs[p][n], rows, load_staged_rhs=staged)
             at = pl.ds(pl.multiple_of(i * TILE, TILE), TILE)
-            kkeep[low, at] = pltpu.matmul_pop(accs_k[0]).astype(BF)
-            vkeep0[:, at] = pltpu.matmul_pop(accs_v[0]).astype(BF)
-            ksend[high, at] = pltpu.matmul_pop(accs_k[1]).astype(BF)
-            vkeep1[:, at] = pltpu.matmul_pop(accs_v[1]).astype(BF)
-            kkeep[high, at] = pltpu.matmul_pop(accs_k[2]).astype(BF)
-            vsend[low, at] = pltpu.matmul_pop(accs_v[2]).astype(BF)
-            ksend[low, at] = pltpu.matmul_pop(accs_k[3]).astype(BF)
-            vsend[high, at] = pltpu.matmul_pop(accs_v[3]).astype(BF)
-
-    pl.run_scoped(
-        multiply, *[pltpu.ACC(unit)((tokens, TILE), F32) for unit in range(2) for _ in range(4)]
-    )
-
-
-def first_kernel(ids, hidden, weight, grad_a, grad_b, *rest):
-    x, *outs = rest[:6]
-    send, own, _ = rest[6:9]
-    held, w, held_a, held_b, hidden_sems, sems, grad_sems = rest[9:]
+            for n in range(len(keys)):
+                for p in range(2):
+                    _, out, row = units[p][n]
+                    out[row : row + tokens, at] = pltpu.matmul_pop(accs[p][n]).astype(BF)
+
+    def run():
+        pl.run_scoped(
+            multiply,
+            *[pltpu.ACC(p)((tokens, TILE), F32) for p in range(2) for _ in units[p]],
+        )
+
+    return start, run
+
+
+def send_parts(tokens, ksend, vsend):
+    return [(3, ksend, 0), (1, ksend, tokens)], [(2, vsend, 0), (3, vsend, tokens)]
+
+
+def keep_parts(tokens, kkeep, vkeep0, vkeep1):
+    return [(0, kkeep, 0), (2, kkeep, tokens)], [(0, vkeep0, 0), (1, vkeep1, 0)]
+
+
+def first_kernel(ids, hidden, weight, x, ksend, vsend, held, w, hidden_sems, sems):
     tokens = x.shape[0] // 4
     rows = tokens // STEPS
+    start, run = multiply_terms(x, weight, 0, w, sems, *send_parts(tokens, ksend, vsend))
 
     def hidden_copy(r):
         at = pl.ds((ids[0] ^ r) * rows, rows)
         return pltpu.make_async_copy(hidden.at[at], held.at[r], hidden_sems.at[r])
 
-    def weight_copy(p, i):
-        at = pl.ds(i * TILE, TILE)
-        return pltpu.make_async_copy(weight.at[p, :, at], w.at[p, i], sems.at[p, i])
-
-    others = [
-        pltpu.make_async_copy(grad_a.at[0], held_a, grad_sems.at[0]),
-        pltpu.make_async_copy(grad_b.at[0], held_b, grad_sems.at[1]),
-    ]
-    for r in range(4):
+    for r in (3, 1, 2, 0):
         hidden_copy(r).start()
-    for i in range(w.shape[1]):
-        for p in range(2):
-            weight_copy(p, i).start()
-    for r in range(4):
+    start()
+    for r in (3, 1, 2, 0):
         hidden_copy(r).wait()
         x[r * tokens : (r + 1) * tokens] = held[r].reshape(tokens, x.shape[1])
-    for copy in others:
-        copy.start()
-
-    def ready(i):
-        for p in range(2):
-            weight_copy(p, i).wait()
-
-    multiply_terms(x, w, outs, ready)
-    for copy in others:
-        copy.wait()
-    wide = grad_a.shape[-1]
-    for out, p in ((send, ids[2] ^ 1), (own, ids[2])):
-        out[:, :wide] = held_a[p].astype(BF)
-        out[:, wide:] = held_b[p].astype(BF)
+    run()
+
+
+def keep_kernel(x, weight, after, kkeep, vkeep0, vkeep1, _, w, sems):
+    del after
+    tokens = x.shape[0] // 4
+    start, run = multiply_terms(x, weight, 0, w, sems, *keep_parts(tokens, kkeep, vkeep0, vkeep1))
+    start()
+    run()
 
 
 def later_kernel(x, weight, after, *rest):
     del after
-    *outs, w, sems = rest
+    ksend, vsend, kkeep, vkeep0, vkeep1, w, sems = rest
+    tokens = x.shape[0] // 4
+    sends = send_parts(tokens, ksend, vsend)
+    keeps = keep_parts(tokens, kkeep, vkeep0, vkeep1)
     base = weight.shape[2] - w.shape[1] * TILE
-
-    def weight_copy(p, i):
-        at = pl.ds(base + i * TILE, TILE)
-        return pltpu.make_async_copy(weight.at[p, :, at], w.at[p, i], sems.at[p, i])
-
-    for i in range(w.shape[1]):
-        for p in range(2):
-            weight_copy(p, i).start()
-
-    def ready(i):
-        for p in range(2):
-            weight_copy(p, i).wait()
-
-    multiply_terms(x, w, outs, ready)
-
-
-def term_shapes(tokens, count):
-    return [jax.ShapeDtypeStruct((n * tokens, count * HD), BF) for n in (2, 2, 2, 1, 1)]
-
-
-def first_terms(ids, hidden, kv_weight, grad_a, grad_b, queries, tokens):
+    parts = [a + b for a, b in zip(sends, keeps)]
+    start, run = multiply_terms(x, weight, base, w, sems, *parts)
+    start()
+    run()
+
+
+SEND, KEEP = (2, 2), (2, 1, 1)
+
+
+def term_shapes(rows, tokens, count):
+    return [jax.ShapeDtypeStruct((n * tokens, count * HD), BF) for n in rows]
+
+
+def weight_scratch(width, count):
+    tiles = count * HD // TILE
+    return [pltpu.VMEM((2, tiles, width, TILE), BF), pltpu.SemaphoreType.DMA((2, tiles))]
+
+
+def first_terms(ids, hidden, kv_weight, tokens):
     width = hidden.shape[2]
-    rank, wide = grad_a.shape[2], grad_a.shape[3] + grad_b.shape[3]
     here = pl.BlockSpec(memory_space=pl.ANY)
-    outs = [jax.ShapeDtypeStruct((4 * tokens, width), BF), *term_shapes(tokens, CHUNKS[0])]
-    outs += [jax.ShapeDtypeStruct((rank, wide), BF)] * 2
-    tiles = CHUNKS[0] * HD // TILE
-    specs = [whole(x.shape) for x in outs] + [here]
-    outs.append(jax.ShapeDtypeStruct(queries.shape, BF))
+    outs = [jax.ShapeDtypeStruct((4 * tokens, width), BF)]
+    outs += [pltpu.VMEM(x.shape, BF) for x in term_shapes(SEND, tokens, CHUNKS[0])]
+    w, sems = weight_scratch(width, CHUNKS[0])
     return pl.pallas_call(
         first_kernel,
         out_shape=outs,
         grid_spec=pltpu.PrefetchScalarGridSpec(
             num_scalar_prefetch=1,
             grid=(1,),
-            in_specs=[here] * 4,
-            out_specs=specs,
+            in_specs=[here] * 2,
+            out_specs=[whole(x.shape) for x in outs],
             scratch_shapes=[
                 pltpu.VMEM((4, tokens // STEPS, STEPS, width), BF),
-                pltpu.VMEM((2, tiles, width, TILE), BF),
-                pltpu.VMEM(grad_a.shape[1:], F32),
-                pltpu.VMEM(grad_b.shape[1:], F32),
+                w,
                 pltpu.SemaphoreType.DMA((4,)),
-                pltpu.SemaphoreType.DMA((2, tiles)),
-                pltpu.SemaphoreType.DMA((2,)),
+                sems,
             ],
         ),
         compiler_params=params(16),
-        cost_estimate=cost(16 * tokens * width * CHUNKS[0] * HD, hidden),
+        cost_estimate=cost(8 * tokens * width * CHUNKS[0] * HD, hidden),
         name="first_terms",
-    )(ids, *map(hbm, (hidden, kv_weight, grad_a, grad_b)))
+    )(ids, *map(hbm, (hidden, kv_weight)))
+
+
+def keep_terms(x, kv_weight, queries, after):
+    tokens, width = x.shape[0] // 4, x.shape[1]
+    here = pl.BlockSpec(memory_space=pl.ANY)
+    outs = [pltpu.HBM(out.shape, BF) for out in term_shapes(KEEP, tokens, CHUNKS[0])]
+    specs = [whole(out.shape) for out in outs] + [here]
+    outs.append(jax.ShapeDtypeStruct(queries.shape, BF))
+    return pl.pallas_call(
+        keep_kernel,
+        out_shape=outs,
+        grid=(1,),
+        in_specs=[whole(x.shape), here, here],
+        out_specs=specs,
+        scratch_shapes=weight_scratch(width, CHUNKS[0]),
+        compiler_params=params(14),
+        cost_estimate=cost(8 * tokens * width * CHUNKS[0] * HD, x),
+        name="keep_terms",
+    )(x, hbm(kv_weight), after)
 
 
 def later_terms(x, kv_weight, after):
-    outs = term_shapes(x.shape[0] // 4, CHUNKS[1])
+    outs = term_shapes(SEND + KEEP, x.shape[0] // 4, CHUNKS[1])
     here = pl.BlockSpec(memory_space=pl.ANY)
-    tiles = CHUNKS[1] * HD // TILE
     return pl.pallas_call(
         later_kernel,
         out_shape=outs,
         grid=(1,),
         in_specs=[whole(x.shape), here, here],
         out_specs=[whole(out.shape) for out in outs],
-        scratch_shapes=[
-            pltpu.VMEM((2, tiles, x.shape[1], TILE), BF),
-            pltpu.SemaphoreType.DMA((2, tiles)),
-        ],
+        scratch_shapes=weight_scratch(x.shape[1], CHUNKS[1]),
         compiler_params=params(12),
         cost_estimate=cost(4 * math.prod(x.shape) * CHUNKS[1] * HD, x, *outs),
         name="later_terms",
@@ -324,6 +335,42 @@
         cost_estimate=cost(0, *[vkeep] * 6),
         name="mid_sums",
     )(kkeep, kcame, vkeep, vcame, *after)
+
+
+def pack_kernel(ids, grad_a, grad_b, after, out):
+    del ids, after
+    wide = grad_a.shape[-1]
+    out[:, :wide] = grad_a[0, 0].astype(BF)
+    out[:, wide:] = grad_b[0, 0].astype(BF)
+
+
+def chip_kernel(ids, grad_a, grad_b, other, out):
+    del ids
+    wide = grad_a.shape[-1]
+    out[:, :wide] = (grad_a[0, 0] + other[:, :wide].astype(F32)).astype(BF)
+    out[:, wide:] = (grad_b[0, 0] + other[:, wide:].astype(F32)).astype(BF)
+
+
+def grad_half(kernel, name, ids, grad_a, grad_b, flip, more, spec):
+    rank, wide = grad_a.shape[2], grad_a.shape[3] + grad_b.shape[3]
+
+    def half(x):
+        return pl.BlockSpec((1, 1) + x.shape[2:], lambda i, ids: (0, ids[2] ^ flip, 0, 0))
+
+    out = jax.ShapeDtypeStruct((rank, wide), BF)
+    return pl.pallas_call(
+        kernel,
+        out_shape=out,
+        grid_spec=pltpu.PrefetchScalarGridSpec(
+            num_scalar_prefetch=1,
+            grid=(1,),
+            in_specs=[half(grad_a), half(grad_b), spec],
+            out_specs=whole(out.shape),
+        ),
+        compiler_params=params(4),
+        cost_estimate=cost(0, *[out] * 4),
+        name=name,
+    )(ids, hbm(grad_a), hbm(grad_b), more)
 
 
 def small_call(kernel, name, ids, args, outs, after=(), scratch=(), copied=0):
@@ -591,13 +638,16 @@
     ids = jnp.stack([lax.axis_index("tensor"), dp // 2, dp % 2]).astype(jnp.int32)
     tables = rotary_tables(key_gain, positions)
 
-    x, *first, packed, own, attended = first_terms(
-        ids, hidden_in, kv_weight, grad_a, grad_b, queries, tokens
-    )
-    half = plus(own, core_flip(packed, count_dp))
+    x, *first = first_terms(ids, hidden_in, kv_weight, tokens)
+    here = pl.BlockSpec(memory_space=pl.ANY)
+    packed = grad_half(pack_kernel, "pack_grads", ids, grad_a, grad_b, 1, first[0], here)
+    other = core_flip(packed, count_dp)
+    half = grad_half(
+        chip_kernel, "chip_grads", ids, grad_a, grad_b, 0, other, whole(other.shape)
+    )
 
     def first_exchange(term, *after):
-        ksend, kkeep, vsend, vkeep0, vkeep1 = term
+        ksend, vsend, kkeep, vkeep0, vkeep1 = term
         kcame, vcame = across(ksend, 1), across(vsend, 2)
         mids = mid_sums(kkeep, kcame, vkeep1, vcame, *after)
         return mids, (kkeep, kcame, vkeep0, vcame)
@@ -612,9 +662,13 @@
         half = plus(half, along_line(half, step, count_dp), *after)
         step *= 2
         if step == 2:
+            *keeps, attended = keep_terms(x, kv_weight, queries, half)
+            first += keeps
             mids, parts = first_exchange(first, half)
             after = (mids[0], tables[0])
     if step == 1:
+        *keeps, attended = keep_terms(x, kv_weight, queries, half)
+        first += keeps
         mids, parts = first_exchange(first, half)
     first = second_exchange(mids, parts)
     other = core_flip(half, count_dp)

time: 63.2 us -> 62.1 us (0.983)
  waiting for transfers between devices: 14.9 us -> 10.9 us
  Pallas kernels: 24.8 us -> 28.6 us
  local copies, waits for them, and re-layouts: 3.16 us -> 2.19 us
    pallas_call x0 -> x3, Pallas kernels: none -> 7.78 us  [the longest x1 3.92 us: keep_terms(): pl.pallas_call(keep_kernel, out_shape=outs, grid=(1,), in_specs=[whole(x....]
    ppermute x2, waiting for transfers between devices: 7.01 us -> 1.99 us  [along_line(): return lax.ppermute(x, 'dp', [(i, i ^ 2 * d) for i in range(count)])]
    pallas_call x1, Pallas kernels: 6.87 us -> 5.48 us  [first_terms(): pl.pallas_call(first_kernel, out_shape=outs, grid_spec=pltpu.PrefetchScal...]
    ppermute x11, waiting for transfers between devices: 7.91 us -> 8.95 us  [across(): return lax.ppermute(x, 'tensor', [(i, i ^ r) for i in range(4)])]
    unnamed x28 -> x24, local copies, waits for them, and re-layouts: 3.05 us -> 2.08 us
    pallas_call x3 -> x2, Pallas kernels: 1.07 us -> 0.1 us  [plus(): pl.pallas_call(plus_kernel, out_shape=out, grid=(1,), in_specs=[whole(a.s...]
    pallas_call x2, Pallas kernels: 1.18 us -> 0.23 us  [mid_sums(): pl.pallas_call(mid_kernel, out_shape=[jax.ShapeDtypeStruct(shape, BF)] *...]
  transfers between devices with their start and end apart: 15 -> 15, of which waited for: 4 -> 5; matrix products, arithmetic and copies ran while one was open for 1% -> 1% of each run, Pallas kernels for 21% -> 30%
where the time goes in v8:
time: 62.1 us; the launch traced here: 61.9 us
  Pallas kernels  28.6 us (46%)
  starting transfers between devices  18.4 us (30%)
  waiting for transfers between devices  10.9 us (18%)
  local copies, waits for them, and re-layouts  2.19 us (4%)
  between operations  0.86 us (1%)
  other arithmetic  0.82 us (1%)
    ppermute x11, starting transfers between devices, across(): return lax.ppermute(x, 'tensor', [(i, i ^ r) for i in range(4)])  14.1 us
    pallas_call x2, Pallas kernels, attend_chunk(): pl.pallas_call(attend_kernel, out_shape=jax.ShapeDtypeStruct(queries.shap...  9.3 us
    ppermute x11, waiting for transfers between devices, across(): return lax.ppermute(x, 'tensor', [(i, i ^ r) for i in range(4)])  8.95 us
    pallas_call x1, Pallas kernels, first_terms(): pl.pallas_call(first_kernel, out_shape=outs, grid_spec=pltpu.PrefetchScal...  5.48 us
    ppermute x2, starting transfers between devices, along_line(): return lax.ppermute(x, 'dp', [(i, i ^ 2 * d) for i in range(count)])  4.29 us
    pallas_call x1, Pallas kernels, later_terms(): pl.pallas_call(later_kernel, out_shape=outs, grid=(1,), in_specs=[whole(x...  4.2 us
    pallas_call x1, Pallas kernels, keep_terms(): pl.pallas_call(keep_kernel, out_shape=outs, grid=(1,), in_specs=[whole(x....  3.92 us
    pallas_call x2, Pallas kernels, grad_half(): pl.pallas_call(kernel, out_shape=out, grid_spec=pltpu.PrefetchScalarGridS...  3.86 us
  transfers between devices with their start and end apart: 15, of which 5 were waited for; matrix products, arithmetic and copies ran while one was open for 1% of the time, Pallas kernels for 30%

profile of v8, /device:TPU:0, one launch (start us, length us, event | category | flops | bytes accessed | tf_op | source)
XLA Modules:
  0.0 61.9 jit_solution(13038978727784452704)
XLA Ops:
  0.7 5.5 %first_terms.1 = (bf16[960,1280]{1,0:T(8,128)(2,1)S(1)}, bf16[480,512]{1,0:T(8,128)(2,1)}, bf16[480,512]{1,0:T(8,128)(2,1)}) custom-call(s32[3]{0:T(128)S(1)} %pad_add_fusion.ids, bf16[240,4,1280]{2,1,0:T(4,128)(2,1)} %hidden.1, bf16[2,1280,1024]{2,1,0:T(8,128)(2,1)} %weight.5), custom_call_target="tpu_custom_call" | custom-call | flops 1258291200 | bytes 2457600 | tf_op jit(solution)/shard_map/first_terms/pallas_call | solution.py:262
  6.2 3.0 %collective-permute-start.5 = (bf16[480,512]{1,0:T(8,128)(2,1)}, bf16[480,512]{1,0:T(8,128)(2,1)S(1)}, u32[]{:S(2)}, u32[]{:S(2)}) collective-permute-start(bf16[480,512]{1,0:T(8,128)(2,1)} %get-tuple-element.26.after), channel_id=1, source_target_pairs={{0,1},{1,0},{2,3},{3,2},{4,5},{5,4},{6,7},{7,6},{8,9},{9,8},{10,11... | collective-permute-start | bytes 1474568 | tf_op jit(solution)/shard_map/ppermute | solution.py:618
  9.2 2.2 %pack_grads.1 = bf16[64,1536]{1,0:T(8,128)(2,1)} custom-call(s32[3]{0:T(128)S(1)} %pad_add_fusion.ids, f32[1,2,64,1280]{3,2,1,0:T(8,128)} %grad_a.3, f32[1,2,64,256]{3,2,1,0:T(8,128)} %grad_b.3, bf16[480,512]{1,0:T(8,128)(2,1)} %get-tuple-element.26.after), custom_call_target="tpu_custom_call" | custom-call | bytes 786432 | tf_op jit(solution)/shard_map/pack_grads/pallas_call | solution.py:361
  11.4 1.5 %collective-permute-start.6 = (bf16[480,512]{1,0:T(8,128)(2,1)}, bf16[480,512]{1,0:T(8,128)(2,1)S(1)}, u32[]{:S(2)}, u32[]{:S(2)}) collective-permute-start(bf16[480,512]{1,0:T(8,128)(2,1)} %get-tuple-element.33), channel_id=1, source_target_pairs={{0,2},{1,3},{2,0},{3,1},{4,6},{5,7},{6,4},{7,5},{8,10},{9,11},{10,... | collective-permute-start | bytes 1474568 | tf_op jit(solution)/shard_map/ppermute | solution.py:618
  13.3 1.6 %chip_grads.1.after.a = bf16[64,1536]{1,0:T(8,128)(2,1)S(1)} custom-call(s32[3]{0:T(128)S(1)} %pad_add_fusion.ids, f32[1,2,64,1280]{3,2,1,0:T(8,128)} %grad_a.3, f32[1,2,64,256]{3,2,1,0:T(8,128)} %grad_b.3, bf16[64,1536]{1,0:T(8,128)(2,1)} %collective-permute-done.other), custom_call_target="tpu_custom_call" | custom-call | bytes 786432 | tf_op jit(solution)/shard_map/chip_grads/pallas_call | solution.py:361
  15.0 1.6 %collective-permute-start.3 = (bf16[64,1536]{1,0:T(8,128)(2,1)S(1)}, bf16[64,1536]{1,0:T(8,128)(2,1)S(1)}, u32[]{:S(2)}, u32[]{:S(2)}) collective-permute-start(bf16[64,1536]{1,0:T(8,128)(2,1)S(1)} %chip_grads.1.after.a), channel_id=1, source_target_pairs={{0,8},{4,12},{8,0},{12,4},{16,24},{20,28},{24,16},{28,20},{1,9},{5... | collective-permute-start | bytes 589832 | tf_op jit(solution)/shard_map/ppermute | solution.py:423
  16.6 4.2 %later_terms.1 = (bf16[480,512]{1,0:T(8,128)(2,1)S(1)}, bf16[480,512]{1,0:T(8,128)(2,1)S(1)}, bf16[480,512]{1,0:T(8,128)(2,1)S(1)}, bf16[240,512]{1,0:T(8,128)(2,1)S(1)}, bf16[240,512]{1,0:T(8,128)(2,1)S(1)}) custom-call(bf16[960,1280]{1,0:T(8,128)(2,1)S(1)} %get-tuple-element.25.x.refs_4_, bf16[2,1280,1024]{2,1,0:T(8,128)(2,1)} %weight.5, ...), custom_call_target="tpu_custom_call" | custom-call | flops 2516582400 | bytes 4423680 | tf_op jit(solution)/shard_map/later_terms/pallas_call | solution.py:305
  20.8 1.5 %collective-permute-start.2 = (bf16[480,512]{1,0:T(8,128)(2,1)S(1)}, bf16[480,512]{1,0:T(8,128)(2,1)S(1)}, u32[]{:S(2)}, u32[]{:S(2)}) collective-permute-start(bf16[480,512]{1,0:T(8,128)(2,1)S(1)} %get-tuple-element.30), channel_id=1, source_target_pairs={{0,2},{1,3},{2,0},{3,1},{4,6},{5,7},{6,4},{7,5},{8,10},{9,11},{10,... | collective-permute-start | bytes 1474568 | tf_op jit(solution)/shard_map/ppermute | solution.py:618
  22.9 2.7 %collective-permute-start.4 = (bf16[64,1536]{1,0:T(8,128)(2,1)S(1)}, bf16[64,1536]{1,0:T(8,128)(2,1)S(1)}, u32[]{:S(2)}, u32[]{:S(2)}) collective-permute-start(bf16[64,1536]{1,0:T(8,128)(2,1)S(1)} %plus.2.after.rest_0_.a), channel_id=1, source_target_pairs={{0,16},{4,20},{8,24},{12,28},{16,0},{20,4},{24,8},{28,12},{1,17},{... | collective-permute-start | bytes 589832 | tf_op jit(solution)/shard_map/ppermute | solution.py:423
  26.1 3.9 %keep_terms.1 = (bf16[480,512]{1,0:T(8,128)(2,1)}, bf16[240,512]{1,0:T(8,128)(2,1)}, bf16[240,512]{1,0:T(8,128)(2,1)}, bf16[60,4,4096]{2,1,0:T(4,128)(2,1)}) custom-call(bf16[960,1280]{1,0:T(8,128)(2,1)S(1)} %get-tuple-element.25.x.refs_4_, bf16[2,1280,1024]{2,1,0:T(8,128)(2,1)} %weight.5, bf16[64,1536]{1,0:T(8,128)(2,1)S(1)} %plus.2.after.rest_0_.a), custom_call_target="tpu_custom_call" | custom-call | flops 1258291200 | bytes 2457600 | tf_op jit(solution)/shard_map/keep_terms/pallas_call | solution.py:289
  30.0 1.1 %copy-done.1 = bf16[480,512]{1,0:T(8,128)(2,1)S(1)} copy-done((bf16[480,512]{1,0:T(8,128)(2,1)S(1)}, bf16[480,512]{1,0:T(8,128)(2,1)}, u32[]{:S(2)}) %copy-start.1) | copy-done | bytes 491544
  31.1 0.9 %copy-done.3 = bf16[240,512]{1,0:T(8,128)(2,1)S(1)} copy-done((bf16[240,512]{1,0:T(8,128)(2,1)S(1)}, bf16[240,512]{1,0:T(8,128)(2,1)}, u32[]{:S(2)}) %copy-start.3) | copy-done | bytes 245784
  32.2 2.0 %collective-permute-done.4.b = bf16[64,1536]{1,0:T(8,128)(2,1)S(1)} collective-permute-done((bf16[64,1536]{1,0:T(8,128)(2,1)S(1)}, bf16[64,1536]{1,0:T(8,128)(2,1)S(1)}, u32[]{:S(2)}, u32[]{:S(2)}) %collective-permute-start.4) | collective-permute-done | bytes 196640 | tf_op jit(solution)/shard_map/ppermute | solution.py:423
  34.3 1.4 %collective-permute-start.14 = (bf16[240,512]{1,0:T(8,128)(2,1)S(1)}, bf16[240,512]{1,0:T(8,128)(2,1)S(1)}, u32[]{:S(2)}, u32[]{:S(2)}) collective-permute-start(bf16[240,512]{1,0:T(8,128)(2,1)S(1)} %get-tuple-element.43), channel_id=1, source_target_pairs={{0,1},{1,0},{2,3},{3,2},{4,5},{5,4},{6,7},{7,6},{8,9},{9,8},{10,11... | collective-permute-start | bytes 737288 | tf_op jit(solution)/shard_map/ppermute | solution.py:618
  35.8 0.7 %collective-permute-start.13 = (bf16[240,512]{1,0:T(8,128)(2,1)S(1)}, bf16[240,512]{1,0:T(8,128)(2,1)S(1)}, u32[]{:S(2)}, u32[]{:S(2)}) collective-permute-start(bf16[240,512]{1,0:T(8,128)(2,1)S(1)} %get-tuple-element.34.rest_0_), channel_id=1, source_target_pairs={{0,2},{1,3},{2,0},{3,1},{4,6},{5,7},{6,4},{7,5},{8,10},{9,11},{10,... | collective-permute-start | bytes 737288 | tf_op jit(solution)/shard_map/ppermute | solution.py:618
  36.5 1.5 %update_factors.1 = (f32[2,64,1280]{2,1,0:T(8,128)}, f32[2,64,256]{2,1,0:T(8,128)}, bf16[256,256]{1,0:T(8,128)(2,1)S(1)}, bf16[256,256]{1,0:T(8,128)(2,1)S(1)}, ...) custom-call(s32[3]{0:T(128)S(1)} %pad_add_fusion.ids, bf16[64,1536]{1,0:T(8,128)(2,1)S(1)} %plus.3.refs_0_, ...), custom_call_target="tpu_custom_call" | custom-call | bytes 3637248 | tf_op jit(solution)/shard_map/update_factors/pallas_call | solution.py:382
  38.8 1.3 %collective-permute-start.9 = (bf16[256,256]{1,0:T(8,128)(2,1)S(1)}, bf16[256,256]{1,0:T(8,128)(2,1)S(1)}, u32[]{:S(2)}, u32[]{:S(2)}) collective-permute-start(bf16[256,256]{1,0:T(8,128)(2,1)S(1)} %get-tuple-element.36), channel_id=1, source_target_pairs={{0,2},{1,3},{2,0},{3,1},{4,6},{5,7},{6,4},{7,5},{8,10},{9,11},{10,... | collective-permute-start | bytes 393224 | tf_op jit(solution)/shard_map/ppermute | solution.py:618
  40.1 1.5 %collective-permute-start.10 = (bf16[256,256]{1,0:T(8,128)(2,1)S(1)}, bf16[256,256]{1,0:T(8,128)(2,1)S(1)}, u32[]{:S(2)}, u32[]{:S(2)}) collective-permute-start(bf16[256,256]{1,0:T(8,128)(2,1)S(1)} %get-tuple-element.37), channel_id=1, source_target_pairs={{0,3},{1,2},{2,1},{3,0},{4,7},{5,6},{6,5},{7,4},{8,11},{9,10},{10,... | collective-permute-start | bytes 393224 | tf_op jit(solution)/shard_map/ppermute | solution.py:618
  41.7 4.3 %collective-permute-done.8.rest_0_.refs_10_ = bf16[256,256]{1,0:T(8,128)(2,1)S(1)} collective-permute-done((bf16[256,256]{1,0:T(8,128)(2,1)S(1)}, bf16[256,256]{1,0:T(8,128)(2,1)S(1)}, u32[]{:S(2)}, u32[]{:S(2)}) %collective-permute-start.8) | collective-permute-done | bytes 131104 | tf_op jit(solution)/shard_map/ppermute | solution.py:618
  45.9 3.5 %collective-permute-done.9.rest_1_.refs_11_ = bf16[256,256]{1,0:T(8,128)(2,1)S(1)} collective-permute-done((bf16[256,256]{1,0:T(8,128)(2,1)S(1)}, bf16[256,256]{1,0:T(8,128)(2,1)S(1)}, u32[]{:S(2)}, u32[]{:S(2)}) %collective-permute-start.9) | collective-permute-done | bytes 131104 | tf_op jit(solution)/shard_map/ppermute | solution.py:618
  49.5 0.8 %collective-permute-start.11 = (bf16[240,512]{1,0:T(8,128)(2,1)S(1)}, bf16[240,512]{1,0:T(8,128)(2,1)S(1)}, u32[]{:S(2)}, u32[]{:S(2)}) collective-permute-start(bf16[240,512]{1,0:T(8,128)(2,1)S(1)} %get-tuple-element.38), channel_id=1, source_target_pairs={{0,2},{1,3},{2,0},{3,1},{4,6},{5,7},{6,4},{7,5},{8,10},{9,11},{10,... | collective-permute-start | bytes 737288 | tf_op jit(solution)/shard_map/ppermute | solution.py:618
  50.3 1.0 %collective-permute-start.12 = (bf16[240,512]{1,0:T(8,128)(2,1)S(1)}, bf16[240,512]{1,0:T(8,128)(2,1)S(1)}, u32[]{:S(2)}, u32[]{:S(2)}) collective-permute-start(bf16[240,512]{1,0:T(8,128)(2,1)S(1)} %get-tuple-element.40), channel_id=1, source_target_pairs={{0,1},{1,0},{2,3},{3,2},{4,5},{5,4},{6,7},{7,6},{8,9},{9,8},{10,11... | collective-permute-start | bytes 737288 | tf_op jit(solution)/shard_map/ppermute | solution.py:618
  51.4 4.7 %attend_chunk.2.refs_15_ = bf16[60,4,4096]{2,1,0:T(4,128)(2,1)} custom-call(s32[3]{0:T(128)S(1)} %pad_add_fusion.ids, s32[1]{0:T(128)} %constant.43.clone.1.first, s32[60]{0:T(128)S(1)} %copy-done.9, bf16[60,4,4096]{2,1,0:T(4,128)(2,1)S(1)} %copy-done.5, bf16[60,16,1024]{2,1,0:T(8,128)(2,1)S(1)} %copy-done.6, ...), custom_call_target="tpu_custom_call", output_to_operand_aliasing={{}: (18, {})} | custom-call | flops 16000000000 | bytes 10846208 | tf_op jit(solution)/shard_map/attend_chunk/pallas_call | solution.py:594
  57.2 4.6 %attend_chunk.3 = bf16[60,4,4096]{2,1,0:T(4,128)(2,1)} custom-call(s32[3]{0:T(128)S(1)} %pad_add_fusion.ids, s32[1]{0:T(128)} %constant.41.clone.1.first, s32[60]{0:T(128)S(1)} %copy-done.9, bf16[60,4,4096]{2,1,0:T(4,128)(2,1)S(1)} %copy-done.5, bf16[60,16,1024]{2,1,0:T(8,128)(2,1)S(1)} %copy-done.6, ...), custom_call_target="tpu_custom_call", output_to_operand_aliasing={{}: (18, {})} | custom-call | flops 16000000000 | bytes 10846208 | tf_op jit(solution)/shard_map/attend_chunk/pallas_call | solution.py:594
  (49 shorter events, 3.8 us)
Async XLA Ops:
  0.7 12.2 %copy-start.10 = (f32[128]{0:T(128)S(1)}, f32[128]{0:T(128)}, u32[]{:S(2)}) copy-start(f32[128]{0:T(128)} %param.18) | copy-start | bytes 1540
  0.7 12.3 %copy-start.11 = (s32[60]{0:T(128)S(1)}, s32[60]{0:T(128)}, u32[]{:S(2)}) copy-start(s32[60]{0:T(128)} %param.23) | copy-start | bytes 724
  6.2 23.8 %collective-permute-start.5 = (bf16[480,512]{1,0:T(8,128)(2,1)}, bf16[480,512]{1,0:T(8,128)(2,1)S(1)}, u32[]{:S(2)}, u32[]{:S(2)}) collective-permute-start(bf16[480,512]{1,0:T(8,128)(2,1)} %get-tuple-element.26.after), channel_id=1, source_target_pairs={{0,1},{1,0},{2,3},{3,2},{4,5},{5,4},{6,7},{7,6},{8,9},{9,8},{10,11... | collective-permute-start | bytes 1474568 | tf_op jit(solution)/shard_map/ppermute | solution.py:618
  11.4 1.9 %collective-permute-start = (bf16[64,1536]{1,0:T(8,128)(2,1)}, bf16[64,1536]{1,0:T(8,128)(2,1)}, u32[]{:S(2)}, u32[]{:S(2)}) collective-permute-start(bf16[64,1536]{1,0:T(8,128)(2,1)} %pack_grads.1), channel_id=1, source_target_pairs={{0,4},{4,0},{8,12},{12,8},{16,20},{20,16},{24,28},{28,24},{1,5},{5... | collective-permute-start | bytes 589832 | tf_op jit(solution)/shard_map/ppermute | solution.py:401
  11.4 18.6 %collective-permute-start.6 = (bf16[480,512]{1,0:T(8,128)(2,1)}, bf16[480,512]{1,0:T(8,128)(2,1)S(1)}, u32[]{:S(2)}, u32[]{:S(2)}) collective-permute-start(bf16[480,512]{1,0:T(8,128)(2,1)} %get-tuple-element.33), channel_id=1, source_target_pairs={{0,2},{1,3},{2,0},{3,1},{4,6},{5,7},{6,4},{7,5},{8,10},{9,11},{10,... | collective-permute-start | bytes 1474568 | tf_op jit(solution)/shard_map/ppermute | solution.py:618
  15.0 7.9 %collective-permute-start.3 = (bf16[64,1536]{1,0:T(8,128)(2,1)S(1)}, bf16[64,1536]{1,0:T(8,128)(2,1)S(1)}, u32[]{:S(2)}, u32[]{:S(2)}) collective-permute-start(bf16[64,1536]{1,0:T(8,128)(2,1)S(1)} %chip_grads.1.after.a), channel_id=1, source_target_pairs={{0,8},{4,12},{8,0},{12,4},{16,24},{20,28},{24,16},{28,20},{1,9},{5... | collective-permute-start | bytes 589832 | tf_op jit(solution)/shard_map/ppermute | solution.py:423
  20.8 17.9 %collective-permute-start.2 = (bf16[480,512]{1,0:T(8,128)(2,1)S(1)}, bf16[480,512]{1,0:T(8,128)(2,1)S(1)}, u32[]{:S(2)}, u32[]{:S(2)}) collective-permute-start(bf16[480,512]{1,0:T(8,128)(2,1)S(1)} %get-tuple-element.30), channel_id=1, source_target_pairs={{0,2},{1,3},{2,0},{3,1},{4,6},{5,7},{6,4},{7,5},{8,10},{9,11},{10,... | collective-permute-start | bytes 1474568 | tf_op jit(solution)/shard_map/ppermute | solution.py:618
  22.3 17.8 %collective-permute-start.1 = (bf16[480,512]{1,0:T(8,128)(2,1)S(1)}, bf16[480,512]{1,0:T(8,128)(2,1)S(1)}, u32[]{:S(2)}, u32[]{:S(2)}) collective-permute-start(bf16[480,512]{1,0:T(8,128)(2,1)S(1)} %get-tuple-element.28.rest_0_), channel_id=1, source_target_pairs={{0,1},{1,0},{2,3},{3,2},{4,5},{5,4},{6,7},{7,6},{8,9},{9,8},{10,11... | collective-permute-start | bytes 1474568 | tf_op jit(solution)/shard_map/ppermute | solution.py:618
  22.9 11.3 %collective-permute-start.4 = (bf16[64,1536]{1,0:T(8,128)(2,1)S(1)}, bf16[64,1536]{1,0:T(8,128)(2,1)S(1)}, u32[]{:S(2)}, u32[]{:S(2)}) collective-permute-start(bf16[64,1536]{1,0:T(8,128)(2,1)S(1)} %plus.2.after.rest_0_.a), channel_id=1, source_target_pairs={{0,16},{4,20},{8,24},{12,28},{16,0},{20,4},{24,8},{28,12},{1,17},{... | collective-permute-start | bytes 589832 | tf_op jit(solution)/shard_map/ppermute | solution.py:423
  26.1 10.4 %copy-start.4 = (f32[2,64,256]{2,1,0:T(8,128)S(1)}, f32[2,64,256]{2,1,0:T(8,128)}, u32[]{:S(2)}) copy-start(f32[2,64,256]{2,1,0:T(8,128)} %refs_3_.1) | copy-start | bytes 393220
  34.2 17.2 %copy-start.7 = (bf16[60,16,1024]{2,1,0:T(8,128)(2,1)S(1)}, bf16[60,16,1024]{2,1,0:T(8,128)(2,1)}, u32[]{:S(2)}) copy-start(bf16[60,16,1024]{2,1,0:T(8,128)(2,1)} %refs_2_.5) | copy-start | bytes 5898244
  34.2 2.3 %collective-permute-start.7 = (bf16[64,1536]{1,0:T(8,128)(2,1)S(1)}, bf16[64,1536]{1,0:T(8,128)(2,1)S(1)}, u32[]{:S(2)}, u32[]{:S(2)}) collective-permute-start(bf16[64,1536]{1,0:T(8,128)(2,1)S(1)} %plus.3.refs_0_), channel_id=1, source_target_pairs={{0,4},{4,0},{8,12},{12,8},{16,20},{20,16},{24,28},{28,24},{1,5},{5... | collective-permute-start | bytes 589832 | tf_op jit(solution)/shard_map/ppermute | solution.py:401
  34.3 17.0 %collective-permute-start.14 = (bf16[240,512]{1,0:T(8,128)(2,1)S(1)}, bf16[240,512]{1,0:T(8,128)(2,1)S(1)}, u32[]{:S(2)}, u32[]{:S(2)}) collective-permute-start(bf16[240,512]{1,0:T(8,128)(2,1)S(1)} %get-tuple-element.43), channel_id=1, source_target_pairs={{0,1},{1,0},{2,3},{3,2},{4,5},{5,4},{6,7},{7,6},{8,9},{9,8},{10,11... | collective-permute-start | bytes 737288 | tf_op jit(solution)/shard_map/ppermute | solution.py:618
  35.8 15.6 %collective-permute-start.13 = (bf16[240,512]{1,0:T(8,128)(2,1)S(1)}, bf16[240,512]{1,0:T(8,128)(2,1)S(1)}, u32[]{:S(2)}, u32[]{:S(2)}) collective-permute-start(bf16[240,512]{1,0:T(8,128)(2,1)S(1)} %get-tuple-element.34.rest_0_), channel_id=1, source_target_pairs={{0,2},{1,3},{2,0},{3,1},{4,6},{5,7},{6,4},{7,5},{8,10},{9,11},{10,... | collective-permute-start | bytes 737288 | tf_op jit(solution)/shard_map/ppermute | solution.py:618
  36.5 14.8 %copy-start.5 = (bf16[60,4,4096]{2,1,0:T(4,128)(2,1)S(1)}, bf16[60,4,4096]{2,1,0:T(4,128)(2,1)}, u32[]{:S(2)}) copy-start(bf16[60,4,4096]{2,1,0:T(4,128)(2,1)} %refs_0_.3) | copy-start | bytes 5898244
  36.5 14.8 %copy-start.6 = (bf16[60,16,1024]{2,1,0:T(8,128)(2,1)S(1)}, bf16[60,16,1024]{2,1,0:T(8,128)(2,1)}, u32[]{:S(2)}) copy-start(bf16[60,16,1024]{2,1,0:T(8,128)(2,1)} %refs_1_.3) | copy-start | bytes 5898244
  38.1 13.3 %copy-start.2 = (bf16[480,512]{1,0:T(8,128)(2,1)S(1)}, bf16[480,512]{1,0:T(8,128)(2,1)}, u32[]{:S(2)}) copy-start(bf16[480,512]{1,0:T(8,128)(2,1)} %get-tuple-element.31.kkeep.refs_3_) | copy-start | bytes 1474564
  38.1 13.3 %copy-start.8 = (bf16[240,512]{1,0:T(8,128)(2,1)S(1)}, bf16[240,512]{1,0:T(8,128)(2,1)}, u32[]{:S(2)}) copy-start(bf16[240,512]{1,0:T(8,128)(2,1)} %get-tuple-element.42.refs_6_) | copy-start | bytes 737284
  38.1 13.3 %copy-start.9 = (s32[60]{0:T(128)S(1)}, s32[60]{0:T(128)}, u32[]{:S(2)}) copy-start(s32[60]{0:T(128)} %lengths.3) | copy-start | bytes 724
  38.1 7.9 %collective-permute-start.8 = (bf16[256,256]{1,0:T(8,128)(2,1)S(1)}, bf16[256,256]{1,0:T(8,128)(2,1)S(1)}, u32[]{:S(2)}, u32[]{:S(2)}) collective-permute-start(bf16[256,256]{1,0:T(8,128)(2,1)S(1)} %get-tuple-element.35), channel_id=1, source_target_pairs={{0,1},{1,0},{2,3},{3,2},{4,5},{5,4},{6,7},{7,6},{8,9},{9,8},{10,11... | collective-permute-start | bytes 393224 | tf_op jit(solution)/shard_map/ppermute | solution.py:618
  38.8 10.6 %collective-permute-start.9 = (bf16[256,256]{1,0:T(8,128)(2,1)S(1)}, bf16[256,256]{1,0:T(8,128)(2,1)S(1)}, u32[]{:S(2)}, u32[]{:S(2)}) collective-permute-start(bf16[256,256]{1,0:T(8,128)(2,1)S(1)} %get-tuple-element.36), channel_id=1, source_target_pairs={{0,2},{1,3},{2,0},{3,1},{4,6},{5,7},{6,4},{7,5},{8,10},{9,11},{10,... | collective-permute-start | bytes 393224 | tf_op jit(solution)/shard_map/ppermute | solution.py:618
  40.1 9.3 %collective-permute-start.10 = (bf16[256,256]{1,0:T(8,128)(2,1)S(1)}, bf16[256,256]{1,0:T(8,128)(2,1)S(1)}, u32[]{:S(2)}, u32[]{:S(2)}) collective-permute-start(bf16[256,256]{1,0:T(8,128)(2,1)S(1)} %get-tuple-element.37), channel_id=1, source_target_pairs={{0,3},{1,2},{2,1},{3,0},{4,7},{5,6},{6,5},{7,4},{8,11},{9,10},{10,... | collective-permute-start | bytes 393224 | tf_op jit(solution)/shard_map/ppermute | solution.py:618
  49.5 7.3 %collective-permute-start.11 = (bf16[240,512]{1,0:T(8,128)(2,1)S(1)}, bf16[240,512]{1,0:T(8,128)(2,1)S(1)}, u32[]{:S(2)}, u32[]{:S(2)}) collective-permute-start(bf16[240,512]{1,0:T(8,128)(2,1)S(1)} %get-tuple-element.38), channel_id=1, source_target_pairs={{0,2},{1,3},{2,0},{3,1},{4,6},{5,7},{6,4},{7,5},{8,10},{9,11},{10,... | collective-permute-start | bytes 737288 | tf_op jit(solution)/shard_map/ppermute | solution.py:618
  50.3 6.9 %collective-permute-start.12 = (bf16[240,512]{1,0:T(8,128)(2,1)S(1)}, bf16[240,512]{1,0:T(8,128)(2,1)S(1)}, u32[]{:S(2)}, u32[]{:S(2)}) collective-permute-start(bf16[240,512]{1,0:T(8,128)(2,1)S(1)} %get-tuple-element.40), channel_id=1, source_target_pairs={{0,1},{1,0},{2,3},{3,2},{4,5},{5,4},{6,7},{7,6},{8,9},{9,8},{10,11... | collective-permute-start | bytes 737288 | tf_op jit(solution)/shard_map/ppermute | solution.py:618
  (3 other events, 8.5 us)

commit v9 on v8

--- a/solution.py
+++ b/solution.py
@@ -202,7 +202,8 @@
     return [(0, kkeep, 0), (2, kkeep, tokens)], [(0, vkeep0, 0), (1, vkeep1, 0)]
 
 
-def first_kernel(ids, hidden, weight, x, ksend, vsend, held, w, hidden_sems, sems):
+def first_kernel(ids, hidden, weight, grad_a, grad_b, x, ksend, vsend, packed, *scratch):
+    held, w, held_a, held_b, hidden_sems, sems, grad_sems = scratch
     tokens = x.shape[0] // 4
     rows = tokens // STEPS
     start, run = multiply_terms(x, weight, 0, w, sems, *send_parts(tokens, ksend, vsend))
@@ -211,9 +212,20 @@
         at = pl.ds((ids[0] ^ r) * rows, rows)
         return pltpu.make_async_copy(hidden.at[at], held.at[r], hidden_sems.at[r])
 
+    grads = [
+        pltpu.make_async_copy(grad_a.at[0, ids[2] ^ 1], held_a, grad_sems.at[0]),
+        pltpu.make_async_copy(grad_b.at[0, ids[2] ^ 1], held_b, grad_sems.at[1]),
+    ]
+    for copy in grads:
+        copy.start()
     for r in (3, 1, 2, 0):
         hidden_copy(r).start()
     start()
+    for copy in grads:
+        copy.wait()
+    wide = grad_a.shape[-1]
+    packed[:, :wide] = held_a[...].astype(BF)
+    packed[:, wide:] = held_b[...].astype(BF)
     for r in (3, 1, 2, 0):
         hidden_copy(r).wait()
         x[r * tokens : (r + 1) * tokens] = held[r].reshape(tokens, x.shape[1])
@@ -253,11 +265,12 @@
     return [pltpu.VMEM((2, tiles, width, TILE), BF), pltpu.SemaphoreType.DMA((2, tiles))]
 
 
-def first_terms(ids, hidden, kv_weight, tokens):
+def first_terms(ids, hidden, kv_weight, grad_a, grad_b, tokens):
     width = hidden.shape[2]
     here = pl.BlockSpec(memory_space=pl.ANY)
     outs = [jax.ShapeDtypeStruct((4 * tokens, width), BF)]
     outs += [pltpu.VMEM(x.shape, BF) for x in term_shapes(SEND, tokens, CHUNKS[0])]
+    outs.append(jax.ShapeDtypeStruct((grad_a.shape[2], grad_a.shape[3] + grad_b.shape[3]), BF))
     w, sems = weight_scratch(width, CHUNKS[0])
     return pl.pallas_call(
         first_kernel,
@@ -265,19 +278,22 @@
         grid_spec=pltpu.PrefetchScalarGridSpec(
             num_scalar_prefetch=1,
             grid=(1,),
-            in_specs=[here] * 2,
+            in_specs=[here] * 4,
             out_specs=[whole(x.shape) for x in outs],
             scratch_shapes=[
                 pltpu.VMEM((4, tokens // STEPS, STEPS, width), BF),
                 w,
+                pltpu.VMEM(grad_a.shape[2:], F32),
+                pltpu.VMEM(grad_b.shape[2:], F32),
                 pltpu.SemaphoreType.DMA((4,)),
                 sems,
+                pltpu.SemaphoreType.DMA((2,)),
             ],
         ),
         compiler_params=params(16),
         cost_estimate=cost(8 * tokens * width * CHUNKS[0] * HD, hidden),
         name="first_terms",
-    )(ids, *map(hbm, (hidden, kv_weight)))
+    )(ids, *map(hbm, (hidden, kv_weight, grad_a, grad_b)))
 
 
 def keep_terms(x, kv_weight, queries, after):
@@ -337,13 +353,6 @@
     )(kkeep, kcame, vkeep, vcame, *after)
 
 
-def pack_kernel(ids, grad_a, grad_b, after, out):
-    del ids, after
-    wide = grad_a.shape[-1]
-    out[:, :wide] = grad_a[0, 0].astype(BF)
-    out[:, wide:] = grad_b[0, 0].astype(BF)
-
-
 def chip_kernel(ids, grad_a, grad_b, other, out):
     del ids
     wide = grad_a.shape[-1]
@@ -351,26 +360,23 @@
     out[:, wide:] = (grad_b[0, 0] + other[:, wide:].astype(F32)).astype(BF)
 
 
-def grad_half(kernel, name, ids, grad_a, grad_b, flip, more, spec):
-    rank, wide = grad_a.shape[2], grad_a.shape[3] + grad_b.shape[3]
-
+def chip_grads(ids, grad_a, grad_b, other):
     def half(x):
-        return pl.BlockSpec((1, 1) + x.shape[2:], lambda i, ids: (0, ids[2] ^ flip, 0, 0))
-
-    out = jax.ShapeDtypeStruct((rank, wide), BF)
+        return pl.BlockSpec((1, 1) + x.shape[2:], lambda i, ids: (0, ids[2], 0, 0))
+
     return pl.pallas_call(
-        kernel,
-        out_shape=out,
+        chip_kernel,
+        out_shape=jax.ShapeDtypeStruct(other.shape, BF),
         grid_spec=pltpu.PrefetchScalarGridSpec(
             num_scalar_prefetch=1,
             grid=(1,),
-            in_specs=[half(grad_a), half(grad_b), spec],
-            out_specs=whole(out.shape),
+            in_specs=[half(grad_a), half(grad_b), whole(other.shape)],
+            out_specs=whole(other.shape),
         ),
         compiler_params=params(4),
-        cost_estimate=cost(0, *[out] * 4),
-        name=name,
-    )(ids, hbm(grad_a), hbm(grad_b), more)
+        cost_estimate=cost(0, *[other] * 4),
+        name="chip_grads",
+    )(ids, hbm(grad_a), hbm(grad_b), other)
 
 
 def small_call(kernel, name, ids, args, outs, after=(), scratch=(), copied=0):
@@ -638,13 +644,8 @@
     ids = jnp.stack([lax.axis_index("tensor"), dp // 2, dp % 2]).astype(jnp.int32)
     tables = rotary_tables(key_gain, positions)
 
-    x, *first = first_terms(ids, hidden_in, kv_weight, tokens)
-    here = pl.BlockSpec(memory_space=pl.ANY)
-    packed = grad_half(pack_kernel, "pack_grads", ids, grad_a, grad_b, 1, first[0], here)
-    other = core_flip(packed, count_dp)
-    half = grad_half(
-        chip_kernel, "chip_grads", ids, grad_a, grad_b, 0, other, whole(other.shape)
-    )
+    x, *first, packed = first_terms(ids, hidden_in, kv_weight, grad_a, grad_b, tokens)
+    half = chip_grads(ids, grad_a, grad_b, core_flip(packed, count_dp))
 
     def first_exchange(term, *after):
         ksend, vsend, kkeep, vkeep0, vkeep1 = term
@@ -676,7 +677,7 @@
         ids, half, other, factor_a, factor_b, x, count_dp
     )
     ub = [sends[0]] + [across(sends[r], r) for r in (1, 2, 3)]
-    second = second_exchange(*first_exchange(second, *ub[1:]))
+    second = second_exchange(*first_exchange(second, ub[1]))
     for start, count, came in ((0, CHUNKS[0], first), (CHUNKS[0], CHUNKS[1], second)):
         attended = attend_chunk(
             ids,

time: 62.1 us -> 56.5 us (0.910)
  waiting for transfers between devices: 10.9 us -> 7.07 us
  Pallas kernels: 28.6 us -> 26.6 us
    ppermute x11, waiting for transfers between devices: 8.95 us -> 5.08 us  [across(): return lax.ppermute(x, 'tensor', [(i, i ^ r) for i in range(4)])]
    pallas_call x2 -> x1, Pallas kernels: 3.86 us -> 1.65 us  [chip_grads(): pl.pallas_call(chip_kernel, out_shape=jax.ShapeDtypeStruct(other.shape, B...]
  transfers between devices with their start and end apart: 15 -> 15, of which waited for: 5 -> 4; matrix products, arithmetic and copies ran while one was open for 1% -> 2% of each run, Pallas kernels for 30% -> 29%
where the time goes in v9:
time: 56.5 us; the launch traced here: 56.3 us
  Pallas kernels  26.6 us (47%)
  starting transfers between devices  18.8 us (33%)
  waiting for transfers between devices  7.07 us (13%)
  local copies, waits for them, and re-layouts  2.19 us (4%)
  between operations  0.85 us (2%)
  other arithmetic  0.82 us (1%)
    ppermute x11, starting transfers between devices, across(): return lax.ppermute(x, 'tensor', [(i, i ^ r) for i in range(4)])  13.9 us
    pallas_call x2, Pallas kernels, attend_chunk(): pl.pallas_call(attend_kernel, out_shape=jax.ShapeDtypeStruct(queries.shap...  9.3 us
    pallas_call x1, Pallas kernels, first_terms(): pl.pallas_call(first_kernel, out_shape=outs, grid_spec=pltpu.PrefetchScal...  5.68 us
    ppermute x11, waiting for transfers between devices, across(): return lax.ppermute(x, 'tensor', [(i, i ^ r) for i in range(4)])  5.08 us
    ppermute x2, starting transfers between devices, along_line(): return lax.ppermute(x, 'dp', [(i, i ^ 2 * d) for i in range(count)])  4.3 us
    pallas_call x1, Pallas kernels, later_terms(): pl.pallas_call(later_kernel, out_shape=outs, grid=(1,), in_specs=[whole(x...  4.2 us
    pallas_call x1, Pallas kernels, keep_terms(): pl.pallas_call(keep_kernel, out_shape=outs, grid=(1,), in_specs=[whole(x....  3.92 us
    unnamed x24, local copies, waits for them, and re-layouts  2.08 us
  transfers between devices with their start and end apart: 15, of which 4 were waited for; matrix products, arithmetic and copies ran while one was open for 2% of the time, Pallas kernels for 29%

profile of v9, /device:TPU:0, one launch (start us, length us, event | category | flops | bytes accessed | tf_op | source)
XLA Modules:
  0.0 56.3 jit_solution(16689764332428917150)
XLA Ops:
  0.7 5.7 %first_terms.1 = (bf16[960,1280]{1,0:T(8,128)(2,1)S(1)}, bf16[480,512]{1,0:T(8,128)(2,1)}, bf16[480,512]{1,0:T(8,128)(2,1)}, bf16[64,1536]{1,0:T(8,128)(2,1)}) custom-call(s32[3]{0:T(128)S(1)} %pad_add_fusion.ids, bf16[240,4,1280]{2,1,0:T(4,128)(2,1)} %hidden.1, bf16[2,1280,1024]{2,1,0:T(8,128)(2,1)} %weight.5, f32[1,2,64,1280]{3,2,1,0:T(8,128)} %grad_a.3, ...), custom_call_target="tpu_custom_call" | custom-call | flops 1258291200 | bytes 2457600 | tf_op jit(solution)/shard_map/first_terms/pallas_call | solution.py:275
  6.9 2.6 %collective-permute-start.5 = (bf16[480,512]{1,0:T(8,128)(2,1)}, bf16[480,512]{1,0:T(8,128)(2,1)S(1)}, u32[]{:S(2)}, u32[]{:S(2)}) collective-permute-start(bf16[480,512]{1,0:T(8,128)(2,1)} %get-tuple-element.33), channel_id=1, source_target_pairs={{0,1},{1,0},{2,3},{3,2},{4,5},{5,4},{6,7},{7,6},{8,9},{9,8},{10,11... | collective-permute-start | bytes 1474568 | tf_op jit(solution)/shard_map/ppermute | solution.py:624
  9.5 1.5 %collective-permute-start.6 = (bf16[480,512]{1,0:T(8,128)(2,1)}, bf16[480,512]{1,0:T(8,128)(2,1)S(1)}, u32[]{:S(2)}, u32[]{:S(2)}) collective-permute-start(bf16[480,512]{1,0:T(8,128)(2,1)} %get-tuple-element.35), channel_id=1, source_target_pairs={{0,2},{1,3},{2,0},{3,1},{4,6},{5,7},{6,4},{7,5},{8,10},{9,11},{10,... | collective-permute-start | bytes 1474568 | tf_op jit(solution)/shard_map/ppermute | solution.py:624
  11.4 1.6 %chip_grads.1.after.a = bf16[64,1536]{1,0:T(8,128)(2,1)S(1)} custom-call(s32[3]{0:T(128)S(1)} %pad_add_fusion.ids, f32[1,2,64,1280]{3,2,1,0:T(8,128)} %grad_a.3, f32[1,2,64,256]{3,2,1,0:T(8,128)} %grad_b.3, bf16[64,1536]{1,0:T(8,128)(2,1)} %collective-permute-done.other), custom_call_target="tpu_custom_call" | custom-call | bytes 786432 | tf_op jit(solution)/shard_map/chip_grads/pallas_call | solution.py:367
  13.0 1.6 %collective-permute-start.3 = (bf16[64,1536]{1,0:T(8,128)(2,1)S(1)}, bf16[64,1536]{1,0:T(8,128)(2,1)S(1)}, u32[]{:S(2)}, u32[]{:S(2)}) collective-permute-start(bf16[64,1536]{1,0:T(8,128)(2,1)S(1)} %chip_grads.1.after.a), channel_id=1, source_target_pairs={{0,8},{4,12},{8,0},{12,4},{16,24},{20,28},{24,16},{28,20},{1,9},{5... | collective-permute-start | bytes 589832 | tf_op jit(solution)/shard_map/ppermute | solution.py:429
  14.7 4.2 %later_terms.1 = (bf16[480,512]{1,0:T(8,128)(2,1)S(1)}, bf16[480,512]{1,0:T(8,128)(2,1)S(1)}, bf16[480,512]{1,0:T(8,128)(2,1)S(1)}, bf16[240,512]{1,0:T(8,128)(2,1)S(1)}, bf16[240,512]{1,0:T(8,128)(2,1)S(1)}) custom-call(bf16[960,1280]{1,0:T(8,128)(2,1)S(1)} %get-tuple-element.26.x.refs_4_, bf16[2,1280,1024]{2,1,0:T(8,128)(2,1)} %weight.5, ...), custom_call_target="tpu_custom_call" | custom-call | flops 2516582400 | bytes 4423680 | tf_op jit(solution)/shard_map/later_terms/pallas_call | solution.py:321
  18.9 0.6 %collective-permute-start.2 = (bf16[480,512]{1,0:T(8,128)(2,1)S(1)}, bf16[480,512]{1,0:T(8,128)(2,1)S(1)}, u32[]{:S(2)}, u32[]{:S(2)}) collective-permute-start(bf16[480,512]{1,0:T(8,128)(2,1)S(1)} %get-tuple-element.31), channel_id=1, source_target_pairs={{0,2},{1,3},{2,0},{3,1},{4,6},{5,7},{6,4},{7,5},{8,10},{9,11},{10,... | collective-permute-start | bytes 1474568 | tf_op jit(solution)/shard_map/ppermute | solution.py:624
  19.5 0.8 %collective-permute-start.1 = (bf16[480,512]{1,0:T(8,128)(2,1)S(1)}, bf16[480,512]{1,0:T(8,128)(2,1)S(1)}, u32[]{:S(2)}, u32[]{:S(2)}) collective-permute-start(bf16[480,512]{1,0:T(8,128)(2,1)S(1)} %get-tuple-element.29.rest_0_), channel_id=1, source_target_pairs={{0,1},{1,0},{2,3},{3,2},{4,5},{5,4},{6,7},{7,6},{8,9},{9,8},{10,11... | collective-permute-start | bytes 1474568 | tf_op jit(solution)/shard_map/ppermute | solution.py:624
  20.3 2.7 %collective-permute-start.4 = (bf16[64,1536]{1,0:T(8,128)(2,1)S(1)}, bf16[64,1536]{1,0:T(8,128)(2,1)S(1)}, u32[]{:S(2)}, u32[]{:S(2)}) collective-permute-start(bf16[64,1536]{1,0:T(8,128)(2,1)S(1)} %plus.2.after.rest_0_.a), channel_id=1, source_target_pairs={{0,16},{4,20},{8,24},{12,28},{16,0},{20,4},{24,8},{28,12},{1,17},{... | collective-permute-start | bytes 589832 | tf_op jit(solution)/shard_map/ppermute | solution.py:429
  23.5 3.9 %keep_terms.1 = (bf16[480,512]{1,0:T(8,128)(2,1)}, bf16[240,512]{1,0:T(8,128)(2,1)}, bf16[240,512]{1,0:T(8,128)(2,1)}, bf16[60,4,4096]{2,1,0:T(4,128)(2,1)}) custom-call(bf16[960,1280]{1,0:T(8,128)(2,1)S(1)} %get-tuple-element.26.x.refs_4_, bf16[2,1280,1024]{2,1,0:T(8,128)(2,1)} %weight.5, bf16[64,1536]{1,0:T(8,128)(2,1)S(1)} %plus.2.after.rest_0_.a), custom_call_target="tpu_custom_call" | custom-call | flops 1258291200 | bytes 2457600 | tf_op jit(solution)/shard_map/keep_terms/pallas_call | solution.py:305
  27.5 1.1 %copy-done.1 = bf16[480,512]{1,0:T(8,128)(2,1)S(1)} copy-done((bf16[480,512]{1,0:T(8,128)(2,1)S(1)}, bf16[480,512]{1,0:T(8,128)(2,1)}, u32[]{:S(2)}) %copy-start.1) | copy-done | bytes 491544
  28.6 0.9 %copy-done.3 = bf16[240,512]{1,0:T(8,128)(2,1)S(1)} copy-done((bf16[240,512]{1,0:T(8,128)(2,1)S(1)}, bf16[240,512]{1,0:T(8,128)(2,1)}, u32[]{:S(2)}) %copy-start.3) | copy-done | bytes 245784
  29.6 2.0 %collective-permute-done.4.b = bf16[64,1536]{1,0:T(8,128)(2,1)S(1)} collective-permute-done((bf16[64,1536]{1,0:T(8,128)(2,1)S(1)}, bf16[64,1536]{1,0:T(8,128)(2,1)S(1)}, u32[]{:S(2)}, u32[]{:S(2)}) %collective-permute-start.4) | collective-permute-done | bytes 196640 | tf_op jit(solution)/shard_map/ppermute | solution.py:429
  31.8 0.9 %collective-permute-start.14 = (bf16[240,512]{1,0:T(8,128)(2,1)S(1)}, bf16[240,512]{1,0:T(8,128)(2,1)S(1)}, u32[]{:S(2)}, u32[]{:S(2)}) collective-permute-start(bf16[240,512]{1,0:T(8,128)(2,1)S(1)} %get-tuple-element.45), channel_id=1, source_target_pairs={{0,1},{1,0},{2,3},{3,2},{4,5},{5,4},{6,7},{7,6},{8,9},{9,8},{10,11... | collective-permute-start | bytes 737288 | tf_op jit(solution)/shard_map/ppermute | solution.py:624
  32.7 1.5 %collective-permute-start.13 = (bf16[240,512]{1,0:T(8,128)(2,1)S(1)}, bf16[240,512]{1,0:T(8,128)(2,1)S(1)}, u32[]{:S(2)}, u32[]{:S(2)}) collective-permute-start(bf16[240,512]{1,0:T(8,128)(2,1)S(1)} %get-tuple-element.36.rest_0_), channel_id=1, source_target_pairs={{0,2},{1,3},{2,0},{3,1},{4,6},{5,7},{6,4},{7,5},{8,10},{9,11},{10,... | collective-permute-start | bytes 737288 | tf_op jit(solution)/shard_map/ppermute | solution.py:624
  34.2 1.5 %update_factors.1 = (f32[2,64,1280]{2,1,0:T(8,128)}, f32[2,64,256]{2,1,0:T(8,128)}, bf16[256,256]{1,0:T(8,128)(2,1)S(1)}, bf16[256,256]{1,0:T(8,128)(2,1)S(1)}, ...) custom-call(s32[3]{0:T(128)S(1)} %pad_add_fusion.ids, bf16[64,1536]{1,0:T(8,128)(2,1)S(1)} %plus.3.refs_0_, ...), custom_call_target="tpu_custom_call" | custom-call | bytes 3637248 | tf_op jit(solution)/shard_map/update_factors/pallas_call | solution.py:388
  35.8 0.6 %collective-permute-start.8 = (bf16[256,256]{1,0:T(8,128)(2,1)S(1)}, bf16[256,256]{1,0:T(8,128)(2,1)S(1)}, u32[]{:S(2)}, u32[]{:S(2)}) collective-permute-start(bf16[256,256]{1,0:T(8,128)(2,1)S(1)} %get-tuple-element.37), channel_id=1, source_target_pairs={{0,1},{1,0},{2,3},{3,2},{4,5},{5,4},{6,7},{7,6},{8,9},{9,8},{10,11... | collective-permute-start | bytes 393224 | tf_op jit(solution)/shard_map/ppermute | solution.py:624
  36.4 1.2 %collective-permute-start.11 = (bf16[256,256]{1,0:T(8,128)(2,1)S(1)}, bf16[256,256]{1,0:T(8,128)(2,1)S(1)}, u32[]{:S(2)}, u32[]{:S(2)}) collective-permute-start(bf16[256,256]{1,0:T(8,128)(2,1)S(1)} %get-tuple-element.42), channel_id=1, source_target_pairs={{0,2},{1,3},{2,0},{3,1},{4,6},{5,7},{6,4},{7,5},{8,10},{9,11},{10,... | collective-permute-start | bytes 393224 | tf_op jit(solution)/shard_map/ppermute | solution.py:624
  37.5 1.8 %collective-permute-start.12 = (bf16[256,256]{1,0:T(8,128)(2,1)S(1)}, bf16[256,256]{1,0:T(8,128)(2,1)S(1)}, u32[]{:S(2)}, u32[]{:S(2)}) collective-permute-start(bf16[256,256]{1,0:T(8,128)(2,1)S(1)} %get-tuple-element.43), channel_id=1, source_target_pairs={{0,3},{1,2},{2,1},{3,0},{4,7},{5,6},{6,5},{7,4},{8,11},{9,10},{10,... | collective-permute-start | bytes 393224 | tf_op jit(solution)/shard_map/ppermute | solution.py:624
  39.3 4.1 %collective-permute-done.8.rest_0_.refs_10_ = bf16[256,256]{1,0:T(8,128)(2,1)S(1)} collective-permute-done((bf16[256,256]{1,0:T(8,128)(2,1)S(1)}, bf16[256,256]{1,0:T(8,128)(2,1)S(1)}, u32[]{:S(2)}, u32[]{:S(2)}) %collective-permute-start.8) | collective-permute-done | bytes 131104 | tf_op jit(solution)/shard_map/ppermute | solution.py:624
  43.6 0.9 %collective-permute-start.9 = (bf16[240,512]{1,0:T(8,128)(2,1)S(1)}, bf16[240,512]{1,0:T(8,128)(2,1)S(1)}, u32[]{:S(2)}, u32[]{:S(2)}) collective-permute-start(bf16[240,512]{1,0:T(8,128)(2,1)S(1)} %get-tuple-element.38), channel_id=1, source_target_pairs={{0,2},{1,3},{2,0},{3,1},{4,6},{5,7},{6,4},{7,5},{8,10},{9,11},{10,... | collective-permute-start | bytes 737288 | tf_op jit(solution)/shard_map/ppermute | solution.py:624
  44.5 1.5 %collective-permute-start.10 = (bf16[240,512]{1,0:T(8,128)(2,1)S(1)}, bf16[240,512]{1,0:T(8,128)(2,1)S(1)}, u32[]{:S(2)}, u32[]{:S(2)}) collective-permute-start(bf16[240,512]{1,0:T(8,128)(2,1)S(1)} %get-tuple-element.40), channel_id=1, source_target_pairs={{0,1},{1,0},{2,3},{3,2},{4,5},{5,4},{6,7},{7,6},{8,9},{9,8},{10,11... | collective-permute-start | bytes 737288 | tf_op jit(solution)/shard_map/ppermute | solution.py:624
  46.5 4.7 %attend_chunk.2.refs_15_ = bf16[60,4,4096]{2,1,0:T(4,128)(2,1)} custom-call(s32[3]{0:T(128)S(1)} %pad_add_fusion.ids, s32[1]{0:T(128)} %constant.43.clone.1.first, s32[60]{0:T(128)S(1)} %copy-done.9, bf16[60,4,4096]{2,1,0:T(4,128)(2,1)S(1)} %copy-done.5, bf16[60,16,1024]{2,1,0:T(8,128)(2,1)S(1)} %copy-done.6, ...), custom_call_target="tpu_custom_call", output_to_operand_aliasing={{}: (18, {})} | custom-call | flops 16000000000 | bytes 10846208 | tf_op jit(solution)/shard_map/attend_chunk/pallas_call | solution.py:600
  51.6 4.6 %attend_chunk.3 = bf16[60,4,4096]{2,1,0:T(4,128)(2,1)} custom-call(s32[3]{0:T(128)S(1)} %pad_add_fusion.ids, s32[1]{0:T(128)} %constant.41.clone.1.first, s32[60]{0:T(128)S(1)} %copy-done.9, bf16[60,4,4096]{2,1,0:T(4,128)(2,1)S(1)} %copy-done.5, bf16[60,16,1024]{2,1,0:T(8,128)(2,1)S(1)} %copy-done.6, ...), custom_call_target="tpu_custom_call", output_to_operand_aliasing={{}: (18, {})} | custom-call | flops 16000000000 | bytes 10846208 | tf_op jit(solution)/shard_map/attend_chunk/pallas_call | solution.py:600
  (48 shorter events, 2.9 us)
Async XLA Ops:
  0.7 10.3 %copy-start.10 = (f32[128]{0:T(128)S(1)}, f32[128]{0:T(128)}, u32[]{:S(2)}) copy-start(f32[128]{0:T(128)} %param.18) | copy-start | bytes 1540
  0.7 10.4 %copy-start.11 = (s32[60]{0:T(128)S(1)}, s32[60]{0:T(128)}, u32[]{:S(2)}) copy-start(s32[60]{0:T(128)} %param.23) | copy-start | bytes 724
  6.4 5.0 %collective-permute-start = (bf16[64,1536]{1,0:T(8,128)(2,1)}, bf16[64,1536]{1,0:T(8,128)(2,1)}, u32[]{:S(2)}, u32[]{:S(2)}) collective-permute-start(bf16[64,1536]{1,0:T(8,128)(2,1)} %get-tuple-element.27), channel_id=1, source_target_pairs={{0,4},{4,0},{8,12},{12,8},{16,20},{20,16},{24,28},{28,24},{1,5},{5... | collective-permute-start | bytes 589832 | tf_op jit(solution)/shard_map/ppermute | solution.py:407
  6.9 20.5 %collective-permute-start.5 = (bf16[480,512]{1,0:T(8,128)(2,1)}, bf16[480,512]{1,0:T(8,128)(2,1)S(1)}, u32[]{:S(2)}, u32[]{:S(2)}) collective-permute-start(bf16[480,512]{1,0:T(8,128)(2,1)} %get-tuple-element.33), channel_id=1, source_target_pairs={{0,1},{1,0},{2,3},{3,2},{4,5},{5,4},{6,7},{7,6},{8,9},{9,8},{10,11... | collective-permute-start | bytes 1474568 | tf_op jit(solution)/shard_map/ppermute | solution.py:624
  9.5 18.0 %collective-permute-start.6 = (bf16[480,512]{1,0:T(8,128)(2,1)}, bf16[480,512]{1,0:T(8,128)(2,1)S(1)}, u32[]{:S(2)}, u32[]{:S(2)}) collective-permute-start(bf16[480,512]{1,0:T(8,128)(2,1)} %get-tuple-element.35), channel_id=1, source_target_pairs={{0,2},{1,3},{2,0},{3,1},{4,6},{5,7},{6,4},{7,5},{8,10},{9,11},{10,... | collective-permute-start | bytes 1474568 | tf_op jit(solution)/shard_map/ppermute | solution.py:624
  13.0 7.3 %collective-permute-start.3 = (bf16[64,1536]{1,0:T(8,128)(2,1)S(1)}, bf16[64,1536]{1,0:T(8,128)(2,1)S(1)}, u32[]{:S(2)}, u32[]{:S(2)}) collective-permute-start(bf16[64,1536]{1,0:T(8,128)(2,1)S(1)} %chip_grads.1.after.a), channel_id=1, source_target_pairs={{0,8},{4,12},{8,0},{12,4},{16,24},{20,28},{24,16},{28,20},{1,9},{5... | collective-permute-start | bytes 589832 | tf_op jit(solution)/shard_map/ppermute | solution.py:429
  18.9 17.5 %collective-permute-start.2 = (bf16[480,512]{1,0:T(8,128)(2,1)S(1)}, bf16[480,512]{1,0:T(8,128)(2,1)S(1)}, u32[]{:S(2)}, u32[]{:S(2)}) collective-permute-start(bf16[480,512]{1,0:T(8,128)(2,1)S(1)} %get-tuple-element.31), channel_id=1, source_target_pairs={{0,2},{1,3},{2,0},{3,1},{4,6},{5,7},{6,4},{7,5},{8,10},{9,11},{10,... | collective-permute-start | bytes 1474568 | tf_op jit(solution)/shard_map/ppermute | solution.py:624
  19.5 18.1 %collective-permute-start.1 = (bf16[480,512]{1,0:T(8,128)(2,1)S(1)}, bf16[480,512]{1,0:T(8,128)(2,1)S(1)}, u32[]{:S(2)}, u32[]{:S(2)}) collective-permute-start(bf16[480,512]{1,0:T(8,128)(2,1)S(1)} %get-tuple-element.29.rest_0_), channel_id=1, source_target_pairs={{0,1},{1,0},{2,3},{3,2},{4,5},{5,4},{6,7},{7,6},{8,9},{9,8},{10,11... | collective-permute-start | bytes 1474568 | tf_op jit(solution)/shard_map/ppermute | solution.py:624
  20.3 11.3 %collective-permute-start.4 = (bf16[64,1536]{1,0:T(8,128)(2,1)S(1)}, bf16[64,1536]{1,0:T(8,128)(2,1)S(1)}, u32[]{:S(2)}, u32[]{:S(2)}) collective-permute-start(bf16[64,1536]{1,0:T(8,128)(2,1)S(1)} %plus.2.after.rest_0_.a), channel_id=1, source_target_pairs={{0,16},{4,20},{8,24},{12,28},{16,0},{20,4},{24,8},{28,12},{1,17},{... | collective-permute-start | bytes 589832 | tf_op jit(solution)/shard_map/ppermute | solution.py:429
  23.5 10.7 %copy-start.4 = (f32[2,64,256]{2,1,0:T(8,128)S(1)}, f32[2,64,256]{2,1,0:T(8,128)}, u32[]{:S(2)}) copy-start(f32[2,64,256]{2,1,0:T(8,128)} %refs_3_.1) | copy-start | bytes 393220
  29.5 16.9 %copy-start.8 = (bf16[240,512]{1,0:T(8,128)(2,1)S(1)}, bf16[240,512]{1,0:T(8,128)(2,1)}, u32[]{:S(2)}) copy-start(bf16[240,512]{1,0:T(8,128)(2,1)} %get-tuple-element.44.refs_6_) | copy-start | bytes 737284
  31.6 14.8 %copy-start.7 = (bf16[60,16,1024]{2,1,0:T(8,128)(2,1)S(1)}, bf16[60,16,1024]{2,1,0:T(8,128)(2,1)}, u32[]{:S(2)}) copy-start(bf16[60,16,1024]{2,1,0:T(8,128)(2,1)} %refs_2_.5) | copy-start | bytes 5898244
  31.7 2.5 %collective-permute-start.7 = (bf16[64,1536]{1,0:T(8,128)(2,1)S(1)}, bf16[64,1536]{1,0:T(8,128)(2,1)S(1)}, u32[]{:S(2)}, u32[]{:S(2)}) collective-permute-start(bf16[64,1536]{1,0:T(8,128)(2,1)S(1)} %plus.3.refs_0_), channel_id=1, source_target_pairs={{0,4},{4,0},{8,12},{12,8},{16,20},{20,16},{24,28},{28,24},{1,5},{5... | collective-permute-start | bytes 589832 | tf_op jit(solution)/shard_map/ppermute | solution.py:407
  31.8 14.7 %copy-start.2 = (bf16[480,512]{1,0:T(8,128)(2,1)S(1)}, bf16[480,512]{1,0:T(8,128)(2,1)}, u32[]{:S(2)}) copy-start(bf16[480,512]{1,0:T(8,128)(2,1)} %get-tuple-element.32.kkeep.refs_3_) | copy-start | bytes 1474564
  31.8 14.7 %copy-start.5 = (bf16[60,4,4096]{2,1,0:T(4,128)(2,1)S(1)}, bf16[60,4,4096]{2,1,0:T(4,128)(2,1)}, u32[]{:S(2)}) copy-start(bf16[60,4,4096]{2,1,0:T(4,128)(2,1)} %refs_0_.3) | copy-start | bytes 5898244
  31.8 14.7 %copy-start.6 = (bf16[60,16,1024]{2,1,0:T(8,128)(2,1)S(1)}, bf16[60,16,1024]{2,1,0:T(8,128)(2,1)}, u32[]{:S(2)}) copy-start(bf16[60,16,1024]{2,1,0:T(8,128)(2,1)} %refs_1_.3) | copy-start | bytes 5898244
  31.8 14.7 %copy-start.9 = (s32[60]{0:T(128)S(1)}, s32[60]{0:T(128)}, u32[]{:S(2)}) copy-start(s32[60]{0:T(128)} %lengths.3) | copy-start | bytes 724
  31.8 12.7 %collective-permute-start.14 = (bf16[240,512]{1,0:T(8,128)(2,1)S(1)}, bf16[240,512]{1,0:T(8,128)(2,1)S(1)}, u32[]{:S(2)}, u32[]{:S(2)}) collective-permute-start(bf16[240,512]{1,0:T(8,128)(2,1)S(1)} %get-tuple-element.45), channel_id=1, source_target_pairs={{0,1},{1,0},{2,3},{3,2},{4,5},{5,4},{6,7},{7,6},{8,9},{9,8},{10,11... | collective-permute-start | bytes 737288 | tf_op jit(solution)/shard_map/ppermute | solution.py:624
  32.7 13.3 %collective-permute-start.13 = (bf16[240,512]{1,0:T(8,128)(2,1)S(1)}, bf16[240,512]{1,0:T(8,128)(2,1)S(1)}, u32[]{:S(2)}, u32[]{:S(2)}) collective-permute-start(bf16[240,512]{1,0:T(8,128)(2,1)S(1)} %get-tuple-element.36.rest_0_), channel_id=1, source_target_pairs={{0,2},{1,3},{2,0},{3,1},{4,6},{5,7},{6,4},{7,5},{8,10},{9,11},{10,... | collective-permute-start | bytes 737288 | tf_op jit(solution)/shard_map/ppermute | solution.py:624
  35.8 7.7 %collective-permute-start.8 = (bf16[256,256]{1,0:T(8,128)(2,1)S(1)}, bf16[256,256]{1,0:T(8,128)(2,1)S(1)}, u32[]{:S(2)}, u32[]{:S(2)}) collective-permute-start(bf16[256,256]{1,0:T(8,128)(2,1)S(1)} %get-tuple-element.37), channel_id=1, source_target_pairs={{0,1},{1,0},{2,3},{3,2},{4,5},{5,4},{6,7},{7,6},{8,9},{9,8},{10,11... | collective-permute-start | bytes 393224 | tf_op jit(solution)/shard_map/ppermute | solution.py:624
  36.4 10.1 %collective-permute-start.11 = (bf16[256,256]{1,0:T(8,128)(2,1)S(1)}, bf16[256,256]{1,0:T(8,128)(2,1)S(1)}, u32[]{:S(2)}, u32[]{:S(2)}) collective-permute-start(bf16[256,256]{1,0:T(8,128)(2,1)S(1)} %get-tuple-element.42), channel_id=1, source_target_pairs={{0,2},{1,3},{2,0},{3,1},{4,6},{5,7},{6,4},{7,5},{8,10},{9,11},{10,... | collective-permute-start | bytes 393224 | tf_op jit(solution)/shard_map/ppermute | solution.py:624
  37.5 8.9 %collective-permute-start.12 = (bf16[256,256]{1,0:T(8,128)(2,1)S(1)}, bf16[256,256]{1,0:T(8,128)(2,1)S(1)}, u32[]{:S(2)}, u32[]{:S(2)}) collective-permute-start(bf16[256,256]{1,0:T(8,128)(2,1)S(1)} %get-tuple-element.43), channel_id=1, source_target_pairs={{0,3},{1,2},{2,1},{3,0},{4,7},{5,6},{6,5},{7,4},{8,11},{9,10},{10,... | collective-permute-start | bytes 393224 | tf_op jit(solution)/shard_map/ppermute | solution.py:624
  43.6 8.1 %collective-permute-start.9 = (bf16[240,512]{1,0:T(8,128)(2,1)S(1)}, bf16[240,512]{1,0:T(8,128)(2,1)S(1)}, u32[]{:S(2)}, u32[]{:S(2)}) collective-permute-start(bf16[240,512]{1,0:T(8,128)(2,1)S(1)} %get-tuple-element.38), channel_id=1, source_target_pairs={{0,2},{1,3},{2,0},{3,1},{4,6},{5,7},{6,4},{7,5},{8,10},{9,11},{10,... | collective-permute-start | bytes 737288 | tf_op jit(solution)/shard_map/ppermute | solution.py:624
  44.5 7.1 %collective-permute-start.10 = (bf16[240,512]{1,0:T(8,128)(2,1)S(1)}, bf16[240,512]{1,0:T(8,128)(2,1)S(1)}, u32[]{:S(2)}, u32[]{:S(2)}) collective-permute-start(bf16[240,512]{1,0:T(8,128)(2,1)S(1)} %get-tuple-element.40), channel_id=1, source_target_pairs={{0,1},{1,0},{2,3},{3,2},{4,5},{5,4},{6,7},{7,6},{8,9},{9,8},{10,11... | collective-permute-start | bytes 737288 | tf_op jit(solution)/shard_map/ppermute | solution.py:624
  (3 other events, 8.8 us)

commit v10 on v9

--- a/solution.py
+++ b/solution.py
@@ -143,9 +143,18 @@
 TILE = 256
 
 
-def multiply_terms(x, weight, base, w, sems, keys, values):
-    tokens = x.shape[0] // 4
-    steps = x.shape[1] // TILE
+def rel_rows(x, x0):
+    def rows(r, at):
+        if r == 0:
+            return x0[:, at]
+        tokens = x.shape[0] // 3
+        return x[(r - 1) * tokens : r * tokens, at]
+
+    return rows
+
+
+def multiply_terms(rows_of, tokens, width, weight, base, w, sems, keys, values):
+    steps = width // TILE
     units = (keys, values)
 
     def copy(p, i):
@@ -175,8 +184,7 @@
                     push(k + 1)
                 for n in range(len(keys)):
                     for p in range(2):
-                        r = units[p][n][0]
-                        rows = x[r * tokens : (r + 1) * tokens, k * TILE : (k + 1) * TILE]
+                        rows = rows_of(units[p][n][0], slice(k * TILE, (k + 1) * TILE))
                         staged = k % 2 if n == 0 else None
                         pltpu.matmul_acc_lhs(accs[p][n], rows, load_staged_rhs=staged)
             at = pl.ds(pl.multiple_of(i * TILE, TILE), TILE)
@@ -204,52 +212,59 @@
 
 def first_kernel(ids, hidden, weight, grad_a, grad_b, x, ksend, vsend, packed, *scratch):
     held, w, held_a, held_b, hidden_sems, sems, grad_sems = scratch
-    tokens = x.shape[0] // 4
+    tokens, width = x.shape[0] // 3, x.shape[1]
     rows = tokens // STEPS
-    start, run = multiply_terms(x, weight, 0, w, sems, *send_parts(tokens, ksend, vsend))
+    parts = send_parts(tokens, ksend, vsend)
+    start, run = multiply_terms(rel_rows(x, None), tokens, width, weight, 0, w, sems, *parts)
 
     def hidden_copy(r):
         at = pl.ds((ids[0] ^ r) * rows, rows)
-        return pltpu.make_async_copy(hidden.at[at], held.at[r], hidden_sems.at[r])
+        return pltpu.make_async_copy(hidden.at[at], held.at[r - 1], hidden_sems.at[r - 1])
 
     grads = [
         pltpu.make_async_copy(grad_a.at[0, ids[2] ^ 1], held_a, grad_sems.at[0]),
         pltpu.make_async_copy(grad_b.at[0, ids[2] ^ 1], held_b, grad_sems.at[1]),
     ]
+    for r in (3, 1, 2):
+        hidden_copy(r).start()
+    start()
     for copy in grads:
         copy.start()
-    for r in (3, 1, 2, 0):
-        hidden_copy(r).start()
-    start()
+    for r in (3, 1, 2):
+        hidden_copy(r).wait()
+        x[(r - 1) * tokens : r * tokens] = held[r - 1].reshape(tokens, width)
     for copy in grads:
         copy.wait()
     wide = grad_a.shape[-1]
     packed[:, :wide] = held_a[...].astype(BF)
     packed[:, wide:] = held_b[...].astype(BF)
-    for r in (3, 1, 2, 0):
-        hidden_copy(r).wait()
-        x[r * tokens : (r + 1) * tokens] = held[r].reshape(tokens, x.shape[1])
     run()
 
 
-def keep_kernel(x, weight, after, kkeep, vkeep0, vkeep1, _, w, sems):
+def keep_kernel(x, x0, weight, after, kkeep, vkeep0, vkeep1, _, w, sems):
     del after
-    tokens = x.shape[0] // 4
-    start, run = multiply_terms(x, weight, 0, w, sems, *keep_parts(tokens, kkeep, vkeep0, vkeep1))
+    tokens, width = x0.shape
+    parts = keep_parts(tokens, kkeep, vkeep0, vkeep1)
+    start, run = multiply_terms(rel_rows(x, x0), tokens, width, weight, 0, w, sems, *parts)
     start()
     run()
 
 
-def later_kernel(x, weight, after, *rest):
+def later_kernel(ids, x, hidden, weight, after, x0, *rest):
     del after
-    ksend, vsend, kkeep, vkeep0, vkeep1, w, sems = rest
-    tokens = x.shape[0] // 4
+    ksend, vsend, kkeep, vkeep0, vkeep1, w, sems, held, hidden_sem = rest
+    tokens, width = x0.shape
+    at = pl.ds(ids[0] * (tokens // STEPS), tokens // STEPS)
+    own = pltpu.make_async_copy(hidden.at[at], held, hidden_sem)
+    own.start()
     sends = send_parts(tokens, ksend, vsend)
     keeps = keep_parts(tokens, kkeep, vkeep0, vkeep1)
     base = weight.shape[2] - w.shape[1] * TILE
     parts = [a + b for a, b in zip(sends, keeps)]
-    start, run = multiply_terms(x, weight, base, w, sems, *parts)
+    start, run = multiply_terms(rel_rows(x, x0), tokens, width, weight, base, w, sems, *parts)
     start()
+    own.wait()
+    x0[...] = held[...].reshape(tokens, width)
     run()
 
 
@@ -268,7 +283,7 @@
 def first_terms(ids, hidden, kv_weight, grad_a, grad_b, tokens):
     width = hidden.shape[2]
     here = pl.BlockSpec(memory_space=pl.ANY)
-    outs = [jax.ShapeDtypeStruct((4 * tokens, width), BF)]
+    outs = [jax.ShapeDtypeStruct((3 * tokens, width), BF)]
     outs += [pltpu.VMEM(x.shape, BF) for x in term_shapes(SEND, tokens, CHUNKS[0])]
     outs.append(jax.ShapeDtypeStruct((grad_a.shape[2], grad_a.shape[3] + grad_b.shape[3]), BF))
     w, sems = weight_scratch(width, CHUNKS[0])
@@ -281,11 +296,11 @@
             in_specs=[here] * 4,
             out_specs=[whole(x.shape) for x in outs],
             scratch_shapes=[
-                pltpu.VMEM((4, tokens // STEPS, STEPS, width), BF),
+                pltpu.VMEM((3, tokens // STEPS, STEPS, width), BF),
                 w,
                 pltpu.VMEM(grad_a.shape[2:], F32),
                 pltpu.VMEM(grad_b.shape[2:], F32),
-                pltpu.SemaphoreType.DMA((4,)),
+                pltpu.SemaphoreType.DMA((3,)),
                 sems,
                 pltpu.SemaphoreType.DMA((2,)),
             ],
@@ -296,8 +311,8 @@
     )(ids, *map(hbm, (hidden, kv_weight, grad_a, grad_b)))
 
 
-def keep_terms(x, kv_weight, queries, after):
-    tokens, width = x.shape[0] // 4, x.shape[1]
+def keep_terms(x, x0, kv_weight, queries, after):
+    tokens, width = x0.shape
     here = pl.BlockSpec(memory_space=pl.ANY)
     outs = [pltpu.HBM(out.shape, BF) for out in term_shapes(KEEP, tokens, CHUNKS[0])]
     specs = [whole(out.shape) for out in outs] + [here]
@@ -306,29 +321,38 @@
         keep_kernel,
         out_shape=outs,
         grid=(1,),
-        in_specs=[whole(x.shape), here, here],
+        in_specs=[whole(x.shape), whole(x0.shape), here, here],
         out_specs=specs,
         scratch_shapes=weight_scratch(width, CHUNKS[0]),
         compiler_params=params(14),
         cost_estimate=cost(8 * tokens * width * CHUNKS[0] * HD, x),
         name="keep_terms",
-    )(x, hbm(kv_weight), after)
-
-
-def later_terms(x, kv_weight, after):
-    outs = term_shapes(SEND + KEEP, x.shape[0] // 4, CHUNKS[1])
+    )(x, x0, hbm(kv_weight), after)
+
+
+def later_terms(ids, x, hidden, kv_weight, after):
+    tokens, width = x.shape[0] // 3, x.shape[1]
+    outs = [jax.ShapeDtypeStruct((tokens, width), BF)]
+    outs += term_shapes(SEND + KEEP, tokens, CHUNKS[1])
     here = pl.BlockSpec(memory_space=pl.ANY)
     return pl.pallas_call(
         later_kernel,
         out_shape=outs,
-        grid=(1,),
-        in_specs=[whole(x.shape), here, here],
-        out_specs=[whole(out.shape) for out in outs],
-        scratch_shapes=weight_scratch(x.shape[1], CHUNKS[1]),
-        compiler_params=params(12),
-        cost_estimate=cost(4 * math.prod(x.shape) * CHUNKS[1] * HD, x, *outs),
+        grid_spec=pltpu.PrefetchScalarGridSpec(
+            num_scalar_prefetch=1,
+            grid=(1,),
+            in_specs=[whole(x.shape), here, here, here],
+            out_specs=[whole(out.shape) for out in outs],
+            scratch_shapes=[
+                *weight_scratch(width, CHUNKS[1]),
+                pltpu.VMEM((tokens // STEPS, STEPS, width), BF),
+                pltpu.SemaphoreType.DMA,
+            ],
+        ),
+        compiler_params=params(13),
+        cost_estimate=cost(16 * tokens * width * CHUNKS[1] * HD, x, *outs),
         name="later_terms",
-    )(x, hbm(kv_weight), after)
+    )(ids, x, hbm(hidden), hbm(kv_weight), after)
 
 
 def mid_kernel(kkeep, kcame, vkeep, vcame, *rest):
@@ -432,7 +456,7 @@
 TOP = 2 * R
 
 
-def update_kernel(rates, ids, half, other, factor_a, factor_b, x, out_a, out_b, *rest):
+def update_kernel(rates, ids, half, other, factor_a, factor_b, x, x0, out_a, out_b, *rest):
     *sends, a, new_a, new_b, sems = rest
     copies = [
         pltpu.make_async_copy(new_a, out_a, sems.at[0]),
@@ -447,7 +471,8 @@
     for p in range(2):
         a[p * R : (p + 1) * R] = new_a[p].astype(BF)
     a[TOP:] = jnp.zeros((TILE - TOP, wide), BF)
-    tokens = x.shape[0] // 4
+    tokens = x0.shape[0]
+    rows_of = rel_rows(x, x0)
 
     def multiply(*accs):
         steps = wide // TILE
@@ -462,7 +487,7 @@
             if k + 1 < steps:
                 push(k + 1)
             for r in range(4):
-                rows = x[r * tokens : (r + 1) * tokens, k * TILE : (k + 1) * TILE]
+                rows = rows_of(r, slice(k * TILE, (k + 1) * TILE))
                 staged = k % 2 if r < 2 else None
                 pltpu.matmul_acc_lhs(accs[r], rows, load_staged_rhs=staged)
         for r, send in enumerate(sends):
@@ -478,7 +503,7 @@
         copy.wait()
 
 
-def updated(ids, half, other, factor_a, factor_b, x, dp, *after):
+def updated(ids, half, other, factor_a, factor_b, x, x0, dp, *after):
     rates = (2.0 / math.sqrt(dp * D), 2.0 / math.sqrt(dp * R))
     outs = [pltpu.HBM(f.shape, F32) for f in (factor_a, factor_b)]
     outs += [jax.ShapeDtypeStruct((2 * TOP, 2 * TOP), BF)] * 4
@@ -486,7 +511,7 @@
         functools.partial(update_kernel, rates),
         "update_factors",
         ids,
-        (half, other, factor_a, factor_b, x),
+        (half, other, factor_a, factor_b, x, x0),
         outs,
         after,
         [
@@ -657,24 +682,24 @@
         kkeep, kcame, vkeep0, vcame = parts
         return kkeep, kcame, across(mids[0], 2), vkeep0, vcame, across(mids[1], 1)
 
-    second = later_terms(x, kv_weight, half)
+    x0, *second = later_terms(ids, x, hidden_in, kv_weight, half)
     step, after = 1, second[:1]
     while 2 * step < count_dp:
         half = plus(half, along_line(half, step, count_dp), *after)
         step *= 2
         if step == 2:
-            *keeps, attended = keep_terms(x, kv_weight, queries, half)
+            *keeps, attended = keep_terms(x, x0, kv_weight, queries, half)
             first += keeps
             mids, parts = first_exchange(first, half)
             after = (mids[0], tables[0])
     if step == 1:
-        *keeps, attended = keep_terms(x, kv_weight, queries, half)
+        *keeps, attended = keep_terms(x, x0, kv_weight, queries, half)
         first += keeps
         mids, parts = first_exchange(first, half)
     first = second_exchange(mids, parts)
     other = core_flip(half, count_dp)
     new_a, new_b, *sends = updated(
-        ids, half, other, factor_a, factor_b, x, count_dp
+        ids, half, other, factor_a, factor_b, x, x0, count_dp
     )
     ub = [sends[0]] + [across(sends[r], r) for r in (1, 2, 3)]
     second = second_exchange(*first_exchange(second, ub[1]))

time: 56.5 us -> 59.2 us (1.048)
  other arithmetic: 0.82 us -> 2.06 us
  waiting for transfers between devices: 7.07 us -> 5.96 us
  starting transfers between devices: 18.8 us -> 19.9 us
  Pallas kernels: 26.6 us -> 27.5 us
    pallas_call x1, Pallas kernels: 4.2 us -> 5.43 us  [later_terms(): pl.pallas_call(later_kernel, out_shape=outs, grid_spec=pltpu.PrefetchScal...]
    ppermute x11, starting transfers between devices: 13.9 us -> 15 us  [across(): return lax.ppermute(x, 'tensor', [(i, i ^ r) for i in range(4)])]
    ppermute x11, waiting for transfers between devices: 5.08 us -> 4.36 us  [across(): return lax.ppermute(x, 'tensor', [(i, i ^ r) for i in range(4)])]
    concatenate x1, other arithmetic: 0.08 us -> 0.75 us  [rotary_tables(): jnp.concatenate([freq, freq])]
    unnamed x24 -> x26, local copies, waits for them, and re-layouts: 2.08 us -> 2.08 us
  transfers between devices with their start and end apart: 15 -> 15, of which waited for: 4 -> 4; matrix products, arithmetic and copies ran while one was open for 2% -> 5% of each run, Pallas kernels for 29% -> 29%
where the time goes in v10:
time: 59.2 us; the launch traced here: 59 us
  Pallas kernels  27.5 us (46%)
  starting transfers between devices  19.9 us (34%)
  waiting for transfers between devices  5.96 us (10%)
  local copies, waits for them, and re-layouts  2.76 us (5%)
  other arithmetic  2.06 us (3%)
  between operations  0.83 us (1%)
    ppermute x11, starting transfers between devices, across(): return lax.ppermute(x, 'tensor', [(i, i ^ r) for i in range(4)])  15 us
    pallas_call x2, Pallas kernels, attend_chunk(): pl.pallas_call(attend_kernel, out_shape=jax.ShapeDtypeStruct(queries.shap...  9.29 us
    pallas_call x1, Pallas kernels, first_terms(): pl.pallas_call(first_kernel, out_shape=outs, grid_spec=pltpu.PrefetchScal...  5.44 us
    pallas_call x1, Pallas kernels, later_terms(): pl.pallas_call(later_kernel, out_shape=outs, grid_spec=pltpu.PrefetchScal...  5.43 us
    ppermute x11, waiting for transfers between devices, across(): return lax.ppermute(x, 'tensor', [(i, i ^ r) for i in range(4)])  4.36 us
    ppermute x2, starting transfers between devices, along_line(): return lax.ppermute(x, 'dp', [(i, i ^ 2 * d) for i in range(count)])  4.3 us
    pallas_call x1, Pallas kernels, keep_terms(): pl.pallas_call(keep_kernel, out_shape=outs, grid=(1,), in_specs=[whole(x....  3.89 us
    unnamed x26, local copies, waits for them, and re-layouts  2.08 us
  transfers between devices with their start and end apart: 15, of which 4 were waited for; matrix products, arithmetic and copies ran while one was open for 5% of the time, Pallas kernels for 29%

profile of v10, /device:TPU:0, one launch (start us, length us, event | category | flops | bytes accessed | tf_op | source)
XLA Modules:
  0.0 59.0 jit_solution(14699436128884680120)
XLA Ops:
  0.7 5.4 %first_terms.1 = (bf16[720,1280]{1,0:T(8,128)(2,1)S(1)}, bf16[480,512]{1,0:T(8,128)(2,1)}, bf16[480,512]{1,0:T(8,128)(2,1)S(1)}, bf16[64,1536]{1,0:T(8,128)(2,1)}) custom-call(s32[3]{0:T(128)S(1)} %pad_add_fusion.ids, bf16[240,4,1280]{2,1,0:T(4,128)(2,1)} %hidden.3, bf16[2,1280,1024]{2,1,0:T(8,128)(2,1)} %weight.5, f32[1,2,64,1280]{3,2,1,0:T(8,128)} %grad_a.3, ...), custom_call_target="tpu_custom_call" | custom-call | flops 1258291200 | bytes 2457600 | tf_op jit(solution)/shard_map/first_terms/pallas_call | solution.py:290
  6.7 2.6 %collective-permute-start.5 = (bf16[480,512]{1,0:T(8,128)(2,1)}, bf16[480,512]{1,0:T(8,128)(2,1)S(1)}, u32[]{:S(2)}, u32[]{:S(2)}) collective-permute-start(bf16[480,512]{1,0:T(8,128)(2,1)} %get-tuple-element.35), channel_id=1, source_target_pairs={{0,1},{1,0},{2,3},{3,2},{4,5},{5,4},{6,7},{7,6},{8,9},{9,8},{10,11... | collective-permute-start | bytes 1474568 | tf_op jit(solution)/shard_map/ppermute | solution.py:649
  9.3 1.5 %collective-permute-start.6 = (bf16[480,512]{1,0:T(8,128)(2,1)S(1)}, bf16[480,512]{1,0:T(8,128)(2,1)S(1)}, u32[]{:S(2)}, u32[]{:S(2)}) collective-permute-start(bf16[480,512]{1,0:T(8,128)(2,1)S(1)} %get-tuple-element.37), channel_id=1, source_target_pairs={{0,2},{1,3},{2,0},{3,1},{4,6},{5,7},{6,4},{7,5},{8,10},{9,11},{10,... | collective-permute-start | bytes 1474568 | tf_op jit(solution)/shard_map/ppermute | solution.py:649
  10.8 0.6 %slice_negate_fusion = (f32[64]{0:T(128)}, f32[64]{0:T(128)}) fusion(f32[128]{0:T(128)S(1)} %copy-done.10), kind=kLoop, calls=%fused_computation.8 | loop fusion | flops 64 | bytes 1024 | tf_op jit(solution)/shard_map/neg | solution.py:644
  11.5 0.7 %convert_element_type.11 = f32[240]{0:T(256)} reshape(f32[60,4]{1,0:T(8,128)S(1)} %add_convert_fusion) | data formatting | bytes 1920 | tf_op jit(solution)/shard_map/convert_element_type | solution.py:643
  12.2 0.7 %pad_maximum_fusion = (f32[128]{0:T(128)S(1)}, f32[128]{0:T(128)S(1)}) fusion(f32[64]{0:T(128)S(1)} %multiply_exponential_fusion, f32[64]{0:T(128)} %get-tuple-element.54, f32[64]{0:T(128)} %get-tuple-element.53), kind=kLoop, calls=%fused_computation.6 | loop fusion | flops 256 | bytes 1792 | tf_op jit(solution)/shard_map/concatenate | solution.py:643
  12.9 1.6 %chip_grads.1.after.a = bf16[64,1536]{1,0:T(8,128)(2,1)S(1)} custom-call(s32[3]{0:T(128)S(1)} %pad_add_fusion.ids, f32[1,2,64,1280]{3,2,1,0:T(8,128)} %grad_a.3, f32[1,2,64,256]{3,2,1,0:T(8,128)} %grad_b.3, bf16[64,1536]{1,0:T(8,128)(2,1)S(1)} %collective-permute-done.other), custom_call_target="tpu_custom_call" | custom-call | bytes 786432 | tf_op jit(solution)/shard_map/chip_grads/pallas_call | solution.py:391
  14.5 1.6 %collective-permute-start.3 = (bf16[64,1536]{1,0:T(8,128)(2,1)S(1)}, bf16[64,1536]{1,0:T(8,128)(2,1)S(1)}, u32[]{:S(2)}, u32[]{:S(2)}) collective-permute-start(bf16[64,1536]{1,0:T(8,128)(2,1)S(1)} %chip_grads.1.after.a), channel_id=1, source_target_pairs={{0,8},{4,12},{8,0},{12,4},{16,24},{20,28},{24,16},{28,20},{1,9},{5... | collective-permute-start | bytes 589832 | tf_op jit(solution)/shard_map/ppermute | solution.py:453
  16.1 5.4 %later_terms.1 = (bf16[240,1280]{1,0:T(8,128)(2,1)S(1)}, bf16[480,512]{1,0:T(8,128)(2,1)S(1)}, bf16[480,512]{1,0:T(8,128)(2,1)S(1)}, bf16[480,512]{1,0:T(8,128)(...) custom-call(s32[3]{0:T(128)S(1)} %pad_add_fusion.ids, ...), custom_call_target="tpu_custom_call" | custom-call | flops 2516582400 | bytes 4423680 | tf_op jit(solution)/shard_map/later_terms/pallas_call | solution.py:338
  22.7 2.7 %collective-permute-start.4 = (bf16[64,1536]{1,0:T(8,128)(2,1)S(1)}, bf16[64,1536]{1,0:T(8,128)(2,1)S(1)}, u32[]{:S(2)}, u32[]{:S(2)}) collective-permute-start(bf16[64,1536]{1,0:T(8,128)(2,1)S(1)} %plus.2.after.rest_0_.a), channel_id=1, source_target_pairs={{0,16},{4,20},{8,24},{12,28},{16,0},{20,4},{24,8},{28,12},{1,17},{... | collective-permute-start | bytes 589832 | tf_op jit(solution)/shard_map/ppermute | solution.py:453
  25.9 3.9 %keep_terms.1 = (bf16[480,512]{1,0:T(8,128)(2,1)}, bf16[240,512]{1,0:T(8,128)(2,1)}, bf16[240,512]{1,0:T(8,128)(2,1)}, bf16[60,4,4096]{2,1,0:T(4,128)(2,1)}) custom-call(bf16[720,1280]{1,0:T(8,128)(2,1)S(1)} %get-tuple-element.27.x.refs_4_, bf16[240,1280]{1,0:T(8,128)(2,1)S(1)} %get-tuple-element.33.x0.refs_5_, bf16[2,1280,1024]{2,1,0:T(8,128)(2,1)} %weight.5, ...), custom_call_target="tpu_custom_call" | custom-call | flops 1258291200 | bytes 1843200 | tf_op jit(solution)/shard_map/keep_terms/pallas_call | solution.py:320
  29.9 1.1 %copy-done.1 = bf16[480,512]{1,0:T(8,128)(2,1)S(1)} copy-done((bf16[480,512]{1,0:T(8,128)(2,1)S(1)}, bf16[480,512]{1,0:T(8,128)(2,1)}, u32[]{:S(2)}) %copy-start.1) | copy-done | bytes 491544
  31.0 0.9 %copy-done.3 = bf16[240,512]{1,0:T(8,128)(2,1)S(1)} copy-done((bf16[240,512]{1,0:T(8,128)(2,1)S(1)}, bf16[240,512]{1,0:T(8,128)(2,1)}, u32[]{:S(2)}) %copy-start.3) | copy-done | bytes 245784
  32.0 1.6 %collective-permute-done.4.b = bf16[64,1536]{1,0:T(8,128)(2,1)S(1)} collective-permute-done((bf16[64,1536]{1,0:T(8,128)(2,1)S(1)}, bf16[64,1536]{1,0:T(8,128)(2,1)S(1)}, u32[]{:S(2)}, u32[]{:S(2)}) %collective-permute-start.4) | collective-permute-done | bytes 196640 | tf_op jit(solution)/shard_map/ppermute | solution.py:453
  33.8 1.6 %collective-permute-start.14 = (bf16[240,512]{1,0:T(8,128)(2,1)S(1)}, bf16[240,512]{1,0:T(8,128)(2,1)S(1)}, u32[]{:S(2)}, u32[]{:S(2)}) collective-permute-start(bf16[240,512]{1,0:T(8,128)(2,1)S(1)} %get-tuple-element.47), channel_id=1, source_target_pairs={{0,1},{1,0},{2,3},{3,2},{4,5},{5,4},{6,7},{7,6},{8,9},{9,8},{10,11... | collective-permute-start | bytes 737288 | tf_op jit(solution)/shard_map/ppermute | solution.py:649
  35.4 1.5 %collective-permute-start.13 = (bf16[240,512]{1,0:T(8,128)(2,1)S(1)}, bf16[240,512]{1,0:T(8,128)(2,1)S(1)}, u32[]{:S(2)}, u32[]{:S(2)}) collective-permute-start(bf16[240,512]{1,0:T(8,128)(2,1)S(1)} %get-tuple-element.38.rest_0_), channel_id=1, source_target_pairs={{0,2},{1,3},{2,0},{3,1},{4,6},{5,7},{6,4},{7,5},{8,10},{9,11},{10,... | collective-permute-start | bytes 737288 | tf_op jit(solution)/shard_map/ppermute | solution.py:649
  36.9 1.5 %update_factors.1 = (f32[2,64,1280]{2,1,0:T(8,128)}, f32[2,64,256]{2,1,0:T(8,128)}, bf16[256,256]{1,0:T(8,128)(2,1)S(1)}, bf16[256,256]{1,0:T(8,128)(2,1)S(1)}, ...) custom-call(s32[3]{0:T(128)S(1)} %pad_add_fusion.ids, bf16[64,1536]{1,0:T(8,128)(2,1)S(1)} %plus.3.refs_0_, ...), custom_call_target="tpu_custom_call" | custom-call | bytes 3637248 | tf_op jit(solution)/shard_map/update_factors/pallas_call | solution.py:412
  39.1 0.8 %collective-permute-start.11 = (bf16[256,256]{1,0:T(8,128)(2,1)S(1)}, bf16[256,256]{1,0:T(8,128)(2,1)S(1)}, u32[]{:S(2)}, u32[]{:S(2)}) collective-permute-start(bf16[256,256]{1,0:T(8,128)(2,1)S(1)} %get-tuple-element.44), channel_id=1, source_target_pairs={{0,2},{1,3},{2,0},{3,1},{4,6},{5,7},{6,4},{7,5},{8,10},{9,11},{10,... | collective-permute-start | bytes 393224 | tf_op jit(solution)/shard_map/ppermute | solution.py:649
  39.8 2.2 %collective-permute-start.12 = (bf16[256,256]{1,0:T(8,128)(2,1)S(1)}, bf16[256,256]{1,0:T(8,128)(2,1)S(1)}, u32[]{:S(2)}, u32[]{:S(2)}) collective-permute-start(bf16[256,256]{1,0:T(8,128)(2,1)S(1)} %get-tuple-element.45), channel_id=1, source_target_pairs={{0,3},{1,2},{2,1},{3,0},{4,7},{5,6},{6,5},{7,4},{8,11},{9,10},{10,... | collective-permute-start | bytes 393224 | tf_op jit(solution)/shard_map/ppermute | solution.py:649
  42.0 3.4 %collective-permute-done.8.rest_0_.refs_10_ = bf16[256,256]{1,0:T(8,128)(2,1)S(1)} collective-permute-done((bf16[256,256]{1,0:T(8,128)(2,1)S(1)}, bf16[256,256]{1,0:T(8,128)(2,1)S(1)}, u32[]{:S(2)}, u32[]{:S(2)}) %collective-permute-start.8) | collective-permute-done | bytes 131104 | tf_op jit(solution)/shard_map/ppermute | solution.py:649
  45.5 1.6 %collective-permute-start.9 = (bf16[240,512]{1,0:T(8,128)(2,1)S(1)}, bf16[240,512]{1,0:T(8,128)(2,1)S(1)}, u32[]{:S(2)}, u32[]{:S(2)}) collective-permute-start(bf16[240,512]{1,0:T(8,128)(2,1)S(1)} %get-tuple-element.40), channel_id=1, source_target_pairs={{0,2},{1,3},{2,0},{3,1},{4,6},{5,7},{6,4},{7,5},{8,10},{9,11},{10,... | collective-permute-start | bytes 737288 | tf_op jit(solution)/shard_map/ppermute | solution.py:649
  47.2 1.5 %collective-permute-start.10 = (bf16[240,512]{1,0:T(8,128)(2,1)S(1)}, bf16[240,512]{1,0:T(8,128)(2,1)S(1)}, u32[]{:S(2)}, u32[]{:S(2)}) collective-permute-start(bf16[240,512]{1,0:T(8,128)(2,1)S(1)} %get-tuple-element.42), channel_id=1, source_target_pairs={{0,1},{1,0},{2,3},{3,2},{4,5},{5,4},{6,7},{7,6},{8,9},{9,8},{10,11... | collective-permute-start | bytes 737288 | tf_op jit(solution)/shard_map/ppermute | solution.py:649
  49.2 4.7 %attend_chunk.2.refs_15_ = bf16[60,4,4096]{2,1,0:T(4,128)(2,1)} custom-call(s32[3]{0:T(128)S(1)} %pad_add_fusion.ids, s32[1]{0:T(128)} %constant.43.clone.1.first, s32[60]{0:T(128)S(1)} %copy-done.9, bf16[60,4,4096]{2,1,0:T(4,128)(2,1)S(1)} %copy-done.5, bf16[60,16,1024]{2,1,0:T(8,128)(2,1)S(1)} %copy-done.6, ...), custom_call_target="tpu_custom_call", output_to_operand_aliasing={{}: (18, {})} | custom-call | flops 16000000000 | bytes 10846208 | tf_op jit(solution)/shard_map/attend_chunk/pallas_call | solution.py:625
  54.3 4.6 %attend_chunk.3 = bf16[60,4,4096]{2,1,0:T(4,128)(2,1)} custom-call(s32[3]{0:T(128)S(1)} %pad_add_fusion.ids, s32[1]{0:T(128)} %constant.41.clone.1.first, s32[60]{0:T(128)S(1)} %copy-done.9, bf16[60,4,4096]{2,1,0:T(4,128)(2,1)S(1)} %copy-done.5, bf16[60,16,1024]{2,1,0:T(8,128)(2,1)S(1)} %copy-done.6, ...), custom_call_target="tpu_custom_call", output_to_operand_aliasing={{}: (18, {})} | custom-call | flops 16000000000 | bytes 10846208 | tf_op jit(solution)/shard_map/attend_chunk/pallas_call | solution.py:625
  (50 shorter events, 4.3 us)
Async XLA Ops:
  0.7 10.1 %copy-start.10 = (f32[128]{0:T(128)S(1)}, f32[128]{0:T(128)}, u32[]{:S(2)}) copy-start(f32[128]{0:T(128)} %param.18) | copy-start | bytes 1540
  0.7 10.7 %copy-start.12 = (s32[60]{0:T(128)S(1)}, s32[60]{0:T(128)}, u32[]{:S(2)}) copy-start(s32[60]{0:T(128)} %param.23) | copy-start | bytes 724
  6.2 6.8 %collective-permute-start = (bf16[64,1536]{1,0:T(8,128)(2,1)}, bf16[64,1536]{1,0:T(8,128)(2,1)S(1)}, u32[]{:S(2)}, u32[]{:S(2)}) collective-permute-start(bf16[64,1536]{1,0:T(8,128)(2,1)} %get-tuple-element.28), channel_id=1, source_target_pairs={{0,4},{4,0},{8,12},{12,8},{16,20},{20,16},{24,28},{28,24},{1,5},{5... | collective-permute-start | bytes 589832 | tf_op jit(solution)/shard_map/ppermute | solution.py:431
  6.7 23.2 %collective-permute-start.5 = (bf16[480,512]{1,0:T(8,128)(2,1)}, bf16[480,512]{1,0:T(8,128)(2,1)S(1)}, u32[]{:S(2)}, u32[]{:S(2)}) collective-permute-start(bf16[480,512]{1,0:T(8,128)(2,1)} %get-tuple-element.35), channel_id=1, source_target_pairs={{0,1},{1,0},{2,3},{3,2},{4,5},{5,4},{6,7},{7,6},{8,9},{9,8},{10,11... | collective-permute-start | bytes 1474568 | tf_op jit(solution)/shard_map/ppermute | solution.py:649
  9.3 20.6 %collective-permute-start.6 = (bf16[480,512]{1,0:T(8,128)(2,1)S(1)}, bf16[480,512]{1,0:T(8,128)(2,1)S(1)}, u32[]{:S(2)}, u32[]{:S(2)}) collective-permute-start(bf16[480,512]{1,0:T(8,128)(2,1)S(1)} %get-tuple-element.37), channel_id=1, source_target_pairs={{0,2},{1,3},{2,0},{3,1},{4,6},{5,7},{6,4},{7,5},{8,10},{9,11},{10,... | collective-permute-start | bytes 1474568 | tf_op jit(solution)/shard_map/ppermute | solution.py:649
  14.5 8.2 %collective-permute-start.3 = (bf16[64,1536]{1,0:T(8,128)(2,1)S(1)}, bf16[64,1536]{1,0:T(8,128)(2,1)S(1)}, u32[]{:S(2)}, u32[]{:S(2)}) collective-permute-start(bf16[64,1536]{1,0:T(8,128)(2,1)S(1)} %chip_grads.1.after.a), channel_id=1, source_target_pairs={{0,8},{4,12},{8,0},{12,4},{16,24},{20,28},{24,16},{28,20},{1,9},{5... | collective-permute-start | bytes 589832 | tf_op jit(solution)/shard_map/ppermute | solution.py:453
  21.6 17.5 %collective-permute-start.2 = (bf16[480,512]{1,0:T(8,128)(2,1)S(1)}, bf16[480,512]{1,0:T(8,128)(2,1)S(1)}, u32[]{:S(2)}, u32[]{:S(2)}) collective-permute-start(bf16[480,512]{1,0:T(8,128)(2,1)S(1)} %get-tuple-element.32), channel_id=1, source_target_pairs={{0,2},{1,3},{2,0},{3,1},{4,6},{5,7},{6,4},{7,5},{8,10},{9,11},{10,... | collective-permute-start | bytes 1474568 | tf_op jit(solution)/shard_map/ppermute | solution.py:649
  22.2 17.7 %collective-permute-start.1 = (bf16[480,512]{1,0:T(8,128)(2,1)S(1)}, bf16[480,512]{1,0:T(8,128)(2,1)S(1)}, u32[]{:S(2)}, u32[]{:S(2)}) collective-permute-start(bf16[480,512]{1,0:T(8,128)(2,1)S(1)} %get-tuple-element.30.rest_0_), channel_id=1, source_target_pairs={{0,1},{1,0},{2,3},{3,2},{4,5},{5,4},{6,7},{7,6},{8,9},{9,8},{10,11... | collective-permute-start | bytes 1474568 | tf_op jit(solution)/shard_map/ppermute | solution.py:649
  22.7 10.9 %collective-permute-start.4 = (bf16[64,1536]{1,0:T(8,128)(2,1)S(1)}, bf16[64,1536]{1,0:T(8,128)(2,1)S(1)}, u32[]{:S(2)}, u32[]{:S(2)}) collective-permute-start(bf16[64,1536]{1,0:T(8,128)(2,1)S(1)} %plus.2.after.rest_0_.a), channel_id=1, source_target_pairs={{0,16},{4,20},{8,24},{12,28},{16,0},{20,4},{24,8},{28,12},{1,17},{... | collective-permute-start | bytes 589832 | tf_op jit(solution)/shard_map/ppermute | solution.py:453
  25.9 11.0 %copy-start.4 = (f32[2,64,256]{2,1,0:T(8,128)S(1)}, f32[2,64,256]{2,1,0:T(8,128)}, u32[]{:S(2)}) copy-start(f32[2,64,256]{2,1,0:T(8,128)} %refs_3_.1) | copy-start | bytes 393220
  31.9 17.2 %copy-start.8 = (bf16[240,512]{1,0:T(8,128)(2,1)S(1)}, bf16[240,512]{1,0:T(8,128)(2,1)}, u32[]{:S(2)}) copy-start(bf16[240,512]{1,0:T(8,128)(2,1)} %get-tuple-element.46.refs_6_) | copy-start | bytes 737284
  33.6 15.5 %copy-start.7 = (bf16[60,16,1024]{2,1,0:T(8,128)(2,1)S(1)}, bf16[60,16,1024]{2,1,0:T(8,128)(2,1)}, u32[]{:S(2)}) copy-start(bf16[60,16,1024]{2,1,0:T(8,128)(2,1)} %refs_2_.5) | copy-start | bytes 5898244
  33.7 3.3 %collective-permute-start.7 = (bf16[64,1536]{1,0:T(8,128)(2,1)S(1)}, bf16[64,1536]{1,0:T(8,128)(2,1)S(1)}, u32[]{:S(2)}, u32[]{:S(2)}) collective-permute-start(bf16[64,1536]{1,0:T(8,128)(2,1)S(1)} %plus.3.refs_0_), channel_id=1, source_target_pairs={{0,4},{4,0},{8,12},{12,8},{16,20},{20,16},{24,28},{28,24},{1,5},{5... | collective-permute-start | bytes 589832 | tf_op jit(solution)/shard_map/ppermute | solution.py:431
  33.7 15.4 %copy-start.2 = (bf16[480,512]{1,0:T(8,128)(2,1)S(1)}, bf16[480,512]{1,0:T(8,128)(2,1)}, u32[]{:S(2)}) copy-start(bf16[480,512]{1,0:T(8,128)(2,1)} %get-tuple-element.34.kkeep.refs_3_) | copy-start | bytes 1474564
  33.7 15.4 %copy-start.5 = (bf16[60,4,4096]{2,1,0:T(4,128)(2,1)S(1)}, bf16[60,4,4096]{2,1,0:T(4,128)(2,1)}, u32[]{:S(2)}) copy-start(bf16[60,4,4096]{2,1,0:T(4,128)(2,1)} %refs_0_.3) | copy-start | bytes 5898244
  33.8 15.4 %copy-start.6 = (bf16[60,16,1024]{2,1,0:T(8,128)(2,1)S(1)}, bf16[60,16,1024]{2,1,0:T(8,128)(2,1)}, u32[]{:S(2)}) copy-start(bf16[60,16,1024]{2,1,0:T(8,128)(2,1)} %refs_1_.3) | copy-start | bytes 5898244
  33.8 15.4 %copy-start.9 = (s32[60]{0:T(128)S(1)}, s32[60]{0:T(128)}, u32[]{:S(2)}) copy-start(s32[60]{0:T(128)} %lengths.3) | copy-start | bytes 724
  33.8 13.4 %collective-permute-start.14 = (bf16[240,512]{1,0:T(8,128)(2,1)S(1)}, bf16[240,512]{1,0:T(8,128)(2,1)S(1)}, u32[]{:S(2)}, u32[]{:S(2)}) collective-permute-start(bf16[240,512]{1,0:T(8,128)(2,1)S(1)} %get-tuple-element.47), channel_id=1, source_target_pairs={{0,1},{1,0},{2,3},{3,2},{4,5},{5,4},{6,7},{7,6},{8,9},{9,8},{10,11... | collective-permute-start | bytes 737288 | tf_op jit(solution)/shard_map/ppermute | solution.py:649
  35.4 13.3 %collective-permute-start.13 = (bf16[240,512]{1,0:T(8,128)(2,1)S(1)}, bf16[240,512]{1,0:T(8,128)(2,1)S(1)}, u32[]{:S(2)}, u32[]{:S(2)}) collective-permute-start(bf16[240,512]{1,0:T(8,128)(2,1)S(1)} %get-tuple-element.38.rest_0_), channel_id=1, source_target_pairs={{0,2},{1,3},{2,0},{3,1},{4,6},{5,7},{6,4},{7,5},{8,10},{9,11},{10,... | collective-permute-start | bytes 737288 | tf_op jit(solution)/shard_map/ppermute | solution.py:649
  38.5 7.0 %collective-permute-start.8 = (bf16[256,256]{1,0:T(8,128)(2,1)S(1)}, bf16[256,256]{1,0:T(8,128)(2,1)S(1)}, u32[]{:S(2)}, u32[]{:S(2)}) collective-permute-start(bf16[256,256]{1,0:T(8,128)(2,1)S(1)} %get-tuple-element.39), channel_id=1, source_target_pairs={{0,1},{1,0},{2,3},{3,2},{4,5},{5,4},{6,7},{7,6},{8,9},{9,8},{10,11... | collective-permute-start | bytes 393224 | tf_op jit(solution)/shard_map/ppermute | solution.py:649
  39.1 10.1 %collective-permute-start.11 = (bf16[256,256]{1,0:T(8,128)(2,1)S(1)}, bf16[256,256]{1,0:T(8,128)(2,1)S(1)}, u32[]{:S(2)}, u32[]{:S(2)}) collective-permute-start(bf16[256,256]{1,0:T(8,128)(2,1)S(1)} %get-tuple-element.44), channel_id=1, source_target_pairs={{0,2},{1,3},{2,0},{3,1},{4,6},{5,7},{6,4},{7,5},{8,10},{9,11},{10,... | collective-permute-start | bytes 393224 | tf_op jit(solution)/shard_map/ppermute | solution.py:649
  39.8 9.3 %collective-permute-start.12 = (bf16[256,256]{1,0:T(8,128)(2,1)S(1)}, bf16[256,256]{1,0:T(8,128)(2,1)S(1)}, u32[]{:S(2)}, u32[]{:S(2)}) collective-permute-start(bf16[256,256]{1,0:T(8,128)(2,1)S(1)} %get-tuple-element.45), channel_id=1, source_target_pairs={{0,3},{1,2},{2,1},{3,0},{4,7},{5,6},{6,5},{7,4},{8,11},{9,10},{10,... | collective-permute-start | bytes 393224 | tf_op jit(solution)/shard_map/ppermute | solution.py:649
  45.5 8.8 %collective-permute-start.9 = (bf16[240,512]{1,0:T(8,128)(2,1)S(1)}, bf16[240,512]{1,0:T(8,128)(2,1)S(1)}, u32[]{:S(2)}, u32[]{:S(2)}) collective-permute-start(bf16[240,512]{1,0:T(8,128)(2,1)S(1)} %get-tuple-element.40), channel_id=1, source_target_pairs={{0,2},{1,3},{2,0},{3,1},{4,6},{5,7},{6,4},{7,5},{8,10},{9,11},{10,... | collective-permute-start | bytes 737288 | tf_op jit(solution)/shard_map/ppermute | solution.py:649
  47.2 7.2 %collective-permute-start.10 = (bf16[240,512]{1,0:T(8,128)(2,1)S(1)}, bf16[240,512]{1,0:T(8,128)(2,1)S(1)}, u32[]{:S(2)}, u32[]{:S(2)}) collective-permute-start(bf16[240,512]{1,0:T(8,128)(2,1)S(1)} %get-tuple-element.42), channel_id=1, source_target_pairs={{0,1},{1,0},{2,3},{3,2},{4,5},{5,4},{6,7},{7,6},{8,9},{9,8},{10,11... | collective-permute-start | bytes 737288 | tf_op jit(solution)/shard_map/ppermute | solution.py:649
  (4 other events, 18.4 us)

commit v11 on v9

--- a/solution.py
+++ b/solution.py
@@ -412,17 +412,28 @@
 
 
 def plus(a, b, *after):
+    return plus_handing(a, b, *after)[0]
+
+
+def plus_handing(a, b, *after, handed=()):
     out = jax.ShapeDtypeStruct(a.shape, BF)
+    here = pl.BlockSpec(memory_space=pl.ANY)
+    count = 2 + len(after)
+
+    def kernel(a, b, *rest):
+        plus_kernel(a, b, rest[len(after) + len(handed)])
+
     return pl.pallas_call(
-        plus_kernel,
-        out_shape=out,
+        kernel,
+        out_shape=[out] + [jax.ShapeDtypeStruct(x.shape, x.dtype) for x in handed],
         grid=(1,),
-        in_specs=[whole(a.shape)] * 2 + [pl.BlockSpec(memory_space=pl.ANY)] * len(after),
-        out_specs=whole(a.shape),
+        in_specs=[whole(a.shape)] * 2 + [here] * (len(after) + len(handed)),
+        out_specs=[whole(a.shape)] + [here] * len(handed),
+        input_output_aliases={count + n: 1 + n for n in range(len(handed))},
         compiler_params=params(2),
         cost_estimate=cost(0, a, b, out),
         name="plus",
-    )(a, b, *after)
+    )(a, b, *after, *handed)
 
 
 def along_line(x, d, count):
@@ -660,7 +671,12 @@
     second = later_terms(x, kv_weight, half)
     step, after = 1, second[:1]
     while 2 * step < count_dp:
-        half = plus(half, along_line(half, step, count_dp), *after)
+        came = along_line(half, step, count_dp)
+        if step == 1:
+            half, *sends = plus_handing(half, came, handed=second[:2])
+            second = [*sends, *second[2:]]
+        else:
+            half = plus(half, came, *after)
         step *= 2
         if step == 2:
             *keeps, attended = keep_terms(x, kv_weight, queries, half)

time: 56.5 us -> 55.8 us (0.988)
  waiting for transfers between devices: 7.07 us -> 6.11 us
    ppermute x2, waiting for transfers between devices: 1.99 us -> 1 us  [along_line(): return lax.ppermute(x, 'dp', [(i, i ^ 2 * d) for i in range(count)])]
  transfers between devices with their start and end apart: 15 -> 15, of which waited for: 4 -> 5; matrix products, arithmetic and copies ran while one was open for 2% -> 2% of each run, Pallas kernels for 29% -> 29%
where the time goes in v11:
time: 55.8 us; the launch traced here: 55.5 us
  Pallas kernels  26.6 us (48%)
  starting transfers between devices  19 us (34%)
  waiting for transfers between devices  6.11 us (11%)
  local copies, waits for them, and re-layouts  2.19 us (4%)
  between operations  0.84 us (2%)
  other arithmetic  0.82 us (1%)
    ppermute x11, starting transfers between devices, across(): return lax.ppermute(x, 'tensor', [(i, i ^ r) for i in range(4)])  14.1 us
    pallas_call x2, Pallas kernels, attend_chunk(): pl.pallas_call(attend_kernel, out_shape=jax.ShapeDtypeStruct(queries.shap...  9.3 us
    pallas_call x1, Pallas kernels, first_terms(): pl.pallas_call(first_kernel, out_shape=outs, grid_spec=pltpu.PrefetchScal...  5.68 us
    ppermute x11, waiting for transfers between devices, across(): return lax.ppermute(x, 'tensor', [(i, i ^ r) for i in range(4)])  5.1 us
    ppermute x2, starting transfers between devices, along_line(): return lax.ppermute(x, 'dp', [(i, i ^ 2 * d) for i in range(count)])  4.3 us
    pallas_call x1, Pallas kernels, later_terms(): pl.pallas_call(later_kernel, out_shape=outs, grid=(1,), in_specs=[whole(x...  4.2 us
    pallas_call x1, Pallas kernels, keep_terms(): pl.pallas_call(keep_kernel, out_shape=outs, grid=(1,), in_specs=[whole(x....  3.93 us
    unnamed x24, local copies, waits for them, and re-layouts  2.08 us
  transfers between devices with their start and end apart: 15, of which 5 were waited for; matrix products, arithmetic and copies ran while one was open for 2% of the time, Pallas kernels for 29%

profile of v11, /device:TPU:0, one launch (start us, length us, event | category | flops | bytes accessed | tf_op | source)
XLA Modules:
  0.0 55.5 jit_solution(11347283949788816777)
XLA Ops:
  0.7 5.7 %first_terms.1 = (bf16[960,1280]{1,0:T(8,128)(2,1)S(1)}, bf16[480,512]{1,0:T(8,128)(2,1)}, bf16[480,512]{1,0:T(8,128)(2,1)}, bf16[64,1536]{1,0:T(8,128)(2,1)}) custom-call(s32[3]{0:T(128)S(1)} %pad_add_fusion.ids, bf16[240,4,1280]{2,1,0:T(4,128)(2,1)} %hidden.1, bf16[2,1280,1024]{2,1,0:T(8,128)(2,1)} %weight.5, f32[1,2,64,1280]{3,2,1,0:T(8,128)} %grad_a.3, ...), custom_call_target="tpu_custom_call" | custom-call | flops 1258291200 | bytes 2457600 | tf_op jit(solution)/shard_map/first_terms/pallas_call | solution.py:275
  6.9 2.6 %collective-permute-start.5 = (bf16[480,512]{1,0:T(8,128)(2,1)}, bf16[480,512]{1,0:T(8,128)(2,1)S(1)}, u32[]{:S(2)}, u32[]{:S(2)}) collective-permute-start(bf16[480,512]{1,0:T(8,128)(2,1)} %get-tuple-element.39), channel_id=1, source_target_pairs={{0,1},{1,0},{2,3},{3,2},{4,5},{5,4},{6,7},{7,6},{8,9},{9,8},{10,11... | collective-permute-start | bytes 1474568 | tf_op jit(solution)/shard_map/ppermute | solution.py:635
  9.5 1.5 %collective-permute-start.6 = (bf16[480,512]{1,0:T(8,128)(2,1)}, bf16[480,512]{1,0:T(8,128)(2,1)S(1)}, u32[]{:S(2)}, u32[]{:S(2)}) collective-permute-start(bf16[480,512]{1,0:T(8,128)(2,1)} %get-tuple-element.41), channel_id=1, source_target_pairs={{0,2},{1,3},{2,0},{3,1},{4,6},{5,7},{6,4},{7,5},{8,10},{9,11},{10,... | collective-permute-start | bytes 1474568 | tf_op jit(solution)/shard_map/ppermute | solution.py:635
  11.4 1.6 %chip_grads.1.after.a = bf16[64,1536]{1,0:T(8,128)(2,1)S(1)} custom-call(s32[3]{0:T(128)S(1)} %pad_add_fusion.ids, f32[1,2,64,1280]{3,2,1,0:T(8,128)} %grad_a.3, f32[1,2,64,256]{3,2,1,0:T(8,128)} %grad_b.3, bf16[64,1536]{1,0:T(8,128)(2,1)} %collective-permute-done.other), custom_call_target="tpu_custom_call" | custom-call | bytes 786432 | tf_op jit(solution)/shard_map/chip_grads/pallas_call | solution.py:367
  13.0 1.6 %collective-permute-start.1 = (bf16[64,1536]{1,0:T(8,128)(2,1)S(1)}, bf16[64,1536]{1,0:T(8,128)(2,1)S(1)}, u32[]{:S(2)}, u32[]{:S(2)}) collective-permute-start(bf16[64,1536]{1,0:T(8,128)(2,1)S(1)} %chip_grads.1.after.a), channel_id=1, source_target_pairs={{0,8},{4,12},{8,0},{12,4},{16,24},{20,28},{24,16},{28,20},{1,9},{5... | collective-permute-start | bytes 589832 | tf_op jit(solution)/shard_map/ppermute | solution.py:440
  14.7 4.2 %later_terms.1 = (bf16[480,512]{1,0:T(8,128)(2,1)S(1)}, bf16[480,512]{1,0:T(8,128)(2,1)S(1)}, bf16[480,512]{1,0:T(8,128)(2,1)S(1)}, bf16[240,512]{1,0:T(8,128)(2,1)S(1)}, bf16[240,512]{1,0:T(8,128)(2,1)S(1)}) custom-call(bf16[960,1280]{1,0:T(8,128)(2,1)S(1)} %get-tuple-element.29.x.refs_4_, bf16[2,1280,1024]{2,1,0:T(8,128)(2,1)} %weight.5, ...), custom_call_target="tpu_custom_call" | custom-call | flops 2516582400 | bytes 4423680 | tf_op jit(solution)/shard_map/later_terms/pallas_call | solution.py:321
  18.9 0.9 %collective-permute-done.1.b = bf16[64,1536]{1,0:T(8,128)(2,1)S(1)} collective-permute-done((bf16[64,1536]{1,0:T(8,128)(2,1)S(1)}, bf16[64,1536]{1,0:T(8,128)(2,1)S(1)}, u32[]{:S(2)}, u32[]{:S(2)}) %collective-permute-start.1) | collective-permute-done | bytes 196640 | tf_op jit(solution)/shard_map/ppermute | solution.py:440
  19.8 2.7 %collective-permute-start.4 = (bf16[64,1536]{1,0:T(8,128)(2,1)S(1)}, bf16[64,1536]{1,0:T(8,128)(2,1)S(1)}, u32[]{:S(2)}, u32[]{:S(2)}) collective-permute-start(bf16[64,1536]{1,0:T(8,128)(2,1)S(1)} %get-tuple-element.37.after.rest_0_.a), channel_id=1, source_target_pairs={{0,16},{4,20},{8,24},{12,28},{16,0},{20,4},{24,8},{28,12},{1,17},{... | collective-permute-start | bytes 589832 | tf_op jit(solution)/shard_map/ppermute | solution.py:440
  22.5 0.5 collective-permute-start.2
  23.0 1.1 %collective-permute-start.3 = (bf16[480,512]{1,0:T(8,128)(2,1)S(1)}, bf16[480,512]{1,0:T(8,128)(2,1)S(1)}, u32[]{:S(2)}, u32[]{:S(2)}) collective-permute-start(bf16[480,512]{1,0:T(8,128)(2,1)S(1)} %get-tuple-element.36), channel_id=1, source_target_pairs={{0,2},{1,3},{2,0},{3,1},{4,6},{5,7},{6,4},{7,5},{8,10},{9,11},{10,... | collective-permute-start | bytes 1474568 | tf_op jit(solution)/shard_map/ppermute | solution.py:635
  24.6 3.9 %keep_terms.1 = (bf16[480,512]{1,0:T(8,128)(2,1)}, bf16[240,512]{1,0:T(8,128)(2,1)}, bf16[240,512]{1,0:T(8,128)(2,1)}, bf16[60,4,4096]{2,1,0:T(4,128)(2,1)}) custom-call(bf16[960,1280]{1,0:T(8,128)(2,1)S(1)} %get-tuple-element.29.x.refs_4_, bf16[2,1280,1024]{2,1,0:T(8,128)(2,1)} %weight.5, bf16[64,1536]{1,0:T(8,128)(2,1)S(1)} %get-tuple-element.37.after.rest_0_.a), custom_call_target="tpu_custom_call" | custom-call | flops 1258291200 | bytes 2457600 | tf_op jit(solution)/shard_map/keep_terms/pallas_call | solution.py:305
  28.6 1.1 %copy-done.1 = bf16[480,512]{1,0:T(8,128)(2,1)S(1)} copy-done((bf16[480,512]{1,0:T(8,128)(2,1)S(1)}, bf16[480,512]{1,0:T(8,128)(2,1)}, u32[]{:S(2)}) %copy-start.1) | copy-done | bytes 491544
  29.7 0.9 %copy-done.3 = bf16[240,512]{1,0:T(8,128)(2,1)S(1)} copy-done((bf16[240,512]{1,0:T(8,128)(2,1)S(1)}, bf16[240,512]{1,0:T(8,128)(2,1)}, u32[]{:S(2)}) %copy-start.3) | copy-done | bytes 245784
  31.0 0.9 %collective-permute-start.14 = (bf16[240,512]{1,0:T(8,128)(2,1)S(1)}, bf16[240,512]{1,0:T(8,128)(2,1)S(1)}, u32[]{:S(2)}, u32[]{:S(2)}) collective-permute-start(bf16[240,512]{1,0:T(8,128)(2,1)S(1)} %get-tuple-element.51), channel_id=1, source_target_pairs={{0,1},{1,0},{2,3},{3,2},{4,5},{5,4},{6,7},{7,6},{8,9},{9,8},{10,11... | collective-permute-start | bytes 737288 | tf_op jit(solution)/shard_map/ppermute | solution.py:635
  32.0 1.5 %collective-permute-start.13 = (bf16[240,512]{1,0:T(8,128)(2,1)S(1)}, bf16[240,512]{1,0:T(8,128)(2,1)S(1)}, u32[]{:S(2)}, u32[]{:S(2)}) collective-permute-start(bf16[240,512]{1,0:T(8,128)(2,1)S(1)} %get-tuple-element.42.rest_0_), channel_id=1, source_target_pairs={{0,2},{1,3},{2,0},{3,1},{4,6},{5,7},{6,4},{7,5},{8,10},{9,11},{10,... | collective-permute-start | bytes 737288 | tf_op jit(solution)/shard_map/ppermute | solution.py:635
  33.5 1.5 %update_factors.1 = (f32[2,64,1280]{2,1,0:T(8,128)}, f32[2,64,256]{2,1,0:T(8,128)}, bf16[256,256]{1,0:T(8,128)(2,1)S(1)}, bf16[256,256]{1,0:T(8,128)(2,1)S(1)}, ...) custom-call(s32[3]{0:T(128)S(1)} %pad_add_fusion.ids, bf16[64,1536]{1,0:T(8,128)(2,1)S(1)} %plus.3.refs_0_, ...), custom_call_target="tpu_custom_call" | custom-call | bytes 3637248 | tf_op jit(solution)/shard_map/update_factors/pallas_call | solution.py:388
  35.0 0.6 %collective-permute-start.8 = (bf16[256,256]{1,0:T(8,128)(2,1)S(1)}, bf16[256,256]{1,0:T(8,128)(2,1)S(1)}, u32[]{:S(2)}, u32[]{:S(2)}) collective-permute-start(bf16[256,256]{1,0:T(8,128)(2,1)S(1)} %get-tuple-element.43), channel_id=1, source_target_pairs={{0,1},{1,0},{2,3},{3,2},{4,5},{5,4},{6,7},{7,6},{8,9},{9,8},{10,11... | collective-permute-start | bytes 393224 | tf_op jit(solution)/shard_map/ppermute | solution.py:635
  35.6 1.1 %collective-permute-start.11 = (bf16[256,256]{1,0:T(8,128)(2,1)S(1)}, bf16[256,256]{1,0:T(8,128)(2,1)S(1)}, u32[]{:S(2)}, u32[]{:S(2)}) collective-permute-start(bf16[256,256]{1,0:T(8,128)(2,1)S(1)} %get-tuple-element.48), channel_id=1, source_target_pairs={{0,2},{1,3},{2,0},{3,1},{4,6},{5,7},{6,4},{7,5},{8,10},{9,11},{10,... | collective-permute-start | bytes 393224 | tf_op jit(solution)/shard_map/ppermute | solution.py:635
  36.8 1.8 %collective-permute-start.12 = (bf16[256,256]{1,0:T(8,128)(2,1)S(1)}, bf16[256,256]{1,0:T(8,128)(2,1)S(1)}, u32[]{:S(2)}, u32[]{:S(2)}) collective-permute-start(bf16[256,256]{1,0:T(8,128)(2,1)S(1)} %get-tuple-element.49), channel_id=1, source_target_pairs={{0,3},{1,2},{2,1},{3,0},{4,7},{5,6},{6,5},{7,4},{8,11},{9,10},{10,... | collective-permute-start | bytes 393224 | tf_op jit(solution)/shard_map/ppermute | solution.py:635
  38.6 4.1 %collective-permute-done.8.rest_0_.refs_10_ = bf16[256,256]{1,0:T(8,128)(2,1)S(1)} collective-permute-done((bf16[256,256]{1,0:T(8,128)(2,1)S(1)}, bf16[256,256]{1,0:T(8,128)(2,1)S(1)}, u32[]{:S(2)}, u32[]{:S(2)}) %collective-permute-start.8) | collective-permute-done | bytes 131104 | tf_op jit(solution)/shard_map/ppermute | solution.py:635
  42.8 0.9 %collective-permute-start.9 = (bf16[240,512]{1,0:T(8,128)(2,1)S(1)}, bf16[240,512]{1,0:T(8,128)(2,1)S(1)}, u32[]{:S(2)}, u32[]{:S(2)}) collective-permute-start(bf16[240,512]{1,0:T(8,128)(2,1)S(1)} %get-tuple-element.44), channel_id=1, source_target_pairs={{0,2},{1,3},{2,0},{3,1},{4,6},{5,7},{6,4},{7,5},{8,10},{9,11},{10,... | collective-permute-start | bytes 737288 | tf_op jit(solution)/shard_map/ppermute | solution.py:635
  43.7 1.5 %collective-permute-start.10 = (bf16[240,512]{1,0:T(8,128)(2,1)S(1)}, bf16[240,512]{1,0:T(8,128)(2,1)S(1)}, u32[]{:S(2)}, u32[]{:S(2)}) collective-permute-start(bf16[240,512]{1,0:T(8,128)(2,1)S(1)} %get-tuple-element.46), channel_id=1, source_target_pairs={{0,1},{1,0},{2,3},{3,2},{4,5},{5,4},{6,7},{7,6},{8,9},{9,8},{10,11... | collective-permute-start | bytes 737288 | tf_op jit(solution)/shard_map/ppermute | solution.py:635
  45.7 4.7 %attend_chunk.2.refs_15_ = bf16[60,4,4096]{2,1,0:T(4,128)(2,1)} custom-call(s32[3]{0:T(128)S(1)} %pad_add_fusion.ids, s32[1]{0:T(128)} %constant.43.clone.1.first, s32[60]{0:T(128)S(1)} %copy-done.9, bf16[60,4,4096]{2,1,0:T(4,128)(2,1)S(1)} %copy-done.5, bf16[60,16,1024]{2,1,0:T(8,128)(2,1)S(1)} %copy-done.6, ...), custom_call_target="tpu_custom_call", output_to_operand_aliasing={{}: (18, {})} | custom-call | flops 16000000000 | bytes 10846208 | tf_op jit(solution)/shard_map/attend_chunk/pallas_call | solution.py:611
  50.9 4.6 %attend_chunk.3 = bf16[60,4,4096]{2,1,0:T(4,128)(2,1)} custom-call(s32[3]{0:T(128)S(1)} %pad_add_fusion.ids, s32[1]{0:T(128)} %constant.41.clone.1.first, s32[60]{0:T(128)S(1)} %copy-done.9, bf16[60,4,4096]{2,1,0:T(4,128)(2,1)S(1)} %copy-done.5, bf16[60,16,1024]{2,1,0:T(8,128)(2,1)S(1)} %copy-done.6, ...), custom_call_target="tpu_custom_call", output_to_operand_aliasing={{}: (18, {})} | custom-call | flops 16000000000 | bytes 10846208 | tf_op jit(solution)/shard_map/attend_chunk/pallas_call | solution.py:611
  (48 shorter events, 3.0 us)
Async XLA Ops:
  0.7 10.3 %copy-start.10 = (f32[128]{0:T(128)S(1)}, f32[128]{0:T(128)}, u32[]{:S(2)}) copy-start(f32[128]{0:T(128)} %param.18) | copy-start | bytes 1540
  0.7 10.4 %copy-start.11 = (s32[60]{0:T(128)S(1)}, s32[60]{0:T(128)}, u32[]{:S(2)}) copy-start(s32[60]{0:T(128)} %param.23) | copy-start | bytes 724
  6.4 5.0 %collective-permute-start = (bf16[64,1536]{1,0:T(8,128)(2,1)}, bf16[64,1536]{1,0:T(8,128)(2,1)}, u32[]{:S(2)}, u32[]{:S(2)}) collective-permute-start(bf16[64,1536]{1,0:T(8,128)(2,1)} %get-tuple-element.30), channel_id=1, source_target_pairs={{0,4},{4,0},{8,12},{12,8},{16,20},{20,16},{24,28},{28,24},{1,5},{5... | collective-permute-start | bytes 589832 | tf_op jit(solution)/shard_map/ppermute | solution.py:407
  6.9 21.6 %collective-permute-start.5 = (bf16[480,512]{1,0:T(8,128)(2,1)}, bf16[480,512]{1,0:T(8,128)(2,1)S(1)}, u32[]{:S(2)}, u32[]{:S(2)}) collective-permute-start(bf16[480,512]{1,0:T(8,128)(2,1)} %get-tuple-element.39), channel_id=1, source_target_pairs={{0,1},{1,0},{2,3},{3,2},{4,5},{5,4},{6,7},{7,6},{8,9},{9,8},{10,11... | collective-permute-start | bytes 1474568 | tf_op jit(solution)/shard_map/ppermute | solution.py:635
  9.5 19.1 %collective-permute-start.6 = (bf16[480,512]{1,0:T(8,128)(2,1)}, bf16[480,512]{1,0:T(8,128)(2,1)S(1)}, u32[]{:S(2)}, u32[]{:S(2)}) collective-permute-start(bf16[480,512]{1,0:T(8,128)(2,1)} %get-tuple-element.41), channel_id=1, source_target_pairs={{0,2},{1,3},{2,0},{3,1},{4,6},{5,7},{6,4},{7,5},{8,10},{9,11},{10,... | collective-permute-start | bytes 1474568 | tf_op jit(solution)/shard_map/ppermute | solution.py:635
  13.0 6.8 %collective-permute-start.1 = (bf16[64,1536]{1,0:T(8,128)(2,1)S(1)}, bf16[64,1536]{1,0:T(8,128)(2,1)S(1)}, u32[]{:S(2)}, u32[]{:S(2)}) collective-permute-start(bf16[64,1536]{1,0:T(8,128)(2,1)S(1)} %chip_grads.1.after.a), channel_id=1, source_target_pairs={{0,8},{4,12},{8,0},{12,4},{16,24},{20,28},{24,16},{28,20},{1,9},{5... | collective-permute-start | bytes 589832 | tf_op jit(solution)/shard_map/ppermute | solution.py:440
  19.8 11.0 %collective-permute-start.4 = (bf16[64,1536]{1,0:T(8,128)(2,1)S(1)}, bf16[64,1536]{1,0:T(8,128)(2,1)S(1)}, u32[]{:S(2)}, u32[]{:S(2)}) collective-permute-start(bf16[64,1536]{1,0:T(8,128)(2,1)S(1)} %get-tuple-element.37.after.rest_0_.a), channel_id=1, source_target_pairs={{0,16},{4,20},{8,24},{12,28},{16,0},{20,4},{24,8},{28,12},{1,17},{... | collective-permute-start | bytes 589832 | tf_op jit(solution)/shard_map/ppermute | solution.py:440
  22.5 13.1 %collective-permute-start.2 = (bf16[480,512]{1,0:T(8,128)(2,1)S(1)}, bf16[480,512]{1,0:T(8,128)(2,1)S(1)}, u32[]{:S(2)}, u32[]{:S(2)}) collective-permute-start(bf16[480,512]{1,0:T(8,128)(2,1)S(1)} %get-tuple-element.34), channel_id=1, source_target_pairs={{0,1},{1,0},{2,3},{3,2},{4,5},{5,4},{6,7},{7,6},{8,9},{9,8},{10,11... | collective-permute-start | bytes 1474568 | tf_op jit(solution)/shard_map/ppermute | solution.py:635
  23.0 13.7 %collective-permute-start.3 = (bf16[480,512]{1,0:T(8,128)(2,1)S(1)}, bf16[480,512]{1,0:T(8,128)(2,1)S(1)}, u32[]{:S(2)}, u32[]{:S(2)}) collective-permute-start(bf16[480,512]{1,0:T(8,128)(2,1)S(1)} %get-tuple-element.36), channel_id=1, source_target_pairs={{0,2},{1,3},{2,0},{3,1},{4,6},{5,7},{6,4},{7,5},{8,10},{9,11},{10,... | collective-permute-start | bytes 1474568 | tf_op jit(solution)/shard_map/ppermute | solution.py:635
  24.6 8.9 %copy-start.4 = (f32[2,64,256]{2,1,0:T(8,128)S(1)}, f32[2,64,256]{2,1,0:T(8,128)}, u32[]{:S(2)}) copy-start(f32[2,64,256]{2,1,0:T(8,128)} %refs_3_.1) | copy-start | bytes 393220
  30.6 15.1 %copy-start.8 = (bf16[240,512]{1,0:T(8,128)(2,1)S(1)}, bf16[240,512]{1,0:T(8,128)(2,1)}, u32[]{:S(2)}) copy-start(bf16[240,512]{1,0:T(8,128)(2,1)} %get-tuple-element.50.refs_6_) | copy-start | bytes 737284
  30.8 14.9 %copy-start.7 = (bf16[60,16,1024]{2,1,0:T(8,128)(2,1)S(1)}, bf16[60,16,1024]{2,1,0:T(8,128)(2,1)}, u32[]{:S(2)}) copy-start(bf16[60,16,1024]{2,1,0:T(8,128)(2,1)} %refs_2_.5) | copy-start | bytes 5898244
  30.9 2.6 %collective-permute-start.7 = (bf16[64,1536]{1,0:T(8,128)(2,1)S(1)}, bf16[64,1536]{1,0:T(8,128)(2,1)S(1)}, u32[]{:S(2)}, u32[]{:S(2)}) collective-permute-start(bf16[64,1536]{1,0:T(8,128)(2,1)S(1)} %plus.3.refs_0_), channel_id=1, source_target_pairs={{0,4},{4,0},{8,12},{12,8},{16,20},{20,16},{24,28},{28,24},{1,5},{5... | collective-permute-start | bytes 589832 | tf_op jit(solution)/shard_map/ppermute | solution.py:407
  31.0 14.7 %copy-start.2 = (bf16[480,512]{1,0:T(8,128)(2,1)S(1)}, bf16[480,512]{1,0:T(8,128)(2,1)}, u32[]{:S(2)}) copy-start(bf16[480,512]{1,0:T(8,128)(2,1)} %get-tuple-element.38.kkeep.refs_3_) | copy-start | bytes 1474564
  31.0 14.7 %copy-start.5 = (bf16[60,4,4096]{2,1,0:T(4,128)(2,1)S(1)}, bf16[60,4,4096]{2,1,0:T(4,128)(2,1)}, u32[]{:S(2)}) copy-start(bf16[60,4,4096]{2,1,0:T(4,128)(2,1)} %refs_0_.3) | copy-start | bytes 5898244
  31.0 14.7 %copy-start.6 = (bf16[60,16,1024]{2,1,0:T(8,128)(2,1)S(1)}, bf16[60,16,1024]{2,1,0:T(8,128)(2,1)}, u32[]{:S(2)}) copy-start(bf16[60,16,1024]{2,1,0:T(8,128)(2,1)} %refs_1_.3) | copy-start | bytes 5898244
  31.0 14.7 %copy-start.9 = (s32[60]{0:T(128)S(1)}, s32[60]{0:T(128)}, u32[]{:S(2)}) copy-start(s32[60]{0:T(128)} %lengths.3) | copy-start | bytes 724
  31.0 12.7 %collective-permute-start.14 = (bf16[240,512]{1,0:T(8,128)(2,1)S(1)}, bf16[240,512]{1,0:T(8,128)(2,1)S(1)}, u32[]{:S(2)}, u32[]{:S(2)}) collective-permute-start(bf16[240,512]{1,0:T(8,128)(2,1)S(1)} %get-tuple-element.51), channel_id=1, source_target_pairs={{0,1},{1,0},{2,3},{3,2},{4,5},{5,4},{6,7},{7,6},{8,9},{9,8},{10,11... | collective-permute-start | bytes 737288 | tf_op jit(solution)/shard_map/ppermute | solution.py:635
  32.0 13.3 %collective-permute-start.13 = (bf16[240,512]{1,0:T(8,128)(2,1)S(1)}, bf16[240,512]{1,0:T(8,128)(2,1)S(1)}, u32[]{:S(2)}, u32[]{:S(2)}) collective-permute-start(bf16[240,512]{1,0:T(8,128)(2,1)S(1)} %get-tuple-element.42.rest_0_), channel_id=1, source_target_pairs={{0,2},{1,3},{2,0},{3,1},{4,6},{5,7},{6,4},{7,5},{8,10},{9,11},{10,... | collective-permute-start | bytes 737288 | tf_op jit(solution)/shard_map/ppermute | solution.py:635
  35.0 7.7 %collective-permute-start.8 = (bf16[256,256]{1,0:T(8,128)(2,1)S(1)}, bf16[256,256]{1,0:T(8,128)(2,1)S(1)}, u32[]{:S(2)}, u32[]{:S(2)}) collective-permute-start(bf16[256,256]{1,0:T(8,128)(2,1)S(1)} %get-tuple-element.43), channel_id=1, source_target_pairs={{0,1},{1,0},{2,3},{3,2},{4,5},{5,4},{6,7},{7,6},{8,9},{9,8},{10,11... | collective-permute-start | bytes 393224 | tf_op jit(solution)/shard_map/ppermute | solution.py:635
  35.6 10.1 %collective-permute-start.11 = (bf16[256,256]{1,0:T(8,128)(2,1)S(1)}, bf16[256,256]{1,0:T(8,128)(2,1)S(1)}, u32[]{:S(2)}, u32[]{:S(2)}) collective-permute-start(bf16[256,256]{1,0:T(8,128)(2,1)S(1)} %get-tuple-element.48), channel_id=1, source_target_pairs={{0,2},{1,3},{2,0},{3,1},{4,6},{5,7},{6,4},{7,5},{8,10},{9,11},{10,... | collective-permute-start | bytes 393224 | tf_op jit(solution)/shard_map/ppermute | solution.py:635
  36.8 8.9 %collective-permute-start.12 = (bf16[256,256]{1,0:T(8,128)(2,1)S(1)}, bf16[256,256]{1,0:T(8,128)(2,1)S(1)}, u32[]{:S(2)}, u32[]{:S(2)}) collective-permute-start(bf16[256,256]{1,0:T(8,128)(2,1)S(1)} %get-tuple-element.49), channel_id=1, source_target_pairs={{0,3},{1,2},{2,1},{3,0},{4,7},{5,6},{6,5},{7,4},{8,11},{9,10},{10,... | collective-permute-start | bytes 393224 | tf_op jit(solution)/shard_map/ppermute | solution.py:635
  42.8 8.0 %collective-permute-start.9 = (bf16[240,512]{1,0:T(8,128)(2,1)S(1)}, bf16[240,512]{1,0:T(8,128)(2,1)S(1)}, u32[]{:S(2)}, u32[]{:S(2)}) collective-permute-start(bf16[240,512]{1,0:T(8,128)(2,1)S(1)} %get-tuple-element.44), channel_id=1, source_target_pairs={{0,2},{1,3},{2,0},{3,1},{4,6},{5,7},{6,4},{7,5},{8,10},{9,11},{10,... | collective-permute-start | bytes 737288 | tf_op jit(solution)/shard_map/ppermute | solution.py:635
  43.7 7.1 %collective-permute-start.10 = (bf16[240,512]{1,0:T(8,128)(2,1)S(1)}, bf16[240,512]{1,0:T(8,128)(2,1)S(1)}, u32[]{:S(2)}, u32[]{:S(2)}) collective-permute-start(bf16[240,512]{1,0:T(8,128)(2,1)S(1)} %get-tuple-element.46), channel_id=1, source_target_pairs={{0,1},{1,0},{2,3},{3,2},{4,5},{5,4},{6,7},{7,6},{8,9},{9,8},{10,11... | collective-permute-start | bytes 737288 | tf_op jit(solution)/shard_map/ppermute | solution.py:635
  (3 other events, 7.0 us)

commit v12 on v11

--- a/solution.py
+++ b/solution.py
@@ -299,7 +299,7 @@
 def keep_terms(x, kv_weight, queries, after):
     tokens, width = x.shape[0] // 4, x.shape[1]
     here = pl.BlockSpec(memory_space=pl.ANY)
-    outs = [pltpu.HBM(out.shape, BF) for out in term_shapes(KEEP, tokens, CHUNKS[0])]
+    outs = term_shapes(KEEP, tokens, CHUNKS[0])
     specs = [whole(out.shape) for out in outs] + [here]
     outs.append(jax.ShapeDtypeStruct(queries.shape, BF))
     return pl.pallas_call(

time: 55.8 us -> 55.6 us (level)
  waiting for transfers between devices: 6.11 us -> 9.98 us
  local copies, waits for them, and re-layouts: 2.19 us -> 0.15 us
  Pallas kernels: 26.6 us -> 25.6 us
  starting transfers between devices: 19 us -> 18 us
    ppermute x2, waiting for transfers between devices: 1 us -> 4.01 us  [along_line(): return lax.ppermute(x, 'dp', [(i, i ^ 2 * d) for i in range(count)])]
    unnamed x24 -> x16, local copies, waits for them, and re-layouts: 2.08 us -> 0.04 us
    pallas_call x1, Pallas kernels: 3.93 us -> 2.95 us  [keep_terms(): pl.pallas_call(keep_kernel, out_shape=outs, grid=(1,), in_specs=[whole(x....]
    ppermute x11, starting transfers between devices: 14.1 us -> 13.1 us  [across(): return lax.ppermute(x, 'tensor', [(i, i ^ r) for i in range(4)])]
    ppermute x11, waiting for transfers between devices: 5.1 us -> 5.97 us  [across(): return lax.ppermute(x, 'tensor', [(i, i ^ r) for i in range(4)])]
  transfers between devices with their start and end apart: 15 -> 15, of which waited for: 5 -> 5; matrix products, arithmetic and copies ran while one was open for 2% -> 2% of each run, Pallas kernels for 29% -> 28%
where the time goes in v12:
time: 55.6 us; the launch traced here: 55.4 us
  Pallas kernels  25.6 us (46%)
  starting transfers between devices  18 us (32%)
  waiting for transfers between devices  9.98 us (18%)
  other arithmetic  0.82 us (1%)
  between operations  0.82 us (1%)
    ppermute x11, starting transfers between devices, across(): return lax.ppermute(x, 'tensor', [(i, i ^ r) for i in range(4)])  13.1 us
    pallas_call x2, Pallas kernels, attend_chunk(): pl.pallas_call(attend_kernel, out_shape=jax.ShapeDtypeStruct(queries.shap...  9.31 us
    ppermute x11, waiting for transfers between devices, across(): return lax.ppermute(x, 'tensor', [(i, i ^ r) for i in range(4)])  5.97 us
    pallas_call x1, Pallas kernels, first_terms(): pl.pallas_call(first_kernel, out_shape=outs, grid_spec=pltpu.PrefetchScal...  5.68 us
    ppermute x2, starting transfers between devices, along_line(): return lax.ppermute(x, 'dp', [(i, i ^ 2 * d) for i in range(count)])  4.3 us
    pallas_call x1, Pallas kernels, later_terms(): pl.pallas_call(later_kernel, out_shape=outs, grid=(1,), in_specs=[whole(x...  4.2 us
    ppermute x2, waiting for transfers between devices, along_line(): return lax.ppermute(x, 'dp', [(i, i ^ 2 * d) for i in range(count)])  4.01 us
    pallas_call x1, Pallas kernels, keep_terms(): pl.pallas_call(keep_kernel, out_shape=outs, grid=(1,), in_specs=[whole(x....  2.95 us
  transfers between devices with their start and end apart: 15, of which 5 were waited for; matrix products, arithmetic and copies ran while one was open for 2% of the time, Pallas kernels for 28%

profile of v12, /device:TPU:0, one launch (start us, length us, event | category | flops | bytes accessed | tf_op | source)
XLA Modules:
  0.0 55.4 jit_solution(876984974852498915)
XLA Ops:
  0.7 5.7 %first_terms.1 = (bf16[960,1280]{1,0:T(8,128)(2,1)S(1)}, bf16[480,512]{1,0:T(8,128)(2,1)}, bf16[480,512]{1,0:T(8,128)(2,1)}, bf16[64,1536]{1,0:T(8,128)(2,1)}) custom-call(s32[3]{0:T(128)S(1)} %pad_add_fusion.ids, bf16[240,4,1280]{2,1,0:T(4,128)(2,1)} %hidden.1, bf16[2,1280,1024]{2,1,0:T(8,128)(2,1)} %weight.5, f32[1,2,64,1280]{3,2,1,0:T(8,128)} %grad_a.3, ...), custom_call_target="tpu_custom_call" | custom-call | flops 1258291200 | bytes 2457600 | tf_op jit(solution)/shard_map/first_terms/pallas_call | solution.py:275
  6.9 2.6 %collective-permute-start.5 = (bf16[480,512]{1,0:T(8,128)(2,1)}, bf16[480,512]{1,0:T(8,128)(2,1)S(1)}, u32[]{:S(2)}, u32[]{:S(2)}) collective-permute-start(bf16[480,512]{1,0:T(8,128)(2,1)} %get-tuple-element.39), channel_id=1, source_target_pairs={{0,1},{1,0},{2,3},{3,2},{4,5},{5,4},{6,7},{7,6},{8,9},{9,8},{10,11... | collective-permute-start | bytes 1474568 | tf_op jit(solution)/shard_map/ppermute | solution.py:635
  9.5 1.5 %collective-permute-start.6 = (bf16[480,512]{1,0:T(8,128)(2,1)}, bf16[480,512]{1,0:T(8,128)(2,1)S(1)}, u32[]{:S(2)}, u32[]{:S(2)}) collective-permute-start(bf16[480,512]{1,0:T(8,128)(2,1)} %get-tuple-element.41), channel_id=1, source_target_pairs={{0,2},{1,3},{2,0},{3,1},{4,6},{5,7},{6,4},{7,5},{8,10},{9,11},{10,... | collective-permute-start | bytes 1474568 | tf_op jit(solution)/shard_map/ppermute | solution.py:635
  11.4 1.6 %chip_grads.1.after.a = bf16[64,1536]{1,0:T(8,128)(2,1)S(1)} custom-call(s32[3]{0:T(128)S(1)} %pad_add_fusion.ids, f32[1,2,64,1280]{3,2,1,0:T(8,128)} %grad_a.3, f32[1,2,64,256]{3,2,1,0:T(8,128)} %grad_b.3, bf16[64,1536]{1,0:T(8,128)(2,1)} %collective-permute-done.other), custom_call_target="tpu_custom_call" | custom-call | bytes 786432 | tf_op jit(solution)/shard_map/chip_grads/pallas_call | solution.py:367
  13.0 1.6 %collective-permute-start.1 = (bf16[64,1536]{1,0:T(8,128)(2,1)S(1)}, bf16[64,1536]{1,0:T(8,128)(2,1)S(1)}, u32[]{:S(2)}, u32[]{:S(2)}) collective-permute-start(bf16[64,1536]{1,0:T(8,128)(2,1)S(1)} %chip_grads.1.after.a), channel_id=1, source_target_pairs={{0,8},{4,12},{8,0},{12,4},{16,24},{20,28},{24,16},{28,20},{1,9},{5... | collective-permute-start | bytes 589832 | tf_op jit(solution)/shard_map/ppermute | solution.py:440
  14.7 4.2 %later_terms.1 = (bf16[480,512]{1,0:T(8,128)(2,1)S(1)}, bf16[480,512]{1,0:T(8,128)(2,1)S(1)}, bf16[480,512]{1,0:T(8,128)(2,1)S(1)}, bf16[240,512]{1,0:T(8,128)(2,1)S(1)}, bf16[240,512]{1,0:T(8,128)(2,1)S(1)}) custom-call(bf16[960,1280]{1,0:T(8,128)(2,1)S(1)} %get-tuple-element.29.x.refs_4_, bf16[2,1280,1024]{2,1,0:T(8,128)(2,1)} %weight.5, ...), custom_call_target="tpu_custom_call" | custom-call | flops 2516582400 | bytes 4423680 | tf_op jit(solution)/shard_map/later_terms/pallas_call | solution.py:321
  18.9 0.9 %collective-permute-done.1.b = bf16[64,1536]{1,0:T(8,128)(2,1)S(1)} collective-permute-done((bf16[64,1536]{1,0:T(8,128)(2,1)S(1)}, bf16[64,1536]{1,0:T(8,128)(2,1)S(1)}, u32[]{:S(2)}, u32[]{:S(2)}) %collective-permute-start.1) | collective-permute-done | bytes 196640 | tf_op jit(solution)/shard_map/ppermute | solution.py:440
  19.8 2.7 %collective-permute-start.4 = (bf16[64,1536]{1,0:T(8,128)(2,1)S(1)}, bf16[64,1536]{1,0:T(8,128)(2,1)S(1)}, u32[]{:S(2)}, u32[]{:S(2)}) collective-permute-start(bf16[64,1536]{1,0:T(8,128)(2,1)S(1)} %get-tuple-element.37.after.rest_0_.a), channel_id=1, source_target_pairs={{0,16},{4,20},{8,24},{12,28},{16,0},{20,4},{24,8},{28,12},{1,17},{... | collective-permute-start | bytes 589832 | tf_op jit(solution)/shard_map/ppermute | solution.py:440
  22.5 0.5 collective-permute-start.2
  23.0 1.1 %collective-permute-start.3 = (bf16[480,512]{1,0:T(8,128)(2,1)S(1)}, bf16[480,512]{1,0:T(8,128)(2,1)S(1)}, u32[]{:S(2)}, u32[]{:S(2)}) collective-permute-start(bf16[480,512]{1,0:T(8,128)(2,1)S(1)} %get-tuple-element.36), channel_id=1, source_target_pairs={{0,2},{1,3},{2,0},{3,1},{4,6},{5,7},{6,4},{7,5},{8,10},{9,11},{10,... | collective-permute-start | bytes 1474568 | tf_op jit(solution)/shard_map/ppermute | solution.py:635
  24.6 3.0 %keep_terms.1 = (bf16[480,512]{1,0:T(8,128)(2,1)S(1)}, bf16[240,512]{1,0:T(8,128)(2,1)S(1)}, bf16[240,512]{1,0:T(8,128)(2,1)S(1)}, bf16[60,4,4096]{2,1,0:T(4,128)(2,1)}) custom-call(bf16[960,1280]{1,0:T(8,128)(2,1)S(1)} %get-tuple-element.29.x.refs_4_, bf16[2,1280,1024]{2,1,0:T(8,128)(2,1)} %weight.5, bf16[64,1536]{1,0:T(8,128)(2,1)S(1)} %get-tuple-element.37.after.rest_0_.a), custom_call_target="tpu_custom_call" | custom-call | flops 1258291200 | bytes 2457600 | tf_op jit(solution)/shard_map/keep_terms/pallas_call | solution.py:305
  27.7 3.1 %collective-permute-done.4.b = bf16[64,1536]{1,0:T(8,128)(2,1)S(1)} collective-permute-done((bf16[64,1536]{1,0:T(8,128)(2,1)S(1)}, bf16[64,1536]{1,0:T(8,128)(2,1)S(1)}, u32[]{:S(2)}, u32[]{:S(2)}) %collective-permute-start.4) | collective-permute-done | bytes 196640 | tf_op jit(solution)/shard_map/ppermute | solution.py:440
  31.0 0.6 %collective-permute-start.14 = (bf16[240,512]{1,0:T(8,128)(2,1)S(1)}, bf16[240,512]{1,0:T(8,128)(2,1)S(1)}, u32[]{:S(2)}, u32[]{:S(2)}) collective-permute-start(bf16[240,512]{1,0:T(8,128)(2,1)S(1)} %get-tuple-element.51), channel_id=1, source_target_pairs={{0,1},{1,0},{2,3},{3,2},{4,5},{5,4},{6,7},{7,6},{8,9},{9,8},{10,11... | collective-permute-start | bytes 737288 | tf_op jit(solution)/shard_map/ppermute | solution.py:635
  31.6 1.3 %collective-permute-start.13 = (bf16[240,512]{1,0:T(8,128)(2,1)S(1)}, bf16[240,512]{1,0:T(8,128)(2,1)S(1)}, u32[]{:S(2)}, u32[]{:S(2)}) collective-permute-start(bf16[240,512]{1,0:T(8,128)(2,1)S(1)} %get-tuple-element.42.rest_0_), channel_id=1, source_target_pairs={{0,2},{1,3},{2,0},{3,1},{4,6},{5,7},{6,4},{7,5},{8,10},{9,11},{10,... | collective-permute-start | bytes 737288 | tf_op jit(solution)/shard_map/ppermute | solution.py:635
  33.0 1.5 %update_factors.1 = (f32[2,64,1280]{2,1,0:T(8,128)}, f32[2,64,256]{2,1,0:T(8,128)}, bf16[256,256]{1,0:T(8,128)(2,1)S(1)}, bf16[256,256]{1,0:T(8,128)(2,1)S(1)}, ...) custom-call(s32[3]{0:T(128)S(1)} %pad_add_fusion.ids, bf16[64,1536]{1,0:T(8,128)(2,1)S(1)} %plus.3.refs_0_, ...), custom_call_target="tpu_custom_call" | custom-call | bytes 3637248 | tf_op jit(solution)/shard_map/update_factors/pallas_call | solution.py:388
  34.5 0.7 %collective-permute-start.8 = (bf16[256,256]{1,0:T(8,128)(2,1)S(1)}, bf16[256,256]{1,0:T(8,128)(2,1)S(1)}, u32[]{:S(2)}, u32[]{:S(2)}) collective-permute-start(bf16[256,256]{1,0:T(8,128)(2,1)S(1)} %get-tuple-element.43), channel_id=1, source_target_pairs={{0,1},{1,0},{2,3},{3,2},{4,5},{5,4},{6,7},{7,6},{8,9},{9,8},{10,11... | collective-permute-start | bytes 393224 | tf_op jit(solution)/shard_map/ppermute | solution.py:635
  35.2 1.5 %collective-permute-start.11 = (bf16[256,256]{1,0:T(8,128)(2,1)S(1)}, bf16[256,256]{1,0:T(8,128)(2,1)S(1)}, u32[]{:S(2)}, u32[]{:S(2)}) collective-permute-start(bf16[256,256]{1,0:T(8,128)(2,1)S(1)} %get-tuple-element.48), channel_id=1, source_target_pairs={{0,2},{1,3},{2,0},{3,1},{4,6},{5,7},{6,4},{7,5},{8,10},{9,11},{10,... | collective-permute-start | bytes 393224 | tf_op jit(solution)/shard_map/ppermute | solution.py:635
  36.7 1.3 %collective-permute-start.12 = (bf16[256,256]{1,0:T(8,128)(2,1)S(1)}, bf16[256,256]{1,0:T(8,128)(2,1)S(1)}, u32[]{:S(2)}, u32[]{:S(2)}) collective-permute-start(bf16[256,256]{1,0:T(8,128)(2,1)S(1)} %get-tuple-element.49), channel_id=1, source_target_pairs={{0,3},{1,2},{2,1},{3,0},{4,7},{5,6},{6,5},{7,4},{8,11},{9,10},{10,... | collective-permute-start | bytes 393224 | tf_op jit(solution)/shard_map/ppermute | solution.py:635
  38.1 4.7 %collective-permute-done.8.rest_0_.refs_10_ = bf16[256,256]{1,0:T(8,128)(2,1)S(1)} collective-permute-done((bf16[256,256]{1,0:T(8,128)(2,1)S(1)}, bf16[256,256]{1,0:T(8,128)(2,1)S(1)}, u32[]{:S(2)}, u32[]{:S(2)}) %collective-permute-start.8) | collective-permute-done | bytes 131104 | tf_op jit(solution)/shard_map/ppermute | solution.py:635
  42.8 0.6 %collective-permute-start.9 = (bf16[240,512]{1,0:T(8,128)(2,1)S(1)}, bf16[240,512]{1,0:T(8,128)(2,1)S(1)}, u32[]{:S(2)}, u32[]{:S(2)}) collective-permute-start(bf16[240,512]{1,0:T(8,128)(2,1)S(1)} %get-tuple-element.44), channel_id=1, source_target_pairs={{0,2},{1,3},{2,0},{3,1},{4,6},{5,7},{6,4},{7,5},{8,10},{9,11},{10,... | collective-permute-start | bytes 737288 | tf_op jit(solution)/shard_map/ppermute | solution.py:635
  43.4 1.4 %collective-permute-start.10 = (bf16[240,512]{1,0:T(8,128)(2,1)S(1)}, bf16[240,512]{1,0:T(8,128)(2,1)S(1)}, u32[]{:S(2)}, u32[]{:S(2)}) collective-permute-start(bf16[240,512]{1,0:T(8,128)(2,1)S(1)} %get-tuple-element.46), channel_id=1, source_target_pairs={{0,1},{1,0},{2,3},{3,2},{4,5},{5,4},{6,7},{7,6},{8,9},{9,8},{10,11... | collective-permute-start | bytes 737288 | tf_op jit(solution)/shard_map/ppermute | solution.py:635
  44.8 0.9 %collective-permute-done.11.refs_11_ = bf16[256,256]{1,0:T(8,128)(2,1)S(1)} collective-permute-done((bf16[256,256]{1,0:T(8,128)(2,1)S(1)}, bf16[256,256]{1,0:T(8,128)(2,1)S(1)}, u32[]{:S(2)}, u32[]{:S(2)}) %collective-permute-start.11) | collective-permute-done | bytes 131104 | tf_op jit(solution)/shard_map/ppermute | solution.py:635
  45.7 4.7 %attend_chunk.2.refs_15_ = bf16[60,4,4096]{2,1,0:T(4,128)(2,1)} custom-call(s32[3]{0:T(128)S(1)} %pad_add_fusion.ids, s32[1]{0:T(128)} %constant.43.clone.1.first, s32[60]{0:T(128)S(1)} %copy-done.5, bf16[60,4,4096]{2,1,0:T(4,128)(2,1)S(1)} %copy-done.2, bf16[60,16,1024]{2,1,0:T(8,128)(2,1)S(1)} %copy-done.3, ...), custom_call_target="tpu_custom_call", output_to_operand_aliasing={{}: (18, {})} | custom-call | flops 16000000000 | bytes 10846208 | tf_op jit(solution)/shard_map/attend_chunk/pallas_call | solution.py:611
  50.8 4.6 %attend_chunk.3 = bf16[60,4,4096]{2,1,0:T(4,128)(2,1)} custom-call(s32[3]{0:T(128)S(1)} %pad_add_fusion.ids, s32[1]{0:T(128)} %constant.41.clone.1.first, s32[60]{0:T(128)S(1)} %copy-done.5, bf16[60,4,4096]{2,1,0:T(4,128)(2,1)S(1)} %copy-done.2, bf16[60,16,1024]{2,1,0:T(8,128)(2,1)S(1)} %copy-done.3, ...), custom_call_target="tpu_custom_call", output_to_operand_aliasing={{}: (18, {})} | custom-call | flops 16000000000 | bytes 10846208 | tf_op jit(solution)/shard_map/attend_chunk/pallas_call | solution.py:611
  (40 shorter events, 2.3 us)
Async XLA Ops:
  0.7 10.3 %copy-start.6 = (f32[128]{0:T(128)S(1)}, f32[128]{0:T(128)}, u32[]{:S(2)}) copy-start(f32[128]{0:T(128)} %param.18) | copy-start | bytes 1540
  0.7 10.4 %copy-start.7 = (s32[60]{0:T(128)S(1)}, s32[60]{0:T(128)}, u32[]{:S(2)}) copy-start(s32[60]{0:T(128)} %param.23) | copy-start | bytes 724
  6.4 5.0 %collective-permute-start = (bf16[64,1536]{1,0:T(8,128)(2,1)}, bf16[64,1536]{1,0:T(8,128)(2,1)}, u32[]{:S(2)}, u32[]{:S(2)}) collective-permute-start(bf16[64,1536]{1,0:T(8,128)(2,1)} %get-tuple-element.30), channel_id=1, source_target_pairs={{0,4},{4,0},{8,12},{12,8},{16,20},{20,16},{24,28},{28,24},{1,5},{5... | collective-permute-start | bytes 589832 | tf_op jit(solution)/shard_map/ppermute | solution.py:407
  6.9 20.7 %collective-permute-start.5 = (bf16[480,512]{1,0:T(8,128)(2,1)}, bf16[480,512]{1,0:T(8,128)(2,1)S(1)}, u32[]{:S(2)}, u32[]{:S(2)}) collective-permute-start(bf16[480,512]{1,0:T(8,128)(2,1)} %get-tuple-element.39), channel_id=1, source_target_pairs={{0,1},{1,0},{2,3},{3,2},{4,5},{5,4},{6,7},{7,6},{8,9},{9,8},{10,11... | collective-permute-start | bytes 1474568 | tf_op jit(solution)/shard_map/ppermute | solution.py:635
  9.5 18.1 %collective-permute-start.6 = (bf16[480,512]{1,0:T(8,128)(2,1)}, bf16[480,512]{1,0:T(8,128)(2,1)S(1)}, u32[]{:S(2)}, u32[]{:S(2)}) collective-permute-start(bf16[480,512]{1,0:T(8,128)(2,1)} %get-tuple-element.41), channel_id=1, source_target_pairs={{0,2},{1,3},{2,0},{3,1},{4,6},{5,7},{6,4},{7,5},{8,10},{9,11},{10,... | collective-permute-start | bytes 1474568 | tf_op jit(solution)/shard_map/ppermute | solution.py:635
  13.0 6.8 %collective-permute-start.1 = (bf16[64,1536]{1,0:T(8,128)(2,1)S(1)}, bf16[64,1536]{1,0:T(8,128)(2,1)S(1)}, u32[]{:S(2)}, u32[]{:S(2)}) collective-permute-start(bf16[64,1536]{1,0:T(8,128)(2,1)S(1)} %chip_grads.1.after.a), channel_id=1, source_target_pairs={{0,8},{4,12},{8,0},{12,4},{16,24},{20,28},{24,16},{28,20},{1,9},{5... | collective-permute-start | bytes 589832 | tf_op jit(solution)/shard_map/ppermute | solution.py:440
  19.8 11.0 %collective-permute-start.4 = (bf16[64,1536]{1,0:T(8,128)(2,1)S(1)}, bf16[64,1536]{1,0:T(8,128)(2,1)S(1)}, u32[]{:S(2)}, u32[]{:S(2)}) collective-permute-start(bf16[64,1536]{1,0:T(8,128)(2,1)S(1)} %get-tuple-element.37.after.rest_0_.a), channel_id=1, source_target_pairs={{0,16},{4,20},{8,24},{12,28},{16,0},{20,4},{24,8},{28,12},{1,17},{... | collective-permute-start | bytes 589832 | tf_op jit(solution)/shard_map/ppermute | solution.py:440
  22.5 12.7 %collective-permute-start.2 = (bf16[480,512]{1,0:T(8,128)(2,1)S(1)}, bf16[480,512]{1,0:T(8,128)(2,1)S(1)}, u32[]{:S(2)}, u32[]{:S(2)}) collective-permute-start(bf16[480,512]{1,0:T(8,128)(2,1)S(1)} %get-tuple-element.34), channel_id=1, source_target_pairs={{0,1},{1,0},{2,3},{3,2},{4,5},{5,4},{6,7},{7,6},{8,9},{9,8},{10,11... | collective-permute-start | bytes 1474568 | tf_op jit(solution)/shard_map/ppermute | solution.py:635
  23.0 13.7 %collective-permute-start.3 = (bf16[480,512]{1,0:T(8,128)(2,1)S(1)}, bf16[480,512]{1,0:T(8,128)(2,1)S(1)}, u32[]{:S(2)}, u32[]{:S(2)}) collective-permute-start(bf16[480,512]{1,0:T(8,128)(2,1)S(1)} %get-tuple-element.36), channel_id=1, source_target_pairs={{0,2},{1,3},{2,0},{3,1},{4,6},{5,7},{6,4},{7,5},{8,10},{9,11},{10,... | collective-permute-start | bytes 1474568 | tf_op jit(solution)/shard_map/ppermute | solution.py:635
  27.6 5.4 %copy-start = (f32[2,64,1280]{2,1,0:T(8,128)S(1)}, f32[2,64,1280]{2,1,0:T(8,128)}, u32[]{:S(2)}) copy-start(f32[2,64,1280]{2,1,0:T(8,128)} %refs_2_.3) | copy-start | bytes 1966084
  27.6 5.4 %copy-start.1 = (f32[2,64,256]{2,1,0:T(8,128)S(1)}, f32[2,64,256]{2,1,0:T(8,128)}, u32[]{:S(2)}) copy-start(f32[2,64,256]{2,1,0:T(8,128)} %refs_3_.1) | copy-start | bytes 393220
  30.8 14.8 %copy-start.4 = (bf16[60,16,1024]{2,1,0:T(8,128)(2,1)S(1)}, bf16[60,16,1024]{2,1,0:T(8,128)(2,1)}, u32[]{:S(2)}) copy-start(bf16[60,16,1024]{2,1,0:T(8,128)(2,1)} %refs_2_.5) | copy-start | bytes 5898244
  30.9 2.1 %collective-permute-start.7 = (bf16[64,1536]{1,0:T(8,128)(2,1)S(1)}, bf16[64,1536]{1,0:T(8,128)(2,1)S(1)}, u32[]{:S(2)}, u32[]{:S(2)}) collective-permute-start(bf16[64,1536]{1,0:T(8,128)(2,1)S(1)} %plus.3.refs_0_), channel_id=1, source_target_pairs={{0,4},{4,0},{8,12},{12,8},{16,20},{20,16},{24,28},{28,24},{1,5},{5... | collective-permute-start | bytes 589832 | tf_op jit(solution)/shard_map/ppermute | solution.py:407
  31.0 14.7 %copy-start.2 = (bf16[60,4,4096]{2,1,0:T(4,128)(2,1)S(1)}, bf16[60,4,4096]{2,1,0:T(4,128)(2,1)}, u32[]{:S(2)}) copy-start(bf16[60,4,4096]{2,1,0:T(4,128)(2,1)} %refs_0_.3) | copy-start | bytes 5898244
  31.0 14.7 %copy-start.3 = (bf16[60,16,1024]{2,1,0:T(8,128)(2,1)S(1)}, bf16[60,16,1024]{2,1,0:T(8,128)(2,1)}, u32[]{:S(2)}) copy-start(bf16[60,16,1024]{2,1,0:T(8,128)(2,1)} %refs_1_.3) | copy-start | bytes 5898244
  31.0 14.7 %copy-start.5 = (s32[60]{0:T(128)S(1)}, s32[60]{0:T(128)}, u32[]{:S(2)}) copy-start(s32[60]{0:T(128)} %lengths.3) | copy-start | bytes 724
  31.0 12.4 %collective-permute-start.14 = (bf16[240,512]{1,0:T(8,128)(2,1)S(1)}, bf16[240,512]{1,0:T(8,128)(2,1)S(1)}, u32[]{:S(2)}, u32[]{:S(2)}) collective-permute-start(bf16[240,512]{1,0:T(8,128)(2,1)S(1)} %get-tuple-element.51), channel_id=1, source_target_pairs={{0,1},{1,0},{2,3},{3,2},{4,5},{5,4},{6,7},{7,6},{8,9},{9,8},{10,11... | collective-permute-start | bytes 737288 | tf_op jit(solution)/shard_map/ppermute | solution.py:635
  31.6 13.2 %collective-permute-start.13 = (bf16[240,512]{1,0:T(8,128)(2,1)S(1)}, bf16[240,512]{1,0:T(8,128)(2,1)S(1)}, u32[]{:S(2)}, u32[]{:S(2)}) collective-permute-start(bf16[240,512]{1,0:T(8,128)(2,1)S(1)} %get-tuple-element.42.rest_0_), channel_id=1, source_target_pairs={{0,2},{1,3},{2,0},{3,1},{4,6},{5,7},{6,4},{7,5},{8,10},{9,11},{10,... | collective-permute-start | bytes 737288 | tf_op jit(solution)/shard_map/ppermute | solution.py:635
  34.5 8.2 %collective-permute-start.8 = (bf16[256,256]{1,0:T(8,128)(2,1)S(1)}, bf16[256,256]{1,0:T(8,128)(2,1)S(1)}, u32[]{:S(2)}, u32[]{:S(2)}) collective-permute-start(bf16[256,256]{1,0:T(8,128)(2,1)S(1)} %get-tuple-element.43), channel_id=1, source_target_pairs={{0,1},{1,0},{2,3},{3,2},{4,5},{5,4},{6,7},{7,6},{8,9},{9,8},{10,11... | collective-permute-start | bytes 393224 | tf_op jit(solution)/shard_map/ppermute | solution.py:635
  35.2 10.4 %collective-permute-start.11 = (bf16[256,256]{1,0:T(8,128)(2,1)S(1)}, bf16[256,256]{1,0:T(8,128)(2,1)S(1)}, u32[]{:S(2)}, u32[]{:S(2)}) collective-permute-start(bf16[256,256]{1,0:T(8,128)(2,1)S(1)} %get-tuple-element.48), channel_id=1, source_target_pairs={{0,2},{1,3},{2,0},{3,1},{4,6},{5,7},{6,4},{7,5},{8,10},{9,11},{10,... | collective-permute-start | bytes 393224 | tf_op jit(solution)/shard_map/ppermute | solution.py:635
  36.7 8.9 %collective-permute-start.12 = (bf16[256,256]{1,0:T(8,128)(2,1)S(1)}, bf16[256,256]{1,0:T(8,128)(2,1)S(1)}, u32[]{:S(2)}, u32[]{:S(2)}) collective-permute-start(bf16[256,256]{1,0:T(8,128)(2,1)S(1)} %get-tuple-element.49), channel_id=1, source_target_pairs={{0,3},{1,2},{2,1},{3,0},{4,7},{5,6},{6,5},{7,4},{8,11},{9,10},{10,... | collective-permute-start | bytes 393224 | tf_op jit(solution)/shard_map/ppermute | solution.py:635
  42.8 7.9 %collective-permute-start.9 = (bf16[240,512]{1,0:T(8,128)(2,1)S(1)}, bf16[240,512]{1,0:T(8,128)(2,1)S(1)}, u32[]{:S(2)}, u32[]{:S(2)}) collective-permute-start(bf16[240,512]{1,0:T(8,128)(2,1)S(1)} %get-tuple-element.44), channel_id=1, source_target_pairs={{0,2},{1,3},{2,0},{3,1},{4,6},{5,7},{6,4},{7,5},{8,10},{9,11},{10,... | collective-permute-start | bytes 737288 | tf_op jit(solution)/shard_map/ppermute | solution.py:635
  43.4 7.4 %collective-permute-start.10 = (bf16[240,512]{1,0:T(8,128)(2,1)S(1)}, bf16[240,512]{1,0:T(8,128)(2,1)S(1)}, u32[]{:S(2)}, u32[]{:S(2)}) collective-permute-start(bf16[240,512]{1,0:T(8,128)(2,1)S(1)} %get-tuple-element.46), channel_id=1, source_target_pairs={{0,1},{1,0},{2,3},{3,2},{4,5},{5,4},{6,7},{7,6},{8,9},{9,8},{10,11... | collective-permute-start | bytes 737288 | tf_op jit(solution)/shard_map/ppermute | solution.py:635
